TPU v7x, 32 devices: a whole 2x2x4 slice. The times are simulated.
32 devices in a mesh: dp: 8 (over z, core), seq: 4 (over y, x).
Axes of the slice: x: 2, y: 2, z: 4, core: 2. Of those that a mesh axis runs over, the one named last changes fastest.
Arguments:
- tokens: bfloat16 [8, 2048, 2048], P('dp', 'seq'), may hold values from -60 to 60
- cotangent: bfloat16 [8, 2048, 2048], P('dp', 'seq'), may hold values from -6 to 6
- lengths: int32 [8], P('dp'), may hold values from 1537 to 2048, as said below
- key_mask: int32 [8, 2048], P('dp', 'seq'), may hold values 0 or 1
- attn_gain: bfloat16 [2048], P(('dp', 'seq')), may hold values from 0.5 to 1.5
- attn_shift: bfloat16 [2048], P(('dp', 'seq')), may hold values from -4 to 4
- qkv_weight: bfloat16 [2048, 6144], P(('dp', 'seq')), may hold values from -0.125 to 0.125
- qv_bias: bfloat16 [4096], P(('dp', 'seq')), may hold values from -4 to 4
- proj_weight: bfloat16 [2048, 2048], P(('dp', 'seq')), may hold values from -1.5 to 1.5
- proj_bias: bfloat16 [2048], P(('dp', 'seq')), may hold values from -4 to 4
- mlp_gain: bfloat16 [2048], P(('dp', 'seq')), may hold values from 0.5 to 1.5
- mlp_shift: bfloat16 [2048], P(('dp', 'seq')), may hold values from -4 to 4
- fc_weight: bfloat16 [2048, 8192], P(('dp', 'seq')), may hold values from -0.125 to 0.125
- fc_bias: bfloat16 [8192], P(('dp', 'seq')), may hold values from -4 to 4
- down_weight: bfloat16 [8192, 2048], P(('dp', 'seq')), may hold values from -0.0625 to 0.0625
- down_bias: bfloat16 [2048], P(('dp', 'seq')), may hold values from -4 to 4
Outputs:
- block_out: bfloat16 [8, 2048, 2048], P('dp', 'seq')
- tokens_grad: float32 [8, 2048, 2048], P('dp', 'seq')
- attn_gain_grad: float32 [2048], P(('dp', 'seq'))
- attn_shift_grad: float32 [2048], P(('dp', 'seq'))
- qkv_weight_grad: float32 [2048, 6144], P(('dp', 'seq'))
- qv_bias_grad: float32 [4096], P(('dp', 'seq'))
- proj_weight_grad: float32 [2048, 2048], P(('dp', 'seq'))
- proj_bias_grad: float32 [2048], P(('dp', 'seq'))
- mlp_gain_grad: float32 [2048], P(('dp', 'seq'))
- mlp_shift_grad: float32 [2048], P(('dp', 'seq'))
- fc_weight_grad: float32 [2048, 8192], P(('dp', 'seq'))
- fc_bias_grad: float32 [8192], P(('dp', 'seq'))
- down_weight_grad: float32 [8192, 2048], P(('dp', 'seq'))
- down_bias_grad: float32 [2048], P(('dp', 'seq'))
Inputs may be any that keep to these rules, and one draw needn't show every extreme that they name: `lengths`: in every draw some sequence has length 2048.
All inputs are finite; a program needn't handle non-finite values. No bound on the sum of `key_mask` on one device may be relied on, other than what follows from the above.
Results may differ from a plain program's by a relative error of at most 0.0094.
Values may be sent and summed in bfloat16 or wider, within the bound.
A program may use at most 448 MiB of HBM per device.

v0:
```python
import math

import jax
import jax.numpy as jnp
from jax import lax
from jax.sharding import PartitionSpec as P

HEADS = 16
HEAD_DIM = 128


EPS = 1e-05
NEG = -1e30


def layer_norm(values, gain, shift):
    average = jnp.mean(values, axis=-1, keepdims=True)
    centred = values - average
    spread = jnp.mean(centred * centred, axis=-1, keepdims=True)
    return centred * lax.rsqrt(spread + EPS) * gain + shift


def gelu_tanh(values):
    return jax.nn.gelu(values, approximate=True)


def inner_rows(left, right):
    return lax.dot_general(
        left, right, (((0,), (0,)), ((), ())), preferred_element_type=jnp.float32
    )


def times_transposed(left, right):
    return lax.dot_general(
        left, right, (((1,), (1,)), ((), ())), preferred_element_type=jnp.float32
    )


def split_heads(matrix, per_step):
    count = matrix.shape[0]
    heads = matrix.shape[1] // HEAD_DIM
    return matrix.reshape(count, heads // per_step, per_step, HEAD_DIM).transpose(1, 2, 0, 3)


def join_heads(grouped):
    count = grouped.shape[2]
    return grouped.transpose(2, 0, 1, 3).reshape(
        count, grouped.shape[0] * grouped.shape[1] * HEAD_DIM
    )


def attend_forward(queries, key_all, value_all, allowed, per_step):
    factor = HEAD_DIM ** (-0.5)

    def one_group(operands):
        query_part, key_part, value_part = operands
        scores = (
            jnp.einsum("gqd,gkd->gqk", query_part, key_part, preferred_element_type=jnp.float32)
            * factor
        )
        scores = jnp.where(allowed, scores, NEG)
        highest = jnp.max(scores, axis=-1, keepdims=True)
        exp_scores = jnp.exp(scores - highest)
        totals = jnp.sum(exp_scores, axis=-1, keepdims=True)
        chances = (exp_scores / totals).astype(jnp.bfloat16)
        outputs = jnp.einsum(
            "gqk,gkd->gqd", chances, value_part, preferred_element_type=jnp.float32
        )
        return (outputs, (highest + jnp.log(totals))[..., 0])

    outputs, log_totals = lax.map(
        one_group,
        (
            split_heads(queries, per_step),
            split_heads(key_all, per_step),
            split_heads(value_all, per_step),
        ),
    )
    return (join_heads(outputs), log_totals)


def attend_backward(queries, key_all, value_all, allowed, log_totals, grad_out, per_step):
    factor = HEAD_DIM ** (-0.5)

    def one_group(operands):
        query_part, key_part, value_part, lse_part, grad_part = operands
        scores = (
            jnp.einsum("gqd,gkd->gqk", query_part, key_part, preferred_element_type=jnp.float32)
            * factor
        )
        scores = jnp.where(allowed, scores, NEG)
        probs = jnp.exp(scores - lse_part[..., None])
        grad_values = jnp.einsum(
            "gqk,gqd->gkd",
            probs.astype(jnp.bfloat16),
            grad_part,
            preferred_element_type=jnp.float32,
        )
        grad_probs = jnp.einsum(
            "gqd,gkd->gqk", grad_part, value_part, preferred_element_type=jnp.float32
        )
        weighted = jnp.sum(probs * grad_probs, axis=-1, keepdims=True)
        grad_scores = (probs * (grad_probs - weighted)).astype(jnp.bfloat16)
        grad_queries = (
            jnp.einsum("gqk,gkd->gqd", grad_scores, key_part, preferred_element_type=jnp.float32)
            * factor
        )
        grad_keys = (
            jnp.einsum("gqk,gqd->gkd", grad_scores, query_part, preferred_element_type=jnp.float32)
            * factor
        )
        return (grad_queries, grad_keys, grad_values)

    grad_queries, grad_keys, grad_values = lax.map(
        one_group,
        (
            split_heads(queries, per_step),
            split_heads(key_all, per_step),
            split_heads(value_all, per_step),
            log_totals,
            split_heads(grad_out, per_step),
        ),
    )
    return (join_heads(grad_queries), join_heads(grad_keys), join_heads(grad_values))


def shards(
    tokens,
    cotangent,
    lengths,
    key_mask,
    attn_gain,
    attn_shift,
    qkv_weight,
    qv_bias,
    proj_weight,
    proj_bias,
    mlp_gain,
    mlp_shift,
    fc_weight,
    fc_bias,
    down_weight,
    down_bias,
):
    seq_count, piece, width = tokens.shape
    seq_devices = lax.axis_size("seq")
    seq_rank = lax.axis_index("seq")
    full_length = piece * seq_devices
    offset = seq_rank * piece
    query_pos = offset + jnp.arange(piece, dtype=jnp.int32)
    key_pos = jnp.arange(full_length, dtype=jnp.int32)
    own_flags = ((key_mask == 1) & (query_pos[None, :] < lengths[:, None])).astype(jnp.bfloat16)
    small = (
        lax.all_gather(attn_gain, ("dp", "seq"), axis=0, tiled=True),
        lax.all_gather(attn_shift, ("dp", "seq"), axis=0, tiled=True),
        lax.all_gather(qv_bias, ("dp", "seq"), axis=0, tiled=True),
        lax.all_gather(proj_weight, ("dp", "seq"), axis=0, tiled=True),
        lax.all_gather(proj_bias, ("dp", "seq"), axis=0, tiled=True),
        lax.all_gather(mlp_gain, ("dp", "seq"), axis=0, tiled=True),
        lax.all_gather(mlp_shift, ("dp", "seq"), axis=0, tiled=True),
        lax.all_gather(fc_bias, ("dp", "seq"), axis=0, tiled=True),
        lax.all_gather(down_bias, ("dp", "seq"), axis=0, tiled=True),
    )
    gain_one = small[0].astype(jnp.float32)
    shift_one = small[1].astype(jnp.float32)
    qv_full = small[2].astype(jnp.float32)
    proj_full = small[3]
    proj_shift = small[4].astype(jnp.float32)
    gain_two = small[5].astype(jnp.float32)
    shift_two = small[6].astype(jnp.float32)
    fc_shift = small[7].astype(jnp.float32)
    down_shift = small[8].astype(jnp.float32)
    flat = tokens.reshape(seq_count * piece, width).astype(jnp.float32)
    normed_one, norm_one_pull = jax.vjp(layer_norm, flat, gain_one, shift_one)
    normed_one = normed_one.astype(jnp.bfloat16)
    upstream = cotangent.reshape(seq_count * piece, width)
    mats = (
        lax.all_gather(qkv_weight, ("dp", "seq"), axis=0, tiled=True),
        lax.all_gather(fc_weight, ("dp", "seq"), axis=0, tiled=True),
        lax.all_gather(down_weight, ("dp", "seq"), axis=0, tiled=True),
    )
    qkv_full = mats[0]
    fc_full = mats[1]
    down_full = mats[2]
    per_step = math.gcd(HEADS, 4)
    causal = key_pos[None, :] <= query_pos[:, None]
    diagonal = key_pos[None, :] == query_pos[:, None]
    qkv_shift = jnp.concatenate(
        [qv_full[:width], jnp.zeros((width,), jnp.float32), qv_full[width:]]
    )
    projected = (
        jnp.dot(normed_one, qkv_full, preferred_element_type=jnp.float32) + qkv_shift
    ).astype(jnp.bfloat16)
    queries = projected[:, :width]
    key_own = projected[:, width : 2 * width].reshape(seq_count, piece, width)
    value_own = projected[:, 2 * width :].reshape(seq_count, piece, width)
    key_all, value_all, flags_all = (
        lax.all_gather(key_own, "seq", axis=1, tiled=True),
        lax.all_gather(value_own, "seq", axis=1, tiled=True),
        lax.all_gather(own_flags, "seq", axis=1, tiled=True),
    )
    seq_index = 0
    allowed = causal & ((flags_all[seq_index][None, :] > 0) | diagonal)
    head_out, log_totals = attend_forward(
        queries, key_all[seq_index], value_all[seq_index], allowed, per_step
    )
    allowed_list = [allowed]
    lse_list = [log_totals]
    attended = head_out.astype(jnp.bfloat16)
    middle = flat + (jnp.dot(attended, proj_full, preferred_element_type=jnp.float32) + proj_shift)
    normed_two, norm_two_pull = jax.vjp(layer_norm, middle, gain_two, shift_two)
    normed_two = normed_two.astype(jnp.bfloat16)
    hidden = jnp.dot(normed_two, fc_full, preferred_element_type=jnp.float32) + fc_shift
    active, gelu_pull = jax.vjp(gelu_tanh, hidden)
    active = active.astype(jnp.bfloat16)
    result = middle + (jnp.dot(active, down_full, preferred_element_type=jnp.float32) + down_shift)
    block_out = result.astype(jnp.bfloat16).reshape(seq_count, piece, width)
    grad_down = inner_rows(active, upstream)
    grad_down_bias = jnp.sum(upstream.astype(jnp.float32), axis=0)
    grad_active = times_transposed(upstream, down_full)
    grad_hidden = gelu_pull(grad_active)[0].astype(jnp.bfloat16)
    grad_fc = inner_rows(normed_two, grad_hidden)
    grad_fc_bias = jnp.sum(grad_hidden.astype(jnp.float32), axis=0)
    grad_normed_two = times_transposed(grad_hidden, fc_full)
    grad_mid_norm, grad_gain_two, grad_shift_two = norm_two_pull(grad_normed_two)
    grad_middle = upstream.astype(jnp.float32) + grad_mid_norm
    mlp_grads = (
        lax.psum_scatter(grad_gain_two, ("dp", "seq"), scatter_dimension=0, tiled=True),
        lax.psum_scatter(grad_shift_two, ("dp", "seq"), scatter_dimension=0, tiled=True),
        lax.psum_scatter(grad_fc, ("dp", "seq"), scatter_dimension=0, tiled=True),
        lax.psum_scatter(grad_fc_bias, ("dp", "seq"), scatter_dimension=0, tiled=True),
        lax.psum_scatter(grad_down, ("dp", "seq"), scatter_dimension=0, tiled=True),
        lax.psum_scatter(grad_down_bias, ("dp", "seq"), scatter_dimension=0, tiled=True),
    )
    grad_mid_low = grad_middle.astype(jnp.bfloat16)
    grad_proj = inner_rows(attended, grad_mid_low)
    grad_proj_bias = jnp.sum(grad_mid_low.astype(jnp.float32), axis=0)
    grad_attended = times_transposed(grad_mid_low, proj_full).astype(jnp.bfloat16)
    seq_index = 0
    grad_queries, grad_keys, grad_values = attend_backward(
        queries,
        key_all[seq_index],
        value_all[seq_index],
        allowed_list[seq_index],
        lse_list[seq_index],
        grad_attended,
        per_step,
    )
    key_grads = [grad_keys]
    value_grads = [grad_values]
    key_share, value_share = (
        lax.psum_scatter(jnp.stack(key_grads), "seq", scatter_dimension=1, tiled=True),
        lax.psum_scatter(jnp.stack(value_grads), "seq", scatter_dimension=1, tiled=True),
    )
    grad_qkv = jnp.concatenate(
        [
            grad_queries.astype(jnp.bfloat16),
            key_share.reshape(seq_count * piece, width).astype(jnp.bfloat16),
            value_share.reshape(seq_count * piece, width).astype(jnp.bfloat16),
        ],
        axis=1,
    )
    grad_qkv_weight = inner_rows(normed_one, grad_qkv)
    column_sums = jnp.sum(grad_qkv.astype(jnp.float32), axis=0)
    grad_qv_bias = jnp.concatenate([column_sums[:width], column_sums[2 * width :]])
    grad_normed_one = times_transposed(grad_qkv, qkv_full)
    grad_flat_norm, grad_gain_one, grad_shift_one = norm_one_pull(grad_normed_one)
    tokens_grad = (grad_middle + grad_flat_norm).reshape(seq_count, piece, width)
    attn_grads = (
        lax.psum_scatter(grad_gain_one, ("dp", "seq"), scatter_dimension=0, tiled=True),
        lax.psum_scatter(grad_shift_one, ("dp", "seq"), scatter_dimension=0, tiled=True),
        lax.psum_scatter(grad_qkv_weight, ("dp", "seq"), scatter_dimension=0, tiled=True),
        lax.psum_scatter(grad_qv_bias, ("dp", "seq"), scatter_dimension=0, tiled=True),
        lax.psum_scatter(grad_proj, ("dp", "seq"), scatter_dimension=0, tiled=True),
        lax.psum_scatter(grad_proj_bias, ("dp", "seq"), scatter_dimension=0, tiled=True),
    )
    outputs = (
        block_out,
        tokens_grad,
        attn_grads[0],
        attn_grads[1],
        attn_grads[2],
        attn_grads[3],
        attn_grads[4],
        attn_grads[5],
        mlp_grads[0],
        mlp_grads[1],
        mlp_grads[2],
        mlp_grads[3],
        mlp_grads[4],
        mlp_grads[5],
    )
    return outputs


def solution(mesh):
    in_specs = (
        P("dp", "seq", None),
        P("dp", "seq", None),
        P("dp"),
        P("dp", "seq"),
        P(("dp", "seq")),
        P(("dp", "seq")),
        P(("dp", "seq"), None),
        P(("dp", "seq")),
        P(("dp", "seq"), None),
        P(("dp", "seq")),
        P(("dp", "seq")),
        P(("dp", "seq")),
        P(("dp", "seq"), None),
        P(("dp", "seq")),
        P(("dp", "seq"), None),
        P(("dp", "seq")),
    )
    out_specs = (
        P("dp", "seq", None),
        P("dp", "seq", None),
        P(("dp", "seq")),
        P(("dp", "seq")),
        P(("dp", "seq"), None),
        P(("dp", "seq")),
        P(("dp", "seq"), None),
        P(("dp", "seq")),
        P(("dp", "seq")),
        P(("dp", "seq")),
        P(("dp", "seq"), None),
        P(("dp", "seq")),
        P(("dp", "seq"), None),
        P(("dp", "seq")),
    )
    return jax.shard_map(shards, mesh=mesh, in_specs=in_specs, out_specs=out_specs, check_vma=False)
```

profile of v0, /device:TPU:0, one launch (start us, length us, event | category | flops | bytes accessed | tf_op | source)
XLA Modules:
  0.0 5283.1 jit_solution(3906840447921936737)
XLA Ops:
  13.1 43.6 all-reduce.15
  56.7 66.8 %all-gather.2 = bf16[32,1,128]{2,1,0:T(2,128)(2,1)S(1)} all-gather(bf16[1,1,128]{2,1,0:T(2,128)(2,1)} %bitcast.214), channel_id=1, replica_groups=mesh['dp'=8,'seq'=4] {'dp','seq'}, dimensions={0}, use_global_device_ids=true | all-gather | bytes 8448 | tf_op jit(solution)/shard_map/all_gather | solution.py:156
  126.8 43.3 all-gather.11.cloned.1.call-done
  170.2 18.2 add_convert_fusion
  196.3 65.7 %all-gather.3 = bf16[32,1,256]{2,1,0:T(2,128)(2,1)S(1)} all-gather(bf16[1,1,256]{2,1,0:T(2,128)(2,1)S(1)} %reshape.197), channel_id=1, replica_groups=mesh['dp'=8,'seq'=4] {'dp','seq'}, dimensions={0}, use_global_device_ids=true | all-gather | bytes 16896 | tf_op jit(solution)/shard_map/all_gather | solution.py:161
  277.8 14.6 reshape_squeeze.9
  301.2 66.6 %all-gather.19.cloned.1.call-done = bf16[2048,2048]{1,0:T(8,128)(2,1)} async-done(((bf16[512,2048]{1,0:T(8,128)(2,1)}), bf16[2048,2048]{1,0:T(8,128)(2,1)}) %all-gather.19.cloned.1.call-update) | async-done | bytes 8388624 | tf_op jit(solution)/shard_map/all_gather | solution.py:198
  367.8 14.4 reshape_squeeze.8
  392.5 77.0 %while.28 = (s32[]{:T(128)}, bf16[4,4,512,128]{2,3,1,0:T(8,128)(2,1)}, f32[4,4,512]{2,1,0:T(4,128)S(1)}, bf16[4,4,512,128]{3,2,1,0:T(8,128)(2,1)}, bf16[4,4,2048...) while((s32[]{:T(128)}, ...), condition=%wide.region_5.6_spmd.clone, body=%wide.region_2.5_spmd.clone.sunk | while | flops 2202007552 | bytes 60364904 | solution.py:71
  482.0 162.3 %all-gather.15.cloned.1.call-done = bf16[2048,8192]{1,0:T(8,128)(2,1)} async-done(((bf16[64,8192]{1,0:T(8,128)(2,1)}), bf16[2048,8192]{1,0:T(8,128)(2,1)}) %all-gather.15.cloned.1.call-update) | async-done | bytes 33554448 | tf_op jit(solution)/shard_map/all_gather | solution.py:179
  644.3 28.4 fusion.100
  672.7 167.3 %all-gather.17.cloned.1.call-done = bf16[8192,2048]{1,0:T(8,128)(2,1)} async-done(((bf16[256,2048]{1,0:T(8,128)(2,1)}), bf16[8192,2048]{1,0:T(8,128)(2,1)}) %all-gather.17.cloned.1.call-update) | async-done | bytes 33554448 | tf_op jit(solution)/shard_map/all_gather | solution.py:180
  840.0 34.3 convert_reduce_fusion
  874.3 27.2 multiply_reduce_fusion.1
  924.3 255.9 %while.29 = (s32[]{:T(128)}, bf16[4,4,512,128]{2,3,1,0:T(8,128)(2,1)}, f32[4,4,2048,128]{2,3,1,0:T(8,128)}, f32[4,4,2048,128]{2,3,1,0:T(8,128)}, bf16[4,4,512,12...) while((s32[]{:T(128)}, ...), condition=%wide.region_12.13_spmd.clone, body=%wide.region_10.12_spmd.clone.sunk | while | flops 5437388800 | bytes 233372832 | solution.py:114
  943.1 12.9 multiply_reduce_fusion.5
  1006.9 12.9 multiply_reduce_fusion.5
  1019.8 12.1 multiply_convert_fusion.5
  1070.7 12.9 multiply_reduce_fusion.5
  1134.6 12.9 multiply_reduce_fusion.5
  1180.9 151.3 %reduce-scatter.9.cloned.1.call-done = f32[1,512,2048]{1,2,0:T(8,128)} async-done(((f32[1,2048,2048]{1,2,0:T(8,128)}), f32[1,512,2048]{1,2,0:T(8,128)}) %reduce-scatter.9.cloned.1.call-update) | async-done | bytes 4194320 | tf_op jit(solution)/shard_map/reduce_scatter | solution.py:253
  1336.0 153.1 %reduce-scatter.7.cloned.1.call-done = f32[1,512,2048]{1,2,0:T(8,128)} async-done(((f32[1,2048,2048]{1,2,0:T(8,128)}), f32[1,512,2048]{1,2,0:T(8,128)}) %reduce-scatter.7.cloned.1.call-update) | async-done | bytes 4194320 | tf_op jit(solution)/shard_map/reduce_scatter | solution.py:252
  1502.1 23.2 fusion.101
  1536.2 12.5 fusion.108
  1549.3 24.1 fusion.94
  1575.0 32.3 fusion.86
  1608.1 32.1 fusion.99
  1640.9 27.9 fusion.84
  1678.9 342.5 %reduce-scatter.13.cloned.1.call-done = f32[64,2048]{1,0:T(8,128)} async-done(((f32[2048,2048]{1,0:T(8,128)}), f32[64,2048]{1,0:T(8,128)}) %reduce-scatter.13.cloned.1.call-update) | async-done | bytes 524304 | tf_op jit(solution)/shard_map/reduce_scatter | solution.py:274
  2021.4 441.0 %reduce-scatter.11.cloned.1.call-done = f32[64,6144]{1,0:T(8,128)} async-done(((f32[2048,6144]{1,0:T(8,128)}), f32[64,6144]{1,0:T(8,128)}) %reduce-scatter.11.cloned.1.call-update) | async-done | bytes 1572880 | tf_op jit(solution)/shard_map/reduce_scatter | solution.py:272
  2462.4 1406.3 %reduce-scatter.17.cloned.1.call-done = f32[256,2048]{1,0:T(8,128)} async-done(((f32[8192,2048]{1,0:T(8,128)}), f32[256,2048]{1,0:T(8,128)}) %reduce-scatter.17.cloned.1.call-update) | async-done | bytes 2097168 | tf_op jit(solution)/shard_map/reduce_scatter | solution.py:232
  3868.7 1407.6 %reduce-scatter.15.cloned.1.call-done = f32[64,8192]{1,0:T(8,128)} async-done(((f32[2048,8192]{1,0:T(8,128)}), f32[64,8192]{1,0:T(8,128)}) %reduce-scatter.15.cloned.1.call-update) | async-done | bytes 2097168 | tf_op jit(solution)/shard_map/reduce_scatter | solution.py:230
  (249 shorter events, 396.3 us)
Async XLA Ops:
  7.2 118.4 %copy-start.5 = (bf16[1,512,2048]{2,1,0:T(8,128)(2,1)S(1)}, bf16[1,512,2048]{2,1,0:T(8,128)(2,1)}, u32[]{:S(2)}) copy-start(bf16[1,512,2048]{2,1,0:T(8,128)(2,1)} %param.20) | copy-start | bytes 6291460
  7.2 163.0 %all-gather.11.cloned.1.call-start = ((), (), s32[]{:S(2)}) async-start(), calls=%async_computation.6 | async-start | bytes 25952256 | tf_op jit(solution)/shard_map/all_gather | solution.py:178
  7.9 269.9 %all-gather.21.cloned.1.call-start = ((), (), s32[]{:S(2)}) async-start(), calls=%async_computation.17 | async-start | bytes 10485760 | tf_op jit(solution)/shard_map/all_gather | solution.py:199
  56.7 131.7 %copy-start.35 = (f32[2048]{0:T(1024)}, f32[2048]{0:T(1024)S(1)}, u32[]{:S(2)}) copy-start(f32[2048]{0:T(1024)S(1)} %convert_element_type.113) | copy-start | bytes 24580
  56.7 131.7 %copy-start.23 = (f32[2048]{0:T(1024)}, f32[2048]{0:T(1024)S(1)}, u32[]{:S(2)}) copy-start(f32[2048]{0:T(1024)S(1)} %convert_element_type.112) | copy-start | bytes 24580
  125.5 62.9 %copy-start.27 = (f32[512]{0:T(512)}, f32[512]{0:T(512)S(1)}, u32[]{:S(2)}) copy-start(f32[512]{0:T(512)S(1)} %broadcast_multiply_fusion.1) | copy-start | bytes 6148
  126.8 61.6 %copy-start.29 = (f32[512]{0:T(512)}, f32[512]{0:T(512)S(1)}, u32[]{:S(2)}) copy-start(f32[512]{0:T(512)S(1)} %fusion.92) | copy-start | bytes 6148
  191.3 71.3 %copy-start.39 = (s32[1,512]{1,0:T(1,128)S(1)}, s32[1,512]{1,0:T(1,128)}, u32[]{:S(2)}) copy-start(s32[1,512]{1,0:T(1,128)} %param.23) | copy-start | bytes 6148
  191.3 176.5 %all-gather.19.cloned.1.call-start = ((), (), s32[]{:S(2)}) async-start(), calls=%async_computation.16 | async-start | bytes 10485760 | tf_op jit(solution)/shard_map/all_gather | solution.py:198
  192.0 277.5 %all-gather.13.cloned.1.call-start = ((), (), s32[]{:S(2)}) async-start(), calls=%async_computation.7 | async-start | bytes 8650752 | tf_op jit(solution)/shard_map/all_gather | solution.py:157
  192.6 451.7 %all-gather.15.cloned.1.call-start = ((), (), s32[]{:S(2)}) async-start(), calls=%async_computation.8 | async-start | bytes 34603008 | tf_op jit(solution)/shard_map/all_gather | solution.py:179
  193.2 646.8 %all-gather.17.cloned.1.call-start = ((), (), s32[]{:S(2)}) async-start(), calls=%async_computation.9 | async-start | bytes 34603008 | tf_op jit(solution)/shard_map/all_gather | solution.py:180
  193.8 1138.5 %reduce-scatter.9.cloned.1.call-start = ((), (), s32[]{:S(2)}) async-start(), calls=%async_computation.11 | async-start | bytes 20971520 | tf_op jit(solution)/shard_map/reduce_scatter | solution.py:253
  392.5 77.1 %copy-start.37 = (f32[2048]{0:T(1024)S(1)}, f32[2048]{0:T(1024)}, u32[]{:S(2)}) copy-start(f32[2048]{0:T(1024)} %convert_element_type.120) | copy-start | bytes 24580
  479.4 164.8 %copy-start.15 = (f32[2048]{0:T(1024)S(1)}, f32[2048]{0:T(1024)}, u32[]{:S(2)}) copy-start(f32[2048]{0:T(1024)} %convert_element_type.121) | copy-start | bytes 24580
  479.4 164.8 %copy-start.21 = (f32[2048]{0:T(1024)S(1)}, f32[2048]{0:T(1024)}, u32[]{:S(2)}) copy-start(f32[2048]{0:T(1024)} %convert_element_type.122) | copy-start | bytes 24580
  479.5 422.0 %copy-start.17 = (f32[512]{0:T(512)}, f32[512]{0:T(512)S(1)}, u32[]{:S(2)}) copy-start(f32[512]{0:T(512)S(1)} %broadcast_multiply_fusion) | copy-start | bytes 6148
  481.9 419.6 %copy-start.19 = (f32[512]{0:T(512)}, f32[512]{0:T(512)S(1)}, u32[]{:S(2)}) copy-start(f32[512]{0:T(512)S(1)} %fusion.93) | copy-start | bytes 6148
  481.9 358.1 %copy-start.10 = (bf16[1,512,2048]{2,1,0:T(8,128)(2,1)S(1)}, bf16[1,512,2048]{2,1,0:T(8,128)(2,1)}, u32[]{:S(2)}) copy-start(bf16[1,512,2048]{2,1,0:T(8,128)(2,1)} %param.21) | copy-start | bytes 6291460
  482.0 358.1 %copy-start.25 = (f32[32,1,256]{2,1,0:T(1,128)S(1)}, f32[32,1,256]{2,1,0:T(1,128)}, u32[]{:S(2)}) copy-start(f32[32,1,256]{2,1,0:T(1,128)} %convert_element_type.143) | copy-start | bytes 98308
  874.3 27.2 copy-start.2
  1180.1 309.0 %reduce-scatter.7.cloned.1.call-start = ((), (), s32[]{:S(2)}) async-start(), calls=%async_computation.10 | async-start | bytes 20971520 | tf_op jit(solution)/shard_map/reduce_scatter | solution.py:252
  1180.9 487.8 %all-reduce.18.cloned.1.call-start = ((), (), s32[]{:S(2)}) async-start(), calls=%async_computation.18 | async-start | bytes 196608
  1491.8 10.2 copy-start.6
  1491.8 10.2 copy-start.24
  1491.8 10.2 copy-start.28
  1502.0 23.2 copy-start.32
  1502.1 23.2 copy-start.30
  1535.9 485.4 %reduce-scatter.13.cloned.1.call-start = ((), (), s32[]{:S(2)}) async-start(), calls=%async_computation.13 | async-start | bytes 17301504 | tf_op jit(solution)/shard_map/reduce_scatter | solution.py:274
  1548.7 913.8 %reduce-scatter.11.cloned.1.call-start = ((), (), s32[]{:S(2)}) async-start(), calls=%async_computation.12 | async-start | bytes 51904512 | tf_op jit(solution)/shard_map/reduce_scatter | solution.py:272
  1573.5 2295.3 %reduce-scatter.17.cloned.1.call-start = ((), (), s32[]{:S(2)}) async-start(), calls=%async_computation.15 | async-start | bytes 69206016 | tf_op jit(solution)/shard_map/reduce_scatter | solution.py:232
  1607.4 3669.0 %reduce-scatter.15.cloned.1.call-start = ((), (), s32[]{:S(2)}) async-start(), calls=%async_computation.14 | async-start | bytes 69206016 | tf_op jit(solution)/shard_map/reduce_scatter | solution.py:230
  (25 other events, 68.9 us)
Sparse Core Ops, SparseCore 0:
  10.9 159.2 all-gather.10
  191.4 86.3 all-gather.20
  280.2 87.5 all-gather.18
  370.5 77.5 all-gather.12
  450.9 193.3 all-gather.14
  647.0 192.9 all-gather.16
  1180.3 151.9 reduce-scatter.8
  1335.3 153.7 reduce-scatter.6
  1536.1 123.7 all-reduce.17
  1662.7 358.6 reduce-scatter.12
  2029.5 432.8 reduce-scatter.10
  2465.3 1403.3 reduce-scatter.16
  3871.8 1404.5 reduce-scatter.14
where the time goes:
time: 5290 us; the launch traced here: 5280 us
  waiting for transfers between devices  4350 us (82%)
  matrix products  465 us (9%)
  blocking collectives  183 us (3%)
  local copies, waits for them, and re-layouts  155 us (3%)
  other arithmetic  114 us (2%)
    reduce_scatter x1, waiting for transfers between devices, shards(): lax.psum_scatter(grad_fc, ('dp', 'seq'), scatter_dimension=0, tiled=True)  1410 us
    reduce_scatter x1, waiting for transfers between devices, shards(): lax.psum_scatter(grad_down, ('dp', 'seq'), scatter_dimension=0, tiled=True)  1410 us
    reduce_scatter x1, waiting for transfers between devices, shards(): lax.psum_scatter(grad_qkv_weight, ('dp', 'seq'), scatter_dimension=0, til...  441 us
    reduce_scatter x1, waiting for transfers between devices, shards(): lax.psum_scatter(grad_proj, ('dp', 'seq'), scatter_dimension=0, tiled=True)  343 us
    all_gather x1, waiting for transfers between devices, shards(): lax.all_gather(down_weight, ('dp', 'seq'), axis=0, tiled=True)  167 us
    all_gather x1, waiting for transfers between devices, shards(): lax.all_gather(fc_weight, ('dp', 'seq'), axis=0, tiled=True)  162 us
    reduce_scatter x1, waiting for transfers between devices, shards(): lax.psum_scatter(jnp.stack(key_grads), 'seq', scatter_dimension=1, tiled=...  153 us
    reduce_scatter x1, waiting for transfers between devices, shards(): lax.psum_scatter(jnp.stack(value_grads), 'seq', scatter_dimension=1, tile...  151 us
  transfers between devices with their start and end apart: 13, of which 11 were waited for; matrix products, arithmetic and copies ran while one was open for 6% of the time, Pallas kernels for 0%

commit v1 on v0

v1 whole, which is shorter than its diff:
```python
import functools
import math

import jax
import jax.numpy as jnp
from jax import lax
from jax.experimental import pallas as pl
from jax.experimental.pallas import tpu as pltpu
from jax.sharding import PartitionSpec as P

HEADS = 16
HEAD_DIM = 128
EPS = 1e-05
NEG = -1e30
FACTOR = HEAD_DIM ** (-0.5)
LOG2E = math.log2(math.e)
F32 = jnp.float32
BF16 = jnp.bfloat16
BOTH = ("dp", "seq")


def nn(left, right):
    return lax.dot_general(left, right, (((1,), (0,)), ((), ())), preferred_element_type=F32)


def nt(left, right):
    return lax.dot_general(left, right, (((1,), (1,)), ((), ())), preferred_element_type=F32)


def tn(left, right):
    return lax.dot_general(left, right, (((0,), (0,)), ((), ())), preferred_element_type=F32)


def scores_of(key_ref, bias_ref, query, rel, piece, diagonal):
    rows = pl.ds(pl.multiple_of(rel * piece, piece), piece)
    scores = nt(key_ref[rows, :], query) * (FACTOR * LOG2E)
    key_bias = bias_ref[rows, :]
    if not diagonal:
        return scores + key_bias
    key_at = lax.broadcasted_iota(jnp.int32, scores.shape, 0)
    query_at = lax.broadcasted_iota(jnp.int32, scores.shape, 1)
    allowed = ((key_at < query_at) & (key_bias > -1.0)) | (key_at == query_at)
    return jnp.where(allowed, scores, NEG)


def forward_kernel(rank_ref, query_ref, key_ref, value_ref, bias_ref, out_ref, lse_ref, score_ref, value_t):
    piece = query_ref.shape[0]
    rank = rank_ref[0]
    step = pl.program_id(1)
    true = lax.bitwise_xor(step, rank)

    @pl.when(step == 0)
    def _():
        value_t[...] = value_ref[...].astype(F32).T.astype(BF16)

    query = query_ref[...]

    def first(at, top):
        scores = scores_of(key_ref, bias_ref, query, lax.bitwise_xor(at, rank), piece, False)
        score_ref[pl.ds(pl.multiple_of(at * piece, piece), piece), :] = scores
        return jnp.maximum(top, jnp.max(scores, axis=0, keepdims=True))

    last = scores_of(key_ref, bias_ref, query, step, piece, True)
    top = lax.fori_loop(0, true, first, jnp.max(last, axis=0, keepdims=True))

    def weigh(scores, rel):
        weights = jnp.exp2(scores - top)
        columns = pl.ds(pl.multiple_of(rel * piece, piece), piece)
        return jnp.sum(weights, axis=0, keepdims=True), nn(value_t[:, columns], weights.astype(BF16))

    def second(at, carry):
        total, out = carry
        more, part = weigh(
            score_ref[pl.ds(pl.multiple_of(at * piece, piece), piece), :], lax.bitwise_xor(at, rank)
        )
        return total + more, out + part

    total, out = lax.fori_loop(0, true, second, weigh(last, step))
    out_ref[...] = (out / total).T.astype(BF16)
    lse_ref[0] = top + jnp.log2(total)


def attend(rank, qkv, key_bias, piece):
    length, heads = qkv.shape[0], qkv.shape[1] // (3 * HEAD_DIM)
    grid_spec = pltpu.PrefetchScalarGridSpec(
        num_scalar_prefetch=1,
        grid=(heads, length // piece),
        in_specs=[
            pl.BlockSpec((piece, HEAD_DIM), lambda h, i, r: (i, 3 * h)),
            pl.BlockSpec((length, HEAD_DIM), lambda h, i, r: (0, 3 * h + 1)),
            pl.BlockSpec((length, HEAD_DIM), lambda h, i, r: (0, 3 * h + 2)),
            pl.BlockSpec((length, 1), lambda h, i, r: (0, 0)),
        ],
        out_specs=[
            pl.BlockSpec((piece, HEAD_DIM), lambda h, i, r: (i, h)),
            pl.BlockSpec((1, 1, piece), lambda h, i, r: (h, 0, i)),
        ],
        scratch_shapes=[pltpu.VMEM((length, piece), F32), pltpu.VMEM((HEAD_DIM, length), BF16)],
    )
    flops = 4 * heads * length * length * HEAD_DIM
    return pl.pallas_call(
        forward_kernel,
        grid_spec=grid_spec,
        out_shape=(
            jax.ShapeDtypeStruct((length, heads * HEAD_DIM), BF16),
            jax.ShapeDtypeStruct((heads, 1, length), F32),
        ),
        compiler_params=pltpu.CompilerParams(
            dimension_semantics=("arbitrary", "arbitrary"), vmem_limit_bytes=48 * 2**20
        ),
        cost_estimate=pl.CostEstimate(
            flops=flops, bytes_accessed=qkv.size * 3, transcendentals=heads * length * length // 2
        ),
    )(rank, qkv, qkv, qkv, key_bias)


def backward_kernel(
    rank_ref, query_ref, grad_ref, lse_ref, key_ref, value_ref, bias_ref, out_ref,
    prob_ref, chance_ref, key_t, key_sum, value_sum,
):
    piece = query_ref.shape[0]
    rank = rank_ref[0]
    step = pl.program_id(1)
    true = lax.bitwise_xor(step, rank)

    @pl.when(step == 0)
    def _():
        key_t[...] = key_ref[...].astype(F32).T.astype(BF16)
        key_sum[...] = jnp.zeros_like(key_sum)
        value_sum[...] = jnp.zeros_like(value_sum)

    query, grad, lse = query_ref[...], grad_ref[...], lse_ref[0]

    def rows_of(block):
        return pl.ds(pl.multiple_of(block * piece, piece), piece)

    def measure(scores, rel):
        rows = rows_of(rel)
        probs = jnp.exp2(scores - lse)
        grad_chances = nt(value_ref[rows, :], grad)
        value_sum[rows, :] += nn(probs.astype(BF16), grad)
        prob_ref[rows, :] = probs
        chance_ref[rows, :] = grad_chances
        return jnp.sum(probs * grad_chances, axis=0, keepdims=True)

    def first(at, weighted):
        rel = lax.bitwise_xor(at, rank)
        scores = scores_of(key_ref, bias_ref, query, rel, piece, False)
        return weighted + measure(scores, rel)

    last = scores_of(key_ref, bias_ref, query, step, piece, True)
    weighted = lax.fori_loop(0, true, first, measure(last, step))

    def second(at, total):
        rel = lax.bitwise_xor(at, rank)
        rows = rows_of(rel)
        grad_scores = (prob_ref[rows, :] * (chance_ref[rows, :] - weighted)).astype(BF16)
        key_sum[rows, :] += nn(grad_scores, query)
        return total + nn(key_t[:, rows], grad_scores)

    total = lax.fori_loop(0, true + 1, second, jnp.zeros((HEAD_DIM, piece), F32))
    out_ref[rows_of(step), 0:HEAD_DIM] = (total * FACTOR).T.astype(BF16)

    @pl.when(step == pl.num_programs(1) - 1)
    def _():
        out_ref[:, HEAD_DIM : 2 * HEAD_DIM] = (key_sum[...] * FACTOR).astype(BF16)
        out_ref[:, 2 * HEAD_DIM :] = value_sum[...].astype(BF16)


def attend_backward(rank, qkv, grad_attended, lse, key_bias, piece):
    length, heads = qkv.shape[0], qkv.shape[1] // (3 * HEAD_DIM)
    grid_spec = pltpu.PrefetchScalarGridSpec(
        num_scalar_prefetch=1,
        grid=(heads, length // piece),
        in_specs=[
            pl.BlockSpec((piece, HEAD_DIM), lambda h, i, r: (i, 3 * h)),
            pl.BlockSpec((piece, HEAD_DIM), lambda h, i, r: (i, h)),
            pl.BlockSpec((1, 1, piece), lambda h, i, r: (h, 0, i)),
            pl.BlockSpec((length, HEAD_DIM), lambda h, i, r: (0, 3 * h + 1)),
            pl.BlockSpec((length, HEAD_DIM), lambda h, i, r: (0, 3 * h + 2)),
            pl.BlockSpec((length, 1), lambda h, i, r: (0, 0)),
        ],
        out_specs=pl.BlockSpec((length, 3 * HEAD_DIM), lambda h, i, r: (0, h)),
        scratch_shapes=[
            pltpu.VMEM((length, piece), F32),
            pltpu.VMEM((length, piece), F32),
            pltpu.VMEM((HEAD_DIM, length), BF16),
            pltpu.VMEM((length, HEAD_DIM), F32),
            pltpu.VMEM((length, HEAD_DIM), F32),
        ],
    )
    flops = 10 * heads * length * length * HEAD_DIM
    return pl.pallas_call(
        backward_kernel,
        grid_spec=grid_spec,
        out_shape=jax.ShapeDtypeStruct(qkv.shape, BF16),
        compiler_params=pltpu.CompilerParams(
            dimension_semantics=("arbitrary", "arbitrary"), vmem_limit_bytes=48 * 2**20
        ),
        cost_estimate=pl.CostEstimate(
            flops=flops, bytes_accessed=qkv.size * 6, transcendentals=heads * length * length // 2
        ),
    )(rank, qkv, grad_attended, lse, qkv, qkv, key_bias)


def shift(value, axis, distance):
    count = lax.axis_size(axis)
    return lax.ppermute(value, axis, [(i, i ^ distance) for i in range(count)])


def gather_blocks(value, axis="seq"):
    return [value] + [shift(value, axis, k) for k in range(1, lax.axis_size(axis))]


def scatter_blocks(blocks, axis="seq"):
    return [blocks[0]] + [shift(blocks[k], axis, k) for k in range(1, lax.axis_size(axis))]


def by_rank(blocks, rank):
    bit = 1
    while bit < len(blocks):
        odd = (rank & bit) != 0
        blocks = [jnp.where(odd, blocks[k ^ bit], blocks[k]) for k in range(len(blocks))]
        bit *= 2
    return blocks


def pick(pieces, at):
    return lax.dynamic_index_in_dim(pieces, at, axis=0, keepdims=False)


def exchange(pieces, rank):
    sent = [pick(pieces, rank ^ k) for k in range(pieces.shape[0])]
    return by_rank(scatter_blocks(sent), rank)


def small_scatter(pieces, dp_rank, seq_rank):
    total = 0.0
    sent = [lax.dynamic_index_in_dim(pieces, seq_rank ^ k, axis=1, keepdims=False) for k in range(pieces.shape[1])]
    for part in scatter_blocks(sent):
        total = total + part
    sent = [pick(total, dp_rank ^ k) for k in range(pieces.shape[0])]
    total = 0.0
    for part in scatter_blocks(sent, "dp"):
        total = total + part
    return total


def swap_pairs(dp_count, seq_count, sub):
    pairs = []
    for d in range(dp_count):
        for s in range(seq_count):
            source = ((d // sub) * sub + s % sub) * seq_count + (s // sub) * sub + d % sub
            pairs.append((source, d * seq_count + s))
    return pairs


def norm_parts(values):
    average = jnp.mean(values, axis=-1, keepdims=True)
    centred = values - average
    scale = lax.rsqrt(jnp.mean(centred * centred, axis=-1, keepdims=True) + EPS)
    return centred * scale, scale


def norm_backward(normed, scale, gain, upstream):
    weighted = upstream * gain
    return scale * (
        weighted
        - jnp.mean(weighted, axis=-1, keepdims=True)
        - normed * jnp.mean(weighted * normed, axis=-1, keepdims=True)
    )


def add_up(parts):
    total = parts[0].astype(F32)
    for part in parts[1:]:
        total = total + part.astype(F32)
    return total


def shards(
    tokens,
    cotangent,
    lengths,
    key_mask,
    attn_gain,
    attn_shift,
    qkv_weight,
    qv_bias,
    proj_weight,
    proj_bias,
    mlp_gain,
    mlp_shift,
    fc_weight,
    fc_bias,
    down_weight,
    down_bias,
):
    _, piece, width = tokens.shape
    dp_count, seq_count = lax.axis_size("dp"), lax.axis_size("seq")
    dp_rank, seq_rank = lax.axis_index("dp"), lax.axis_index("seq")
    length = piece * seq_count
    own_heads = HEADS // seq_count
    rows = qkv_weight.shape[0]
    sub = HEAD_DIM // proj_weight.shape[0]
    high = seq_count // sub
    block = down_weight.shape[0]
    rank = jnp.reshape(seq_rank, (1,)).astype(jnp.int32)
    swap = swap_pairs(dp_count, seq_count, sub)

    qkv_pieces = (
        qkv_weight.reshape(rows, 3, own_heads, sub, high, HEAD_DIM)
        .transpose(4, 3, 0, 2, 1, 5)
        .reshape(seq_count, rows, own_heads * 3 * HEAD_DIM)
    )
    qkv_rows = jnp.concatenate(exchange(qkv_pieces, seq_rank), axis=0)
    qkv_full = lax.all_gather(qkv_rows, "dp", axis=0, tiled=True)
    tokens_own = tokens[0]
    token_blocks = gather_blocks(tokens_own)
    proj_full = lax.all_gather(lax.ppermute(proj_weight, BOTH, swap), "dp", axis=0, tiled=True)
    down_full = lax.all_gather(down_weight, "dp", axis=0, tiled=True)
    fc_pieces = (
        fc_weight.reshape(rows, dp_count, seq_count, block)
        .transpose(2, 0, 1, 3)
        .reshape(seq_count, rows, dp_count * block)
    )
    fc_rows = jnp.concatenate(exchange(fc_pieces, seq_rank), axis=0)
    fc_full = lax.all_gather(fc_rows, "dp", axis=0, tiled=True)

    small = (attn_gain, attn_shift, qv_bias, proj_bias, mlp_gain, mlp_shift, fc_bias, down_bias)
    sizes = [item.shape[0] for item in small]
    packed = jnp.concatenate(small)
    packed = jnp.stack(by_rank(gather_blocks(packed), seq_rank))
    packed = jnp.stack(by_rank(gather_blocks(packed, "dp"), dp_rank)).astype(F32)
    parts, start = [], 0
    for size in sizes:
        parts.append(packed[:, :, start : start + size])
        start += size
    whole = [part.reshape(-1) for part in parts]
    gain_one, shift_one, qv_full, proj_shift, gain_two, shift_two, _, down_shift = whole
    fc_shift = lax.dynamic_index_in_dim(parts[6], seq_rank, axis=1, keepdims=False).reshape(-1)
    rank_low, rank_high = seq_rank % sub, seq_rank // sub
    qv_heads = qv_full.reshape(2, own_heads, sub, high, HEAD_DIM)
    qv_own = lax.dynamic_index_in_dim(
        lax.dynamic_index_in_dim(qv_heads, rank_low, axis=2, keepdims=False), rank_high, axis=2, keepdims=False
    )
    qkv_shift = jnp.stack([qv_own[0], jnp.zeros_like(qv_own[0]), qv_own[1]], axis=1).reshape(-1)

    positions = seq_rank * piece + jnp.arange(piece, dtype=jnp.int32)
    own_flags = ((key_mask[0] == 1) & (positions < lengths[0])).astype(BF16)
    flags = jnp.concatenate(gather_blocks(own_flags))
    key_bias = jnp.where(flags > 0, 0.0, NEG).astype(F32)[:, None]

    own = tokens_own.astype(F32)
    cot_own, token_blocks[-1] = lax.optimization_barrier((cotangent[0], token_blocks[-1]))
    cot_blocks = gather_blocks(cot_own)
    token_all = jnp.concatenate(token_blocks, axis=0).astype(F32)
    normed_one = (norm_parts(token_all)[0] * gain_one + shift_one).astype(BF16)
    qkv = (nn(normed_one, qkv_full) + qkv_shift).astype(BF16)
    attended, lse = attend(rank, qkv, key_bias, piece)
    proj_terms = [
        nn(attended[k * piece : (k + 1) * piece], proj_full).astype(BF16) for k in range(seq_count)
    ]
    middle = own + (add_up(scatter_blocks(proj_terms)) + proj_shift)
    unit_two, scale_two = norm_parts(middle)
    normed_two = (unit_two * gain_two + shift_two).astype(BF16)

    normed_two_all = jnp.concatenate(gather_blocks(normed_two), axis=0)
    cot_all = jnp.concatenate(cot_blocks, axis=0)
    grad_active = nt(cot_all, down_full)
    hidden = nn(normed_two_all, fc_full) + fc_shift
    active, gelu_pull = jax.vjp(lambda h: jax.nn.gelu(h, approximate=True), hidden)
    active = active.astype(BF16)
    grad_hidden = gelu_pull(grad_active)[0].astype(BF16)
    grad_two_terms = [
        nt(grad_hidden[k * piece : (k + 1) * piece], fc_full).astype(BF16) for k in range(seq_count)
    ]
    upstream_two = add_up(scatter_blocks(grad_two_terms))
    cot_f32 = cotangent[0].astype(F32)
    grad_middle = cot_f32 + norm_backward(unit_two, scale_two, gain_two, upstream_two)
    grad_mid_low = grad_middle.astype(BF16)
    grad_mid_blocks = gather_blocks(grad_mid_low)

    grad_down = tn(active, cot_all).astype(BF16)
    grad_down = lax.psum_scatter(grad_down, "dp", scatter_dimension=0, tiled=True).astype(F32)
    grad_fc = tn(normed_two_all, grad_hidden).astype(BF16)
    grad_fc = lax.psum_scatter(grad_fc, "dp", scatter_dimension=0, tiled=True)
    grad_fc = exchange(grad_fc.reshape(seq_count, rows, dp_count * block), seq_rank)
    grad_fc = jnp.stack([item.reshape(rows, dp_count, block) for item in grad_fc], axis=2)
    grad_fc = grad_fc.reshape(fc_weight.shape).astype(F32)
    down_terms = [
        nn(active[k * piece : (k + 1) * piece], down_full).astype(BF16) for k in range(seq_count)
    ]
    block_out = (middle + (add_up(scatter_blocks(down_terms)) + down_shift)).astype(BF16)

    grad_mid_all = jnp.concatenate(grad_mid_blocks, axis=0)
    grad_proj = tn(attended, grad_mid_all).astype(BF16)
    grad_proj = lax.psum_scatter(grad_proj, "dp", scatter_dimension=0, tiled=True)
    grad_proj = lax.ppermute(grad_proj, BOTH, swap).astype(F32)
    grad_attended = nt(grad_mid_all, proj_full).astype(BF16)
    grad_qkv = attend_backward(rank, qkv, grad_attended, lse, key_bias, piece)
    grad_qkv_weight = tn(normed_one, grad_qkv).astype(BF16)
    grad_qkv_weight = lax.psum_scatter(grad_qkv_weight, "dp", scatter_dimension=0, tiled=True)
    grad_qkv_weight = exchange(grad_qkv_weight.reshape(seq_count, rows, -1), seq_rank)
    grad_qkv_weight = (
        jnp.stack(grad_qkv_weight)
        .reshape(high, sub, rows, own_heads, 3, HEAD_DIM)
        .transpose(2, 4, 3, 1, 0, 5)
        .reshape(qkv_weight.shape)
        .astype(F32)
    )
    grad_one_terms = [
        nt(grad_qkv[k * piece : (k + 1) * piece], qkv_full).astype(BF16) for k in range(seq_count)
    ]
    upstream_one = add_up(scatter_blocks(grad_one_terms))
    unit_one, scale_one = norm_parts(own)
    tokens_grad = grad_middle + norm_backward(unit_one, scale_one, gain_one, upstream_one)

    def spread(vector):
        return vector.reshape(dp_count, seq_count, -1)

    def at_rank(vector):
        here = (jnp.arange(seq_count) == seq_rank).astype(F32)
        return vector.reshape(dp_count, 1, -1) * here[None, :, None]

    early = (
        spread(jnp.sum(grad_mid_low.astype(F32), axis=0)),
        spread(jnp.sum(upstream_two * unit_two, axis=0)),
        spread(jnp.sum(upstream_two, axis=0)),
        spread(jnp.sum(cot_f32, axis=0)),
        at_rank(jnp.sum(grad_hidden.astype(F32), axis=0)),
    )
    early = small_scatter(jnp.concatenate(early, axis=2), dp_rank, seq_rank)
    column_sums = jnp.sum(grad_qkv.astype(F32), axis=0).reshape(own_heads, 3, HEAD_DIM)
    qv_sums = jnp.stack([column_sums[:, 0], column_sums[:, 2]])[:, :, None, None, :]
    here = (jnp.arange(sub) == rank_low)[:, None] & (jnp.arange(high) == rank_high)[None, :]
    qv_sums = qv_sums * here.astype(F32)[None, None, :, :, None]
    late = (
        spread(jnp.sum(upstream_one * unit_one, axis=0)),
        spread(jnp.sum(upstream_one, axis=0)),
        spread(qv_sums),
    )
    late = small_scatter(jnp.concatenate(late, axis=2), dp_rank, seq_rank)
    share = attn_gain.shape[0]
    return (
        block_out[None],
        tokens_grad[None],
        late[:share],
        late[share : 2 * share],
        grad_qkv_weight,
        late[2 * share :],
        grad_proj,
        early[:share],
        early[share : 2 * share],
        early[2 * share : 3 * share],
        grad_fc,
        early[4 * share :],
        grad_down,
        early[3 * share : 4 * share],
    )


def solution(mesh):
    in_specs = (
        P("dp", "seq", None),
        P("dp", "seq", None),
        P("dp"),
        P("dp", "seq"),
        P(BOTH),
        P(BOTH),
        P(BOTH, None),
        P(BOTH),
        P(BOTH, None),
        P(BOTH),
        P(BOTH),
        P(BOTH),
        P(BOTH, None),
        P(BOTH),
        P(BOTH, None),
        P(BOTH),
    )
    out_specs = (
        P("dp", "seq", None),
        P("dp", "seq", None),
        P(BOTH),
        P(BOTH),
        P(BOTH, None),
        P(BOTH),
        P(BOTH, None),
        P(BOTH),
        P(BOTH),
        P(BOTH),
        P(BOTH, None),
        P(BOTH),
        P(BOTH, None),
        P(BOTH),
    )
    return jax.shard_map(shards, mesh=mesh, in_specs=in_specs, out_specs=out_specs, check_vma=False)
```

time: 5290 us -> 1250 us (0.24)
  waiting for transfers between devices: 4350 us -> 685 us
  blocking collectives: 183 us -> 0 us
  matrix products: 465 us -> 293 us
  local copies, waits for them, and re-layouts: 155 us -> 34.7 us
  starting transfers between devices: 0.9 us -> 97 us
  Pallas kernels: 0 us -> 79 us
  other arithmetic: 114 us -> 40.5 us
    reduce_scatter x6 -> x4, waiting for transfers between devices: 3900 us -> 0.01 us  [the longest x1 0.01 us: shards(): lax.psum_scatter(grad_proj, 'dp', scatter_dimension=0, tiled=True)]
    ppermute x0 -> x71, waiting for transfers between devices: none -> 684 us  [the longest x69 684 us: shift(): return lax.ppermute(value, axis, [(i, i ^ distance) for i in range(count)])]
    all_gather x6 -> x4, waiting for transfers between devices: 443 us -> 0.05 us  [the longest x1 0.02 us: shards(): qkv_full = lax.all_gather(qkv_rows, 'dp', axis=0, tiled=True)]
    dot_general x40 -> x24, matrix products: 465 us -> 293 us  [the longest x10 117 us: nt(): lax.dot_general(left, right, (((1,), (1,)), ((), ())), preferred_element_...]
    all_gather x3 -> x0, blocking collectives: 139 us -> none  [the longest x1 66.8 us: shards(): lax.all_gather(qv_bias, ('dp', 'seq'), axis=0, tiled=True)]
    ppermute x0 -> x71, starting transfers between devices: none -> 96.5 us  [the longest x69 94 us: shift(): return lax.ppermute(value, axis, [(i, i ^ distance) for i in range(count)])]
    pallas_call x0 -> x2, Pallas kernels: none -> 79 us  [the longest x1 48.3 us: attend_backward(): pl.pallas_call(backward_kernel, grid_spec=grid_spec, out_shape=jax.ShapeD...]
  transfers between devices with their start and end apart: 13 -> 79, of which waited for: 11 -> 26; matrix products, arithmetic and copies ran while one was open for 6% -> 22% of each run, Pallas kernels for 0% -> 6%
where the time goes in v1:
time: 1250 us; the launch traced here: 1240 us
  waiting for transfers between devices  685 us (55%)
  matrix products  293 us (23%)
  starting transfers between devices  97 us (8%)
  Pallas kernels  79 us (6%)
  other arithmetic  40.5 us (3%)
  local copies, waits for them, and re-layouts  34.7 us (3%)
  between operations  16.2 us (1%)
    ppermute x69, waiting for transfers between devices, shift(): return lax.ppermute(value, axis, [(i, i ^ distance) for i in range(count)])  684 us
    dot_general x10, matrix products, nt(): lax.dot_general(left, right, (((1,), (1,)), ((), ())), preferred_element_...  117 us
    dot_general x10, matrix products, nn(): lax.dot_general(left, right, (((1,), (0,)), ((), ())), preferred_element_...  101 us
    ppermute x69, starting transfers between devices, shift(): return lax.ppermute(value, axis, [(i, i ^ distance) for i in range(count)])  94 us
    dot_general x4, matrix products, tn(): lax.dot_general(left, right, (((0,), (0,)), ((), ())), preferred_element_...  74.8 us
    pallas_call x1, Pallas kernels, attend_backward(): pl.pallas_call(backward_kernel, grid_spec=grid_spec, out_shape=jax.ShapeD...  48.3 us
    pallas_call x1, Pallas kernels, attend(): pl.pallas_call(forward_kernel, grid_spec=grid_spec, out_shape=(jax.ShapeD...  30.7 us
  transfers between devices with their start and end apart: 79, of which 26 were waited for; matrix products, arithmetic and copies ran while one was open for 22% of the time, Pallas kernels for 6%

profile of v1, /device:TPU:0, one launch (start us, length us, event | category | flops | bytes accessed | tf_op | source)
XLA Modules:
  0.0 1244.8 jit_solution(5988172872464167552)
XLA Ops:
  28.9 8.3 collective-permute-start.28
  77.3 43.5 %collective-permute-done.2 = bf16[512,2048]{1,0:T(8,128)(2,1)} collective-permute-done((bf16[512,2048]{1,0:T(8,128)(2,1)S(1)}, bf16[512,2048]{1,0:T(8,128)(2,1)}, u32[]{:S(2)}, u32[]{:S(2)}) %collective-permute-start.2) | collective-permute-done | bytes 2097184 | tf_op jit(solution)/shard_map/ppermute | solution.py:208
  120.8 44.2 %collective-permute-done.1 = bf16[512,2048]{1,0:T(8,128)(2,1)} collective-permute-done((bf16[512,2048]{1,0:T(8,128)(2,1)S(1)}, bf16[512,2048]{1,0:T(8,128)(2,1)}, u32[]{:S(2)}, u32[]{:S(2)}) %collective-permute-start.1) | collective-permute-done | bytes 2097184 | tf_op jit(solution)/shard_map/ppermute | solution.py:208
  174.8 22.6 %add_convert_fusion.query_ref.key_ref.value_ref = bf16[2048,1536]{1,0:T(8,128)(2,1)} fusion(bf16[2048,1536]{1,0:T(8,128)(2,1)} %all-gather.5.cloned.1.call-done, f32[1536]{0:T(1024)S(1)} %add.323, f32[2048]{0:T(1024)S(1)} %add.313, f32[2048]{0:T(1024)S(1)} %mul.188, f32[2048]{0:T(1024)S(1)} %add_rsqrt_fusion, f32[2048]{0:T(1024)S(1)} %broadcast_multiply_fusion.2, ...), kind=kOutput, calls=%fused_computation.20 | convolution fusion | flops 12945719296 | bytes 21010432 | tf_op jit(solution)/shard_map/dot_general | solution.py:23
  197.4 30.7 %shard_map.263 = (bf16[2048,512]{1,0:T(8,128)(2,1)S(1)}, f32[4,1,2048]{2,1,0:T(1,128)S(1)}) custom-call(s32[1]{0:T(128)} %bitcast.1.rank_ref, bf16[2048,1536]{1,0:T(8,128)(2,1)} %add_convert_fusion.query_ref.key_ref.value_ref, bf16[2048,1536]{1,0:T(8,128)(2,1)} %add_convert_fusion.query_ref.key_ref.value_ref, ...), custom_call_target="tpu_custom_call" | custom-call | flops 8589934592 | bytes 9437184 | tf_op jit(solution)/shard_map/pallas_call | solution.py:101
  247.3 34.0 %collective-permute-done.20 = bf16[512,2048]{1,0:T(8,128)(2,1)} collective-permute-done((bf16[512,2048]{1,0:T(8,128)(2,1)}, bf16[512,2048]{1,0:T(8,128)(2,1)}, u32[]{:S(2)}, u32[]{:S(2)}) %collective-permute-start.20) | collective-permute-done | bytes 2097184 | tf_op jit(solution)/shard_map/ppermute | solution.py:208
  282.4 92.4 %collective-permute-done.21 = bf16[512,2048]{1,0:T(8,128)(2,1)} collective-permute-done((bf16[512,2048]{1,0:T(8,128)(2,1)}, bf16[512,2048]{1,0:T(8,128)(2,1)}, u32[]{:S(2)}, u32[]{:S(2)}) %collective-permute-start.21) | collective-permute-done | bytes 2097184 | tf_op jit(solution)/shard_map/ppermute | solution.py:208
  385.0 31.0 %collective-permute-done.32 = bf16[512,2048]{1,0:T(8,128)(2,1)S(1)} collective-permute-done((bf16[512,2048]{1,0:T(8,128)(2,1)}, bf16[512,2048]{1,0:T(8,128)(2,1)S(1)}, u32[]{:S(2)}, u32[]{:S(2)}) %collective-permute-start.32) | collective-permute-done | bytes 2097184 | tf_op jit(solution)/shard_map/ppermute | solution.py:208
  420.1 44.6 %collective-permute-done.33 = bf16[512,2048]{1,0:T(8,128)(2,1)S(1)} collective-permute-done((bf16[512,2048]{1,0:T(8,128)(2,1)S(1)}, bf16[512,2048]{1,0:T(8,128)(2,1)S(1)}, u32[]{:S(2)}, u32[]{:S(2)}) %collective-permute-start.33) | collective-permute-done | bytes 2097184 | tf_op jit(solution)/shard_map/ppermute | solution.py:208
  467.8 41.1 %collective-permute-done.24 = bf16[512,2048]{1,0:T(8,128)(2,1)} collective-permute-done((bf16[512,2048]{1,0:T(8,128)(2,1)}, bf16[512,2048]{1,0:T(8,128)(2,1)}, u32[]{:S(2)}, u32[]{:S(2)}) %collective-permute-start.24) | collective-permute-done | bytes 2097184 | tf_op jit(solution)/shard_map/ppermute | solution.py:208
  508.9 28.1 %fusion.40 = f32[2048,2048]{1,0:T(8,128)} fusion(bf16[2048,2048]{1,0:T(8,128)(2,1)} %all-gather.9.cloned.1.call-done, bf16[512,2048]{1,0:T(8,128)(2,1)} %collective-permute-done.25, bf16[512,2048]{1,0:T(8,128)(2,1)} %collective-permute-done.24, bf16[512,2048]{1,0:T(8,128)(2,1)} %collective-permute-done.23, bf16[512,2048]{1,0:T(8,128)(2,1)} %add_convert_fusion.2), kind=kOutput, calls=%fused_computation.86 | convolution fusion | flops 17213423616 | bytes 33554432 | tf_op jit(solution)/shard_map/dot_general | solution.py:23
  537.0 38.4 %convert_reduce_fusion.1 = (f32[2048]{0:T(1024)}, bf16[2048,2048]{1,0:T(8,128)(2,1)}, bf16[2048,2048]{1,0:T(8,128)(2,1)}) fusion(f32[2048,2048]{1,0:T(8,128)} %fusion.40, f32[2048]{0:T(1024)S(1)} %bitcast.259, bf16[2048,2048]{1,0:T(8,128)(2,1)} %constant_dynamic-update-slice_fusion.8, bf16[2048,2048]{1,0:T(8,128)(2,1)} %all-gather.11.cloned.1.call-done), kind=kOutput, calls=%fused_computation.17 | convolution fusion | flops 17284724736 | bytes 50348032 | tf_op jit(solution)/shard_map/dot_general | solution.py:27
  575.4 10.0 convolution_convert_fusion.11
  604.2 30.1 %collective-permute-done.35 = bf16[512,2048]{1,0:T(8,128)(2,1)} collective-permute-done((bf16[512,2048]{1,0:T(8,128)(2,1)}, bf16[512,2048]{1,0:T(8,128)(2,1)}, u32[]{:S(2)}, u32[]{:S(2)}) %collective-permute-start.35) | collective-permute-done | bytes 2097184 | tf_op jit(solution)/shard_map/ppermute | solution.py:208
  634.3 50.6 %collective-permute-done.36 = bf16[512,2048]{1,0:T(8,128)(2,1)} collective-permute-done((bf16[512,2048]{1,0:T(8,128)(2,1)}, bf16[512,2048]{1,0:T(8,128)(2,1)}, u32[]{:S(2)}, u32[]{:S(2)}) %collective-permute-start.36) | collective-permute-done | bytes 2097184 | tf_op jit(solution)/shard_map/ppermute | solution.py:208
  684.9 14.5 %multiply_reduce_fusion = (f32[2048]{0:T(1024)}, f32[512]{0:T(512)S(1)}, f32[512]{0:T(512)S(1)}, f32[2048]{0:T(1024)}, f32[512,2048]{1,0:T(8,128)}) fusion(f32[512,2048]{1,0:T(8,128)S(1)} %copy-done.1, f32[512]{0:T(512)S(1)} %add_rsqrt_fusion.2, f32[512]{0:T(512)S(1)} %broadcast_multiply_fusion.8, f32[2048]{0:T(1024)S(1)} %mul.195, ...), kind=kOutput, calls=%fused_computation.44 | convolution fusion | flops 4312787968 | bytes 25198592 | tf_op jit(solution)/shard_map/dot_general | solution.py:27
  709.0 46.0 %collective-permute-done.40 = bf16[512,2048]{1,0:T(8,128)(2,1)S(1)} collective-permute-done((bf16[512,2048]{1,0:T(8,128)(2,1)S(1)}, bf16[512,2048]{1,0:T(8,128)(2,1)S(1)}, u32[]{:S(2)}, u32[]{:S(2)}) %collective-permute-start.40) | collective-permute-done | bytes 2097184 | tf_op jit(solution)/shard_map/ppermute | solution.py:208
  755.0 41.8 %collective-permute-done.39 = bf16[512,2048]{1,0:T(8,128)(2,1)S(1)} collective-permute-done((bf16[512,2048]{1,0:T(8,128)(2,1)S(1)}, bf16[512,2048]{1,0:T(8,128)(2,1)S(1)}, u32[]{:S(2)}, u32[]{:S(2)}) %collective-permute-start.39) | collective-permute-done | bytes 2097184 | tf_op jit(solution)/shard_map/ppermute | solution.py:208
  805.5 9.6 convolution_convert_fusion.8.grad_ref
  815.2 48.3 %shard_map.264 = bf16[2048,1536]{1,0:T(8,128)(2,1)} custom-call(s32[1]{0:T(128)} %bitcast.1.rank_ref, bf16[2048,1536]{1,0:T(8,128)(2,1)} %add_convert_fusion.query_ref.key_ref.value_ref, bf16[2048,512]{1,0:T(8,128)(2,1)S(1)} %convolution_convert_fusion.8.grad_ref, f32[4,1,2048]{2,1,0:T(1,128)S(1)} %get-tuple-element.21.lse_ref, ...), custom_call_target="tpu_custom_call" | custom-call | flops 21474836480 | bytes 18874368 | tf_op jit(solution)/shard_map/pallas_call | solution.py:193
  863.5 20.8 %convolution_convert_fusion.2 = bf16[2048,1536]{1,0:T(8,128)(2,1)} fusion(bf16[2048,1536]{1,0:T(8,128)(2,1)} %shard_map.264, f32[2048]{0:T(1024)S(1)} %copy-done.23, f32[2048]{0:T(1024)S(1)} %copy-done.14, f32[2048]{0:T(1024)S(1)} %copy-done.27, f32[2048]{0:T(1024)S(1)} %copy-done.18, bf16[512,2048]{1,0:T(8,128)(2,1)} %collective-permute-done.2, ...), kind=kOutput, calls=%fused_computation.26 | convolution fusion | flops 12942573568 | bytes 21004288 | tf_op jit(solution)/shard_map/dot_general | solution.py:31
  884.3 23.7 %convolution_convert_fusion.1 = bf16[2048,2048]{1,0:T(8,128)(2,1)} fusion(bf16[2048,2048]{1,0:T(8,128)(2,1)} %get-tuple-element.31, bf16[512,2048]{1,0:T(8,128)(2,1)} %collective-permute-done.25, bf16[512,2048]{1,0:T(8,128)(2,1)} %collective-permute-done.24, bf16[512,2048]{1,0:T(8,128)(2,1)} %collective-permute-done.23, bf16[512,2048]{1,0:T(8,128)(2,1)} %add_convert_fusion.2), kind=kOutput, calls=%fused_computation.25 | convolution fusion | flops 17217617920 | bytes 25165824 | tf_op jit(solution)/shard_map/dot_general | solution.py:31
  908.1 24.2 %convolution_convert_fusion = bf16[2048,2048]{1,0:T(8,128)(2,1)} fusion(bf16[2048,2048]{1,0:T(8,128)(2,1)} %get-tuple-element.47, bf16[2048,2048]{1,0:T(8,128)(2,1)} %constant_dynamic-update-slice_fusion.8), kind=kOutput, calls=%fused_computation.24 | convolution fusion | flops 17184063488 | bytes 25165824 | tf_op jit(solution)/shard_map/dot_general | solution.py:31
  933.2 10.0 convolution_convert_fusion.15
  945.2 9.9 convolution_convert_fusion.14
  957.6 9.8 convolution_convert_fusion.13
  968.7 23.5 %collective-permute-done.58 = f32[8,512]{1,0:T(8,128)S(1)} collective-permute-done((f32[8,512]{1,0:T(8,128)S(1)}, f32[8,512]{1,0:T(8,128)S(1)}, u32[]{:S(2)}, u32[]{:S(2)}) %collective-permute-start.58) | collective-permute-done | bytes 16416 | tf_op jit(solution)/shard_map/ppermute | solution.py:208
  994.2 54.1 %collective-permute-done.59 = f32[8,512]{1,0:T(8,128)S(1)} collective-permute-done((f32[8,512]{1,0:T(8,128)S(1)}, f32[8,512]{1,0:T(8,128)S(1)}, u32[]{:S(2)}, u32[]{:S(2)}) %collective-permute-start.59) | collective-permute-done | bytes 16416 | tf_op jit(solution)/shard_map/ppermute | solution.py:208
  1078.2 8.6 fusion.25
  1089.0 34.4 %collective-permute-done.41 = bf16[512,2048]{1,0:T(8,128)(2,1)} collective-permute-done((bf16[512,2048]{1,0:T(8,128)(2,1)}, bf16[512,2048]{1,0:T(8,128)(2,1)}, u32[]{:S(2)}, u32[]{:S(2)}) %collective-permute-start.41) | collective-permute-done | bytes 2097184 | tf_op jit(solution)/shard_map/ppermute | solution.py:208
  1123.5 44.0 %collective-permute-done.42 = bf16[512,2048]{1,0:T(8,128)(2,1)} collective-permute-done((bf16[512,2048]{1,0:T(8,128)(2,1)}, bf16[512,2048]{1,0:T(8,128)(2,1)}, u32[]{:S(2)}, u32[]{:S(2)}) %collective-permute-start.42) | collective-permute-done | bytes 2097184 | tf_op jit(solution)/shard_map/ppermute | solution.py:208
  1167.5 11.4 fusion.23
  (392 shorter events, 244.6 us)
Async XLA Ops:
  7.2 167.5 %all-gather.5.cloned.1.call-start = ((), (), s32[]{:S(2)}) async-start(), calls=%async_computation.4 | async-start | bytes 7077888 | tf_op jit(solution)/shard_map/all_gather | solution.py:317
  25.7 202.5 %all-gather.7.cloned.1.call-start = ((), (), s32[]{:S(2)}) async-start(), calls=%async_computation.5 | async-start | bytes 2359296 | tf_op jit(solution)/shard_map/all_gather | solution.py:320
  27.2 440.6 %all-gather.9.cloned.1.call-start = ((), (), s32[]{:S(2)}) async-start(), calls=%async_computation.6 | async-start | bytes 9437184 | tf_op jit(solution)/shard_map/all_gather | solution.py:328
  50.8 486.2 %all-gather.11.cloned.1.call-start = ((), (), s32[]{:S(2)}) async-start(), calls=%async_computation.7 | async-start | bytes 9437184 | tf_op jit(solution)/shard_map/all_gather | solution.py:321
  58.2 1141.5 %reduce-scatter.7.cloned.1.call-start = ((), (), s32[]{:S(2)}) async-start(), calls=%async_computation.9 | async-start | bytes 2359296 | tf_op jit(solution)/shard_map/reduce_scatter | solution.py:398
  71.3 49.6 %collective-permute-start.2 = (bf16[512,2048]{1,0:T(8,128)(2,1)S(1)}, bf16[512,2048]{1,0:T(8,128)(2,1)}, u32[]{:S(2)}, u32[]{:S(2)}) collective-permute-start(bf16[512,2048]{1,0:T(8,128)(2,1)S(1)} %bitcast.224), channel_id=1, source_target_pairs={{0,3},{1,2},{2,1},{3,0},{4,7},{5,6},{6,5},{7,4},{8,11},{9,10},{10,... | collective-permute-start | bytes 6291464 | tf_op jit(solution)/shard_map/ppermute | solution.py:208
  72.5 92.5 %collective-permute-start.1 = (bf16[512,2048]{1,0:T(8,128)(2,1)S(1)}, bf16[512,2048]{1,0:T(8,128)(2,1)}, u32[]{:S(2)}, u32[]{:S(2)}) collective-permute-start(bf16[512,2048]{1,0:T(8,128)(2,1)S(1)} %bitcast.225), channel_id=1, source_target_pairs={{0,2},{1,3},{2,0},{3,1},{4,6},{5,7},{6,4},{7,5},{8,10},{9,11},{10,... | collective-permute-start | bytes 6291464 | tf_op jit(solution)/shard_map/ppermute | solution.py:208
  73.3 91.7 %collective-permute-start = (bf16[512,2048]{1,0:T(8,128)(2,1)S(1)}, bf16[512,2048]{1,0:T(8,128)(2,1)}, u32[]{:S(2)}, u32[]{:S(2)}) collective-permute-start(bf16[512,2048]{1,0:T(8,128)(2,1)S(1)} %bitcast.226), channel_id=1, source_target_pairs={{0,1},{1,0},{2,3},{3,2},{4,5},{5,4},{6,7},{7,6},{8,9},{9,8},{10,11... | collective-permute-start | bytes 6291464 | tf_op jit(solution)/shard_map/ppermute | solution.py:208
  235.9 138.9 %collective-permute-start.21 = (bf16[512,2048]{1,0:T(8,128)(2,1)}, bf16[512,2048]{1,0:T(8,128)(2,1)}, u32[]{:S(2)}, u32[]{:S(2)}) collective-permute-start(bf16[512,2048]{1,0:T(8,128)(2,1)} %convolution_convert_fusion.18), channel_id=1, source_target_pairs={{0,2},{1,3},{2,0},{3,1},{4,6},{5,7},{6,4},{7,5},{8,10},{9,11},{10,... | collective-permute-start | bytes 6291464 | tf_op jit(solution)/shard_map/ppermute | solution.py:208
  240.8 134.1 %collective-permute-start.22 = (bf16[512,2048]{1,0:T(8,128)(2,1)}, bf16[512,2048]{1,0:T(8,128)(2,1)}, u32[]{:S(2)}, u32[]{:S(2)}) collective-permute-start(bf16[512,2048]{1,0:T(8,128)(2,1)} %convolution_convert_fusion.17), channel_id=1, source_target_pairs={{0,3},{1,2},{2,1},{3,0},{4,7},{5,6},{6,5},{7,4},{8,11},{9,10},{10,... | collective-permute-start | bytes 6291464 | tf_op jit(solution)/shard_map/ppermute | solution.py:208
  241.7 224.5 %collective-permute-start.34 = (bf16[512,2048]{1,0:T(8,128)(2,1)}, bf16[512,2048]{1,0:T(8,128)(2,1)S(1)}, u32[]{:S(2)}, u32[]{:S(2)}) collective-permute-start(bf16[512,2048]{1,0:T(8,128)(2,1)} %bitcast.232), channel_id=1, source_target_pairs={{0,3},{1,2},{2,1},{3,0},{4,7},{5,6},{6,5},{7,4},{8,11},{9,10},{10,... | collective-permute-start | bytes 6291464 | tf_op jit(solution)/shard_map/ppermute | solution.py:208
  244.4 171.7 %collective-permute-start.32 = (bf16[512,2048]{1,0:T(8,128)(2,1)}, bf16[512,2048]{1,0:T(8,128)(2,1)S(1)}, u32[]{:S(2)}, u32[]{:S(2)}) collective-permute-start(bf16[512,2048]{1,0:T(8,128)(2,1)} %bitcast.233), channel_id=1, source_target_pairs={{0,1},{1,0},{2,3},{3,2},{4,5},{5,4},{6,7},{7,6},{8,9},{9,8},{10,11... | collective-permute-start | bytes 6291464 | tf_op jit(solution)/shard_map/ppermute | solution.py:208
  281.3 183.4 %collective-permute-start.33 = (bf16[512,2048]{1,0:T(8,128)(2,1)S(1)}, bf16[512,2048]{1,0:T(8,128)(2,1)S(1)}, u32[]{:S(2)}, u32[]{:S(2)}) collective-permute-start(bf16[512,2048]{1,0:T(8,128)(2,1)S(1)} %bitcast.234), channel_id=1, source_target_pairs={{0,2},{1,3},{2,0},{3,1},{4,6},{5,7},{6,4},{7,5},{8,10},{9,11},{10,... | collective-permute-start | bytes 6291464 | tf_op jit(solution)/shard_map/ppermute | solution.py:208
  382.6 85.2 %collective-permute-start.25 = (bf16[512,2048]{1,0:T(8,128)(2,1)}, bf16[512,2048]{1,0:T(8,128)(2,1)}, u32[]{:S(2)}, u32[]{:S(2)}) collective-permute-start(bf16[512,2048]{1,0:T(8,128)(2,1)} %add_convert_fusion.2), channel_id=1, source_target_pairs={{0,3},{1,2},{2,1},{3,0},{4,7},{5,6},{6,5},{7,4},{8,11},{9,10},{10,... | collective-permute-start | bytes 6291464 | tf_op jit(solution)/shard_map/ppermute | solution.py:208
  384.2 124.7 %collective-permute-start.24 = (bf16[512,2048]{1,0:T(8,128)(2,1)}, bf16[512,2048]{1,0:T(8,128)(2,1)}, u32[]{:S(2)}, u32[]{:S(2)}) collective-permute-start(bf16[512,2048]{1,0:T(8,128)(2,1)} %add_convert_fusion.2), channel_id=1, source_target_pairs={{0,2},{1,3},{2,0},{3,1},{4,6},{5,7},{6,4},{7,5},{8,10},{9,11},{10,... | collective-permute-start | bytes 6291464 | tf_op jit(solution)/shard_map/ppermute | solution.py:208
  416.0 92.8 %collective-permute-start.23 = (bf16[512,2048]{1,0:T(8,128)(2,1)}, bf16[512,2048]{1,0:T(8,128)(2,1)}, u32[]{:S(2)}, u32[]{:S(2)}) collective-permute-start(bf16[512,2048]{1,0:T(8,128)(2,1)} %add_convert_fusion.2), channel_id=1, source_target_pairs={{0,1},{1,0},{2,3},{3,2},{4,5},{5,4},{6,7},{7,6},{8,9},{9,8},{10,11... | collective-permute-start | bytes 6291464 | tf_op jit(solution)/shard_map/ppermute | solution.py:208
  585.4 48.9 %collective-permute-start.35 = (bf16[512,2048]{1,0:T(8,128)(2,1)}, bf16[512,2048]{1,0:T(8,128)(2,1)}, u32[]{:S(2)}, u32[]{:S(2)}) collective-permute-start(bf16[512,2048]{1,0:T(8,128)(2,1)} %convolution_convert_fusion.11), channel_id=1, source_target_pairs={{0,1},{1,0},{2,3},{3,2},{4,5},{5,4},{6,7},{7,6},{8,9},{9,8},{10,11... | collective-permute-start | bytes 6291464 | tf_op jit(solution)/shard_map/ppermute | solution.py:208
  593.3 91.6 %collective-permute-start.36 = (bf16[512,2048]{1,0:T(8,128)(2,1)}, bf16[512,2048]{1,0:T(8,128)(2,1)}, u32[]{:S(2)}, u32[]{:S(2)}) collective-permute-start(bf16[512,2048]{1,0:T(8,128)(2,1)} %convolution_convert_fusion.10), channel_id=1, source_target_pairs={{0,2},{1,3},{2,0},{3,1},{4,6},{5,7},{6,4},{7,5},{8,10},{9,11},{10,... | collective-permute-start | bytes 6291464 | tf_op jit(solution)/shard_map/ppermute | solution.py:208
  602.5 82.3 %collective-permute-start.37 = (bf16[512,2048]{1,0:T(8,128)(2,1)}, bf16[512,2048]{1,0:T(8,128)(2,1)}, u32[]{:S(2)}, u32[]{:S(2)}) collective-permute-start(bf16[512,2048]{1,0:T(8,128)(2,1)} %convolution_convert_fusion.9), channel_id=1, source_target_pairs={{0,3},{1,2},{2,1},{3,0},{4,7},{5,6},{6,5},{7,4},{8,11},{9,10},{10,... | collective-permute-start | bytes 6291464 | tf_op jit(solution)/shard_map/ppermute | solution.py:208
  705.5 49.5 %collective-permute-start.40 = (bf16[512,2048]{1,0:T(8,128)(2,1)S(1)}, bf16[512,2048]{1,0:T(8,128)(2,1)S(1)}, u32[]{:S(2)}, u32[]{:S(2)}) collective-permute-start(bf16[512,2048]{1,0:T(8,128)(2,1)S(1)} %get-tuple-element.33), channel_id=1, source_target_pairs={{0,3},{1,2},{2,1},{3,0},{4,7},{5,6},{6,5},{7,4},{8,11},{9,10},{10,... | collective-permute-start | bytes 6291464 | tf_op jit(solution)/shard_map/ppermute | solution.py:208
  708.1 88.6 %collective-permute-start.39 = (bf16[512,2048]{1,0:T(8,128)(2,1)S(1)}, bf16[512,2048]{1,0:T(8,128)(2,1)S(1)}, u32[]{:S(2)}, u32[]{:S(2)}) collective-permute-start(bf16[512,2048]{1,0:T(8,128)(2,1)S(1)} %get-tuple-element.33), channel_id=1, source_target_pairs={{0,2},{1,3},{2,0},{3,1},{4,6},{5,7},{6,4},{7,5},{8,10},{9,11},{10,... | collective-permute-start | bytes 6291464 | tf_op jit(solution)/shard_map/ppermute | solution.py:208
  708.7 88.5 %collective-permute-start.38 = (bf16[512,2048]{1,0:T(8,128)(2,1)S(1)}, bf16[512,2048]{1,0:T(8,128)(2,1)S(1)}, u32[]{:S(2)}, u32[]{:S(2)}) collective-permute-start(bf16[512,2048]{1,0:T(8,128)(2,1)S(1)} %get-tuple-element.33), channel_id=1, source_target_pairs={{0,1},{1,0},{2,3},{3,2},{4,5},{5,4},{6,7},{7,6},{8,9},{9,8},{10,11... | collective-permute-start | bytes 6291464 | tf_op jit(solution)/shard_map/ppermute | solution.py:208
  805.4 398.1 %reduce-scatter.5.cloned.1.call-start = ((), (), s32[]{:S(2)}) async-start(), calls=%async_computation.8 | async-start | bytes 7077888 | tf_op jit(solution)/shard_map/reduce_scatter | solution.py:403
  884.3 328.6 %reduce-scatter.9.cloned.1.call-start = ((), (), s32[]{:S(2)}) async-start(), calls=%async_computation.10 | async-start | bytes 9437184 | tf_op jit(solution)/shard_map/reduce_scatter | solution.py:387
  908.1 308.4 %reduce-scatter.11.cloned.1.call-start = ((), (), s32[]{:S(2)}) async-start(), calls=%async_computation.11 | async-start | bytes 9437184 | tf_op jit(solution)/shard_map/reduce_scatter | solution.py:385
  943.2 118.5 %collective-permute-start.29 = (bf16[512,2048]{1,0:T(8,128)(2,1)}, bf16[512,2048]{1,0:T(8,128)(2,1)}, u32[]{:S(2)}, u32[]{:S(2)}) collective-permute-start(bf16[512,2048]{1,0:T(8,128)(2,1)} %convolution_convert_fusion.15), channel_id=1, source_target_pairs={{0,1},{1,0},{2,3},{3,2},{4,5},{5,4},{6,7},{7,6},{8,9},{9,8},{10,11... | collective-permute-start | bytes 6291464 | tf_op jit(solution)/shard_map/ppermute | solution.py:208
  955.1 106.9 %collective-permute-start.30 = (bf16[512,2048]{1,0:T(8,128)(2,1)}, bf16[512,2048]{1,0:T(8,128)(2,1)}, u32[]{:S(2)}, u32[]{:S(2)}) collective-permute-start(bf16[512,2048]{1,0:T(8,128)(2,1)} %convolution_convert_fusion.14), channel_id=1, source_target_pairs={{0,2},{1,3},{2,0},{3,1},{4,6},{5,7},{6,4},{7,5},{8,10},{9,11},{10,... | collective-permute-start | bytes 6291464 | tf_op jit(solution)/shard_map/ppermute | solution.py:208
  967.4 94.6 %collective-permute-start.31 = (bf16[512,2048]{1,0:T(8,128)(2,1)S(1)}, bf16[512,2048]{1,0:T(8,128)(2,1)S(1)}, u32[]{:S(2)}, u32[]{:S(2)}) collective-permute-start(bf16[512,2048]{1,0:T(8,128)(2,1)S(1)} %convolution_convert_fusion.13), channel_id=1, source_target_pairs={{0,3},{1,2},{2,1},{3,0},{4,7},{5,6},{6,5},{7,4},{8,11},{9,10},{10,... | collective-permute-start | bytes 6291464 | tf_op jit(solution)/shard_map/ppermute | solution.py:208
  968.6 79.7 %collective-permute-start.59 = (f32[8,512]{1,0:T(8,128)S(1)}, f32[8,512]{1,0:T(8,128)S(1)}, u32[]{:S(2)}, u32[]{:S(2)}) collective-permute-start(f32[8,512]{1,0:T(8,128)S(1)} %bitcast.256), channel_id=1, source_target_pairs={{0,2},{1,3},{2,0},{3,1},{4,6},{5,7},{6,4},{7,5},{8,10},{9,11},{10,... | collective-permute-start | bytes 49160 | tf_op jit(solution)/shard_map/ppermute | solution.py:208
  992.2 56.1 %collective-permute-start.60 = (f32[8,512]{1,0:T(8,128)S(1)}, f32[8,512]{1,0:T(8,128)S(1)}, u32[]{:S(2)}, u32[]{:S(2)}) collective-permute-start(f32[8,512]{1,0:T(8,128)S(1)} %bitcast.254), channel_id=1, source_target_pairs={{0,3},{1,2},{2,1},{3,0},{4,7},{5,6},{6,5},{7,4},{8,11},{9,10},{10,... | collective-permute-start | bytes 49160 | tf_op jit(solution)/shard_map/ppermute | solution.py:208
  1074.8 92.6 %collective-permute-start.42 = (bf16[512,2048]{1,0:T(8,128)(2,1)}, bf16[512,2048]{1,0:T(8,128)(2,1)}, u32[]{:S(2)}, u32[]{:S(2)}) collective-permute-start(bf16[512,2048]{1,0:T(8,128)(2,1)} %convolution_convert_fusion.5), channel_id=1, source_target_pairs={{0,2},{1,3},{2,0},{3,1},{4,6},{5,7},{6,4},{7,5},{8,10},{9,11},{10,... | collective-permute-start | bytes 6291464 | tf_op jit(solution)/shard_map/ppermute | solution.py:208
  1076.4 91.1 %collective-permute-start.43 = (bf16[512,2048]{1,0:T(8,128)(2,1)}, bf16[512,2048]{1,0:T(8,128)(2,1)}, u32[]{:S(2)}, u32[]{:S(2)}) collective-permute-start(bf16[512,2048]{1,0:T(8,128)(2,1)} %convolution_convert_fusion.4), channel_id=1, source_target_pairs={{0,3},{1,2},{2,1},{3,0},{4,7},{5,6},{6,5},{7,4},{8,11},{9,10},{10,... | collective-permute-start | bytes 6291464 | tf_op jit(solution)/shard_map/ppermute | solution.py:208
  (97 other events, 2592.5 us)
Sparse Core Ops, SparseCore 0:
  25.8 66.0 all-gather.4
  94.0 27.7 all-gather.6
  123.9 81.5 all-gather.8
  207.0 80.5 all-gather.10
  805.6 36.5 reduce-scatter.6
  884.4 70.6 reduce-scatter.4
  957.4 87.9 reduce-scatter.8
  1047.7 88.1 reduce-scatter.10

commit v2 on v1

v2 whole, which is shorter than its diff:
```python
import functools
import math

import jax
import jax.numpy as jnp
from jax import lax
from jax.experimental import pallas as pl
from jax.experimental.pallas import tpu as pltpu
from jax.sharding import PartitionSpec as P

HEADS = 16
HEAD_DIM = 128
EPS = 1e-05
NEG = -1e30
FACTOR = HEAD_DIM ** (-0.5)
LOG2E = math.log2(math.e)
F32 = jnp.float32
BF16 = jnp.bfloat16
BOTH = ("dp", "seq")


def nn(left, right):
    return lax.dot_general(left, right, (((1,), (0,)), ((), ())), preferred_element_type=F32)


def nt(left, right):
    return lax.dot_general(left, right, (((1,), (1,)), ((), ())), preferred_element_type=F32)


def tn(left, right):
    return lax.dot_general(left, right, (((0,), (0,)), ((), ())), preferred_element_type=F32)


def params(limit_mib=56):
    return pltpu.CompilerParams(dimension_semantics=("arbitrary",), vmem_limit_bytes=limit_mib * 2**20)


def cost(flops, moved, exps=0):
    return pl.CostEstimate(flops=int(flops), bytes_accessed=int(moved), transcendentals=int(exps))


def call_on_block(kernel, grid, inputs, fresh, shared, previous, scratch, estimate, rank=None):
    arrays = [item for item, _ in inputs]
    specs = [spec for _, spec in inputs]
    aliases = {}
    lead = 0 if rank is None else 1
    if previous is not None:
        for at, item in enumerate(previous):
            aliases[lead + len(arrays)] = len(fresh) + at
            arrays.append(item)
            specs.append(pl.BlockSpec(memory_space=pl.ANY))
    count = len(inputs)
    skipped = 0 if previous is None else len(previous)

    def body(*refs):
        refs = list(refs)
        kernel(*refs[: lead + count], *refs[lead + count + skipped :])

    out_specs = [spec for _, spec in fresh] + [spec for _, spec in shared]
    out_shape = [shape for shape, _ in fresh] + [shape for shape, _ in shared]
    if rank is None:
        results = pl.pallas_call(
            body, grid=grid, in_specs=specs, out_specs=out_specs, out_shape=out_shape, scratch_shapes=scratch,
            input_output_aliases=aliases, compiler_params=params(), cost_estimate=estimate,
        )(*arrays)
    else:
        results = pl.pallas_call(
            body,
            grid_spec=pltpu.PrefetchScalarGridSpec(
                num_scalar_prefetch=1, grid=grid, in_specs=specs, out_specs=out_specs, scratch_shapes=scratch
            ),
            out_shape=out_shape, input_output_aliases=aliases, compiler_params=params(), cost_estimate=estimate,
        )(rank, *arrays)
    return results[: len(fresh)], results[len(fresh) :]


def norm_parts(values):
    average = jnp.mean(values, axis=-1, keepdims=True)
    centred = values - average
    scale = lax.rsqrt(jnp.mean(centred * centred, axis=-1, keepdims=True) + EPS)
    return centred * scale, scale


def norm_backward(normed, scale, gain, upstream):
    weighted = upstream * gain
    return scale * (
        weighted
        - jnp.mean(weighted, axis=-1, keepdims=True)
        - normed * jnp.mean(weighted * normed, axis=-1, keepdims=True)
    )


def project_kernel(x, gain, shift_, wq, wk, wv, bias, normed, q, k, v, k_t, v_t):
    columns = wq.shape[1]
    rows = (norm_parts(x[...].astype(F32))[0] * gain[...] + shift_[...]).astype(BF16)
    normed[...] = rows
    q[...] = (nn(rows, wq[...]) + bias[:, :columns]).astype(BF16)
    keys = nn(rows, wk[...])
    k[...] = keys.astype(BF16)
    k_t[...] = keys.T.astype(BF16)
    values = nn(rows, wv[...]) + bias[:, columns:]
    v[...] = values.astype(BF16)
    v_t[...] = values.T.astype(BF16)


def project(at, x, gain, shift_, weights, bias, count, previous):
    piece, width = x.shape
    columns = weights[0].shape[1]
    tile = min(256, piece)
    steps = piece // tile
    whole = lambda shape: pl.BlockSpec(shape, lambda i: (0, 0))
    rows = lambda n: pl.BlockSpec((tile, n), lambda i: (at * steps + i, 0))
    turned = pl.BlockSpec((columns, tile), lambda i: (0, at * steps + i))
    length = piece * count
    inputs = [
        (x, pl.BlockSpec((tile, width), lambda i: (i, 0))),
        (gain, whole((1, width))),
        (shift_, whole((1, width))),
        *[(item, whole((width, columns))) for item in weights],
        (bias, whole((1, 2 * columns))),
    ]
    shape = lambda *dims: jax.ShapeDtypeStruct(dims, BF16)
    shared = [(shape(length, width), rows(width))] + [(shape(length, columns), rows(columns))] * 3
    shared += [(shape(columns, length), turned)] * 2
    return call_on_block(
        project_kernel, (steps,), inputs, [], shared, previous, [],
        cost(6 * piece * width * columns, 4 * piece * width + 6 * width * columns + 10 * piece * columns),
    )[1]


def rows_of(block, piece):
    return pl.ds(pl.multiple_of(block * piece, piece), piece)


def scores_of(key_ref, bias_ref, query, rel, piece, diagonal):
    rows = rows_of(rel, piece)
    scores = nt(key_ref[rows, :], query) * (FACTOR * LOG2E)
    key_bias = bias_ref[rows, :]
    if not diagonal:
        return scores + key_bias
    key_at = lax.broadcasted_iota(jnp.int32, scores.shape, 0)
    query_at = lax.broadcasted_iota(jnp.int32, scores.shape, 1)
    allowed = ((key_at < query_at) & (key_bias > -1.0)) | (key_at == query_at)
    return jnp.where(allowed, scores, NEG)


def attend_kernel(at, rank_ref, query_ref, key_ref, value_t, bias_ref, proj_ref, part_ref, attended, lse_ref, score_ref, sum_ref):
    piece = query_ref.shape[0]
    rank = rank_ref[0]
    head = pl.program_id(0)
    true = lax.bitwise_xor(at, rank)
    query = query_ref[...]

    def first(block, top):
        scores = scores_of(key_ref, bias_ref, query, lax.bitwise_xor(block, rank), piece, False)
        score_ref[rows_of(block, piece), :] = scores
        return jnp.maximum(top, jnp.max(scores, axis=0, keepdims=True))

    last = scores_of(key_ref, bias_ref, query, at, piece, True)
    top = lax.fori_loop(0, true, first, jnp.max(last, axis=0, keepdims=True))

    def weigh(scores, rel):
        weights = jnp.exp2(scores - top)
        return jnp.sum(weights, axis=0, keepdims=True), nn(value_t[:, rows_of(rel, piece)], weights.astype(BF16))

    def second(block, carry):
        total, out = carry
        more, part = weigh(score_ref[rows_of(block, piece), :], lax.bitwise_xor(block, rank))
        return total + more, out + part

    total, out = lax.fori_loop(0, true, second, weigh(last, at))
    result = (out / total).T.astype(BF16)
    attended[...] = result
    lse_ref[0] = top + jnp.log2(total)
    term = nn(result, proj_ref[...])

    @pl.when(head == 0)
    def _():
        sum_ref[...] = term

    @pl.when(head > 0)
    def _():
        sum_ref[...] += term

    @pl.when(head == pl.num_programs(0) - 1)
    def _():
        part_ref[...] = sum_ref[...].astype(BF16)


def attend(at, rank, q, k, v_t, key_bias, proj, piece, previous):
    length, columns = q.shape
    heads, width = columns // HEAD_DIM, proj.shape[1]
    inputs = [
        (q, pl.BlockSpec((piece, HEAD_DIM), lambda h, r: (at, h))),
        (k, pl.BlockSpec((length, HEAD_DIM), lambda h, r: (0, h))),
        (v_t, pl.BlockSpec((HEAD_DIM, length), lambda h, r: (h, 0))),
        (key_bias, pl.BlockSpec((length, 1), lambda h, r: (0, 0))),
        (proj, pl.BlockSpec((HEAD_DIM, width), lambda h, r: (h, 0))),
    ]
    fresh = [(jax.ShapeDtypeStruct((piece, width), BF16), pl.BlockSpec((piece, width), lambda h, r: (0, 0)))]
    shared = [
        (jax.ShapeDtypeStruct((length, columns), BF16), pl.BlockSpec((piece, HEAD_DIM), lambda h, r: (at, h))),
        (jax.ShapeDtypeStruct((heads, 1, length), F32), pl.BlockSpec((1, 1, piece), lambda h, r: (h, 0, at))),
    ]
    scratch = [pltpu.VMEM((length, piece), F32), pltpu.VMEM((piece, width), F32)]
    (part,), shared = call_on_block(
        functools.partial(attend_kernel, at), (heads,), inputs, fresh, shared, previous, scratch,
        cost(
            2 * length * piece * columns * 1.3 + 2 * piece * columns * width, 6 * length * columns + 2 * width * columns,
            heads * length * piece * 0.6,
        ), rank,
    )
    return part, shared


def feed_kernel(normed, cot, fc, bias, down, part, active_out, hidden_out, normed_out, cot_out, sum_ref):
    step = pl.program_id(0)
    weights = fc[...]
    hidden = nn(normed[...], weights) + bias[...]
    grad_active = nt(cot[...], down[...])
    inner = math.sqrt(2 / math.pi) * (hidden + 0.044715 * (hidden * hidden * hidden))
    bent = jnp.tanh(inner)
    half = 0.5 * (1.0 + bent)
    active_out[...] = (hidden * half).astype(BF16)
    slope = half + (0.5 * hidden) * (1.0 - bent * bent) * (
        math.sqrt(2 / math.pi) * (1.0 + (3 * 0.044715) * (hidden * hidden))
    )
    grad_hidden = (grad_active * slope).astype(BF16)
    hidden_out[...] = grad_hidden
    term = nt(grad_hidden, weights)

    @pl.when(step == 0)
    def _():
        sum_ref[...] = term
        normed_out[...] = normed[...]
        cot_out[...] = cot[...]

    @pl.when(step > 0)
    def _():
        sum_ref[...] += term

    @pl.when(step == pl.num_programs(0) - 1)
    def _():
        part[...] = sum_ref[...].astype(BF16)


def feed(at, normed, cot, fc, bias, down, count, previous):
    piece, width = normed.shape
    inner = fc.shape[1]
    tile = min(512, inner)
    length = piece * count
    rows = pl.BlockSpec((piece, width), lambda j: (0, 0))
    inputs = [
        (normed, rows),
        (cot, rows),
        (fc, pl.BlockSpec((width, tile), lambda j: (0, j))),
        (bias, pl.BlockSpec((1, tile), lambda j: (0, j))),
        (down, pl.BlockSpec((tile, width), lambda j: (j, 0))),
    ]
    shape = lambda n: jax.ShapeDtypeStruct((length, n), BF16)
    columns = pl.BlockSpec((piece, tile), lambda j: (at, j))
    here = pl.BlockSpec((piece, width), lambda j: (at, 0))
    fresh = [(jax.ShapeDtypeStruct((piece, width), BF16), rows)]
    shared = [(shape(inner), columns), (shape(inner), columns), (shape(width), here), (shape(width), here)]
    (part,), shared = call_on_block(
        feed_kernel, (inner // tile,), inputs, fresh, shared, previous, [pltpu.VMEM((piece, width), F32)],
        cost(6 * piece * width * inner, 4 * width * inner + 10 * piece * width + 4 * piece * inner, piece * inner),
    )
    return part, shared


def retreat_kernel(
    at, first_call, last_call, rank_ref, low_ref, proj_ref, query_ref, lse_ref, key_ref, value_ref, key_t, bias_ref, *rest
):
    rest = list(rest)
    key_in, value_in = (None, None) if first_call else (rest.pop(0), rest.pop(0))
    key_out, value_out, query_out, low_out, prob_ref, chance_ref, key_sum, value_sum = rest
    piece = query_ref.shape[0]
    rank = rank_ref[0]
    true = lax.bitwise_xor(at, rank)

    @pl.when(pl.program_id(0) == 0)
    def _():
        low_out[...] = low_ref[...]

    if first_call:
        key_sum[...] = jnp.zeros_like(key_sum)
        value_sum[...] = jnp.zeros_like(value_sum)
    else:
        key_sum[...] = key_in[...]
        value_sum[...] = value_in[...]
    query, lse = query_ref[...], lse_ref[0]
    grad = nt(low_ref[...], proj_ref[...]).astype(BF16)

    def measure(scores, rel):
        rows = rows_of(rel, piece)
        probs = jnp.exp2(scores - lse)
        grad_chances = nt(value_ref[rows, :], grad)
        value_sum[rows, :] += nn(probs.astype(BF16), grad)
        prob_ref[rows, :] = probs
        chance_ref[rows, :] = grad_chances
        return jnp.sum(probs * grad_chances, axis=0, keepdims=True)

    def first(block, weighted):
        rel = lax.bitwise_xor(block, rank)
        return weighted + measure(scores_of(key_ref, bias_ref, query, rel, piece, False), rel)

    last = scores_of(key_ref, bias_ref, query, at, piece, True)
    weighted = lax.fori_loop(0, true, first, measure(last, at))

    def second(block, total):
        rows = rows_of(lax.bitwise_xor(block, rank), piece)
        grad_scores = (prob_ref[rows, :] * (chance_ref[rows, :] - weighted)).astype(BF16)
        key_sum[rows, :] += nn(grad_scores, query)
        return total + nn(key_t[:, rows], grad_scores)

    total = lax.fori_loop(0, true + 1, second, jnp.zeros((HEAD_DIM, piece), F32))
    query_out[...] = (total * FACTOR).T.astype(BF16)
    if last_call:
        key_out[...] = (key_sum[...] * FACTOR).astype(BF16)
        value_out[...] = value_sum[...].astype(BF16)
    else:
        key_out[...] = key_sum[...]
        value_out[...] = value_sum[...]


def retreat(at, rank, low, proj, q, lse, k, v, k_t, key_bias, sums, previous, last_call):
    length, columns = q.shape
    piece, width = low.shape
    heads = columns // HEAD_DIM
    tall = pl.BlockSpec((length, HEAD_DIM), lambda h, r: (0, h))
    part = pl.BlockSpec((piece, HEAD_DIM), lambda h, r: (at, h))
    inputs = [
        (low, pl.BlockSpec((piece, width), lambda h, r: (0, 0))),
        (proj, pl.BlockSpec((HEAD_DIM, width), lambda h, r: (h, 0))),
        (q, part),
        (lse, pl.BlockSpec((1, 1, piece), lambda h, r: (h, 0, at))),
        (k, tall),
        (v, tall),
        (k_t, pl.BlockSpec((HEAD_DIM, length), lambda h, r: (h, 0))),
        (key_bias, pl.BlockSpec((length, 1), lambda h, r: (0, 0))),
    ]
    if sums is not None:
        inputs += [(item, tall) for item in sums]
    kind = BF16 if last_call else F32
    fresh = [(jax.ShapeDtypeStruct((length, columns), kind), tall)] * 2
    shared = [
        (jax.ShapeDtypeStruct((length, columns), BF16), part),
        (jax.ShapeDtypeStruct((length, width), BF16), pl.BlockSpec((piece, width), lambda h, r: (at, 0))),
    ]
    scratch = [pltpu.VMEM((length, piece), F32)] * 2 + [pltpu.VMEM((length, HEAD_DIM), F32)] * 2
    return call_on_block(
        functools.partial(retreat_kernel, at, sums is None, last_call), (heads,), inputs, fresh, shared, previous,
        scratch,
        cost(
            5 * 1.3 * length * piece * columns + 2 * piece * columns * width, 20 * length * columns,
            heads * length * piece * 0.6,
        ), rank,
    )


def back_kernel(dq, dk, dv, wq, wk, wv, out):
    out[...] = (nt(dq[...], wq[...]) + nt(dk[...], wk[...]) + nt(dv[...], wv[...])).astype(BF16)


def back(at, grads, weights, piece):
    columns, width = grads[0].shape[1], weights[0].shape[0]
    tile = min(512, width)
    return pl.pallas_call(
        back_kernel,
        grid=(width // tile,),
        in_specs=[pl.BlockSpec((piece, columns), lambda j: (at, 0))] * 3
        + [pl.BlockSpec((tile, columns), lambda j: (j, 0))] * 3,
        out_specs=pl.BlockSpec((piece, tile), lambda j: (0, j)),
        out_shape=jax.ShapeDtypeStruct((piece, width), BF16),
        compiler_params=params(),
        cost_estimate=cost(6 * piece * width * columns, 6 * width * columns + 6 * piece * columns + 2 * piece * width),
    )(*grads, *weights)


def part_specs(parts, tile, steps, width):
    arrays, specs = [], []
    for part in parts:
        if isinstance(part, tuple):
            middle = steps // 2
            arrays += list(part)
            specs.append(pl.BlockSpec((tile, width), lambda i: (jnp.minimum(i, middle - 1), 0)))
            specs.append(pl.BlockSpec((tile, width), lambda i: (jnp.maximum(i - middle, 0), 0)))
        else:
            arrays.append(part)
            specs.append(pl.BlockSpec((tile, width), lambda i: (i, 0)))
    return arrays, specs


def add_parts(kinds, refs):
    total = None
    upper = pl.program_id(0) < pl.num_programs(0) // 2
    for kind in kinds:
        if kind:
            high, low = refs.pop(0)[...], refs.pop(0)[...]
            term = jnp.where(upper, high.astype(F32), low.astype(F32))
        else:
            term = refs.pop(0)[...].astype(F32)
        total = term if total is None else total + term
    return total


def rowwise(kernel, parts, rows, vectors, outputs, sums):
    count, width = rows[0].shape
    tile = min(128, count // 2)
    steps = count // tile
    arrays, specs = part_specs(parts, tile, steps, width)
    kinds = [isinstance(part, tuple) for part in parts]
    specs += [pl.BlockSpec((tile, width), lambda i: (i, 0))] * len(rows)
    specs += [pl.BlockSpec((1, width), lambda i: (0, 0))] * len(vectors)

    def body(*refs):
        refs = list(refs)
        total = add_parts(kinds, refs)
        tiles = [refs.pop(0)[...] for _ in rows]
        given = [refs.pop(0)[...] for _ in vectors]
        results = kernel(total, tiles, given)
        for result, _ in zip(results, outputs):
            refs.pop(0)[...] = result
        for result in results[len(outputs) :]:
            ref = refs.pop(0)
            column = jnp.sum(result, axis=0, keepdims=True)

            @pl.when(pl.program_id(0) == 0)
            def _():
                ref[...] = column

            @pl.when(pl.program_id(0) > 0)
            def _():
                ref[...] += column

    return pl.pallas_call(
        body,
        grid=(steps,),
        in_specs=specs,
        out_specs=[pl.BlockSpec((tile, width), lambda i: (i, 0))] * len(outputs)
        + [pl.BlockSpec((1, width), lambda i: (0, 0))] * sums,
        out_shape=[jax.ShapeDtypeStruct((count, width), kind) for kind in outputs]
        + [jax.ShapeDtypeStruct((1, width), F32)] * sums,
        compiler_params=params(),
        cost_estimate=cost(20 * count * width, count * width * (2 * len(arrays) + 4 * len(rows) + 4 * len(outputs))),
    )(*arrays, *rows, *vectors)


def middle_kernel(total, rows, vectors):
    (tokens,), (bias, gain, shift_) = rows, vectors
    middle = tokens.astype(F32) + (total + bias)
    return middle, (norm_parts(middle)[0] * gain + shift_).astype(BF16)


def out_kernel(total, rows, vectors):
    return (((rows[0] + (total + vectors[0])).astype(BF16)),)


def middle_back_kernel(total, rows, vectors):
    (middle, cot), (gain,) = rows, vectors
    normed, scale = norm_parts(middle)
    cot = cot.astype(F32)
    grad = cot + norm_backward(normed, scale, gain, total)
    low = grad.astype(BF16)
    return grad, low, total * normed, total, low.astype(F32), cot


def tokens_back_kernel(total, rows, vectors):
    (tokens, grad_middle), (gain,) = rows, vectors
    normed, scale = norm_parts(tokens.astype(F32))
    return grad_middle + norm_backward(normed, scale, gain, total), total * normed, total


def lay_out(rank, blocks, width, places):
    rows = blocks[0][0].shape[0]
    count, each = len(blocks), len(blocks[0])
    unit = places[1]

    def body(rank_ref, *refs):
        out = refs[-1]
        for k in range(count):
            source = lax.bitwise_xor(k, rank_ref[0])
            for array, column, target in places[0](source):
                out[:, pl.ds(pl.multiple_of(target * unit, unit), unit)] = refs[k * each + array][
                    :, column * unit : (column + 1) * unit
                ].astype(F32)

    arrays = [item for block in blocks for item in block]
    return pl.pallas_call(
        body,
        grid_spec=pltpu.PrefetchScalarGridSpec(
            num_scalar_prefetch=1,
            grid=(1,),
            in_specs=[pl.BlockSpec(item.shape, lambda i, r: (0, 0)) for item in arrays],
            out_specs=pl.BlockSpec((rows, width), lambda i, r: (0, 0)),
        ),
        out_shape=jax.ShapeDtypeStruct((rows, width), F32),
        compiler_params=params(),
        cost_estimate=cost(rows * width, 6 * rows * width),
    )(rank, *arrays)


def after(value, *others):
    return lax.optimization_barrier((value, *others))[0]


def shift(value, axis, distance):
    count = lax.axis_size(axis)
    return lax.ppermute(value, axis, [(i, i ^ distance) for i in range(count)])


def gather_blocks(value, axis="seq"):
    return [value] + [shift(value, axis, k) for k in range(1, lax.axis_size(axis))]


def scatter_blocks(blocks, axis="seq"):
    return [blocks[0]] + [shift(blocks[k], axis, k) for k in range(1, lax.axis_size(axis))]


def gather_plane(value):
    if lax.axis_size("seq") != 4:
        return gather_blocks(value)
    half = value.shape[0] // 2
    one, two = shift(value, "seq", 1), shift(value, "seq", 2)
    three = jnp.concatenate([shift(one[:half], "seq", 2), shift(two[half:], "seq", 1)], axis=0)
    return [value, one, two, three]


def scatter_plane(blocks):
    if lax.axis_size("seq") != 4:
        return scatter_blocks(blocks)
    half = blocks[0].shape[0] // 2
    up, low = shift(blocks[3][:half], "seq", 1), shift(blocks[3][half:], "seq", 2)
    one = shift(blocks[1][:half], "seq", 1)
    two = shift(blocks[2][half:], "seq", 2)
    one_low = (blocks[1][half:].astype(F32) + low.astype(F32)).astype(BF16)
    two_up = (blocks[2][:half].astype(F32) + up.astype(F32)).astype(BF16)
    return [blocks[0], (one, shift(one_low, "seq", 1)), (shift(two_up, "seq", 2), two)]


def by_rank(blocks, rank):
    bit = 1
    while bit < len(blocks):
        odd = (rank & bit) != 0
        blocks = [jnp.where(odd, blocks[k ^ bit], blocks[k]) for k in range(len(blocks))]
        bit *= 2
    return blocks


def pick(pieces, at):
    return lax.dynamic_index_in_dim(pieces, at, axis=0, keepdims=False)


def exchange(pieces, rank):
    return scatter_blocks([pick(pieces, rank ^ k) for k in range(pieces.shape[0])])


def small_scatter(pieces, dp_rank, seq_rank):
    total = 0.0
    sent = [lax.dynamic_index_in_dim(pieces, seq_rank ^ k, axis=1, keepdims=False) for k in range(pieces.shape[1])]
    for part in scatter_blocks(sent):
        total = total + part
    sent = [pick(total, dp_rank ^ k) for k in range(pieces.shape[0])]
    total = 0.0
    for part in scatter_blocks(sent, "dp"):
        total = total + part
    return total


def swap_pairs(dp_count, seq_count, sub):
    pairs = []
    for d in range(dp_count):
        for s in range(seq_count):
            source = ((d // sub) * sub + s % sub) * seq_count + (s // sub) * sub + d % sub
            pairs.append((source, d * seq_count + s))
    return pairs


def gather_dp(value):
    return lax.all_gather(value, "dp", axis=0, tiled=True)


def scatter_dp(value):
    return lax.psum_scatter(value, "dp", scatter_dimension=0, tiled=True)


def shards(
    tokens,
    cotangent,
    lengths,
    key_mask,
    attn_gain,
    attn_shift,
    qkv_weight,
    qv_bias,
    proj_weight,
    proj_bias,
    mlp_gain,
    mlp_shift,
    fc_weight,
    fc_bias,
    down_weight,
    down_bias,
):
    _, piece, width = tokens.shape
    dp_count, seq_count = lax.axis_size("dp"), lax.axis_size("seq")
    dp_rank, seq_rank = lax.axis_index("dp"), lax.axis_index("seq")
    own_heads = HEADS // seq_count
    own_width = own_heads * HEAD_DIM
    rows = qkv_weight.shape[0]
    sub = HEAD_DIM // proj_weight.shape[0]
    high = seq_count // sub
    block = down_weight.shape[0]
    rank = jnp.reshape(seq_rank, (1,)).astype(jnp.int32)
    swap = swap_pairs(dp_count, seq_count, sub)
    order = list(range(seq_count - 1, -1, -1))
    if seq_count == 4:
        order = [3, 1, 2, 0]

    qkv_pieces = (
        qkv_weight.reshape(rows, 3, own_heads, sub, high, HEAD_DIM)
        .transpose(4, 3, 0, 1, 2, 5)
        .reshape(seq_count, rows, 3 * own_width)
    )
    qkv_rows = jnp.concatenate(by_rank(exchange(qkv_pieces, seq_rank), seq_rank), axis=0)
    weights = [gather_dp(qkv_rows[:, i * own_width : (i + 1) * own_width]) for i in range(3)]
    tokens_own = after(tokens[0], qkv_pieces)
    token_blocks = gather_plane(tokens_own)

    small = (attn_gain, attn_shift, qv_bias, proj_bias, mlp_gain, mlp_shift, fc_bias, down_bias)
    sizes = [item.shape[0] for item in small]
    positions = seq_rank * piece + jnp.arange(piece, dtype=jnp.int32)
    own_flags = ((key_mask[0] == 1) & (positions < lengths[0])).astype(BF16)
    packed = after(jnp.concatenate(small + (own_flags,)), qkv_rows)
    blocks = gather_blocks(packed)
    flags = jnp.concatenate([item[-piece:] for item in blocks])
    key_bias = jnp.where(flags > 0, 0.0, NEG).astype(F32)[:, None]
    packed = jnp.stack(by_rank([item[:-piece] for item in blocks], seq_rank))
    packed = jnp.stack(by_rank(gather_blocks(packed, "dp"), dp_rank)).astype(F32)
    parts, start = [], 0
    for size in sizes:
        parts.append(packed[:, :, start : start + size])
        start += size
    whole = [part.reshape(1, -1) for part in parts]
    gain_one, shift_one, qv_full, proj_shift, gain_two, shift_two, _, down_shift = whole
    fc_shift = lax.dynamic_index_in_dim(parts[6], seq_rank, axis=1, keepdims=False).reshape(1, -1)
    rank_low, rank_high = seq_rank % sub, seq_rank // sub
    qv_heads = qv_full.reshape(2, own_heads, sub, high, HEAD_DIM)
    qv_own = lax.dynamic_index_in_dim(
        lax.dynamic_index_in_dim(qv_heads, rank_low, axis=2, keepdims=False), rank_high, axis=2, keepdims=False
    )
    qv_own = qv_own.reshape(1, -1)

    proj_full = gather_dp(lax.ppermute(after(proj_weight, qkv_rows), BOTH, swap))
    fc_pieces = (
        after(fc_weight, qkv_rows)
        .reshape(rows, dp_count, seq_count, block)
        .transpose(2, 0, 1, 3)
        .reshape(seq_count, rows, dp_count * block)
    )
    fc_rows = jnp.concatenate(by_rank(exchange(fc_pieces, seq_rank), seq_rank), axis=0)
    fc_full = gather_dp(fc_rows)
    down_full = gather_dp(after(down_weight, fc_rows))

    cot_blocks = gather_plane(after(cotangent[0], token_blocks[-1]))
    shared = None
    for k in range(seq_count):
        shared = project(k, token_blocks[k], gain_one, shift_one, weights, qv_own, seq_count, shared)
    normed_one, q, keys, values, keys_t, values_t = shared
    proj_terms, shared = [None] * seq_count, None
    for k in order:
        proj_terms[k], shared = attend(k, rank, q, keys, values_t, key_bias, proj_full, piece, shared)
    attended, lse = shared
    middle, normed_two = rowwise(
        middle_kernel, scatter_plane(proj_terms), [tokens_own], [proj_shift, gain_two, shift_two], [F32, BF16], 0
    )

    normed_blocks = gather_plane(normed_two)
    grad_terms, shared = [], None
    for k in range(seq_count):
        term, shared = feed(k, normed_blocks[k], cot_blocks[k], fc_full, fc_shift, down_full, seq_count, shared)
        grad_terms.append(term)
    active, grad_hidden, normed_all, cot_all = shared
    grad_down = tn(active, cot_all).astype(BF16)
    grad_fc = tn(normed_all, grad_hidden).astype(BF16)
    received = scatter_plane(grad_terms)
    received[0] = after(received[0], grad_down, grad_fc)
    grad_middle, grad_mid_low, *sums_two = rowwise(
        middle_back_kernel, received, [middle, cotangent[0]], [gain_two], [F32, BF16], 4
    )
    low_blocks = gather_plane(grad_mid_low)
    grad_down = scatter_dp(grad_down)
    grad_fc = scatter_dp(grad_fc)
    down_terms = [
        nn(active[k * piece : (k + 1) * piece], down_full).astype(BF16) for k in range(seq_count)
    ]
    low_blocks[1], *down_terms = lax.optimization_barrier((low_blocks[1], *down_terms))
    down_terms, _ = lax.optimization_barrier((down_terms, low_blocks[-1]))

    sums, shared = None, None
    for k in range(seq_count):
        sums, shared = retreat(
            k, rank, low_blocks[k], proj_full, q, lse, keys, values, keys_t, key_bias, sums, shared, k == seq_count - 1
        )
    grad_q, low_all = shared
    grads = [grad_q, sums[0], sums[1]]
    grad_qkv = [scatter_dp(tn(normed_one, item).astype(BF16)) for item in grads]
    back_terms = [None] * seq_count
    for k in order:
        back_terms[k] = back(k, grads, weights, piece)
    tokens_grad, *sums_one = rowwise(
        tokens_back_kernel, scatter_plane(back_terms), [tokens_own, grad_middle], [gain_one], [F32], 2
    )
    (block_out,) = rowwise(out_kernel, scatter_plane(down_terms), [middle], [down_shift], [BF16], 0)
    grad_proj = scatter_dp(tn(attended, low_all).astype(BF16))
    grad_proj = lax.ppermute(grad_proj, BOTH, swap).astype(F32)

    blocks = exchange(grad_fc.reshape(seq_count, rows, dp_count * block), seq_rank)
    if block % 128 == 0:
        fc_places = lambda s: [(0, d, d * seq_count + s) for d in range(dp_count)]
        grad_fc = lay_out(rank, [[item] for item in blocks], fc_weight.shape[1], (fc_places, block))
    else:
        blocks = [item.reshape(rows, dp_count, block) for item in by_rank(blocks, seq_rank)]
        grad_fc = jnp.stack(blocks, axis=2).reshape(fc_weight.shape).astype(F32)
    blocks = list(zip(*[exchange(item.reshape(seq_count, rows, own_width), seq_rank) for item in grad_qkv]))
    qkv_places = lambda s: [
        (part, head, part * HEADS + (head * sub + s % sub) * high + s // sub)
        for part in range(3)
        for head in range(own_heads)
    ]
    grad_qkv_weight = lay_out(rank, blocks, qkv_weight.shape[1], (qkv_places, HEAD_DIM))

    def spread(vector):
        return vector.reshape(dp_count, seq_count, -1)

    here = (jnp.arange(seq_count) == seq_rank).astype(F32)
    hidden_sums = jnp.sum(grad_hidden.astype(F32), axis=0).reshape(dp_count, 1, -1) * here[None, :, None]
    early = jnp.concatenate([spread(item) for item in sums_two] + [hidden_sums], axis=2)
    early = small_scatter(early, dp_rank, seq_rank)
    qv_sums = jnp.stack([jnp.sum(item.astype(F32), axis=0) for item in (grads[0], grads[2])])
    here = (jnp.arange(sub) == rank_low)[:, None] & (jnp.arange(high) == rank_high)[None, :]
    qv_sums = qv_sums.reshape(2, own_heads, 1, 1, HEAD_DIM) * here.astype(F32)[None, None, :, :, None]
    late = jnp.concatenate([spread(item) for item in sums_one] + [spread(qv_sums)], axis=2)
    late = small_scatter(late, dp_rank, seq_rank)
    share = attn_gain.shape[0]
    return (
        block_out[None],
        tokens_grad[None],
        late[:share],
        late[share : 2 * share],
        grad_qkv_weight,
        late[2 * share :],
        grad_proj,
        early[2 * share : 3 * share],
        early[:share],
        early[share : 2 * share],
        grad_fc,
        early[4 * share :],
        grad_down.astype(F32),
        early[3 * share : 4 * share],
    )


def solution(mesh):
    in_specs = (
        P("dp", "seq", None),
        P("dp", "seq", None),
        P("dp"),
        P("dp", "seq"),
        P(BOTH),
        P(BOTH),
        P(BOTH, None),
        P(BOTH),
        P(BOTH, None),
        P(BOTH),
        P(BOTH),
        P(BOTH),
        P(BOTH, None),
        P(BOTH),
        P(BOTH, None),
        P(BOTH),
    )
    out_specs = (
        P("dp", "seq", None),
        P("dp", "seq", None),
        P(BOTH),
        P(BOTH),
        P(BOTH, None),
        P(BOTH),
        P(BOTH, None),
        P(BOTH),
        P(BOTH),
        P(BOTH),
        P(BOTH, None),
        P(BOTH),
        P(BOTH, None),
        P(BOTH),
    )
    return jax.shard_map(shards, mesh=mesh, in_specs=in_specs, out_specs=out_specs, check_vma=False)
```

time: 1250 us -> 1130 us (0.904)
  Pallas kernels: 79 us -> 341 us
  waiting for transfers between devices: 685 us -> 442 us
  matrix products: 293 us -> 124 us
  local copies, waits for them, and re-layouts: 34.7 us -> 58.9 us
  other arithmetic: 40.5 us -> 26.8 us
    ppermute x69 -> x88, waiting for transfers between devices: 684 us -> 388 us  [shift(): return lax.ppermute(value, axis, [(i, i ^ distance) for i in range(count)])]
    pallas_call x2 -> x26, Pallas kernels: 79 us -> 341 us  [the longest x8 142 us: call_on_block(): pl.pallas_call(body, grid_spec=pltpu.PrefetchScalarGridSpec(num_scalar_pr...]
    dot_general x10 -> x0, matrix products: 117 us -> none  [nt(): lax.dot_general(left, right, (((1,), (1,)), ((), ())), preferred_element_...]
    dot_general x10 -> x4, matrix products: 101 us -> 37.9 us  [nn(): lax.dot_general(left, right, (((1,), (0,)), ((), ())), preferred_element_...]
    reduce_scatter x4 -> x6, waiting for transfers between devices: 0.01 us -> 51.4 us  [scatter_dp(): return lax.psum_scatter(value, 'dp', scatter_dimension=0, tiled=True)]
    slice x1 -> x25, local copies, waits for them, and re-layouts: 0.01 us -> 22.7 us  [the longest x4 7.95 us: scatter_plane(): blocks[3][:half]]
    reduce_sum x7 -> x2, other arithmetic: 22.7 us -> 5.37 us  [the longest x1 4.76 us: shards(): jnp.sum(grad_hidden.astype(F32), axis=0).reshape(dp_count, 1, -1)]
    ppermute x69 -> x88, starting transfers between devices: 94 us -> 106 us  [shift(): return lax.ppermute(value, axis, [(i, i ^ distance) for i in range(count)])]
  transfers between devices with their start and end apart: 79 -> 102, of which waited for: 26 -> 38; matrix products, arithmetic and copies ran while one was open for 22% -> 16% of each run, Pallas kernels for 6% -> 19%
where the time goes in v2:
time: 1130 us; the launch traced here: 1120 us
  waiting for transfers between devices  442 us (39%)
  Pallas kernels  341 us (30%)
  matrix products  124 us (11%)
  starting transfers between devices  109 us (10%)
  local copies, waits for them, and re-layouts  58.9 us (5%)
  other arithmetic  26.8 us (2%)
  between operations  16.6 us (1%)
    ppermute x88, waiting for transfers between devices, shift(): return lax.ppermute(value, axis, [(i, i ^ distance) for i in range(count)])  388 us
    pallas_call x8, Pallas kernels, call_on_block(): pl.pallas_call(body, grid_spec=pltpu.PrefetchScalarGridSpec(num_scalar_pr...  142 us
    pallas_call x8, Pallas kernels, call_on_block(): pl.pallas_call(body, grid=grid, in_specs=specs, out_specs=out_specs, out_...  128 us
    ppermute x88, starting transfers between devices, shift(): return lax.ppermute(value, axis, [(i, i ^ distance) for i in range(count)])  106 us
    dot_general x6, matrix products, tn(): lax.dot_general(left, right, (((0,), (0,)), ((), ())), preferred_element_...  85.9 us
    reduce_scatter x6, waiting for transfers between devices, scatter_dp(): return lax.psum_scatter(value, 'dp', scatter_dimension=0, tiled=True)  51.4 us
    dot_general x4, matrix products, nn(): lax.dot_general(left, right, (((1,), (0,)), ((), ())), preferred_element_...  37.9 us
    pallas_call x4, Pallas kernels, rowwise(): pl.pallas_call(body, grid=(steps,), in_specs=specs, out_specs=[pl.BlockSp...  35.6 us
  transfers between devices with their start and end apart: 102, of which 38 were waited for; matrix products, arithmetic and copies ran while one was open for 16% of the time, Pallas kernels for 19%

profile of v2, /device:TPU:0, one launch (start us, length us, event | category | flops | bytes accessed | tf_op | source)
XLA Modules:
  0.0 1118.8 jit_solution(6420402659129262735)
XLA Ops:
  58.6 42.4 %collective-permute-done.7 = bf16[1280]{0:T(1024)(128)(2,1)S(1)} collective-permute-done((bf16[1280]{0:T(1024)(128)(2,1)S(1)}, bf16[1280]{0:T(1024)(128)(2,1)S(1)}, u32[]{:S(2)}, u32[]{:S(2)}) %collective-permute-start.7) | collective-permute-done | bytes 2592 | tf_op jit(solution)/shard_map/ppermute | solution.py:510
  123.2 18.8 %collective-permute-done.1 = bf16[256,2048]{1,0:T(8,128)(2,1)S(1)} collective-permute-done((bf16[256,2048]{1,0:T(8,128)(2,1)}, bf16[256,2048]{1,0:T(8,128)(2,1)S(1)}, u32[]{:S(2)}, u32[]{:S(2)}) %collective-permute-start.1) | collective-permute-done | bytes 1048608 | tf_op jit(solution)/shard_map/ppermute | solution.py:510
  184.6 18.5 %shard_map.267 = (bf16[512,2048]{1,0:T(8,128)(2,1)}, bf16[2048,512]{1,0:T(8,128)(2,1)}, f32[4,1,2048]{2,1,0:T(1,128)}) custom-call(s32[1]{0:T(128)} %bitcast.refs_0_.rank_ref, bf16[2048,512]{1,0:T(8,128)(2,1)} %get-tuple-element.133.refs_1_.refs_3_, bf16[2048,512]{1,0:T(8,128)(2,1)} %get-tuple-element.134.refs_2_.refs_5_, ...), custom_call_target="tpu_custom_call" | custom-call | flops 2469606144 | bytes 8388608 | tf_op jit(solution)/shard_map/pallas_call | solution.py:67
  205.0 13.4 %shard_map.268 = (bf16[512,2048]{1,0:T(8,128)(2,1)}, bf16[2048,512]{1,0:T(8,128)(2,1)}, f32[4,1,2048]{2,1,0:T(1,128)}) custom-call(s32[1]{0:T(128)} %bitcast.refs_0_.rank_ref, bf16[2048,512]{1,0:T(8,128)(2,1)} %get-tuple-element.133.refs_1_.refs_3_, ...), custom_call_target="tpu_custom_call", output_to_operand_aliasing={{1}: (6, {}), {2}: (7, {})} | custom-call | flops 2469606144 | bytes 8388608 | tf_op jit(solution)/shard_map/pallas_call | solution.py:67
  218.4 15.9 %shard_map.269 = (bf16[512,2048]{1,0:T(8,128)(2,1)}, bf16[2048,512]{1,0:T(8,128)(2,1)}, f32[4,1,2048]{2,1,0:T(1,128)}) custom-call(s32[1]{0:T(128)} %bitcast.refs_0_.rank_ref, bf16[2048,512]{1,0:T(8,128)(2,1)} %get-tuple-element.133.refs_1_.refs_3_, ...), custom_call_target="tpu_custom_call", output_to_operand_aliasing={{1}: (6, {}), {2}: (7, {})} | custom-call | flops 2469606144 | bytes 8388608 | tf_op jit(solution)/shard_map/pallas_call | solution.py:67
  246.1 16.0 %collective-permute-done.23.refs_4_ = bf16[256,2048]{1,0:T(8,128)(2,1)S(1)} collective-permute-done((bf16[256,2048]{1,0:T(8,128)(2,1)S(1)}, bf16[256,2048]{1,0:T(8,128)(2,1)S(1)}, u32[]{:S(2)}, u32[]{:S(2)}) %collective-permute-start.23) | collective-permute-done | bytes 1048608 | tf_op jit(solution)/shard_map/ppermute | solution.py:510
  266.0 10.6 shard_map.270
  297.8 35.0 %collective-permute-done.31.refs_1_ = bf16[512,2048]{1,0:T(8,128)(2,1)} collective-permute-done((bf16[512,2048]{1,0:T(8,128)(2,1)}, bf16[512,2048]{1,0:T(8,128)(2,1)}, u32[]{:S(2)}, u32[]{:S(2)}) %collective-permute-start.31) | collective-permute-done | bytes 2097184 | tf_op jit(solution)/shard_map/ppermute | solution.py:510
  336.7 40.9 %collective-permute-done.27.refs_0_ = bf16[512,2048]{1,0:T(8,128)(2,1)S(1)} collective-permute-done((bf16[512,2048]{1,0:T(8,128)(2,1)}, bf16[512,2048]{1,0:T(8,128)(2,1)S(1)}, u32[]{:S(2)}, u32[]{:S(2)}) %collective-permute-start.27) | collective-permute-done | bytes 2097184 | tf_op jit(solution)/shard_map/ppermute | solution.py:510
  382.4 14.4 %collective-permute-done.32 = bf16[256,2048]{1,0:T(8,128)(2,1)S(1)} collective-permute-done((bf16[256,2048]{1,0:T(8,128)(2,1)S(1)}, bf16[256,2048]{1,0:T(8,128)(2,1)S(1)}, u32[]{:S(2)}, u32[]{:S(2)}) %collective-permute-start.32) | collective-permute-done | bytes 1048608 | tf_op jit(solution)/shard_map/ppermute | solution.py:510
  401.6 16.0 %collective-permute-done.28 = bf16[256,2048]{1,0:T(8,128)(2,1)S(1)} collective-permute-done((bf16[256,2048]{1,0:T(8,128)(2,1)S(1)}, bf16[256,2048]{1,0:T(8,128)(2,1)S(1)}, u32[]{:S(2)}, u32[]{:S(2)}) %collective-permute-start.28) | collective-permute-done | bytes 1048608 | tf_op jit(solution)/shard_map/ppermute | solution.py:510
  421.8 22.7 %shard_map.272 = (bf16[512,2048]{1,0:T(8,128)(2,1)}, bf16[2048,2048]{1,0:T(8,128)(2,1)}, bf16[2048,2048]{1,0:T(8,128)(2,1)}, bf16[2048,2048]{1,0:T(8,128)(2,1)}, bf16[2048,2048]{1,0:T(8,128)(2,1)}) custom-call(bf16[512,2048]{1,0:T(8,128)(2,1)} %get-tuple-element.147.refs_0_, bf16[512,2048]{1,0:T(8,128)(2,1)} %bitcast.18.refs_1_.refs_6_, ...), custom_call_target="tpu_custom_call" | custom-call | flops 12884901888 | bytes 31457280 | tf_op jit(solution)/shard_map/pallas_call | solution.py:62
  444.5 22.4 %shard_map.273 = (bf16[512,2048]{1,0:T(8,128)(2,1)}, bf16[2048,2048]{1,0:T(8,128)(2,1)}, bf16[2048,2048]{1,0:T(8,128)(2,1)}, bf16[2048,2048]{1,0:T(8,128)(2,1)}, bf16[2048,2048]{1,0:T(8,128)(2,1)}) custom-call(bf16[512,2048]{1,0:T(8,128)(2,1)} %copy-done.10, ...), custom_call_target="tpu_custom_call", output_to_operand_aliasing={{1}: (5, {}), {2}: (6, {}), {3}: (7, {}), {4}: (8, {})} | custom-call | flops 12884901888 | bytes 31457280 | tf_op jit(solution)/shard_map/pallas_call | solution.py:62
  466.9 22.4 %shard_map.274 = (bf16[512,2048]{1,0:T(8,128)(2,1)}, bf16[2048,2048]{1,0:T(8,128)(2,1)}, bf16[2048,2048]{1,0:T(8,128)(2,1)}, bf16[2048,2048]{1,0:T(8,128)(2,1)}, bf16[2048,2048]{1,0:T(8,128)(2,1)}) custom-call(bf16[512,2048]{1,0:T(8,128)(2,1)} %copy-done.9, ...), custom_call_target="tpu_custom_call", output_to_operand_aliasing={{1}: (5, {}), {2}: (6, {}), {3}: (7, {}), {4}: (8, {})} | custom-call | flops 12884901888 | bytes 31457280 | tf_op jit(solution)/shard_map/pallas_call | solution.py:62
  489.2 22.6 %shard_map.275 = (bf16[512,2048]{1,0:T(8,128)(2,1)}, bf16[2048,2048]{1,0:T(8,128)(2,1)}, bf16[2048,2048]{1,0:T(8,128)(2,1)}, bf16[2048,2048]{1,0:T(8,128)(2,1)}, bf16[2048,2048]{1,0:T(8,128)(2,1)}) custom-call(bf16[512,2048]{1,0:T(8,128)(2,1)} %pad_maximum_fusion.refs_0_, ...), custom_call_target="tpu_custom_call", output_to_operand_aliasing={{1}: (5, {}), {2}: (6, {}), {3}: (7, {}), {4}: (8, {})} | custom-call | flops 12884901888 | bytes 31457280 | tf_op jit(solution)/shard_map/pallas_call | solution.py:62
  519.9 23.8 %convolution_convert_fusion = bf16[2048,2048]{1,0:T(8,128)(2,1)} fusion(bf16[2048,2048]{1,0:T(8,128)(2,1)} %get-tuple-element.166, bf16[2048,2048]{1,0:T(8,128)(2,1)} %get-tuple-element.167), kind=kOutput, calls=%fused_computation.1 | convolution fusion | flops 17184063488 | bytes 25165824 | tf_op jit(solution)/shard_map/dot_general | solution.py:31
  543.6 23.9 %convolution_convert_fusion.1 = bf16[2048,2048]{1,0:T(8,128)(2,1)} fusion(bf16[2048,2048]{1,0:T(8,128)(2,1)} %get-tuple-element.164, bf16[2048,2048]{1,0:T(8,128)(2,1)} %get-tuple-element.165), kind=kOutput, calls=%fused_computation.2 | convolution fusion | flops 17184063488 | bytes 25165824 | tf_op jit(solution)/shard_map/dot_general | solution.py:31
  592.4 11.5 %collective-permute-done.35.refs_1_ = bf16[256,2048]{1,0:T(8,128)(2,1)S(1)} collective-permute-done((bf16[256,2048]{1,0:T(8,128)(2,1)S(1)}, bf16[256,2048]{1,0:T(8,128)(2,1)S(1)}, u32[]{:S(2)}, u32[]{:S(2)}) %collective-permute-start.35) | collective-permute-done | bytes 1048608 | tf_op jit(solution)/shard_map/ppermute | solution.py:510
  603.9 18.1 %collective-permute-done.37.refs_2_ = bf16[256,2048]{1,0:T(8,128)(2,1)S(1)} collective-permute-done((bf16[256,2048]{1,0:T(8,128)(2,1)S(1)}, bf16[256,2048]{1,0:T(8,128)(2,1)S(1)}, u32[]{:S(2)}, u32[]{:S(2)}) %collective-permute-start.37) | collective-permute-done | bytes 1048608 | tf_op jit(solution)/shard_map/ppermute | solution.py:510
  622.9 12.0 %shard_map.276 = (f32[512,2048]{1,0:T(8,128)}, bf16[512,2048]{1,0:T(8,128)(2,1)}, f32[1,2048]{1,0:T(1,128)}, f32[1,2048]{1,0:T(1,128)}, f32[1,2048]{1,0:T(1,128)}, /*index=5*/f32[1,2048]{1,0:T(1,128)}) custom-call(bf16[512,2048]{1,0:T(8,128)(2,1)} %get-tuple-element.168.refs_0_, bf16[256,2048]{1,0:T(8,128)(2,1)} %copy-done.26, bf16[256,2048]{1,0:T(8,128)(2,1)} %copy-done.29, ...), custom_call_target="tpu_custom_call" | custom-call | flops 20971520 | bytes 27262976 | tf_op jit(solution)/shard_map/pallas_call | solution.py:437
  636.5 10.6 convolution_convert_fusion.8
  654.5 24.0 %collective-permute-done.41.refs_1_ = bf16[512,2048]{1,0:T(8,128)(2,1)S(1)} collective-permute-done((bf16[512,2048]{1,0:T(8,128)(2,1)}, bf16[512,2048]{1,0:T(8,128)(2,1)S(1)}, u32[]{:S(2)}, u32[]{:S(2)}) %collective-permute-start.41) | collective-permute-done | bytes 2097184 | tf_op jit(solution)/shard_map/ppermute | solution.py:510
  679.7 14.7 %shard_map.278 = (f32[2048,512]{1,0:T(8,128)}, f32[2048,512]{1,0:T(8,128)}, bf16[2048,512]{1,0:T(8,128)(2,1)}, bf16[2048,2048]{1,0:T(8,128)(2,1)}) custom-call(s32[1]{0:T(128)} %bitcast.refs_0_.rank_ref, bf16[512,2048]{1,0:T(8,128)(2,1)} %get-tuple-element.173.refs_1_, bf16[512,2048]{1,0:T(8,128)(2,1)} %all-gather.13.cloned.1.call-done.refs_5_.refs_2_, ...), custom_call_target="tpu_custom_call" | custom-call | flops 4563402752 | bytes 20971520 | tf_op jit(solution)/shard_map/pallas_call | solution.py:67
  699.6 19.3 %shard_map.279 = (f32[2048,512]{1,0:T(8,128)}, f32[2048,512]{1,0:T(8,128)}, bf16[2048,512]{1,0:T(8,128)(2,1)}, bf16[2048,2048]{1,0:T(8,128)(2,1)}) custom-call(s32[1]{0:T(128)} %bitcast.refs_0_.rank_ref, bf16[512,2048]{1,0:T(8,128)(2,1)} %copy-done.12, ...), custom_call_target="tpu_custom_call", output_to_operand_aliasing={{2}: (11, {}), {3}: (12, {})} | custom-call | flops 4563402752 | bytes 20971520 | tf_op jit(solution)/shard_map/pallas_call | solution.py:67
  718.9 23.0 %shard_map.280 = (f32[2048,512]{1,0:T(8,128)}, f32[2048,512]{1,0:T(8,128)}, bf16[2048,512]{1,0:T(8,128)(2,1)}, bf16[2048,2048]{1,0:T(8,128)(2,1)}) custom-call(s32[1]{0:T(128)} %bitcast.refs_0_.rank_ref, bf16[512,2048]{1,0:T(8,128)(2,1)} %copy-done.11, ...), custom_call_target="tpu_custom_call", output_to_operand_aliasing={{2}: (11, {}), {3}: (12, {})} | custom-call | flops 4563402752 | bytes 20971520 | tf_op jit(solution)/shard_map/pallas_call | solution.py:67
  743.5 27.0 %shard_map.281 = (bf16[2048,512]{1,0:T(8,128)(2,1)}, bf16[2048,512]{1,0:T(8,128)(2,1)}, bf16[2048,512]{1,0:T(8,128)(2,1)}, bf16[2048,2048]{1,0:T(8,128)(2,1)}) custom-call(s32[1]{0:T(128)} %bitcast.refs_0_.rank_ref, bf16[512,2048]{1,0:T(8,128)(2,1)} %copy-done.14, ...), custom_call_target="tpu_custom_call", output_to_operand_aliasing={{2}: (11, {}), {3}: (12, {})} | custom-call | flops 4563402752 | bytes 20971520 | tf_op jit(solution)/shard_map/pallas_call | solution.py:67
  877.8 31.4 %collective-permute-done.52 = bf16[256,2048]{1,0:T(8,128)(2,1)S(1)} collective-permute-done((bf16[256,2048]{1,0:T(8,128)(2,1)S(1)}, bf16[256,2048]{1,0:T(8,128)(2,1)S(1)}, u32[]{:S(2)}, u32[]{:S(2)}) %collective-permute-start.52) | collective-permute-done | bytes 1048608 | tf_op jit(solution)/shard_map/ppermute | solution.py:510
  909.6 11.4 %collective-permute-done.48 = bf16[256,2048]{1,0:T(8,128)(2,1)S(1)} collective-permute-done((bf16[256,2048]{1,0:T(8,128)(2,1)S(1)}, bf16[256,2048]{1,0:T(8,128)(2,1)S(1)}, u32[]{:S(2)}, u32[]{:S(2)}) %collective-permute-start.48) | collective-permute-done | bytes 1048608 | tf_op jit(solution)/shard_map/ppermute | solution.py:510
  932.6 21.5 %collective-permute-done.55.refs_3_ = bf16[256,2048]{1,0:T(8,128)(2,1)S(1)} collective-permute-done((bf16[256,2048]{1,0:T(8,128)(2,1)S(1)}, bf16[256,2048]{1,0:T(8,128)(2,1)S(1)}, u32[]{:S(2)}, u32[]{:S(2)}) %collective-permute-start.55) | collective-permute-done | bytes 1048608 | tf_op jit(solution)/shard_map/ppermute | solution.py:510
  984.2 14.4 %collective-permute-done.49.refs_3_ = bf16[256,2048]{1,0:T(8,128)(2,1)} collective-permute-done((bf16[256,2048]{1,0:T(8,128)(2,1)S(1)}, bf16[256,2048]{1,0:T(8,128)(2,1)}, u32[]{:S(2)}, u32[]{:S(2)}) %collective-permute-start.49) | collective-permute-done | bytes 1048608 | tf_op jit(solution)/shard_map/ppermute | solution.py:510
  1037.4 12.4 %collective-permute-done.73.refs_9_ = bf16[64,512]{1,0:T(8,128)(2,1)S(1)} collective-permute-done((bf16[64,512]{1,0:T(8,128)(2,1)S(1)}, bf16[64,512]{1,0:T(8,128)(2,1)S(1)}, u32[]{:S(2)}, u32[]{:S(2)}) %collective-permute-start.73) | collective-permute-done | bytes 65568 | tf_op jit(solution)/shard_map/ppermute | solution.py:510
  1053.7 51.4 %reduce-scatter.17.cloned.1.call-done = bf16[256,2048]{1,0:T(8,128)(2,1)} async-done(((bf16[2048,2048]{1,0:T(8,128)(2,1)}), bf16[256,2048]{1,0:T(8,128)(2,1)}) %reduce-scatter.17.cloned.1.call-update) | async-done | bytes 1048592 | tf_op jit(solution)/shard_map/reduce_scatter | solution.py:585
  (476 shorter events, 420.0 us)
Async XLA Ops:
  7.2 139.7 %all-gather.11.cloned.1.call-start = ((), (), s32[]{:S(2)}) async-start(), calls=%async_computation.8 | async-start | bytes 2359296 | tf_op jit(solution)/shard_map/all_gather | solution.py:581
  25.0 121.9 %all-gather.7.cloned.1.call-start = ((), (), s32[]{:S(2)}) async-start(), calls=%async_computation.6 | async-start | bytes 2359296 | tf_op jit(solution)/shard_map/all_gather | solution.py:581
  25.7 121.2 %all-gather.9.cloned.1.call-start = ((), (), s32[]{:S(2)}) async-start(), calls=%async_computation.7 | async-start | bytes 2359296 | tf_op jit(solution)/shard_map/all_gather | solution.py:581
  26.5 158.1 %all-gather.13.cloned.1.call-start = ((), (), s32[]{:S(2)}) async-start(), calls=%async_computation.9 | async-start | bytes 2359296 | tf_op jit(solution)/shard_map/all_gather | solution.py:581
  27.9 393.8 %all-gather.17.cloned.1.call-start = ((), (), s32[]{:S(2)}) async-start(), calls=%async_computation.11 | async-start | bytes 9437184 | tf_op jit(solution)/shard_map/all_gather | solution.py:581
  51.8 369.9 %all-gather.15.cloned.1.call-start = ((), (), s32[]{:S(2)}) async-start(), calls=%async_computation.10 | async-start | bytes 9437184 | tf_op jit(solution)/shard_map/all_gather | solution.py:581
  52.4 957.4 %reduce-scatter.11.cloned.1.call-start = ((), (), s32[]{:S(2)}) async-start(), calls=%async_computation.14 | async-start | bytes 2359296 | tf_op jit(solution)/shard_map/reduce_scatter | solution.py:585
  52.7 61.5 %collective-permute-start = (bf16[512,2048]{1,0:T(8,128)(2,1)S(1)}, bf16[512,2048]{1,0:T(8,128)(2,1)}, u32[]{:S(2)}, u32[]{:S(2)}) collective-permute-start(bf16[512,2048]{1,0:T(8,128)(2,1)S(1)} %bitcast.172), channel_id=1, source_target_pairs={{0,1},{1,0},{2,3},{3,2},{4,5},{5,4},{6,7},{7,6},{8,9},{9,8},{10,11... | collective-permute-start | bytes 6291464 | tf_op jit(solution)/shard_map/ppermute | solution.py:510
  58.0 60.0 %collective-permute-start.2 = (bf16[512,2048]{1,0:T(8,128)(2,1)S(1)}, bf16[512,2048]{1,0:T(8,128)(2,1)}, u32[]{:S(2)}, u32[]{:S(2)}) collective-permute-start(bf16[512,2048]{1,0:T(8,128)(2,1)S(1)} %bitcast.173), channel_id=1, source_target_pairs={{0,2},{1,3},{2,0},{3,1},{4,6},{5,7},{6,4},{7,5},{8,10},{9,11},{10,... | collective-permute-start | bytes 6291464 | tf_op jit(solution)/shard_map/ppermute | solution.py:510
  244.0 88.7 %collective-permute-start.31 = (bf16[512,2048]{1,0:T(8,128)(2,1)}, bf16[512,2048]{1,0:T(8,128)(2,1)}, u32[]{:S(2)}, u32[]{:S(2)}) collective-permute-start(bf16[512,2048]{1,0:T(8,128)(2,1)} %bitcast.18.refs_1_.refs_6_), channel_id=1, source_target_pairs={{0,1},{1,0},{2,3},{3,2},{4,5},{5,4},{6,7},{7,6},{8,9},{9,8},{10,11... | collective-permute-start | bytes 6291464 | tf_op jit(solution)/shard_map/ppermute | solution.py:510
  262.0 72.4 %collective-permute-start.33 = (bf16[512,2048]{1,0:T(8,128)(2,1)}, bf16[512,2048]{1,0:T(8,128)(2,1)S(1)}, u32[]{:S(2)}, u32[]{:S(2)}) collective-permute-start(bf16[512,2048]{1,0:T(8,128)(2,1)} %bitcast.18.refs_1_.refs_6_), channel_id=1, source_target_pairs={{0,2},{1,3},{2,0},{3,1},{4,6},{5,7},{6,4},{7,5},{8,10},{9,11},{10,... | collective-permute-start | bytes 6291464 | tf_op jit(solution)/shard_map/ppermute | solution.py:510
  295.3 82.2 %collective-permute-start.27 = (bf16[512,2048]{1,0:T(8,128)(2,1)}, bf16[512,2048]{1,0:T(8,128)(2,1)S(1)}, u32[]{:S(2)}, u32[]{:S(2)}) collective-permute-start(bf16[512,2048]{1,0:T(8,128)(2,1)} %get-tuple-element.147.refs_0_), channel_id=1, source_target_pairs={{0,1},{1,0},{2,3},{3,2},{4,5},{5,4},{6,7},{7,6},{8,9},{9,8},{10,11... | collective-permute-start | bytes 6291464 | tf_op jit(solution)/shard_map/ppermute | solution.py:510
  297.4 80.7 %collective-permute-start.29 = (bf16[512,2048]{1,0:T(8,128)(2,1)}, bf16[512,2048]{1,0:T(8,128)(2,1)S(1)}, u32[]{:S(2)}, u32[]{:S(2)}) collective-permute-start(bf16[512,2048]{1,0:T(8,128)(2,1)} %get-tuple-element.147.refs_0_), channel_id=1, source_target_pairs={{0,2},{1,3},{2,0},{3,1},{4,6},{5,7},{6,4},{7,5},{8,10},{9,11},{10,... | collective-permute-start | bytes 6291464 | tf_op jit(solution)/shard_map/ppermute | solution.py:510
  334.0 62.9 %collective-permute-start.32 = (bf16[256,2048]{1,0:T(8,128)(2,1)S(1)}, bf16[256,2048]{1,0:T(8,128)(2,1)S(1)}, u32[]{:S(2)}, u32[]{:S(2)}) collective-permute-start(bf16[256,2048]{1,0:T(8,128)(2,1)S(1)} %slice.272), channel_id=1, source_target_pairs={{0,2},{1,3},{2,0},{3,1},{4,6},{5,7},{6,4},{7,5},{8,10},{9,11},{10,... | collective-permute-start | bytes 3145736 | tf_op jit(solution)/shard_map/ppermute | solution.py:510
  334.6 65.4 %collective-permute-start.34 = (bf16[256,2048]{1,0:T(8,128)(2,1)S(1)}, bf16[256,2048]{1,0:T(8,128)(2,1)S(1)}, u32[]{:S(2)}, u32[]{:S(2)}) collective-permute-start(bf16[256,2048]{1,0:T(8,128)(2,1)S(1)} %slice.273), channel_id=1, source_target_pairs={{0,1},{1,0},{2,3},{3,2},{4,5},{5,4},{6,7},{7,6},{8,9},{9,8},{10,11... | collective-permute-start | bytes 3145736 | tf_op jit(solution)/shard_map/ppermute | solution.py:510
  515.1 63.0 %collective-permute-start.38 = (bf16[256,2048]{1,0:T(8,128)(2,1)}, bf16[256,2048]{1,0:T(8,128)(2,1)}, u32[]{:S(2)}, u32[]{:S(2)}) collective-permute-start(bf16[256,2048]{1,0:T(8,128)(2,1)} %get-tuple-element.226), channel_id=1, source_target_pairs={{0,1},{1,0},{2,3},{3,2},{4,5},{5,4},{6,7},{7,6},{8,9},{9,8},{10,11... | collective-permute-start | bytes 3145736 | tf_op jit(solution)/shard_map/ppermute | solution.py:510
  516.8 63.6 %collective-permute-start.36 = (bf16[256,2048]{1,0:T(8,128)(2,1)}, bf16[256,2048]{1,0:T(8,128)(2,1)S(1)}, u32[]{:S(2)}, u32[]{:S(2)}) collective-permute-start(bf16[256,2048]{1,0:T(8,128)(2,1)} %get-tuple-element.227), channel_id=1, source_target_pairs={{0,2},{1,3},{2,0},{3,1},{4,6},{5,7},{6,4},{7,5},{8,10},{9,11},{10,... | collective-permute-start | bytes 3145736 | tf_op jit(solution)/shard_map/ppermute | solution.py:510
  518.4 73.9 %collective-permute-start.40 = (bf16[256,2048]{1,0:T(8,128)(2,1)}, bf16[256,2048]{1,0:T(8,128)(2,1)}, u32[]{:S(2)}, u32[]{:S(2)}) collective-permute-start(bf16[256,2048]{1,0:T(8,128)(2,1)} %slice.224), channel_id=1, source_target_pairs={{0,2},{1,3},{2,0},{3,1},{4,6},{5,7},{6,4},{7,5},{8,10},{9,11},{10,... | collective-permute-start | bytes 3145736 | tf_op jit(solution)/shard_map/ppermute | solution.py:510
  678.6 63.3 %collective-permute-start.42 = (bf16[256,2048]{1,0:T(8,128)(2,1)S(1)}, bf16[256,2048]{1,0:T(8,128)(2,1)S(1)}, u32[]{:S(2)}, u32[]{:S(2)}) collective-permute-start(bf16[256,2048]{1,0:T(8,128)(2,1)S(1)} %slice.274), channel_id=1, source_target_pairs={{0,2},{1,3},{2,0},{3,1},{4,6},{5,7},{6,4},{7,5},{8,10},{9,11},{10,... | collective-permute-start | bytes 3145736 | tf_op jit(solution)/shard_map/ppermute | solution.py:510
  780.5 230.9 %reduce-scatter.9.cloned.1.call-start = ((), (), s32[]{:S(2)}) async-start(), calls=%async_computation.13 | async-start | bytes 2359296 | tf_op jit(solution)/shard_map/reduce_scatter | solution.py:585
  791.7 225.5 %reduce-scatter.7.cloned.1.call-start = ((), (), s32[]{:S(2)}) async-start(), calls=%async_computation.12 | async-start | bytes 2359296 | tf_op jit(solution)/shard_map/reduce_scatter | solution.py:585
  802.8 222.7 %reduce-scatter.15.cloned.1.call-start = ((), (), s32[]{:S(2)}) async-start(), calls=%async_computation.16 | async-start | bytes 9437184 | tf_op jit(solution)/shard_map/reduce_scatter | solution.py:585
  803.4 224.5 %reduce-scatter.13.cloned.1.call-start = ((), (), s32[]{:S(2)}) async-start(), calls=%async_computation.15 | async-start | bytes 2359296 | tf_op jit(solution)/shard_map/reduce_scatter | solution.py:585
  813.6 291.6 %reduce-scatter.17.cloned.1.call-start = ((), (), s32[]{:S(2)}) async-start(), calls=%async_computation.17 | async-start | bytes 9437184 | tf_op jit(solution)/shard_map/reduce_scatter | solution.py:585
  860.6 61.1 %collective-permute-start.56 = (bf16[256,2048]{1,0:T(8,128)(2,1)S(1)}, bf16[256,2048]{1,0:T(8,128)(2,1)}, u32[]{:S(2)}, u32[]{:S(2)}) collective-permute-start(bf16[256,2048]{1,0:T(8,128)(2,1)S(1)} %slice.282), channel_id=1, source_target_pairs={{0,2},{1,3},{2,0},{3,1},{4,6},{5,7},{6,4},{7,5},{8,10},{9,11},{10,... | collective-permute-start | bytes 3145736 | tf_op jit(solution)/shard_map/ppermute | solution.py:510
  871.8 60.4 %collective-permute-start.51 = (bf16[256,2048]{1,0:T(8,128)(2,1)S(1)}, bf16[256,2048]{1,0:T(8,128)(2,1)S(1)}, u32[]{:S(2)}, u32[]{:S(2)}) collective-permute-start(bf16[256,2048]{1,0:T(8,128)(2,1)S(1)} %slice.277), channel_id=1, source_target_pairs={{0,1},{1,0},{2,3},{3,2},{4,5},{5,4},{6,7},{7,6},{8,9},{9,8},{10,11... | collective-permute-start | bytes 3145736 | tf_op jit(solution)/shard_map/ppermute | solution.py:510
  909.2 72.3 %collective-permute-start.45 = (bf16[256,2048]{1,0:T(8,128)(2,1)}, bf16[256,2048]{1,0:T(8,128)(2,1)}, u32[]{:S(2)}, u32[]{:S(2)}) collective-permute-start(bf16[256,2048]{1,0:T(8,128)(2,1)} %slice.231), channel_id=1, source_target_pairs={{0,1},{1,0},{2,3},{3,2},{4,5},{5,4},{6,7},{7,6},{8,9},{9,8},{10,11... | collective-permute-start | bytes 3145736 | tf_op jit(solution)/shard_map/ppermute | solution.py:510
  921.8 60.1 %collective-permute-start.50 = (bf16[256,2048]{1,0:T(8,128)(2,1)S(1)}, bf16[256,2048]{1,0:T(8,128)(2,1)}, u32[]{:S(2)}, u32[]{:S(2)}) collective-permute-start(bf16[256,2048]{1,0:T(8,128)(2,1)S(1)} %slice.236), channel_id=1, source_target_pairs={{0,2},{1,3},{2,0},{3,1},{4,6},{5,7},{6,4},{7,5},{8,10},{9,11},{10,... | collective-permute-start | bytes 3145736 | tf_op jit(solution)/shard_map/ppermute | solution.py:510
  932.1 66.5 %collective-permute-start.49 = (bf16[256,2048]{1,0:T(8,128)(2,1)S(1)}, bf16[256,2048]{1,0:T(8,128)(2,1)}, u32[]{:S(2)}, u32[]{:S(2)}) collective-permute-start(bf16[256,2048]{1,0:T(8,128)(2,1)S(1)} %add_convert_fusion.2), channel_id=1, source_target_pairs={{0,2},{1,3},{2,0},{3,1},{4,6},{5,7},{6,4},{7,5},{8,10},{9,11},{10,... | collective-permute-start | bytes 3145736 | tf_op jit(solution)/shard_map/ppermute | solution.py:510
  1029.5 78.5 %collective-permute-start.87 = (bf16[64,2048]{1,0:T(8,128)(2,1)S(1)}, bf16[64,2048]{1,0:T(8,128)(2,1)S(1)}, u32[]{:S(2)}, u32[]{:S(2)}) collective-permute-start(bf16[64,2048]{1,0:T(8,128)(2,1)S(1)} %get-tuple-element.240), channel_id=1, source_target_pairs={{0,1},{1,0},{2,3},{3,2},{4,5},{5,4},{6,7},{7,6},{8,9},{9,8},{10,11... | collective-permute-start | bytes 786440 | tf_op jit(solution)/shard_map/ppermute | solution.py:510
  1031.5 76.4 %collective-permute-start.88 = (bf16[64,2048]{1,0:T(8,128)(2,1)S(1)}, bf16[64,2048]{1,0:T(8,128)(2,1)S(1)}, u32[]{:S(2)}, u32[]{:S(2)}) collective-permute-start(bf16[64,2048]{1,0:T(8,128)(2,1)S(1)} %get-tuple-element.239), channel_id=1, source_target_pairs={{0,2},{1,3},{2,0},{3,1},{4,6},{5,7},{6,4},{7,5},{8,10},{9,11},{10,... | collective-permute-start | bytes 786440 | tf_op jit(solution)/shard_map/ppermute | solution.py:510
  1033.3 74.7 %collective-permute-start.89 = (bf16[64,2048]{1,0:T(8,128)(2,1)S(1)}, bf16[64,2048]{1,0:T(8,128)(2,1)S(1)}, u32[]{:S(2)}, u32[]{:S(2)}) collective-permute-start(bf16[64,2048]{1,0:T(8,128)(2,1)S(1)} %get-tuple-element.238), channel_id=1, source_target_pairs={{0,3},{1,2},{2,1},{3,0},{4,7},{5,6},{6,5},{7,4},{8,11},{9,10},{10,... | collective-permute-start | bytes 786440 | tf_op jit(solution)/shard_map/ppermute | solution.py:510
  (130 other events, 1958.2 us)
Sparse Core Ops, SparseCore 0:
  25.1 29.5 all-gather.10
  56.8 28.5 all-gather.6
  87.7 30.1 all-gather.8
  119.3 27.9 all-gather.12
  148.8 81.5 all-gather.16
  231.8 80.5 all-gather.14
  780.6 33.6 reduce-scatter.10
  816.5 34.4 reduce-scatter.8
  853.3 34.3 reduce-scatter.6
  889.8 88.3 reduce-scatter.14
  980.5 33.9 reduce-scatter.12
  1016.6 88.4 reduce-scatter.16

commit v3 on v2

--- a/solution.py
+++ b/solution.py
@@ -17,6 +17,7 @@
 F32 = jnp.float32
 BF16 = jnp.bfloat16
 BOTH = ("dp", "seq")
+MESH = pl.DeviceIdType.MESH
 
 
 def nn(left, right):
@@ -103,8 +104,8 @@
     v_t[...] = values.T.astype(BF16)
 
 
-def project(at, x, gain, shift_, weights, bias, count, previous):
-    piece, width = x.shape
+def project(at, x, first, gain, shift_, weights, bias, piece, count, previous):
+    width = x.shape[1]
     columns = weights[0].shape[1]
     tile = min(256, piece)
     steps = piece // tile
@@ -113,7 +114,7 @@
     turned = pl.BlockSpec((columns, tile), lambda i: (0, at * steps + i))
     length = piece * count
     inputs = [
-        (x, pl.BlockSpec((tile, width), lambda i: (i, 0))),
+        (x, pl.BlockSpec((tile, width), lambda i: (first * steps + i, 0))),
         (gain, whole((1, width))),
         (shift_, whole((1, width))),
         *[(item, whole((width, columns))) for item in weights],
@@ -501,6 +502,399 @@
     )(rank, *arrays)
 
 
+def neighbours():
+    rank = lax.axis_index("seq")
+    return rank + 1 - 2 * lax.rem(rank, 2), rank + 2 - 4 * lax.rem(lax.div(rank, 2), 2)
+
+
+def remote(source, target, send, receive, axis, device):
+    return pltpu.make_async_remote_copy(
+        src_ref=source, dst_ref=target, send_sem=send, recv_sem=receive, device_id={axis: device}, device_id_type=MESH
+    )
+
+
+def greet(axis, device):
+    pl.semaphore_signal(pltpu.get_barrier_semaphore(), inc=1, device_id={axis: device}, device_id_type=MESH)
+
+
+def opening_kernel(
+    tokens, cot, down, fc_pieces, token_all, cot_all, down_full, fc_rows,
+    local, send, receive, right_send, right_receive, left_send, left_receive, mate_send, mate_receive,
+):
+    piece = tokens.shape[0]
+    half = piece // 2
+    rows = down.shape[0]
+    fine = fc_pieces.shape[1]
+    me, place = lax.axis_index("seq"), lax.axis_index("dp")
+    one, two = neighbours()
+    three = 3 - me
+    stages = lax.axis_size("dp") // 2
+    level, core = lax.div(place, 2), lax.rem(place, 2)
+    mate = place + 1 - 2 * core
+    above, below = level < stages - 1, level > 0
+
+    for device in (one, two, three):
+        greet("seq", device)
+    greet("dp", mate)
+    pl.when(above)(lambda: greet("dp", place + 2))
+    pl.when(below)(lambda: greet("dp", place - 2))
+    pl.semaphore_wait(pltpu.get_barrier_semaphore(), 4 + above.astype(jnp.int32) + below.astype(jnp.int32))
+
+    def block(ref, at, start=0, size=piece):
+        return ref.at[pl.ds(at * piece + start, size)]
+
+    def pair(source, target, at):
+        return (
+            remote(source, block(target, 1), send.at[at], receive.at[at], "seq", one),
+            remote(source, block(target, 2), send.at[at + 1], receive.at[at + 1], "seq", two),
+        )
+
+    token_one, token_two = pair(tokens, token_all, 0)
+    token_three = (
+        remote(block(token_all, 1, 0, half), block(token_all, 3, 0, half), send.at[2], receive.at[2], "seq", two),
+        remote(block(token_all, 2, half, half), block(token_all, 3, half, half), send.at[3], receive.at[3], "seq", one),
+    )
+    cot_one, cot_two = pair(cot, cot_all, 4)
+    mine = fc_rows.at[pl.ds(me * fine, fine)]
+    pieces = [
+        remote(fc_pieces.at[device], mine, send.at[6 + i], receive.at[6 + i], "seq", device)
+        for i, device in enumerate((one, two, three))
+    ]
+    shard = lambda ref, at: ref.at[pl.ds((2 * at + core) * rows, rows)]
+    kept = [
+        pltpu.make_async_copy(tokens, block(token_all, 0), local.at[0]),
+        pltpu.make_async_copy(cot, block(cot_all, 0), local.at[1]),
+        pltpu.make_async_copy(down, shard(down_full, level), local.at[2]),
+        pltpu.make_async_copy(fc_pieces.at[me], mine, local.at[3]),
+    ]
+
+    def right(step):
+        at = level - (step - 1)
+        source = down if step == 1 else shard(down_full, at)
+        return remote(source, shard(down_full, at), right_send.at[step - 1], right_receive.at[step - 1], "dp", place + 2)
+
+    def left(step):
+        at = level + (step - 1)
+        source = down if step == 1 else shard(down_full, at)
+        return remote(source, shard(down_full, at), left_send.at[step - 1], left_receive.at[step - 1], "dp", place - 2)
+
+    def across(index, at):
+        return remote(shard(down_full, at), shard(down_full, at), mate_send.at[index], mate_receive.at[index], "dp", mate)
+
+    right_sends = lambda step: above & (level >= step - 1)
+    left_sends = lambda step: below & (level <= stages - step)
+    right_gets = lambda step: level >= step
+    left_gets = lambda step: level + step <= stages - 1
+
+    def relay(step):
+        pl.when(right_sends(step))(lambda: right(step).start())
+        pl.when(left_sends(step))(lambda: left(step).start())
+
+    def take(step):
+        @pl.when(right_gets(step))
+        def _():
+            remote(down, shard(down_full, level - step), right_send.at[step - 1], right_receive.at[step - 1], "dp", mate).wait_recv()
+            across(step, level - step).start()
+
+        @pl.when(left_gets(step))
+        def _():
+            remote(down, shard(down_full, level + step), left_send.at[step - 1], left_receive.at[step - 1], "dp", mate).wait_recv()
+            across(stages - 1 + step, level + step).start()
+
+    token_one.start()
+    token_two.start()
+    relay(1)
+    for copy in pieces + kept:
+        copy.start()
+    remote(down, shard(down_full, level), mate_send.at[0], mate_receive.at[0], "dp", mate).start()
+    take(1)
+    relay(2)
+    token_one.wait_recv()
+    token_two.wait_recv()
+    for copy in token_three:
+        copy.start()
+    take(2)
+    relay(3)
+    for copy in token_three:
+        copy.wait_recv()
+    cot_one.start()
+    cot_two.start()
+    take(3)
+    for copy in kept:
+        copy.wait()
+    for copy in pieces:
+        copy.wait()
+    token_one.wait_send()
+    token_two.wait_send()
+    for copy in token_three:
+        copy.wait_send()
+    for step in range(1, stages):
+        pl.when(right_sends(step))(lambda step=step: right(step).wait_send())
+        pl.when(left_sends(step))(lambda step=step: left(step).wait_send())
+
+        @pl.when(right_gets(step))
+        def _(step=step):
+            across(step, level - step).wait()
+
+        @pl.when(left_gets(step))
+        def _(step=step):
+            across(stages - 1 + step, level + step).wait()
+
+    remote(down, shard(down_full, level), mate_send.at[0], mate_receive.at[0], "dp", mate).wait()
+    cot_one.wait()
+    cot_two.wait()
+
+
+def opening(tokens, cot, down, fc_pieces, seq_count, dp_count):
+    piece, width = tokens.shape
+    steps = dp_count // 2 - 1
+    anywhere = pl.BlockSpec(memory_space=pl.ANY)
+    shape = lambda rows, columns: jax.ShapeDtypeStruct((rows, columns), BF16)
+    dma = pltpu.SemaphoreType.DMA
+    return pl.pallas_call(
+        opening_kernel,
+        in_specs=[anywhere] * 4,
+        out_specs=[anywhere] * 4,
+        out_shape=[
+            shape(piece * seq_count, width),
+            shape(piece * seq_count, width),
+            shape(down.shape[0] * dp_count, width),
+            shape(seq_count * fc_pieces.shape[1], fc_pieces.shape[2]),
+        ],
+        scratch_shapes=[
+            dma((4,)), dma((9,)), dma((9,)), dma((steps,)), dma((steps,)), dma((steps,)), dma((steps,)),
+            dma((2 * steps + 1,)), dma((2 * steps + 1,)),
+        ],
+        compiler_params=pltpu.CompilerParams(collective_id=0, has_side_effects=True),
+        cost_estimate=cost(0, 10 * piece * seq_count * width),
+    )(tokens, cot, down, fc_pieces)
+
+
+def plane_kernel(
+    normed, cot_in, fc, bias, down, middle, gain,
+    grad_middle, low, sums, active, hidden_grad, normed_all, cot_all, terms,
+    normed_buf, cot_buf, sum_ref, joined, passed, arrived, load, local, send, receive,
+):
+    piece, width = normed.shape
+    half = piece // 2
+    inner = fc.shape[1]
+    tile = min(512, inner)
+    last = inner // tile - 1
+    one, two = neighbours()
+    for device in (one, two):
+        greet("seq", device)
+    pl.semaphore_wait(pltpu.get_barrier_semaphore(), 2)
+
+    up, lower = pl.ds(0, half), pl.ds(half, half)
+    rows = lambda k, start=0, size=piece: pl.ds(k * piece + start, size)
+
+    def copy(index, source, target, device):
+        return remote(source, target, send.at[index], receive.at[index], "seq", device)
+
+    normed_one = copy(0, normed, normed_buf.at[1], one)
+    normed_two = copy(1, normed, normed_buf.at[2], two)
+    normed_three = (
+        copy(2, normed_buf.at[1, up], normed_buf.at[3, up], two),
+        copy(3, normed_buf.at[2, lower], normed_buf.at[3, lower], one),
+    )
+    cot_three = (
+        copy(4, cot_buf.at[1, up], cot_buf.at[3, up], two),
+        copy(5, cot_buf.at[2, lower], cot_buf.at[3, lower], one),
+    )
+    across = (copy(6, cot_buf.at[0, up], passed.at[0], one), copy(7, cot_buf.at[0, lower], passed.at[1], two))
+    plain_one = copy(8, cot_buf.at[1, up], arrived.at[0, up], one)
+    plain_two = copy(9, cot_buf.at[2, lower], arrived.at[1, lower], two)
+    joined_one = copy(10, joined.at[0], arrived.at[0, lower], one)
+    joined_two = copy(11, joined.at[1], arrived.at[1, up], two)
+
+    loads = [pltpu.make_async_copy(cot_in.at[rows(k)], cot_buf.at[k], load.at[k]) for k in range(3)]
+    own = pltpu.make_async_copy(normed, normed_buf.at[0], load.at[3])
+    keeps = [pltpu.make_async_copy(normed_buf.at[k], normed_all.at[rows(k)], local.at[k]) for k in range(4)]
+    keep_cot = pltpu.make_async_copy(cot_buf.at[3], cot_all.at[rows(3)], local.at[4])
+
+    normed_one.start()
+    normed_two.start()
+    own.start()
+    for item in loads:
+        item.start()
+
+    def feed_body(fc_tile, down_tile, active_tile, hidden_tile):
+        k, j = pl.program_id(0), pl.program_id(1)
+
+        @pl.when((k == 0) & (j == 0))
+        def _():
+            own.wait()
+            loads[0].wait()
+            keeps[0].start()
+
+        @pl.when((k == 1) & (j == 0))
+        def _():
+            normed_one.wait_recv()
+            normed_two.wait_recv()
+            for item in normed_three:
+                item.start()
+            loads[1].wait()
+            loads[2].wait()
+            for item in cot_three:
+                item.start()
+            keeps[1].start()
+            keeps[2].start()
+
+        @pl.when((k == 3) & (j == 0))
+        def _():
+            for item in normed_three + cot_three:
+                item.wait_recv()
+            keeps[3].start()
+            keep_cot.start()
+
+        weights = fc_tile[...]
+        hidden = nn(normed_buf[k], weights) + bias[:, pl.ds(pl.multiple_of(j * tile, tile), tile)]
+        grad_active = nt(cot_buf[k], down_tile[...])
+        square = hidden * hidden
+        bent = jnp.tanh(math.sqrt(2 / math.pi) * (hidden + 0.044715 * (square * hidden)))
+        share = 0.5 * (1.0 + bent)
+        active_tile[...] = (hidden * share).astype(BF16)
+        slope = share + (0.5 * hidden) * (1.0 - bent * bent) * (
+            math.sqrt(2 / math.pi) * (1.0 + (3 * 0.044715) * square)
+        )
+        grad_hidden = (grad_active * slope).astype(BF16)
+        hidden_tile[...] = grad_hidden
+        term = nt(grad_hidden, weights)
+
+        @pl.when(j == 0)
+        def _():
+            sum_ref[...] = term
+
+        @pl.when(j > 0)
+        def _():
+            sum_ref[...] += term
+
+        @pl.when((j == last) & (k == 0))
+        def _():
+            arrived[2] = sum_ref[...].astype(BF16)
+
+        @pl.when((j == last) & (k == 1))
+        def _():
+            cot_three[0].wait_send()
+            cot_buf[1] = sum_ref[...].astype(BF16)
+            plain_one.start()
+
+        @pl.when((j == last) & (k == 2))
+        def _():
+            cot_three[1].wait_send()
+            cot_buf[2] = sum_ref[...].astype(BF16)
+            plain_two.start()
+
+        @pl.when((j == last) & (k == 3))
+        def _():
+            cot_buf[0] = sum_ref[...].astype(BF16)
+            for item in across:
+                item.start()
+
+    pltpu.emit_pipeline(
+        feed_body,
+        grid=(4, inner // tile),
+        in_specs=[
+            pl.BlockSpec((width, tile), lambda k, j: (0, j)),
+            pl.BlockSpec((tile, width), lambda k, j: (j, 0)),
+        ],
+        out_specs=[pl.BlockSpec((piece, tile), lambda k, j: (k, j))] * 2,
+    )(fc, down, active, hidden_grad)
+
+    narrow = min(512, width)
+
+    def down_body(active_rows, down_columns, out):
+        out[...] = nn(active_rows[...], down_columns[...]).astype(BF16)
+
+    def multiply_down(start):
+        pltpu.emit_pipeline(
+            down_body,
+            grid=(2, width // narrow),
+            in_specs=[
+                pl.BlockSpec((piece, inner), lambda k, j: (start + k, 0)),
+                pl.BlockSpec((inner, narrow), lambda k, j: (0, j)),
+            ],
+            out_specs=[pl.BlockSpec((piece, narrow), lambda k, j: (start + k, j))],
+        )(active, down, terms)
+
+    multiply_down(0)
+    for item in across:
+        item.wait_recv()
+    joined[0] = (cot_buf[1, half:].astype(F32) + passed[1].astype(F32)).astype(BF16)
+    joined[1] = (cot_buf[2, :half].astype(F32) + passed[0].astype(F32)).astype(BF16)
+    joined_one.start()
+    joined_two.start()
+    multiply_down(2)
+    for item in (plain_one, plain_two, joined_one, joined_two):
+        item.wait_recv()
+
+    part = min(128, piece)
+
+    def norm_body(middle_tile, cot_tile, grad_tile, low_tile):
+        i = pl.program_id(0)
+        here = pl.ds(pl.multiple_of(i * part, part), part)
+        upstream = (
+            arrived[2, here, :].astype(F32) + arrived[0, here, :].astype(F32) + arrived[1, here, :].astype(F32)
+        )
+        values = middle_tile[...]
+        unit, scale = norm_parts(values)
+        cot = cot_tile[...].astype(F32)
+        grad = cot + norm_backward(unit, scale, gain[...], upstream)
+        rounded = grad.astype(BF16)
+        grad_tile[...] = grad
+        low_tile[...] = rounded
+        for at, item in enumerate((upstream * unit, upstream, rounded.astype(F32), cot)):
+            column = jnp.sum(item, axis=0, keepdims=True)
+
+            @pl.when(i == 0)
+            def _():
+                sums[at : at + 1, :] = column
+
+            @pl.when(i > 0)
+            def _():
+                sums[at : at + 1, :] += column
+
+    line = pl.BlockSpec((part, width), lambda i: (i, 0))
+    pltpu.emit_pipeline(norm_body, grid=(piece // part,), in_specs=[line] * 2, out_specs=[line] * 2)(
+        middle, cot_in, grad_middle, low
+    )
+    for item in keeps + [keep_cot]:
+        item.wait()
+    for item in (normed_one, normed_two, *normed_three, *across, plain_one, plain_two, joined_one, joined_two):
+        item.wait_send()
+
+
+def feed_plane(normed, cot_all, fc, bias, down, middle, gain):
+    piece, width = normed.shape
+    length, inner = cot_all.shape[0], fc.shape[1]
+    half = piece // 2
+    anywhere = pl.BlockSpec(memory_space=pl.ANY)
+    inside = pl.BlockSpec(memory_space=pltpu.VMEM)
+    shape = lambda rows, columns, kind=BF16: jax.ShapeDtypeStruct((rows, columns), kind)
+    dma = pltpu.SemaphoreType.DMA
+    return pl.pallas_call(
+        plane_kernel,
+        in_specs=[anywhere, anywhere, anywhere, inside, anywhere, anywhere, inside],
+        out_specs=[anywhere, anywhere, inside] + [anywhere] * 5,
+        out_shape=[
+            shape(piece, width, F32), shape(piece, width), shape(4, width, F32), shape(length, inner),
+            shape(length, inner), shape(length, width), shape(length, width), shape(length, width),
+        ],
+        scratch_shapes=[
+            pltpu.VMEM((4, piece, width), BF16),
+            pltpu.VMEM((4, piece, width), BF16),
+            pltpu.VMEM((piece, width), F32),
+            pltpu.VMEM((2, half, width), BF16),
+            pltpu.VMEM((2, half, width), BF16),
+            pltpu.VMEM((3, piece, width), BF16),
+            dma((4,)), dma((5,)), dma((12,)), dma((12,)),
+        ],
+        input_output_aliases={1: 6},
+        compiler_params=pltpu.CompilerParams(collective_id=1, has_side_effects=True, vmem_limit_bytes=60 * 2**20),
+        cost_estimate=cost(8 * length * width * inner, 10 * length * width),
+    )(normed, cot_all, fc, bias, down, middle, gain)
+
+
 def after(value, *others):
     return lax.optimization_barrier((value, *others))[0]
 
@@ -618,6 +1012,7 @@
     if seq_count == 4:
         order = [3, 1, 2, 0]
 
+    in_plane = seq_count == 4 and dp_count == 8
     qkv_pieces = (
         qkv_weight.reshape(rows, 3, own_heads, sub, high, HEAD_DIM)
         .transpose(4, 3, 0, 1, 2, 5)
@@ -625,14 +1020,13 @@
     )
     qkv_rows = jnp.concatenate(by_rank(exchange(qkv_pieces, seq_rank), seq_rank), axis=0)
     weights = [gather_dp(qkv_rows[:, i * own_width : (i + 1) * own_width]) for i in range(3)]
-    tokens_own = after(tokens[0], qkv_pieces)
-    token_blocks = gather_plane(tokens_own)
+    tokens_own, cot_own = tokens[0], cotangent[0]
 
     small = (attn_gain, attn_shift, qv_bias, proj_bias, mlp_gain, mlp_shift, fc_bias, down_bias)
     sizes = [item.shape[0] for item in small]
     positions = seq_rank * piece + jnp.arange(piece, dtype=jnp.int32)
     own_flags = ((key_mask[0] == 1) & (positions < lengths[0])).astype(BF16)
-    packed = after(jnp.concatenate(small + (own_flags,)), qkv_rows)
+    packed = jnp.concatenate(small + (own_flags,))
     blocks = gather_blocks(packed)
     flags = jnp.concatenate([item[-piece:] for item in blocks])
     key_bias = jnp.where(flags > 0, 0.0, NEG).astype(F32)[:, None]
@@ -652,21 +1046,27 @@
     )
     qv_own = qv_own.reshape(1, -1)
 
-    proj_full = gather_dp(lax.ppermute(after(proj_weight, qkv_rows), BOTH, swap))
+    proj_full = gather_dp(lax.ppermute(proj_weight, BOTH, swap))
     fc_pieces = (
-        after(fc_weight, qkv_rows)
-        .reshape(rows, dp_count, seq_count, block)
+        fc_weight.reshape(rows, dp_count, seq_count, block)
         .transpose(2, 0, 1, 3)
         .reshape(seq_count, rows, dp_count * block)
     )
-    fc_rows = jnp.concatenate(by_rank(exchange(fc_pieces, seq_rank), seq_rank), axis=0)
+    shared = None
+    if in_plane:
+        token_all, cot_all, down_full, fc_rows = opening(
+            after(tokens_own, qkv_rows, packed), cot_own, down_weight, fc_pieces, seq_count, dp_count
+        )
+        for k in range(seq_count):
+            shared = project(k, token_all, k, gain_one, shift_one, weights, qv_own, piece, seq_count, shared)
+    else:
+        token_blocks = gather_blocks(tokens_own)
+        cot_blocks = gather_blocks(after(cot_own, token_blocks[-1]))
+        down_full = gather_dp(down_weight)
+        fc_rows = jnp.concatenate(by_rank(exchange(fc_pieces, seq_rank), seq_rank), axis=0)
+        for k in range(seq_count):
+            shared = project(k, token_blocks[k], 0, gain_one, shift_one, weights, qv_own, piece, seq_count, shared)
     fc_full = gather_dp(fc_rows)
-    down_full = gather_dp(after(down_weight, fc_rows))
-
-    cot_blocks = gather_plane(after(cotangent[0], token_blocks[-1]))
-    shared = None
-    for k in range(seq_count):
-        shared = project(k, token_blocks[k], gain_one, shift_one, weights, qv_own, seq_count, shared)
     normed_one, q, keys, values, keys_t, values_t = shared
     proj_terms, shared = [None] * seq_count, None
     for k in order:
@@ -676,27 +1076,33 @@
         middle_kernel, scatter_plane(proj_terms), [tokens_own], [proj_shift, gain_two, shift_two], [F32, BF16], 0
     )
 
-    normed_blocks = gather_plane(normed_two)
-    grad_terms, shared = [], None
-    for k in range(seq_count):
-        term, shared = feed(k, normed_blocks[k], cot_blocks[k], fc_full, fc_shift, down_full, seq_count, shared)
-        grad_terms.append(term)
-    active, grad_hidden, normed_all, cot_all = shared
+    if in_plane:
+        grad_middle, grad_mid_low, sums_two, active, grad_hidden, normed_all, cot_all, down_terms = feed_plane(
+            normed_two, cot_all, fc_full, fc_shift, down_full, middle, gain_two
+        )
+        sums_two = [sums_two[i] for i in range(4)]
+        down_terms = [down_terms[k * piece : (k + 1) * piece] for k in range(seq_count)]
+    else:
+        normed_blocks = gather_blocks(normed_two)
+        grad_terms, shared = [], None
+        for k in range(seq_count):
+            term, shared = feed(k, normed_blocks[k], cot_blocks[k], fc_full, fc_shift, down_full, seq_count, shared)
+            grad_terms.append(term)
+        active, grad_hidden, normed_all, cot_all = shared
+        grad_middle, grad_mid_low, *sums_two = rowwise(
+            middle_back_kernel, scatter_blocks(grad_terms), [middle, cot_own], [gain_two], [F32, BF16], 4
+        )
+        down_terms = [
+            nn(active[k * piece : (k + 1) * piece], down_full).astype(BF16) for k in range(seq_count)
+        ]
+    low_blocks = gather_plane(grad_mid_low)
     grad_down = tn(active, cot_all).astype(BF16)
     grad_fc = tn(normed_all, grad_hidden).astype(BF16)
-    received = scatter_plane(grad_terms)
-    received[0] = after(received[0], grad_down, grad_fc)
-    grad_middle, grad_mid_low, *sums_two = rowwise(
-        middle_back_kernel, received, [middle, cotangent[0]], [gain_two], [F32, BF16], 4
-    )
-    low_blocks = gather_plane(grad_mid_low)
+    low_blocks[1] = after(low_blocks[1], grad_down, grad_fc)
     grad_down = scatter_dp(grad_down)
     grad_fc = scatter_dp(grad_fc)
-    down_terms = [
-        nn(active[k * piece : (k + 1) * piece], down_full).astype(BF16) for k in range(seq_count)
-    ]
-    low_blocks[1], *down_terms = lax.optimization_barrier((low_blocks[1], *down_terms))
     down_terms, _ = lax.optimization_barrier((down_terms, low_blocks[-1]))
+    block_out = rowwise(out_kernel, scatter_plane(down_terms), [middle], [down_shift], [BF16], 0)[0]
 
     sums, shared = None, None
     for k in range(seq_count):
@@ -705,6 +1111,7 @@
         )
     grad_q, low_all = shared
     grads = [grad_q, sums[0], sums[1]]
+    normed_one = after(normed_one, grad_down)
     grad_qkv = [scatter_dp(tn(normed_one, item).astype(BF16)) for item in grads]
     back_terms = [None] * seq_count
     for k in order:
@@ -712,7 +1119,6 @@
     tokens_grad, *sums_one = rowwise(
         tokens_back_kernel, scatter_plane(back_terms), [tokens_own, grad_middle], [gain_one], [F32], 2
     )
-    (block_out,) = rowwise(out_kernel, scatter_plane(down_terms), [middle], [down_shift], [BF16], 0)
     grad_proj = scatter_dp(tn(attended, low_all).astype(BF16))
     grad_proj = lax.ppermute(grad_proj, BOTH, swap).astype(F32)
 

time: 1130 us -> 1040 us (0.920)
  waiting for transfers between devices: 442 us -> 180 us
  Pallas kernels: 341 us -> 597 us
  matrix products: 124 us -> 86.4 us
  starting transfers between devices: 109 us -> 84.8 us
    pallas_call x0 -> x2, Pallas kernels: none -> 356 us  [the longest x1 187 us: feed_plane(): pl.pallas_call(plane_kernel, in_specs=[anywhere, anywhere, anywhere, insi...]
    ppermute x88 -> x67, waiting for transfers between devices: 388 us -> 178 us  [shift(): return lax.ppermute(value, axis, [(i, i ^ distance) for i in range(count)])]
    pallas_call x8 -> x4, Pallas kernels: 128 us -> 38.2 us  [call_on_block(): pl.pallas_call(body, grid=grid, in_specs=specs, out_specs=out_specs, out_...]
    reduce_scatter x6, waiting for transfers between devices: 51.4 us -> 0.05 us  [scatter_dp(): return lax.psum_scatter(value, 'dp', scatter_dimension=0, tiled=True)]
    dot_general x4 -> x0, matrix products: 37.9 us -> none  [nn(): lax.dot_general(left, right, (((1,), (0,)), ((), ())), preferred_element_...]
    ppermute x88 -> x67, starting transfers between devices: 106 us -> 81.5 us  [shift(): return lax.ppermute(value, axis, [(i, i ^ distance) for i in range(count)])]
    pallas_call x4 -> x3, Pallas kernels: 35.6 us -> 23.7 us  [rowwise(): pl.pallas_call(body, grid=(steps,), in_specs=specs, out_specs=[pl.BlockSp...]
  transfers between devices with their start and end apart: 102 -> 80, of which waited for: 38 -> 22; matrix products, arithmetic and copies ran while one was open for 16% -> 12% of each run, Pallas kernels for 19% -> 39%
where the time goes in v3:
time: 1040 us
  Pallas kernels  597 us (57%)
  waiting for transfers between devices  180 us (17%)
  matrix products  86.4 us (8%)
  starting transfers between devices  84.8 us (8%)
  local copies, waits for them, and re-layouts  54.3 us (5%)
  other arithmetic  18.9 us (2%)
  between operations  16 us (2%)
    pallas_call x1, Pallas kernels, feed_plane(): pl.pallas_call(plane_kernel, in_specs=[anywhere, anywhere, anywhere, insi...  187 us
    ppermute x67, waiting for transfers between devices, shift(): return lax.ppermute(value, axis, [(i, i ^ distance) for i in range(count)])  178 us
    pallas_call x1, Pallas kernels, opening(): pl.pallas_call(opening_kernel, in_specs=[anywhere] * 4, out_specs=[anywhe...  170 us
    pallas_call x8, Pallas kernels, call_on_block(): pl.pallas_call(body, grid_spec=pltpu.PrefetchScalarGridSpec(num_scalar_pr...  143 us
    dot_general x6, matrix products, tn(): lax.dot_general(left, right, (((0,), (0,)), ((), ())), preferred_element_...  86.4 us
    ppermute x67, starting transfers between devices, shift(): return lax.ppermute(value, axis, [(i, i ^ distance) for i in range(count)])  81.5 us
    pallas_call x4, Pallas kernels, call_on_block(): pl.pallas_call(body, grid=grid, in_specs=specs, out_specs=out_specs, out_...  38.2 us
    pallas_call x4, Pallas kernels, back(): pl.pallas_call(back_kernel, grid=(width // tile,), in_specs=[pl.BlockSpec...  30.8 us
  transfers between devices with their start and end apart: 80, of which 22 were waited for; matrix products, arithmetic and copies ran while one was open for 12% of the time, Pallas kernels for 39%

profile of v3, /device:TPU:0, one launch (start us, length us, event | category | flops | bytes accessed | tf_op | source)
XLA Modules:
  0.0 1037.8 jit_solution(11770773264210175033)
XLA Ops:
  29.2 8.2 collective-permute-start.5
  56.1 169.6 %shard_map.263 = (bf16[2048,2048]{1,0:T(8,128)(2,1)}, bf16[2048,2048]{1,0:T(8,128)(2,1)}, bf16[2048,2048]{1,0:T(8,128)(2,1)}, bf16[256,2048]{1,0:T(8,128)(2,1)}) custom-call(bf16[512,2048]{1,0:T(8,128)(2,1)} %bitcast.148, bf16[512,2048]{1,0:T(8,128)(2,1)} %bitcast.153, bf16[256,2048]{1,0:T(8,128)(2,1)} %down.1, bf16[4,64,2048]{2,1,0:T(8,128)(2,1)} %reshape.214.fc_pieces), custom_call_target="tpu_custom_call" | custom-call | bytes 41943040 | tf_op jit(solution)/shard_map/pallas_call | solution.py:654
  230.6 10.1 shard_map.264
  240.7 9.3 shard_map.265
  250.0 9.4 shard_map.266
  259.3 9.5 shard_map.267
  268.8 18.5 %shard_map.268 = (bf16[512,2048]{1,0:T(8,128)(2,1)}, bf16[2048,512]{1,0:T(8,128)(2,1)}, f32[4,1,2048]{2,1,0:T(1,128)}) custom-call(s32[1]{0:T(128)} %bitcast.refs_0_.rank_ref, bf16[2048,512]{1,0:T(8,128)(2,1)} %get-tuple-element.110.refs_1_.refs_3_, bf16[2048,512]{1,0:T(8,128)(2,1)} %get-tuple-element.111.refs_2_.refs_5_, ...), custom_call_target="tpu_custom_call" | custom-call | flops 2469606144 | bytes 8388608 | tf_op jit(solution)/shard_map/pallas_call | solution.py:68
  289.2 13.4 %shard_map.269 = (bf16[512,2048]{1,0:T(8,128)(2,1)}, bf16[2048,512]{1,0:T(8,128)(2,1)}, f32[4,1,2048]{2,1,0:T(1,128)}) custom-call(s32[1]{0:T(128)} %bitcast.refs_0_.rank_ref, bf16[2048,512]{1,0:T(8,128)(2,1)} %get-tuple-element.110.refs_1_.refs_3_, ...), custom_call_target="tpu_custom_call", output_to_operand_aliasing={{1}: (6, {}), {2}: (7, {})} | custom-call | flops 2469606144 | bytes 8388608 | tf_op jit(solution)/shard_map/pallas_call | solution.py:68
  305.0 15.9 %shard_map.270 = (bf16[512,2048]{1,0:T(8,128)(2,1)}, bf16[2048,512]{1,0:T(8,128)(2,1)}, f32[4,1,2048]{2,1,0:T(1,128)}) custom-call(s32[1]{0:T(128)} %bitcast.refs_0_.rank_ref, bf16[2048,512]{1,0:T(8,128)(2,1)} %get-tuple-element.110.refs_1_.refs_3_, ...), custom_call_target="tpu_custom_call", output_to_operand_aliasing={{1}: (6, {}), {2}: (7, {})} | custom-call | flops 2469606144 | bytes 8388608 | tf_op jit(solution)/shard_map/pallas_call | solution.py:68
  335.5 10.5 %shard_map.271 = (bf16[512,2048]{1,0:T(8,128)(2,1)}, bf16[2048,512]{1,0:T(8,128)(2,1)}, f32[4,1,2048]{2,1,0:T(1,128)}) custom-call(s32[1]{0:T(128)} %bitcast.refs_0_.rank_ref, bf16[2048,512]{1,0:T(8,128)(2,1)} %get-tuple-element.110.refs_1_.refs_3_, ...), custom_call_target="tpu_custom_call", output_to_operand_aliasing={{1}: (6, {}), {2}: (7, {})} | custom-call | flops 2469606144 | bytes 8388608 | tf_op jit(solution)/shard_map/pallas_call | solution.py:68
  349.6 21.3 %collective-permute-done.18.refs_3_ = bf16[256,2048]{1,0:T(8,128)(2,1)S(1)} collective-permute-done((bf16[256,2048]{1,0:T(8,128)(2,1)}, bf16[256,2048]{1,0:T(8,128)(2,1)S(1)}, u32[]{:S(2)}, u32[]{:S(2)}) %collective-permute-start.18) | collective-permute-done | bytes 1048608 | tf_op jit(solution)/shard_map/ppermute | solution.py:904
  379.4 186.5 %shard_map.273 = (f32[512,2048]{1,0:T(8,128)}, bf16[512,2048]{1,0:T(8,128)(2,1)}, f32[4,2048]{1,0:T(4,128)}, bf16[2048,2048]{1,0:T(8,128)(2,1)}, bf16[2048,2048]...) custom-call(bf16[512,2048]{1,0:T(8,128)(2,1)} %get-tuple-element.123, ...), custom_call_target="tpu_custom_call", output_to_operand_aliasing={{6}: (1, {})} | custom-call | flops 68719476736 | bytes 41943040 | tf_op jit(solution)/shard_map/pallas_call | solution.py:875
  565.9 23.8 %convolution_convert_fusion.1 = bf16[2048,2048]{1,0:T(8,128)(2,1)} fusion(bf16[2048,2048]{1,0:T(8,128)(2,1)} %get-tuple-element.137, bf16[2048,2048]{1,0:T(8,128)(2,1)} %get-tuple-element.138), kind=kOutput, calls=%fused_computation.2 | convolution fusion | flops 17184063488 | bytes 25165824 | tf_op jit(solution)/shard_map/dot_general | solution.py:32
  589.8 24.4 %convolution_convert_fusion = bf16[2048,2048]{1,0:T(8,128)(2,1)} fusion(bf16[2048,2048]{1,0:T(8,128)(2,1)} %get-tuple-element.139, bf16[2048,2048]{1,0:T(8,128)(2,1)} %get-tuple-element.140), kind=kOutput, calls=%fused_computation.1 | convolution fusion | flops 17184063488 | bytes 25165824 | tf_op jit(solution)/shard_map/dot_general | solution.py:32
  615.9 42.7 %collective-permute-done.20.refs_1_ = bf16[512,2048]{1,0:T(8,128)(2,1)S(1)} collective-permute-done((bf16[512,2048]{1,0:T(8,128)(2,1)}, bf16[512,2048]{1,0:T(8,128)(2,1)S(1)}, u32[]{:S(2)}, u32[]{:S(2)}) %collective-permute-start.20) | collective-permute-done | bytes 2097184 | tf_op jit(solution)/shard_map/ppermute | solution.py:904
  659.1 15.1 %shard_map.275 = (f32[2048,512]{1,0:T(8,128)}, f32[2048,512]{1,0:T(8,128)}, bf16[2048,512]{1,0:T(8,128)(2,1)}, bf16[2048,2048]{1,0:T(8,128)(2,1)}) custom-call(s32[1]{0:T(128)} %bitcast.refs_0_.rank_ref, bf16[512,2048]{1,0:T(8,128)(2,1)} %get-tuple-element.129.refs_1_, bf16[512,2048]{1,0:T(8,128)(2,1)} %all-gather.12.cloned.1.call-done.refs_5_.refs_2_, ...), custom_call_target="tpu_custom_call" | custom-call | flops 4563402752 | bytes 20971520 | tf_op jit(solution)/shard_map/pallas_call | solution.py:68
  680.8 19.8 %shard_map.276 = (f32[2048,512]{1,0:T(8,128)}, f32[2048,512]{1,0:T(8,128)}, bf16[2048,512]{1,0:T(8,128)(2,1)}, bf16[2048,2048]{1,0:T(8,128)(2,1)}) custom-call(s32[1]{0:T(128)} %bitcast.refs_0_.rank_ref, bf16[512,2048]{1,0:T(8,128)(2,1)} %copy-done.10, ...), custom_call_target="tpu_custom_call", output_to_operand_aliasing={{2}: (11, {}), {3}: (12, {})} | custom-call | flops 4563402752 | bytes 20971520 | tf_op jit(solution)/shard_map/pallas_call | solution.py:68
  700.6 23.1 %shard_map.277 = (f32[2048,512]{1,0:T(8,128)}, f32[2048,512]{1,0:T(8,128)}, bf16[2048,512]{1,0:T(8,128)(2,1)}, bf16[2048,2048]{1,0:T(8,128)(2,1)}) custom-call(s32[1]{0:T(128)} %bitcast.refs_0_.rank_ref, bf16[512,2048]{1,0:T(8,128)(2,1)} %copy-done.9, ...), custom_call_target="tpu_custom_call", output_to_operand_aliasing={{2}: (11, {}), {3}: (12, {})} | custom-call | flops 4563402752 | bytes 20971520 | tf_op jit(solution)/shard_map/pallas_call | solution.py:68
  725.4 27.0 %shard_map.278 = (bf16[2048,512]{1,0:T(8,128)(2,1)}, bf16[2048,512]{1,0:T(8,128)(2,1)}, bf16[2048,512]{1,0:T(8,128)(2,1)}, bf16[2048,2048]{1,0:T(8,128)(2,1)}) custom-call(s32[1]{0:T(128)} %bitcast.refs_0_.rank_ref, bf16[512,2048]{1,0:T(8,128)(2,1)} %copy-done.11, ...), custom_call_target="tpu_custom_call", output_to_operand_aliasing={{2}: (11, {}), {3}: (12, {})} | custom-call | flops 4563402752 | bytes 20971520 | tf_op jit(solution)/shard_map/pallas_call | solution.py:68
  752.4 9.6 convolution_convert_fusion.2
  763.6 9.5 convolution_convert_fusion.4
  788.5 9.6 convolution_convert_fusion.3
  802.2 7.7 shard_map.281
  814.4 7.6 shard_map.282
  821.9 7.7 shard_map.280
  832.8 9.5 convolution_convert_fusion.5
  842.3 7.8 shard_map.279.refs_0_
  860.9 18.8 %collective-permute-done.27 = bf16[256,2048]{1,0:T(8,128)(2,1)S(1)} collective-permute-done((bf16[256,2048]{1,0:T(8,128)(2,1)S(1)}, bf16[256,2048]{1,0:T(8,128)(2,1)S(1)}, u32[]{:S(2)}, u32[]{:S(2)}) %collective-permute-start.27) | collective-permute-done | bytes 1048608 | tf_op jit(solution)/shard_map/ppermute | solution.py:904
  888.4 17.4 %collective-permute-done.35.refs_4_ = bf16[256,2048]{1,0:T(8,128)(2,1)S(1)} collective-permute-done((bf16[256,2048]{1,0:T(8,128)(2,1)S(1)}, bf16[256,2048]{1,0:T(8,128)(2,1)S(1)}, u32[]{:S(2)}, u32[]{:S(2)}) %collective-permute-start.35) | collective-permute-done | bytes 1048608 | tf_op jit(solution)/shard_map/ppermute | solution.py:904
  907.0 21.3 %collective-permute-done.34.refs_3_ = bf16[256,2048]{1,0:T(8,128)(2,1)S(1)} collective-permute-done((bf16[256,2048]{1,0:T(8,128)(2,1)S(1)}, bf16[256,2048]{1,0:T(8,128)(2,1)S(1)}, u32[]{:S(2)}, u32[]{:S(2)}) %collective-permute-start.34) | collective-permute-done | bytes 1048608 | tf_op jit(solution)/shard_map/ppermute | solution.py:904
  929.7 9.5 shard_map.283
  951.7 16.3 %collective-permute-done.36 = f32[8,256]{1,0:T(8,128)S(1)} collective-permute-done((f32[8,256]{1,0:T(8,128)S(1)}, f32[8,256]{1,0:T(8,128)S(1)}, u32[]{:S(2)}, u32[]{:S(2)}) %collective-permute-start.36) | collective-permute-done | bytes 8224 | tf_op jit(solution)/shard_map/ppermute | solution.py:904
  (387 shorter events, 211.4 us)
Async XLA Ops:
  7.2 223.4 %all-gather.10.cloned.1.call-start = ((), (), s32[]{:S(2)}) async-start(), calls=%async_computation.8 | async-start | bytes 2359296 | tf_op jit(solution)/shard_map/all_gather | solution.py:975
  25.3 205.3 %all-gather.8.cloned.1.call-start = ((), (), s32[]{:S(2)}) async-start(), calls=%async_computation.7 | async-start | bytes 2359296 | tf_op jit(solution)/shard_map/all_gather | solution.py:975
  26.0 204.5 %all-gather.6.cloned.1.call-start = ((), (), s32[]{:S(2)}) async-start(), calls=%async_computation.6 | async-start | bytes 2359296 | tf_op jit(solution)/shard_map/all_gather | solution.py:975
  26.8 242.0 %all-gather.12.cloned.1.call-start = ((), (), s32[]{:S(2)}) async-start(), calls=%async_computation.9 | async-start | bytes 2359296 | tf_op jit(solution)/shard_map/all_gather | solution.py:975
  28.3 351.1 %all-gather.14.cloned.1.call-start = ((), (), s32[]{:S(2)}) async-start(), calls=%async_computation.10 | async-start | bytes 9437184 | tf_op jit(solution)/shard_map/all_gather | solution.py:975
  225.7 536.4 %reduce-scatter.7.cloned.1.call-start = ((), (), s32[]{:S(2)}) async-start(), calls=%async_computation.11 | async-start | bytes 9437184 | tf_op jit(solution)/shard_map/reduce_scatter | solution.py:979
  289.2 37.6 %collective-permute-start.15 = (bf16[256,2048]{1,0:T(8,128)(2,1)S(1)}, bf16[256,2048]{1,0:T(8,128)(2,1)S(1)}, u32[]{:S(2)}, u32[]{:S(2)}) collective-permute-start(bf16[256,2048]{1,0:T(8,128)(2,1)S(1)} %get-tuple-element.189), channel_id=1, source_target_pairs={{0,2},{1,3},{2,0},{3,1},{4,6},{5,7},{6,4},{7,5},{8,10},{9,11},{10,... | collective-permute-start | bytes 3145736 | tf_op jit(solution)/shard_map/ppermute | solution.py:904
  305.0 41.0 %collective-permute-start.14 = (bf16[256,2048]{1,0:T(8,128)(2,1)}, bf16[256,2048]{1,0:T(8,128)(2,1)S(1)}, u32[]{:S(2)}, u32[]{:S(2)}) collective-permute-start(bf16[256,2048]{1,0:T(8,128)(2,1)} %slice.173), channel_id=1, source_target_pairs={{0,1},{1,0},{2,3},{3,2},{4,5},{5,4},{6,7},{7,6},{8,9},{9,8},{10,11... | collective-permute-start | bytes 3145736 | tf_op jit(solution)/shard_map/ppermute | solution.py:904
  326.6 44.3 %collective-permute-start.18 = (bf16[256,2048]{1,0:T(8,128)(2,1)}, bf16[256,2048]{1,0:T(8,128)(2,1)S(1)}, u32[]{:S(2)}, u32[]{:S(2)}) collective-permute-start(bf16[256,2048]{1,0:T(8,128)(2,1)} %add_convert_fusion.4), channel_id=1, source_target_pairs={{0,2},{1,3},{2,0},{3,1},{4,6},{5,7},{6,4},{7,5},{8,10},{9,11},{10,... | collective-permute-start | bytes 3145736 | tf_op jit(solution)/shard_map/ppermute | solution.py:904
  328.1 42.8 %collective-permute-start.16 = (bf16[256,2048]{1,0:T(8,128)(2,1)}, bf16[256,2048]{1,0:T(8,128)(2,1)}, u32[]{:S(2)}, u32[]{:S(2)}) collective-permute-start(bf16[256,2048]{1,0:T(8,128)(2,1)} %add_convert_fusion.5), channel_id=1, source_target_pairs={{0,1},{1,0},{2,3},{3,2},{4,5},{5,4},{6,7},{7,6},{8,9},{9,8},{10,11... | collective-permute-start | bytes 3145736 | tf_op jit(solution)/shard_map/ppermute | solution.py:904
  589.8 402.7 %reduce-scatter.17.cloned.1.call-start = ((), (), s32[]{:S(2)}) async-start(), calls=%async_computation.16 | async-start | bytes 9437184 | tf_op jit(solution)/shard_map/reduce_scatter | solution.py:979
  614.2 380.3 %reduce-scatter.15.cloned.1.call-start = ((), (), s32[]{:S(2)}) async-start(), calls=%async_computation.15 | async-start | bytes 2359296 | tf_op jit(solution)/shard_map/reduce_scatter | solution.py:979
  614.3 44.3 %collective-permute-start.20 = (bf16[512,2048]{1,0:T(8,128)(2,1)}, bf16[512,2048]{1,0:T(8,128)(2,1)S(1)}, u32[]{:S(2)}, u32[]{:S(2)}) collective-permute-start(bf16[512,2048]{1,0:T(8,128)(2,1)} %get-tuple-element.129.refs_1_), channel_id=1, source_target_pairs={{0,1},{1,0},{2,3},{3,2},{4,5},{5,4},{6,7},{7,6},{8,9},{9,8},{10,11... | collective-permute-start | bytes 6291464 | tf_op jit(solution)/shard_map/ppermute | solution.py:904
  614.3 59.8 %collective-permute-start.22 = (bf16[512,2048]{1,0:T(8,128)(2,1)}, bf16[512,2048]{1,0:T(8,128)(2,1)S(1)}, u32[]{:S(2)}, u32[]{:S(2)}) collective-permute-start(bf16[512,2048]{1,0:T(8,128)(2,1)} %get-tuple-element.129.refs_1_), channel_id=1, source_target_pairs={{0,2},{1,3},{2,0},{3,1},{4,6},{5,7},{6,4},{7,5},{8,10},{9,11},{10,... | collective-permute-start | bytes 6291464 | tf_op jit(solution)/shard_map/ppermute | solution.py:904
  658.7 65.0 %collective-permute-start.21 = (bf16[256,2048]{1,0:T(8,128)(2,1)S(1)}, bf16[256,2048]{1,0:T(8,128)(2,1)S(1)}, u32[]{:S(2)}, u32[]{:S(2)}) collective-permute-start(bf16[256,2048]{1,0:T(8,128)(2,1)S(1)} %slice.230), channel_id=1, source_target_pairs={{0,2},{1,3},{2,0},{3,1},{4,6},{5,7},{6,4},{7,5},{8,10},{9,11},{10,... | collective-permute-start | bytes 3145736 | tf_op jit(solution)/shard_map/ppermute | solution.py:904
  675.4 48.5 %collective-permute-start.23 = (bf16[256,2048]{1,0:T(8,128)(2,1)}, bf16[256,2048]{1,0:T(8,128)(2,1)S(1)}, u32[]{:S(2)}, u32[]{:S(2)}) collective-permute-start(bf16[256,2048]{1,0:T(8,128)(2,1)} %slice.231), channel_id=1, source_target_pairs={{0,1},{1,0},{2,3},{3,2},{4,5},{5,4},{6,7},{7,6},{8,9},{9,8},{10,11... | collective-permute-start | bytes 3145736 | tf_op jit(solution)/shard_map/ppermute | solution.py:904
  762.0 237.8 %reduce-scatter.11.cloned.1.call-start = ((), (), s32[]{:S(2)}) async-start(), calls=%async_computation.13 | async-start | bytes 2359296 | tf_op jit(solution)/shard_map/reduce_scatter | solution.py:979
  773.1 230.5 %reduce-scatter.13.cloned.1.call-start = ((), (), s32[]{:S(2)}) async-start(), calls=%async_computation.14 | async-start | bytes 2359296 | tf_op jit(solution)/shard_map/reduce_scatter | solution.py:979
  798.1 215.1 %reduce-scatter.9.cloned.1.call-start = ((), (), s32[]{:S(2)}) async-start(), calls=%async_computation.12 | async-start | bytes 2359296 | tf_op jit(solution)/shard_map/reduce_scatter | solution.py:979
  798.2 60.5 %collective-permute-start.65 = (f32[512]{0:T(512)S(1)}, f32[512]{0:T(512)S(1)}, u32[]{:S(2)}, u32[]{:S(2)}) collective-permute-start(f32[512]{0:T(512)S(1)} %bitcast.182), channel_id=1, source_target_pairs={{0,28},{4,24},{8,20},{12,16},{16,12},{20,8},{24,4},{28,0},{1,29},{... | collective-permute-start | bytes 6152 | tf_op jit(solution)/shard_map/ppermute | solution.py:904
  798.3 61.5 %collective-permute-start.59 = (f32[512]{0:T(512)S(1)}, f32[512]{0:T(512)S(1)}, u32[]{:S(2)}, u32[]{:S(2)}) collective-permute-start(f32[512]{0:T(512)S(1)} %bitcast.181), channel_id=1, source_target_pairs={{0,4},{4,0},{8,12},{12,8},{16,20},{20,16},{24,28},{28,24},{1,5},{5... | collective-permute-start | bytes 6152 | tf_op jit(solution)/shard_map/ppermute | solution.py:904
  799.0 60.9 %collective-permute-start.64 = (f32[512]{0:T(512)S(1)}, f32[512]{0:T(512)S(1)}, u32[]{:S(2)}, u32[]{:S(2)}) collective-permute-start(f32[512]{0:T(512)S(1)} %bitcast.180), channel_id=1, source_target_pairs={{0,24},{4,28},{8,16},{12,20},{16,8},{20,12},{24,0},{28,4},{1,25},{... | collective-permute-start | bytes 6152 | tf_op jit(solution)/shard_map/ppermute | solution.py:904
  813.2 40.2 %collective-permute-start.33 = (bf16[256,2048]{1,0:T(8,128)(2,1)}, bf16[256,2048]{1,0:T(8,128)(2,1)}, u32[]{:S(2)}, u32[]{:S(2)}) collective-permute-start(bf16[256,2048]{1,0:T(8,128)(2,1)} %get-tuple-element.184), channel_id=1, source_target_pairs={{0,1},{1,0},{2,3},{3,2},{4,5},{5,4},{6,7},{7,6},{8,9},{9,8},{10,11... | collective-permute-start | bytes 3145736 | tf_op jit(solution)/shard_map/ppermute | solution.py:904
  813.3 43.9 %collective-permute-start.31 = (bf16[256,2048]{1,0:T(8,128)(2,1)}, bf16[256,2048]{1,0:T(8,128)(2,1)S(1)}, u32[]{:S(2)}, u32[]{:S(2)}) collective-permute-start(bf16[256,2048]{1,0:T(8,128)(2,1)} %get-tuple-element.185), channel_id=1, source_target_pairs={{0,2},{1,3},{2,0},{3,1},{4,6},{5,7},{6,4},{7,5},{8,10},{9,11},{10,... | collective-permute-start | bytes 3145736 | tf_op jit(solution)/shard_map/ppermute | solution.py:904
  858.7 47.1 %collective-permute-start.35 = (bf16[256,2048]{1,0:T(8,128)(2,1)S(1)}, bf16[256,2048]{1,0:T(8,128)(2,1)S(1)}, u32[]{:S(2)}, u32[]{:S(2)}) collective-permute-start(bf16[256,2048]{1,0:T(8,128)(2,1)S(1)} %slice.238), channel_id=1, source_target_pairs={{0,2},{1,3},{2,0},{3,1},{4,6},{5,7},{6,4},{7,5},{8,10},{9,11},{10,... | collective-permute-start | bytes 3145736 | tf_op jit(solution)/shard_map/ppermute | solution.py:904
  859.7 46.2 %collective-permute-start.30 = (bf16[256,2048]{1,0:T(8,128)(2,1)S(1)}, bf16[256,2048]{1,0:T(8,128)(2,1)S(1)}, u32[]{:S(2)}, u32[]{:S(2)}) collective-permute-start(bf16[256,2048]{1,0:T(8,128)(2,1)S(1)} %slice.233), channel_id=1, source_target_pairs={{0,1},{1,0},{2,3},{3,2},{4,5},{5,4},{6,7},{7,6},{8,9},{9,8},{10,11... | collective-permute-start | bytes 3145736 | tf_op jit(solution)/shard_map/ppermute | solution.py:904
  859.9 68.4 %collective-permute-start.34 = (bf16[256,2048]{1,0:T(8,128)(2,1)S(1)}, bf16[256,2048]{1,0:T(8,128)(2,1)S(1)}, u32[]{:S(2)}, u32[]{:S(2)}) collective-permute-start(bf16[256,2048]{1,0:T(8,128)(2,1)S(1)} %add_convert_fusion), channel_id=1, source_target_pairs={{0,2},{1,3},{2,0},{3,1},{4,6},{5,7},{6,4},{7,5},{8,10},{9,11},{10,... | collective-permute-start | bytes 3145736 | tf_op jit(solution)/shard_map/ppermute | solution.py:904
  879.7 48.8 %collective-permute-start.32 = (bf16[256,2048]{1,0:T(8,128)(2,1)S(1)}, bf16[256,2048]{1,0:T(8,128)(2,1)S(1)}, u32[]{:S(2)}, u32[]{:S(2)}) collective-permute-start(bf16[256,2048]{1,0:T(8,128)(2,1)S(1)} %add_convert_fusion.1), channel_id=1, source_target_pairs={{0,1},{1,0},{2,3},{3,2},{4,5},{5,4},{6,7},{7,6},{8,9},{9,8},{10,11... | collective-permute-start | bytes 3145736 | tf_op jit(solution)/shard_map/ppermute | solution.py:904
  887.4 89.0 %collective-permute-start.29 = (bf16[256,2048]{1,0:T(8,128)(2,1)}, bf16[256,2048]{1,0:T(8,128)(2,1)S(1)}, u32[]{:S(2)}, u32[]{:S(2)}) collective-permute-start(bf16[256,2048]{1,0:T(8,128)(2,1)} %slice.194), channel_id=1, source_target_pairs={{0,2},{1,3},{2,0},{3,1},{4,6},{5,7},{6,4},{7,5},{8,10},{9,11},{10,... | collective-permute-start | bytes 3145736 | tf_op jit(solution)/shard_map/ppermute | solution.py:904
  905.8 71.4 %collective-permute-start.24 = (bf16[256,2048]{1,0:T(8,128)(2,1)}, bf16[256,2048]{1,0:T(8,128)(2,1)S(1)}, u32[]{:S(2)}, u32[]{:S(2)}) collective-permute-start(bf16[256,2048]{1,0:T(8,128)(2,1)} %slice.189), channel_id=1, source_target_pairs={{0,1},{1,0},{2,3},{3,2},{4,5},{5,4},{6,7},{7,6},{8,9},{9,8},{10,11... | collective-permute-start | bytes 3145736 | tf_op jit(solution)/shard_map/ppermute | solution.py:904
  905.9 71.3 %collective-permute-start.28 = (bf16[256,2048]{1,0:T(8,128)(2,1)S(1)}, bf16[256,2048]{1,0:T(8,128)(2,1)}, u32[]{:S(2)}, u32[]{:S(2)}) collective-permute-start(bf16[256,2048]{1,0:T(8,128)(2,1)S(1)} %add_convert_fusion.2), channel_id=1, source_target_pairs={{0,2},{1,3},{2,0},{3,1},{4,6},{5,7},{6,4},{7,5},{8,10},{9,11},{10,... | collective-permute-start | bytes 3145736 | tf_op jit(solution)/shard_map/ppermute | solution.py:904
  928.3 48.9 %collective-permute-start.26 = (bf16[256,2048]{1,0:T(8,128)(2,1)}, bf16[256,2048]{1,0:T(8,128)(2,1)}, u32[]{:S(2)}, u32[]{:S(2)}) collective-permute-start(bf16[256,2048]{1,0:T(8,128)(2,1)} %add_convert_fusion.3), channel_id=1, source_target_pairs={{0,1},{1,0},{2,3},{3,2},{4,5},{5,4},{6,7},{7,6},{8,9},{9,8},{10,11... | collective-permute-start | bytes 3145736 | tf_op jit(solution)/shard_map/ppermute | solution.py:904
  (100 other events, 964.0 us)
Sparse Core Ops, SparseCore 0:
  25.4 30.8 all-gather.9
  58.5 40.2 all-gather.7
  101.0 37.3 all-gather.5
  139.9 35.7 all-gather.11
  225.8 80.0 all-gather.13
  589.9 87.3 reduce-scatter.6
  679.5 87.9 reduce-scatter.16
  769.8 34.1 reduce-scatter.14
  806.3 34.1 reduce-scatter.10
  842.6 34.6 reduce-scatter.12
  879.6 34.3 reduce-scatter.8

commit v4 on v3

--- a/solution.py
+++ b/solution.py
@@ -104,28 +104,26 @@
     v_t[...] = values.T.astype(BF16)
 
 
-def project(at, x, first, gain, shift_, weights, bias, piece, count, previous):
-    width = x.shape[1]
-    columns = weights[0].shape[1]
-    tile = min(256, piece)
-    steps = piece // tile
+def project(at, x, first, rows_here, gain, shift_, weight, bias, count, previous):
+    width, columns = x.shape[1], weight.shape[1] // 3
+    tile = min(256, rows_here)
+    steps = rows_here // tile
     whole = lambda shape: pl.BlockSpec(shape, lambda i: (0, 0))
     rows = lambda n: pl.BlockSpec((tile, n), lambda i: (at * steps + i, 0))
     turned = pl.BlockSpec((columns, tile), lambda i: (0, at * steps + i))
-    length = piece * count
     inputs = [
         (x, pl.BlockSpec((tile, width), lambda i: (first * steps + i, 0))),
         (gain, whole((1, width))),
         (shift_, whole((1, width))),
-        *[(item, whole((width, columns))) for item in weights],
+        *[(weight, pl.BlockSpec((width, columns), lambda i, part=part: (0, part))) for part in range(3)],
         (bias, whole((1, 2 * columns))),
     ]
     shape = lambda *dims: jax.ShapeDtypeStruct(dims, BF16)
-    shared = [(shape(length, width), rows(width))] + [(shape(length, columns), rows(columns))] * 3
-    shared += [(shape(columns, length), turned)] * 2
+    shared = [(shape(count, width), rows(width))] + [(shape(count, columns), rows(columns))] * 3
+    shared += [(shape(columns, count), turned)] * 2
     return call_on_block(
         project_kernel, (steps,), inputs, [], shared, previous, [],
-        cost(6 * piece * width * columns, 4 * piece * width + 6 * width * columns + 10 * piece * columns),
+        cost(6 * rows_here * width * columns, 4 * rows_here * width + 6 * width * columns + 10 * rows_here * columns),
     )[1]
 
 
@@ -360,23 +358,25 @@
     )
 
 
-def back_kernel(dq, dk, dv, wq, wk, wv, out):
-    out[...] = (nt(dq[...], wq[...]) + nt(dk[...], wk[...]) + nt(dv[...], wv[...])).astype(BF16)
-
-
-def back(at, grads, weights, piece):
-    columns, width = grads[0].shape[1], weights[0].shape[0]
+def back_kernel(grads, weight, out):
+    out[...] = nt(grads[...], weight[...]).astype(BF16)
+
+
+def back(at, grads, weight, piece):
+    columns, width = grads.shape[1], weight.shape[0]
     tile = min(512, width)
     return pl.pallas_call(
         back_kernel,
         grid=(width // tile,),
-        in_specs=[pl.BlockSpec((piece, columns), lambda j: (at, 0))] * 3
-        + [pl.BlockSpec((tile, columns), lambda j: (j, 0))] * 3,
+        in_specs=[
+            pl.BlockSpec((piece, columns), lambda j: (at, 0)),
+            pl.BlockSpec((tile, columns), lambda j: (j, 0)),
+        ],
         out_specs=pl.BlockSpec((piece, tile), lambda j: (0, j)),
         out_shape=jax.ShapeDtypeStruct((piece, width), BF16),
         compiler_params=params(),
-        cost_estimate=cost(6 * piece * width * columns, 6 * width * columns + 6 * piece * columns + 2 * piece * width),
-    )(*grads, *weights)
+        cost_estimate=cost(2 * piece * width * columns, 2 * width * columns + 2 * piece * (columns + width)),
+    )(grads, weight)
 
 
 def part_specs(parts, tile, steps, width):
@@ -518,13 +518,11 @@
 
 
 def opening_kernel(
-    tokens, cot, down, fc_pieces, token_all, cot_all, down_full, fc_rows,
-    local, send, receive, right_send, right_receive, left_send, left_receive, mate_send, mate_receive,
+    tokens, qkv_pieces, fc_pieces, small, token_all, qkv_full, fc_rows, small_full,
+    qkv_rows, small_rows, local, send, receive, up_send, up_receive, down_send, down_receive, mate_send, mate_receive,
 ):
     piece = tokens.shape[0]
     half = piece // 2
-    rows = down.shape[0]
-    fine = fc_pieces.shape[1]
     me, place = lax.axis_index("seq"), lax.axis_index("dp")
     one, two = neighbours()
     three = 3 - me
@@ -543,141 +541,338 @@
     def block(ref, at, start=0, size=piece):
         return ref.at[pl.ds(at * piece + start, size)]
 
-    def pair(source, target, at):
-        return (
-            remote(source, block(target, 1), send.at[at], receive.at[at], "seq", one),
-            remote(source, block(target, 2), send.at[at + 1], receive.at[at + 1], "seq", two),
-        )
-
-    token_one, token_two = pair(tokens, token_all, 0)
+    def spread(pieces, target, at):
+        rows = target.shape[0] // 4
+        mine = target.at[pl.ds(me * rows, rows)]
+        source = lambda device: pieces if pieces is small else pieces.at[device]
+        copies = [
+            remote(source(device), mine, send.at[at + i], receive.at[at + i], "seq", device)
+            for i, device in enumerate((one, two, three))
+        ]
+        return copies, source(me), mine
+
+    qkv_copies, qkv_own, qkv_mine = spread(qkv_pieces, qkv_rows, 0)
+    small_copies, small_own, small_mine = spread(small, small_rows, 3)
+    fc_copies, fc_own, fc_mine = spread(fc_pieces, fc_rows, 6)
+    token_one = remote(tokens, block(token_all, 1), send.at[9], receive.at[9], "seq", one)
+    token_two = remote(tokens, block(token_all, 2), send.at[10], receive.at[10], "seq", two)
     token_three = (
-        remote(block(token_all, 1, 0, half), block(token_all, 3, 0, half), send.at[2], receive.at[2], "seq", two),
-        remote(block(token_all, 2, half, half), block(token_all, 3, half, half), send.at[3], receive.at[3], "seq", one),
-    )
-    cot_one, cot_two = pair(cot, cot_all, 4)
-    mine = fc_rows.at[pl.ds(me * fine, fine)]
-    pieces = [
-        remote(fc_pieces.at[device], mine, send.at[6 + i], receive.at[6 + i], "seq", device)
-        for i, device in enumerate((one, two, three))
-    ]
-    shard = lambda ref, at: ref.at[pl.ds((2 * at + core) * rows, rows)]
-    kept = [
-        pltpu.make_async_copy(tokens, block(token_all, 0), local.at[0]),
-        pltpu.make_async_copy(cot, block(cot_all, 0), local.at[1]),
-        pltpu.make_async_copy(down, shard(down_full, level), local.at[2]),
-        pltpu.make_async_copy(fc_pieces.at[me], mine, local.at[3]),
-    ]
-
-    def right(step):
+        remote(block(token_all, 1, 0, half), block(token_all, 3, 0, half), send.at[11], receive.at[11], "seq", two),
+        remote(block(token_all, 2, half, half), block(token_all, 3, half, half), send.at[12], receive.at[12], "seq", one),
+    )
+    first_kept = [pltpu.make_async_copy(qkv_own, qkv_mine, local.at[0]), pltpu.make_async_copy(small_own, small_mine, local.at[1])]
+    later_kept = [pltpu.make_async_copy(fc_own, fc_mine, local.at[2]), pltpu.make_async_copy(tokens, block(token_all, 0), local.at[3])]
+
+    chains = ((qkv_rows, qkv_full), (small_rows, small_full))
+
+    def shard(array, at):
+        rows = chains[array][0].shape[0]
+        return chains[array][1].at[pl.ds((2 * at + core) * rows, rows)]
+
+    def rising(array, step, device):
         at = level - (step - 1)
-        source = down if step == 1 else shard(down_full, at)
-        return remote(source, shard(down_full, at), right_send.at[step - 1], right_receive.at[step - 1], "dp", place + 2)
-
-    def left(step):
+        source = chains[array][0] if step == 1 else shard(array, at)
+        return remote(source, shard(array, at), up_send.at[array, step - 1], up_receive.at[array, step - 1], "dp", device)
+
+    def falling(array, step, device):
         at = level + (step - 1)
-        source = down if step == 1 else shard(down_full, at)
-        return remote(source, shard(down_full, at), left_send.at[step - 1], left_receive.at[step - 1], "dp", place - 2)
-
-    def across(index, at):
-        return remote(shard(down_full, at), shard(down_full, at), mate_send.at[index], mate_receive.at[index], "dp", mate)
-
-    right_sends = lambda step: above & (level >= step - 1)
-    left_sends = lambda step: below & (level <= stages - step)
-    right_gets = lambda step: level >= step
-    left_gets = lambda step: level + step <= stages - 1
+        source = chains[array][0] if step == 1 else shard(array, at)
+        return remote(source, shard(array, at), down_send.at[array, step - 1], down_receive.at[array, step - 1], "dp", device)
+
+    def across(array, index, at):
+        source = chains[array][0] if index == 0 else shard(array, at)
+        return remote(source, shard(array, at), mate_send.at[array, index], mate_receive.at[array, index], "dp", mate)
+
+    rises = lambda step: above & (level >= step - 1)
+    falls = lambda step: below & (level <= stages - step)
+    from_below = lambda step: level >= step
+    from_above = lambda step: level + step <= stages - 1
 
     def relay(step):
-        pl.when(right_sends(step))(lambda: right(step).start())
-        pl.when(left_sends(step))(lambda: left(step).start())
+        @pl.when(rises(step))
+        def _():
+            for array in (1, 0):
+                rising(array, step, place + 2).start()
+
+        @pl.when(falls(step))
+        def _():
+            for array in (1, 0):
+                falling(array, step, place - 2).start()
 
     def take(step):
-        @pl.when(right_gets(step))
-        def _():
-            remote(down, shard(down_full, level - step), right_send.at[step - 1], right_receive.at[step - 1], "dp", mate).wait_recv()
-            across(step, level - step).start()
-
-        @pl.when(left_gets(step))
-        def _():
-            remote(down, shard(down_full, level + step), left_send.at[step - 1], left_receive.at[step - 1], "dp", mate).wait_recv()
-            across(stages - 1 + step, level + step).start()
-
+        @pl.when(from_below(step))
+        def _():
+            for array in (1, 0):
+                got = shard(array, level - step)
+                remote(got, got, up_send.at[array, step - 1], up_receive.at[array, step - 1], "dp", mate).wait_recv()
+                across(array, step, level - step).start()
+
+        @pl.when(from_above(step))
+        def _():
+            for array in (1, 0):
+                got = shard(array, level + step)
+                remote(got, got, down_send.at[array, step - 1], down_receive.at[array, step - 1], "dp", mate).wait_recv()
+                across(array, stages - 1 + step, level + step).start()
+
+    for copy in qkv_copies + small_copies + first_kept:
+        copy.start()
     token_one.start()
     token_two.start()
+    for copy in qkv_copies + small_copies:
+        copy.wait_recv()
+    for copy in first_kept:
+        copy.wait()
     relay(1)
-    for copy in pieces + kept:
+    own_full = [pltpu.make_async_copy(chains[array][0], shard(array, level), local.at[4 + array]) for array in range(2)]
+    for array in range(2):
+        across(array, 0, level).start()
+        own_full[array].start()
+    for copy in fc_copies + later_kept:
         copy.start()
-    remote(down, shard(down_full, level), mate_send.at[0], mate_receive.at[0], "dp", mate).start()
     take(1)
     relay(2)
+    take(2)
+    relay(3)
     token_one.wait_recv()
     token_two.wait_recv()
     for copy in token_three:
         copy.start()
-    take(2)
-    relay(3)
-    for copy in token_three:
+    take(3)
+    for copy in later_kept + own_full:
+        copy.wait()
+    for copy in fc_copies:
         copy.wait_recv()
-    cot_one.start()
-    cot_two.start()
-    take(3)
-    for copy in kept:
-        copy.wait()
-    for copy in pieces:
-        copy.wait()
+    for copy in qkv_copies + small_copies + fc_copies:
+        copy.wait_send()
     token_one.wait_send()
     token_two.wait_send()
+    for step in range(1, stages):
+
+        @pl.when(rises(step))
+        def _(step=step):
+            for array in range(2):
+                rising(array, step, place + 2).wait_send()
+
+        @pl.when(falls(step))
+        def _(step=step):
+            for array in range(2):
+                falling(array, step, place - 2).wait_send()
+
+        @pl.when(from_below(step))
+        def _(step=step):
+            for array in range(2):
+                across(array, step, level - step).wait()
+
+        @pl.when(from_above(step))
+        def _(step=step):
+            for array in range(2):
+                across(array, stages - 1 + step, level + step).wait()
+
+    for array in range(2):
+        across(array, 0, level).wait()
     for copy in token_three:
-        copy.wait_send()
-    for step in range(1, stages):
-        pl.when(right_sends(step))(lambda step=step: right(step).wait_send())
-        pl.when(left_sends(step))(lambda step=step: left(step).wait_send())
-
-        @pl.when(right_gets(step))
-        def _(step=step):
-            across(step, level - step).wait()
-
-        @pl.when(left_gets(step))
-        def _(step=step):
-            across(stages - 1 + step, level + step).wait()
-
-    remote(down, shard(down_full, level), mate_send.at[0], mate_receive.at[0], "dp", mate).wait()
-    cot_one.wait()
-    cot_two.wait()
-
-
-def opening(tokens, cot, down, fc_pieces, seq_count, dp_count):
+        copy.wait()
+
+
+def opening(tokens, qkv_pieces, fc_pieces, small, dp_count):
     piece, width = tokens.shape
     steps = dp_count // 2 - 1
     anywhere = pl.BlockSpec(memory_space=pl.ANY)
     shape = lambda rows, columns: jax.ShapeDtypeStruct((rows, columns), BF16)
     dma = pltpu.SemaphoreType.DMA
+    inside = pl.BlockSpec(memory_space=pltpu.VMEM)
+    rows, columns = 4 * qkv_pieces.shape[1], qkv_pieces.shape[2]
+    fine = 4 * small.shape[0]
     return pl.pallas_call(
         opening_kernel,
-        in_specs=[anywhere] * 4,
+        in_specs=[inside] * 4,
         out_specs=[anywhere] * 4,
         out_shape=[
-            shape(piece * seq_count, width),
-            shape(piece * seq_count, width),
-            shape(down.shape[0] * dp_count, width),
-            shape(seq_count * fc_pieces.shape[1], fc_pieces.shape[2]),
+            shape(4 * piece, width),
+            shape(rows * dp_count, columns),
+            shape(4 * fc_pieces.shape[1], fc_pieces.shape[2]),
+            shape(fine * dp_count, small.shape[1]),
         ],
         scratch_shapes=[
-            dma((4,)), dma((9,)), dma((9,)), dma((steps,)), dma((steps,)), dma((steps,)), dma((steps,)),
-            dma((2 * steps + 1,)), dma((2 * steps + 1,)),
+            pltpu.VMEM((rows, columns), BF16), pltpu.VMEM((fine, small.shape[1]), BF16),
+            dma((6,)), dma((13,)), dma((13,)), dma((2, steps)), dma((2, steps)), dma((2, steps)), dma((2, steps)),
+            dma((2, 2 * steps + 1)), dma((2, 2 * steps + 1)),
         ],
-        compiler_params=pltpu.CompilerParams(collective_id=0, has_side_effects=True),
-        cost_estimate=cost(0, 10 * piece * seq_count * width),
-    )(tokens, cot, down, fc_pieces)
+        compiler_params=pltpu.CompilerParams(collective_id=0, has_side_effects=True, vmem_limit_bytes=32 * 2**20),
+        cost_estimate=cost(0, 10 * 4 * piece * width),
+    )(tokens, qkv_pieces, fc_pieces, small)
+
+
+def flip(first, second):
+    low = lax.rem(first + second, 2)
+    high = lax.rem(lax.div(first, 2) + lax.div(second, 2), 2)
+    return 2 * high + low
+
+
+def attend_plane_kernel(
+    q, k, v_t, tokens, cot_one, cot_two, key_bias, proj, vectors,
+    middle, normed, attended, lse, cot_three,
+    score_ref, joint, terms, passed, joined, arrived, send, receive,
+):
+    piece, width = tokens.shape
+    half = piece // 2
+    heads = q.shape[1] // HEAD_DIM
+    rank = lax.axis_index("seq")
+    one, two = neighbours()
+    for device in (one, two):
+        greet("seq", device)
+    pl.semaphore_wait(pltpu.get_barrier_semaphore(), 2)
+    up, lower = pl.ds(0, half), pl.ds(half, half)
+
+    def copy(index, source, target, device):
+        return remote(source, target, send.at[index], receive.at[index], "seq", device)
+
+    cot_copies = (copy(0, cot_one.at[up], cot_three.at[up], two), copy(1, cot_two.at[lower], cot_three.at[lower], one))
+    across = (copy(2, terms.at[3, up], passed.at[0], one), copy(3, terms.at[3, lower], passed.at[1], two))
+    plain_one = copy(4, terms.at[1, up], arrived.at[0, up], one)
+    plain_two = copy(5, terms.at[2, lower], arrived.at[1, lower], two)
+    joined_one = copy(6, joined.at[0], arrived.at[0, lower], one)
+    joined_two = copy(7, joined.at[1], arrived.at[1, up], two)
+    for item in cot_copies:
+        item.start()
+
+    def body(query_ref, key_ref, value_t, attended_tile, lse_tile):
+        group, head = pl.program_id(0), pl.program_id(1)
+        at = 3 - group
+        true = flip(at, rank)
+        query = query_ref[...]
+
+        def first(block, top):
+            scores = scores_of(key_ref, key_bias, query, flip(block, rank), piece, False)
+            score_ref[rows_of(block, piece), :] = scores
+            return jnp.maximum(top, jnp.max(scores, axis=0, keepdims=True))
+
+        last = scores_of(key_ref, key_bias, query, at, piece, True)
+        top = lax.fori_loop(0, true, first, jnp.max(last, axis=0, keepdims=True))
+
+        def weigh(scores, rel):
+            weights = jnp.exp2(scores - top)
+            return jnp.sum(weights, axis=0, keepdims=True), nn(value_t[:, rows_of(rel, piece)], weights.astype(BF16))
+
+        def second(block, carry):
+            total, out = carry
+            more, part = weigh(score_ref[rows_of(block, piece), :], flip(block, rank))
+            return total + more, out + part
+
+        total, out = lax.fori_loop(0, true, second, weigh(last, at))
+        result = (out / total).T.astype(BF16)
+        attended_tile[...] = result
+        lse_tile[0] = top + jnp.log2(total)
+        joint[:, pl.ds(pl.multiple_of(head * HEAD_DIM, HEAD_DIM), HEAD_DIM)] = result
+
+        @pl.when(head == heads - 1)
+        def _():
+            terms[at] = nn(joint[...], proj[...]).astype(BF16)
+
+        @pl.when((head == heads - 1) & (group == 0))
+        def _():
+            for item in across:
+                item.start()
+
+        @pl.when((head == heads - 1) & (group == 1))
+        def _():
+            plain_two.start()
+
+        @pl.when((head == heads - 1) & (group == 2))
+        def _():
+            plain_one.start()
+            for item in across:
+                item.wait_recv()
+            joined[0] = (terms[1, half:].astype(F32) + passed[1].astype(F32)).astype(BF16)
+            joined[1] = (terms[2, :half].astype(F32) + passed[0].astype(F32)).astype(BF16)
+            joined_one.start()
+            joined_two.start()
+
+    length = q.shape[0]
+    pltpu.emit_pipeline(
+        body,
+        grid=(4, heads),
+        in_specs=[
+            pl.BlockSpec((piece, HEAD_DIM), lambda g, h: (3 - g, h)),
+            pl.BlockSpec((length, HEAD_DIM), lambda g, h: (0, h)),
+            pl.BlockSpec((HEAD_DIM, length), lambda g, h: (h, 0)),
+        ],
+        out_specs=[
+            pl.BlockSpec((piece, HEAD_DIM), lambda g, h: (3 - g, h)),
+            pl.BlockSpec((1, 1, piece), lambda g, h: (h, 0, 3 - g)),
+        ],
+    )(q, k, v_t, attended, lse)
+
+    for item in (plain_one, plain_two, joined_one, joined_two):
+        item.wait_recv()
+    part = min(128, piece)
+
+    def norm_body(token_tile, middle_tile, normed_tile):
+        here = pl.ds(pl.multiple_of(pl.program_id(0) * part, part), part)
+        total = terms[0, here, :].astype(F32) + arrived[0, here, :].astype(F32) + arrived[1, here, :].astype(F32)
+        values = token_tile[...].astype(F32) + (total + vectors[0:1, :])
+        middle_tile[...] = values
+        normed_tile[...] = (norm_parts(values)[0] * vectors[1:2, :] + vectors[2:3, :]).astype(BF16)
+
+    line = pl.BlockSpec((part, width), lambda i: (i, 0))
+    pltpu.emit_pipeline(norm_body, grid=(piece // part,), in_specs=[line], out_specs=[line] * 2)(tokens, middle, normed)
+    for item in cot_copies:
+        item.wait()
+    for item in (*across, plain_one, plain_two, joined_one, joined_two):
+        item.wait_send()
+
+
+def attend_plane(q, k, v_t, tokens, cots, key_bias, proj, vectors):
+    piece, width = tokens.shape
+    length, columns = q.shape
+    heads, half = columns // HEAD_DIM, piece // 2
+    anywhere = pl.BlockSpec(memory_space=pl.ANY)
+    inside = pl.BlockSpec(memory_space=pltpu.VMEM)
+    shape = lambda *dims: jax.ShapeDtypeStruct(dims, BF16)
+    dma = pltpu.SemaphoreType.DMA
+    return pl.pallas_call(
+        attend_plane_kernel,
+        in_specs=[anywhere] * 6 + [inside] * 3,
+        out_specs=[anywhere] * 5,
+        out_shape=[
+            jax.ShapeDtypeStruct((piece, width), F32), shape(piece, width), shape(length, columns),
+            jax.ShapeDtypeStruct((heads, 1, length), F32), shape(piece, width),
+        ],
+        scratch_shapes=[
+            pltpu.VMEM((length, piece), F32),
+            pltpu.VMEM((piece, columns), BF16),
+            pltpu.VMEM((4, piece, width), BF16),
+            pltpu.VMEM((2, half, width), BF16),
+            pltpu.VMEM((2, half, width), BF16),
+            pltpu.VMEM((2, piece, width), BF16),
+            dma((8,)), dma((8,)),
+        ],
+        compiler_params=pltpu.CompilerParams(collective_id=2, has_side_effects=True, vmem_limit_bytes=56 * 2**20),
+        cost_estimate=cost(3 * length * length * columns + 2 * length * columns * width, 10 * length * width, heads * length * length // 2),
+    )(q, k, v_t, tokens, *cots, key_bias, proj, vectors)
+
+
+def sum_rows(ref, at, columns, value, first):
+    total = jnp.sum(value, axis=0, keepdims=True)
+
+    @pl.when(first)
+    def _():
+        ref[at : at + 1, columns] = total
+
+    @pl.when(jnp.logical_not(first))
+    def _():
+        ref[at : at + 1, columns] += total
 
 
 def plane_kernel(
-    normed, cot_in, fc, bias, down, middle, gain,
-    grad_middle, low, sums, active, hidden_grad, normed_all, cot_all, terms,
+    normed, cot_own, cot_one, cot_two, cot_three, fc, bias, down, middle, gain,
+    grad_middle, low_all, sums, hidden_sums, active, hidden_grad, normed_all, cot_all, terms, grad_down, grad_fc,
     normed_buf, cot_buf, sum_ref, joined, passed, arrived, load, local, send, receive,
 ):
     piece, width = normed.shape
     half = piece // 2
     inner = fc.shape[1]
+    length = normed_all.shape[0]
     tile = min(512, inner)
     last = inner // tile - 1
     one, two = neighbours()
@@ -697,20 +892,25 @@
         copy(2, normed_buf.at[1, up], normed_buf.at[3, up], two),
         copy(3, normed_buf.at[2, lower], normed_buf.at[3, lower], one),
     )
-    cot_three = (
-        copy(4, cot_buf.at[1, up], cot_buf.at[3, up], two),
-        copy(5, cot_buf.at[2, lower], cot_buf.at[3, lower], one),
-    )
-    across = (copy(6, cot_buf.at[0, up], passed.at[0], one), copy(7, cot_buf.at[0, lower], passed.at[1], two))
-    plain_one = copy(8, cot_buf.at[1, up], arrived.at[0, up], one)
-    plain_two = copy(9, cot_buf.at[2, lower], arrived.at[1, lower], two)
-    joined_one = copy(10, joined.at[0], arrived.at[0, lower], one)
-    joined_two = copy(11, joined.at[1], arrived.at[1, up], two)
-
-    loads = [pltpu.make_async_copy(cot_in.at[rows(k)], cot_buf.at[k], load.at[k]) for k in range(3)]
-    own = pltpu.make_async_copy(normed, normed_buf.at[0], load.at[3])
+    across = (copy(4, cot_buf.at[3, up], passed.at[0], one), copy(5, cot_buf.at[3, lower], passed.at[1], two))
+    plain_one = copy(6, cot_buf.at[1, up], arrived.at[0, up], one)
+    plain_two = copy(7, cot_buf.at[2, lower], arrived.at[1, lower], two)
+    joined_one = copy(8, joined.at[0], arrived.at[0, lower], one)
+    joined_two = copy(9, joined.at[1], arrived.at[1, up], two)
+    low_one = copy(10, low_all.at[rows(0)], low_all.at[rows(1)], one)
+    low_two = copy(11, low_all.at[rows(0)], low_all.at[rows(2)], two)
+    low_three = (
+        copy(12, low_all.at[rows(1, 0, half)], low_all.at[rows(3, 0, half)], two),
+        copy(13, low_all.at[rows(2, half, half)], low_all.at[rows(3, half, half)], one),
+    )
+
+    loads = [
+        pltpu.make_async_copy(source, cot_buf.at[k], load.at[k])
+        for k, source in enumerate((cot_own, cot_one, cot_two, cot_three))
+    ]
+    own = pltpu.make_async_copy(normed, normed_buf.at[0], load.at[4])
     keeps = [pltpu.make_async_copy(normed_buf.at[k], normed_all.at[rows(k)], local.at[k]) for k in range(4)]
-    keep_cot = pltpu.make_async_copy(cot_buf.at[3], cot_all.at[rows(3)], local.at[4])
+    keeps_cot = [pltpu.make_async_copy(cot_buf.at[k], cot_all.at[rows(k)], local.at[4 + k]) for k in range(4)]
 
     normed_one.start()
     normed_two.start()
@@ -724,8 +924,11 @@
         @pl.when((k == 0) & (j == 0))
         def _():
             own.wait()
-            loads[0].wait()
             keeps[0].start()
+            for item in loads:
+                item.wait()
+            for item in keeps_cot:
+                item.start()
 
         @pl.when((k == 1) & (j == 0))
         def _():
@@ -733,22 +936,18 @@
             normed_two.wait_recv()
             for item in normed_three:
                 item.start()
-            loads[1].wait()
-            loads[2].wait()
-            for item in cot_three:
-                item.start()
             keeps[1].start()
             keeps[2].start()
 
         @pl.when((k == 3) & (j == 0))
         def _():
-            for item in normed_three + cot_three:
+            for item in normed_three:
                 item.wait_recv()
             keeps[3].start()
-            keep_cot.start()
 
         weights = fc_tile[...]
-        hidden = nn(normed_buf[k], weights) + bias[:, pl.ds(pl.multiple_of(j * tile, tile), tile)]
+        columns = pl.ds(pl.multiple_of(j * tile, tile), tile)
+        hidden = nn(normed_buf[k], weights) + bias[:, columns]
         grad_active = nt(cot_buf[k], down_tile[...])
         square = hidden * hidden
         bent = jnp.tanh(math.sqrt(2 / math.pi) * (hidden + 0.044715 * (square * hidden)))
@@ -759,6 +958,7 @@
         )
         grad_hidden = (grad_active * slope).astype(BF16)
         hidden_tile[...] = grad_hidden
+        sum_rows(hidden_sums, 0, columns, grad_hidden.astype(F32), k == 0)
         term = nt(grad_hidden, weights)
 
         @pl.when(j == 0)
@@ -771,23 +971,23 @@
 
         @pl.when((j == last) & (k == 0))
         def _():
+            for item in keeps_cot:
+                item.wait()
             arrived[2] = sum_ref[...].astype(BF16)
 
         @pl.when((j == last) & (k == 1))
         def _():
-            cot_three[0].wait_send()
             cot_buf[1] = sum_ref[...].astype(BF16)
             plain_one.start()
 
         @pl.when((j == last) & (k == 2))
         def _():
-            cot_three[1].wait_send()
             cot_buf[2] = sum_ref[...].astype(BF16)
             plain_two.start()
 
         @pl.when((j == last) & (k == 3))
         def _():
-            cot_buf[0] = sum_ref[...].astype(BF16)
+            cot_buf[3] = sum_ref[...].astype(BF16)
             for item in across:
                 item.start()
 
@@ -824,6 +1024,8 @@
     joined[1] = (cot_buf[2, :half].astype(F32) + passed[0].astype(F32)).astype(BF16)
     joined_one.start()
     joined_two.start()
+    for item in keeps:
+        item.wait()
     multiply_down(2)
     for item in (plain_one, plain_two, joined_one, joined_two):
         item.wait_recv()
@@ -836,49 +1038,68 @@
         upstream = (
             arrived[2, here, :].astype(F32) + arrived[0, here, :].astype(F32) + arrived[1, here, :].astype(F32)
         )
-        values = middle_tile[...]
-        unit, scale = norm_parts(values)
+        unit, scale = norm_parts(middle_tile[...])
         cot = cot_tile[...].astype(F32)
         grad = cot + norm_backward(unit, scale, gain[...], upstream)
         rounded = grad.astype(BF16)
         grad_tile[...] = grad
         low_tile[...] = rounded
         for at, item in enumerate((upstream * unit, upstream, rounded.astype(F32), cot)):
-            column = jnp.sum(item, axis=0, keepdims=True)
-
-            @pl.when(i == 0)
-            def _():
-                sums[at : at + 1, :] = column
-
-            @pl.when(i > 0)
-            def _():
-                sums[at : at + 1, :] += column
+            sum_rows(sums, at, slice(None), item, i == 0)
 
     line = pl.BlockSpec((part, width), lambda i: (i, 0))
     pltpu.emit_pipeline(norm_body, grid=(piece // part,), in_specs=[line] * 2, out_specs=[line] * 2)(
-        middle, cot_in, grad_middle, low
-    )
-    for item in keeps + [keep_cot]:
+        middle, cot_own, grad_middle, low_all
+    )
+    low_one.start()
+    low_two.start()
+
+    wide, tall = min(1024, width), min(1024, inner)
+
+    def outer_body(left, right, out):
+        out[...] = tn(left[...], right[...]).astype(BF16)
+
+    def outer(left, right, out, shape):
+        pltpu.emit_pipeline(
+            outer_body,
+            grid=(out.shape[0] // shape[0], out.shape[1] // shape[1]),
+            in_specs=[
+                pl.BlockSpec((length, shape[0]), lambda i, j: (0, i)),
+                pl.BlockSpec((length, shape[1]), lambda i, j: (0, j)),
+            ],
+            out_specs=[pl.BlockSpec(shape, lambda i, j: (i, j))],
+        )(left, right, out)
+
+    outer(active, cot_all, grad_down, (tall, wide))
+    low_one.wait_recv()
+    low_two.wait_recv()
+    for item in low_three:
+        item.start()
+    outer(normed_all, hidden_grad, grad_fc, (wide, tall))
+    for item in low_three:
         item.wait()
-    for item in (normed_one, normed_two, *normed_three, *across, plain_one, plain_two, joined_one, joined_two):
+    for item in (
+        normed_one, normed_two, *normed_three, *across, plain_one, plain_two, joined_one, joined_two, low_one, low_two
+    ):
         item.wait_send()
 
 
-def feed_plane(normed, cot_all, fc, bias, down, middle, gain):
+def feed_plane(normed, cots, fc, bias, down, middle, gain):
     piece, width = normed.shape
-    length, inner = cot_all.shape[0], fc.shape[1]
-    half = piece // 2
+    inner = fc.shape[1]
+    length, half = 4 * piece, piece // 2
     anywhere = pl.BlockSpec(memory_space=pl.ANY)
     inside = pl.BlockSpec(memory_space=pltpu.VMEM)
     shape = lambda rows, columns, kind=BF16: jax.ShapeDtypeStruct((rows, columns), kind)
     dma = pltpu.SemaphoreType.DMA
     return pl.pallas_call(
         plane_kernel,
-        in_specs=[anywhere, anywhere, anywhere, inside, anywhere, anywhere, inside],
-        out_specs=[anywhere, anywhere, inside] + [anywhere] * 5,
+        in_specs=[anywhere] * 6 + [inside, anywhere, anywhere, inside],
+        out_specs=[anywhere, anywhere, inside, inside] + [anywhere] * 7,
         out_shape=[
-            shape(piece, width, F32), shape(piece, width), shape(4, width, F32), shape(length, inner),
-            shape(length, inner), shape(length, width), shape(length, width), shape(length, width),
+            shape(piece, width, F32), shape(length, width), shape(4, width, F32), shape(1, inner, F32),
+            shape(length, inner), shape(length, inner), shape(length, width), shape(length, width),
+            shape(length, width), shape(inner, width), shape(width, inner),
         ],
         scratch_shapes=[
             pltpu.VMEM((4, piece, width), BF16),
@@ -887,12 +1108,257 @@
             pltpu.VMEM((2, half, width), BF16),
             pltpu.VMEM((2, half, width), BF16),
             pltpu.VMEM((3, piece, width), BF16),
-            dma((4,)), dma((5,)), dma((12,)), dma((12,)),
+            dma((5,)), dma((8,)), dma((14,)), dma((14,)),
         ],
-        input_output_aliases={1: 6},
         compiler_params=pltpu.CompilerParams(collective_id=1, has_side_effects=True, vmem_limit_bytes=60 * 2**20),
-        cost_estimate=cost(8 * length * width * inner, 10 * length * width),
-    )(normed, cot_all, fc, bias, down, middle, gain)
+        cost_estimate=cost(12 * length * width * inner, 10 * length * width),
+    )(normed, *cots, fc, bias, down, middle, gain)
+
+
+def retreat_plane_kernel(
+    low_all, q, k, v, k_t, lse, terms, middle, key_bias, proj, down_shift,
+    grads, column_sums, block_out,
+    prob_ref, chance_ref, grad_ref, key_sum, value_sum, rounded, own, passed, joined, arrived,
+    load, local, send, receive,
+):
+    piece, width = middle.shape
+    half = piece // 2
+    length, columns = q.shape
+    heads = columns // HEAD_DIM
+    rank = lax.axis_index("seq")
+    one, two = neighbours()
+    for device in (one, two):
+        greet("seq", device)
+    pl.semaphore_wait(pltpu.get_barrier_semaphore(), 2)
+    up, lower = pl.ds(0, half), pl.ds(half, half)
+    rows = lambda at, start=0, size=piece: pl.ds(at * piece + start, size)
+
+    def copy(index, source, target, device):
+        return remote(source, target, send.at[index], receive.at[index], "seq", device)
+
+    across = (
+        copy(0, terms.at[rows(3, 0, half)], passed.at[0], one),
+        copy(1, terms.at[rows(3, half, half)], passed.at[1], two),
+    )
+    plain_one = copy(2, terms.at[rows(1, 0, half)], arrived.at[0, up], one)
+    plain_two = copy(3, terms.at[rows(2, half, half)], arrived.at[1, lower], two)
+    joined_one = copy(4, joined.at[0], arrived.at[0, lower], one)
+    joined_two = copy(5, joined.at[1], arrived.at[1, up], two)
+    loads = (
+        pltpu.make_async_copy(terms.at[rows(1, half, half)], own.at[0], load.at[0]),
+        pltpu.make_async_copy(terms.at[rows(2, 0, half)], own.at[1], load.at[1]),
+    )
+    for item in (*across, plain_one, plain_two, *loads):
+        item.start()
+    key_sum[...] = jnp.zeros_like(key_sum)
+    value_sum[...] = jnp.zeros_like(value_sum)
+
+    def body(low_ref, query_ref, key_ref, value_ref, key_t, lse_ref, query_out):
+        at, head = pl.program_id(0), pl.program_id(1)
+        true = flip(at, rank)
+        here = pl.ds(pl.multiple_of(head * HEAD_DIM, HEAD_DIM), HEAD_DIM)
+
+        @pl.when(head == 0)
+        def _():
+            grad_ref[...] = nt(low_ref[...], proj[...]).astype(BF16)
+
+        @pl.when((at == 1) & (head == 2))
+        def _():
+            for item in (*across,):
+                item.wait_recv()
+            for item in loads:
+                item.wait()
+            joined[0] = (own[0].astype(F32) + passed[1].astype(F32)).astype(BF16)
+            joined[1] = (own[1].astype(F32) + passed[0].astype(F32)).astype(BF16)
+            joined_one.start()
+            joined_two.start()
+
+        query, grad, base = query_ref[...], grad_ref[:, here], lse_ref[0]
+
+        def measure(scores, rel):
+            block = rows_of(rel, piece)
+            probs = jnp.exp2(scores - base)
+            grad_chances = nt(value_ref[block, :], grad)
+            value_sum[block, here] += nn(probs.astype(BF16), grad)
+            prob_ref[block, :] = probs
+            chance_ref[block, :] = grad_chances
+            return jnp.sum(probs * grad_chances, axis=0, keepdims=True)
+
+        def first(block, weighted):
+            rel = flip(block, rank)
+            return weighted + measure(scores_of(key_ref, key_bias, query, rel, piece, False), rel)
+
+        last = scores_of(key_ref, key_bias, query, at, piece, True)
+        weighted = lax.fori_loop(0, true, first, measure(last, at))
+
+        def second(block, total):
+            block = rows_of(flip(block, rank), piece)
+            grad_scores = (prob_ref[block, :] * (chance_ref[block, :] - weighted)).astype(BF16)
+            key_sum[block, here] += nn(grad_scores, query)
+            return total + nn(key_t[:, block], grad_scores)
+
+        total = lax.fori_loop(0, true + 1, second, jnp.zeros((HEAD_DIM, piece), F32))
+        result = (total * FACTOR).T.astype(BF16)
+        query_out[...] = result
+        sum_rows(column_sums, 0, here, result.astype(F32), at == 0)
+
+    pltpu.emit_pipeline(
+        body,
+        grid=(4, heads),
+        in_specs=[
+            pl.BlockSpec((piece, width), lambda g, h: (g, 0)),
+            pl.BlockSpec((piece, HEAD_DIM), lambda g, h: (g, h)),
+            pl.BlockSpec((length, HEAD_DIM), lambda g, h: (0, h)),
+            pl.BlockSpec((length, HEAD_DIM), lambda g, h: (0, h)),
+            pl.BlockSpec((HEAD_DIM, length), lambda g, h: (h, 0)),
+            pl.BlockSpec((1, 1, piece), lambda g, h: (h, 0, g)),
+        ],
+        out_specs=[pl.BlockSpec((piece, HEAD_DIM), lambda g, h: (g, h))],
+    )(low_all, q, k, v, k_t, lse, grads)
+
+    rounded[:, :columns] = (key_sum[...] * FACTOR).astype(BF16)
+    values = value_sum[...].astype(BF16)
+    rounded[:, columns:] = values
+    column_sums[1:2, :] = jnp.sum(values.astype(F32), axis=0, keepdims=True)
+    keep = pltpu.make_async_copy(rounded, grads.at[:, pl.ds(columns, 2 * columns)], local.at[0])
+    keep.start()
+    for item in (plain_one, plain_two, joined_one, joined_two):
+        item.wait_recv()
+    part = min(128, piece)
+
+    def out_body(middle_tile, term_tile, out):
+        here = pl.ds(pl.multiple_of(pl.program_id(0) * part, part), part)
+        total = term_tile[...].astype(F32) + arrived[0, here, :].astype(F32) + arrived[1, here, :].astype(F32)
+        out[...] = (middle_tile[...] + (total + down_shift[...])).astype(BF16)
+
+    line = pl.BlockSpec((part, width), lambda i: (i, 0))
+    pltpu.emit_pipeline(out_body, grid=(piece // part,), in_specs=[line] * 2, out_specs=[line])(middle, terms, block_out)
+    keep.wait()
+    for item in (*across, plain_one, plain_two, joined_one, joined_two):
+        item.wait_send()
+
+
+def retreat_plane(low_all, q, k, v, k_t, lse, terms, middle, key_bias, proj, down_shift):
+    piece, width = middle.shape
+    length, columns = q.shape
+    half = piece // 2
+    anywhere = pl.BlockSpec(memory_space=pl.ANY)
+    inside = pl.BlockSpec(memory_space=pltpu.VMEM)
+    dma = pltpu.SemaphoreType.DMA
+    return pl.pallas_call(
+        retreat_plane_kernel,
+        in_specs=[anywhere] * 8 + [inside] * 3,
+        out_specs=[anywhere, inside, anywhere],
+        out_shape=[
+            jax.ShapeDtypeStruct((length, 3 * columns), BF16),
+            jax.ShapeDtypeStruct((2, columns), F32),
+            jax.ShapeDtypeStruct((piece, width), BF16),
+        ],
+        scratch_shapes=[
+            pltpu.VMEM((length, piece), F32),
+            pltpu.VMEM((length, piece), F32),
+            pltpu.VMEM((piece, columns), BF16),
+            pltpu.VMEM((length, columns), F32),
+            pltpu.VMEM((length, columns), F32),
+            pltpu.VMEM((length, 2 * columns), BF16),
+            pltpu.VMEM((2, half, width), BF16),
+            pltpu.VMEM((2, half, width), BF16),
+            pltpu.VMEM((2, half, width), BF16),
+            pltpu.VMEM((2, piece, width), BF16),
+            dma((2,)), dma((1,)), dma((6,)), dma((6,)),
+        ],
+        compiler_params=pltpu.CompilerParams(collective_id=3, has_side_effects=True, vmem_limit_bytes=60 * 2**20),
+        cost_estimate=cost(8 * length * length * columns + 2 * length * columns * width, 10 * length * width),
+    )(low_all, q, k, v, k_t, lse, terms, middle, key_bias, proj, down_shift)
+
+
+def closing_kernel(
+    grads, weight, tokens, grad_middle, gain, tokens_grad, sums,
+    terms, passed, joined, arrived, send, receive,
+):
+    piece, width = tokens.shape
+    half = piece // 2
+    one, two = neighbours()
+    for device in (one, two):
+        greet("seq", device)
+    pl.semaphore_wait(pltpu.get_barrier_semaphore(), 2)
+    up, lower = pl.ds(0, half), pl.ds(half, half)
+
+    def copy(index, source, target, device):
+        return remote(source, target, send.at[index], receive.at[index], "seq", device)
+
+    across = (copy(0, terms.at[3, up], passed.at[0], one), copy(1, terms.at[3, lower], passed.at[1], two))
+    plain_one = copy(2, terms.at[1, up], arrived.at[0, up], one)
+    plain_two = copy(3, terms.at[2, lower], arrived.at[1, lower], two)
+    joined_one = copy(4, joined.at[0], arrived.at[0, lower], one)
+    joined_two = copy(5, joined.at[1], arrived.at[1, up], two)
+
+    @pl.loop(0, 4)
+    def _(step):
+        at = 3 - step
+        terms[at] = nt(grads[pl.ds(pl.multiple_of(at * piece, piece), piece), :], weight[...]).astype(BF16)
+
+        @pl.when(step == 0)
+        def _():
+            for item in across:
+                item.start()
+
+        @pl.when(step == 1)
+        def _():
+            plain_two.start()
+
+        @pl.when(step == 2)
+        def _():
+            plain_one.start()
+
+    for item in across:
+        item.wait_recv()
+    joined[0] = (terms[1, half:].astype(F32) + passed[1].astype(F32)).astype(BF16)
+    joined[1] = (terms[2, :half].astype(F32) + passed[0].astype(F32)).astype(BF16)
+    joined_one.start()
+    joined_two.start()
+    for item in (plain_one, plain_two, joined_one, joined_two):
+        item.wait_recv()
+    part = min(128, piece)
+
+    def norm_body(token_tile, middle_tile, out):
+        i = pl.program_id(0)
+        here = pl.ds(pl.multiple_of(i * part, part), part)
+        upstream = terms[0, here, :].astype(F32) + arrived[0, here, :].astype(F32) + arrived[1, here, :].astype(F32)
+        unit, scale = norm_parts(token_tile[...].astype(F32))
+        out[...] = middle_tile[...] + norm_backward(unit, scale, gain[...], upstream)
+        for at, item in enumerate((upstream * unit, upstream)):
+            sum_rows(sums, at, slice(None), item, i == 0)
+
+    line = pl.BlockSpec((part, width), lambda i: (i, 0))
+    pltpu.emit_pipeline(norm_body, grid=(piece // part,), in_specs=[line] * 2, out_specs=[line])(
+        tokens, grad_middle, tokens_grad
+    )
+    for item in (*across, plain_one, plain_two, joined_one, joined_two):
+        item.wait_send()
+
+
+def closing(grads, weight, tokens, grad_middle, gain):
+    piece, width = tokens.shape
+    half = piece // 2
+    anywhere = pl.BlockSpec(memory_space=pl.ANY)
+    inside = pl.BlockSpec(memory_space=pltpu.VMEM)
+    dma = pltpu.SemaphoreType.DMA
+    return pl.pallas_call(
+        closing_kernel,
+        in_specs=[inside, inside, anywhere, anywhere, inside],
+        out_specs=[anywhere, inside],
+        out_shape=[jax.ShapeDtypeStruct((piece, width), F32), jax.ShapeDtypeStruct((2, width), F32)],
+        scratch_shapes=[
+            pltpu.VMEM((4, piece, width), BF16),
+            pltpu.VMEM((2, half, width), BF16),
+            pltpu.VMEM((2, half, width), BF16),
+            pltpu.VMEM((2, piece, width), BF16),
+            dma((6,)), dma((6,)),
+        ],
+        compiler_params=pltpu.CompilerParams(collective_id=4, has_side_effects=True, vmem_limit_bytes=60 * 2**20),
+        cost_estimate=cost(8 * piece * width * grads.shape[1], 10 * piece * width),
+    )(grads, weight, tokens, grad_middle, gain)
 
 
 def after(value, *others):
@@ -1018,8 +1484,6 @@
         .transpose(4, 3, 0, 1, 2, 5)
         .reshape(seq_count, rows, 3 * own_width)
     )
-    qkv_rows = jnp.concatenate(by_rank(exchange(qkv_pieces, seq_rank), seq_rank), axis=0)
-    weights = [gather_dp(qkv_rows[:, i * own_width : (i + 1) * own_width]) for i in range(3)]
     tokens_own, cot_own = tokens[0], cotangent[0]
 
     small = (attn_gain, attn_shift, qv_bias, proj_bias, mlp_gain, mlp_shift, fc_bias, down_bias)
@@ -1027,11 +1491,29 @@
     positions = seq_rank * piece + jnp.arange(piece, dtype=jnp.int32)
     own_flags = ((key_mask[0] == 1) & (positions < lengths[0])).astype(BF16)
     packed = jnp.concatenate(small + (own_flags,))
-    blocks = gather_blocks(packed)
-    flags = jnp.concatenate([item[-piece:] for item in blocks])
+    fc_pieces = (
+        fc_weight.reshape(rows, dp_count, seq_count, block)
+        .transpose(2, 0, 1, 3)
+        .reshape(seq_count, rows, dp_count * block)
+    )
+    if in_plane:
+        room = -(-packed.shape[0] // 2048) * 2048
+        small_rows = jnp.pad(packed, (0, room - packed.shape[0])).reshape(room // 128, 128)
+        token_all, qkv_full, fc_rows, small_full = opening(
+            tokens_own, qkv_pieces, fc_pieces, small_rows, dp_count
+        )
+        packed = small_full.reshape(dp_count, seq_count, room)
+        flags = lax.dynamic_index_in_dim(packed, dp_rank, axis=0, keepdims=False)
+        flags = jnp.concatenate(by_rank([flags[s, sum(sizes) : sum(sizes) + piece] for s in range(seq_count)], seq_rank))
+        packed = packed[:, :, : sum(sizes)].astype(F32)
+    else:
+        qkv_full = gather_dp(jnp.concatenate(by_rank(exchange(qkv_pieces, seq_rank), seq_rank), axis=0))
+        blocks = gather_blocks(packed)
+        flags = jnp.concatenate([item[-piece:] for item in blocks])
+        packed = jnp.stack(by_rank([item[:-piece] for item in blocks], seq_rank))
+        packed = jnp.stack(by_rank(gather_blocks(packed, "dp"), dp_rank)).astype(F32)
+        fc_rows = jnp.concatenate(by_rank(exchange(fc_pieces, seq_rank), seq_rank), axis=0)
     key_bias = jnp.where(flags > 0, 0.0, NEG).astype(F32)[:, None]
-    packed = jnp.stack(by_rank([item[:-piece] for item in blocks], seq_rank))
-    packed = jnp.stack(by_rank(gather_blocks(packed, "dp"), dp_rank)).astype(F32)
     parts, start = [], 0
     for size in sizes:
         parts.append(packed[:, :, start : start + size])
@@ -1046,42 +1528,44 @@
     )
     qv_own = qv_own.reshape(1, -1)
 
+    length = piece * seq_count
     proj_full = gather_dp(lax.ppermute(proj_weight, BOTH, swap))
-    fc_pieces = (
-        fc_weight.reshape(rows, dp_count, seq_count, block)
-        .transpose(2, 0, 1, 3)
-        .reshape(seq_count, rows, dp_count * block)
-    )
+    down_full = gather_dp(after(down_weight, fc_rows) if in_plane else down_weight)
+    fc_full = gather_dp(fc_rows)
     shared = None
     if in_plane:
-        token_all, cot_all, down_full, fc_rows = opening(
-            after(tokens_own, qkv_rows, packed), cot_own, down_weight, fc_pieces, seq_count, dp_count
-        )
-        for k in range(seq_count):
-            shared = project(k, token_all, k, gain_one, shift_one, weights, qv_own, piece, seq_count, shared)
+        cot_own, token_all = lax.optimization_barrier((cot_own, token_all))
+        cots = (shift(cot_own, "seq", 1), shift(cot_own, "seq", 2))
+        shared = project(0, token_all, 0, length, gain_one, shift_one, qkv_full, qv_own, length, None)
     else:
         token_blocks = gather_blocks(tokens_own)
         cot_blocks = gather_blocks(after(cot_own, token_blocks[-1]))
-        down_full = gather_dp(down_weight)
-        fc_rows = jnp.concatenate(by_rank(exchange(fc_pieces, seq_rank), seq_rank), axis=0)
         for k in range(seq_count):
-            shared = project(k, token_blocks[k], 0, gain_one, shift_one, weights, qv_own, piece, seq_count, shared)
-    fc_full = gather_dp(fc_rows)
+            shared = project(k, token_blocks[k], 0, piece, gain_one, shift_one, qkv_full, qv_own, length, shared)
     normed_one, q, keys, values, keys_t, values_t = shared
-    proj_terms, shared = [None] * seq_count, None
-    for k in order:
-        proj_terms[k], shared = attend(k, rank, q, keys, values_t, key_bias, proj_full, piece, shared)
-    attended, lse = shared
-    middle, normed_two = rowwise(
-        middle_kernel, scatter_plane(proj_terms), [tokens_own], [proj_shift, gain_two, shift_two], [F32, BF16], 0
-    )
-
     if in_plane:
-        grad_middle, grad_mid_low, sums_two, active, grad_hidden, normed_all, cot_all, down_terms = feed_plane(
-            normed_two, cot_all, fc_full, fc_shift, down_full, middle, gain_two
+        middle, normed_two, attended, lse, cot_three = attend_plane(
+            q, keys, values_t, tokens_own, cots, key_bias, proj_full,
+            jnp.concatenate([proj_shift, gain_two, shift_two], axis=0),
+        )
+    else:
+        proj_terms, shared = [None] * seq_count, None
+        for k in order:
+            proj_terms[k], shared = attend(k, rank, q, keys, values_t, key_bias, proj_full, piece, shared)
+        attended, lse = shared
+        middle, normed_two = rowwise(
+            middle_kernel, scatter_blocks(proj_terms), [tokens_own], [proj_shift, gain_two, shift_two], [F32, BF16], 0
+        )
+
+    if in_plane:
+        grad_middle, low_all, sums_two, hidden_sums, _, _, _, _, down_terms, grad_down, grad_fc = feed_plane(
+            normed_two, (cot_own, *cots, cot_three), fc_full, fc_shift, down_full, middle, gain_two
         )
         sums_two = [sums_two[i] for i in range(4)]
-        down_terms = [down_terms[k * piece : (k + 1) * piece] for k in range(seq_count)]
+        grad_down, grad_fc = scatter_dp(grad_down), scatter_dp(grad_fc)
+        grads, qv_sums, block_out = retreat_plane(
+            low_all, q, keys, values, keys_t, lse, down_terms, middle, key_bias, proj_full, down_shift
+        )
     else:
         normed_blocks = gather_blocks(normed_two)
         grad_terms, shared = [], None
@@ -1095,32 +1579,33 @@
         down_terms = [
             nn(active[k * piece : (k + 1) * piece], down_full).astype(BF16) for k in range(seq_count)
         ]
-    low_blocks = gather_plane(grad_mid_low)
-    grad_down = tn(active, cot_all).astype(BF16)
-    grad_fc = tn(normed_all, grad_hidden).astype(BF16)
-    low_blocks[1] = after(low_blocks[1], grad_down, grad_fc)
-    grad_down = scatter_dp(grad_down)
-    grad_fc = scatter_dp(grad_fc)
-    down_terms, _ = lax.optimization_barrier((down_terms, low_blocks[-1]))
-    block_out = rowwise(out_kernel, scatter_plane(down_terms), [middle], [down_shift], [BF16], 0)[0]
-
-    sums, shared = None, None
-    for k in range(seq_count):
-        sums, shared = retreat(
-            k, rank, low_blocks[k], proj_full, q, lse, keys, values, keys_t, key_bias, sums, shared, k == seq_count - 1
-        )
-    grad_q, low_all = shared
-    grads = [grad_q, sums[0], sums[1]]
-    normed_one = after(normed_one, grad_down)
-    grad_qkv = [scatter_dp(tn(normed_one, item).astype(BF16)) for item in grads]
-    back_terms = [None] * seq_count
-    for k in order:
-        back_terms[k] = back(k, grads, weights, piece)
-    tokens_grad, *sums_one = rowwise(
-        tokens_back_kernel, scatter_plane(back_terms), [tokens_own, grad_middle], [gain_one], [F32], 2
-    )
+        low_blocks = gather_blocks(grad_mid_low)
+        grad_down = scatter_dp(tn(active, cot_all).astype(BF16))
+        grad_fc = scatter_dp(tn(normed_all, grad_hidden).astype(BF16))
+        hidden_sums = jnp.sum(grad_hidden.astype(F32), axis=0)
+        block_out = rowwise(out_kernel, scatter_blocks(down_terms), [middle], [down_shift], [BF16], 0)[0]
+        sums, shared = None, None
+        for k in range(seq_count):
+            sums, shared = retreat(
+                k, rank, low_blocks[k], proj_full, q, lse, keys, values, keys_t, key_bias, sums, shared,
+                k == seq_count - 1,
+            )
+        grad_q, low_all = shared
+        grads = jnp.concatenate([grad_q, sums[0], sums[1]], axis=1)
+        qv_sums = jnp.stack([jnp.sum(item.astype(F32), axis=0) for item in (grad_q, sums[1])])
+    grad_qkv = scatter_dp(tn(normed_one, grads).astype(BF16))
     grad_proj = scatter_dp(tn(attended, low_all).astype(BF16))
     grad_proj = lax.ppermute(grad_proj, BOTH, swap).astype(F32)
+    if in_plane:
+        tokens_grad, sums_one = closing(grads, qkv_full, tokens_own, grad_middle, gain_one)
+        sums_one = [sums_one[i] for i in range(2)]
+    else:
+        back_terms = [None] * seq_count
+        for k in order:
+            back_terms[k] = back(k, grads, qkv_full, piece)
+        tokens_grad, *sums_one = rowwise(
+            tokens_back_kernel, scatter_blocks(back_terms), [tokens_own, grad_middle], [gain_one], [F32], 2
+        )
 
     blocks = exchange(grad_fc.reshape(seq_count, rows, dp_count * block), seq_rank)
     if block % 128 == 0:
@@ -1129,9 +1614,9 @@
     else:
         blocks = [item.reshape(rows, dp_count, block) for item in by_rank(blocks, seq_rank)]
         grad_fc = jnp.stack(blocks, axis=2).reshape(fc_weight.shape).astype(F32)
-    blocks = list(zip(*[exchange(item.reshape(seq_count, rows, own_width), seq_rank) for item in grad_qkv]))
+    blocks = [[item] for item in exchange(grad_qkv.reshape(seq_count, rows, 3 * own_width), seq_rank)]
     qkv_places = lambda s: [
-        (part, head, part * HEADS + (head * sub + s % sub) * high + s // sub)
+        (0, part * own_heads + head, part * HEADS + (head * sub + s % sub) * high + s // sub)
         for part in range(3)
         for head in range(own_heads)
     ]
@@ -1141,10 +1626,9 @@
         return vector.reshape(dp_count, seq_count, -1)
 
     here = (jnp.arange(seq_count) == seq_rank).astype(F32)
-    hidden_sums = jnp.sum(grad_hidden.astype(F32), axis=0).reshape(dp_count, 1, -1) * here[None, :, None]
+    hidden_sums = hidden_sums.reshape(dp_count, 1, -1) * here[None, :, None]
     early = jnp.concatenate([spread(item) for item in sums_two] + [hidden_sums], axis=2)
     early = small_scatter(early, dp_rank, seq_rank)
-    qv_sums = jnp.stack([jnp.sum(item.astype(F32), axis=0) for item in (grads[0], grads[2])])
     here = (jnp.arange(sub) == rank_low)[:, None] & (jnp.arange(high) == rank_high)[None, :]
     qv_sums = qv_sums.reshape(2, own_heads, 1, 1, HEAD_DIM) * here.astype(F32)[None, None, :, :, None]
     late = jnp.concatenate([spread(item) for item in sums_one] + [spread(qv_sums)], axis=2)

time: 1040 us -> 920 us (0.88)
  matrix products: 86.4 us -> 29.3 us
  starting transfers between devices: 84.8 us -> 37.6 us
  local copies, waits for them, and re-layouts: 54.3 us -> 33.3 us
  Pallas kernels: 597 us -> 617 us
  other arithmetic: 18.9 us -> 6.41 us
    ppermute x67 -> x28, waiting for transfers between devices: 178 us -> 30 us  [shift(): return lax.ppermute(value, axis, [(i, i ^ distance) for i in range(count)])]
    reduce_scatter x6 -> x4, waiting for transfers between devices: 0.05 us -> 127 us  [scatter_dp(): return lax.psum_scatter(value, 'dp', scatter_dimension=0, tiled=True)]
    dot_general x6 -> x2, matrix products: 86.4 us -> 29.3 us  [tn(): lax.dot_general(left, right, (((0,), (0,)), ((), ())), preferred_element_...]
    ppermute x67 -> x28, starting transfers between devices: 81.5 us -> 34 us  [shift(): return lax.ppermute(value, axis, [(i, i ^ distance) for i in range(count)])]
    pallas_call x17 -> x5, Pallas kernels: 554 us -> 586 us  [the longest x1 230 us: feed_plane(): pl.pallas_call(plane_kernel, in_specs=[anywhere] * 6 + [inside, anywhere,...]
    slice x16 -> x1, local copies, waits for them, and re-layouts: 21.8 us -> 0.84 us  [shards(): sums_one = [sums_one[i] for i in range(2)]]
    all_gather x5 -> x3, waiting for transfers between devices: 0.03 us -> 16.9 us  [gather_dp(): return lax.all_gather(value, 'dp', axis=0, tiled=True)]
    pallas_call x4 -> x1, Pallas kernels: 38.2 us -> 24.6 us  [call_on_block(): pl.pallas_call(body, grid=grid, in_specs=specs, out_specs=out_specs, out_...]
  transfers between devices with their start and end apart: 80 -> 37, of which waited for: 22 -> 11; matrix products, arithmetic and copies ran while one was open for 12% -> 4% of each run, Pallas kernels for 39% -> 34%
where the time goes in v4:
time: 920 us; the launch traced here: 915 us
  Pallas kernels  617 us (67%)
  waiting for transfers between devices  176 us (19%)
  starting transfers between devices  37.6 us (4%)
  local copies, waits for them, and re-layouts  33.3 us (4%)
  matrix products  29.3 us (3%)
  between operations  15.6 us (2%)
    pallas_call x1, Pallas kernels, feed_plane(): pl.pallas_call(plane_kernel, in_specs=[anywhere] * 6 + [inside, anywhere,...  230 us
    reduce_scatter x4, waiting for transfers between devices, scatter_dp(): return lax.psum_scatter(value, 'dp', scatter_dimension=0, tiled=True)  127 us
    pallas_call x1, Pallas kernels, opening(): pl.pallas_call(opening_kernel, in_specs=[inside] * 4, out_specs=[anywhere...  99.3 us
    pallas_call x1, Pallas kernels, attend_plane(): pl.pallas_call(attend_plane_kernel, in_specs=[anywhere] * 6 + [inside] *...  98.7 us
    pallas_call x1, Pallas kernels, closing(): pl.pallas_call(closing_kernel, in_specs=[inside, inside, anywhere, anywhe...  82.4 us
    pallas_call x1, Pallas kernels, retreat_plane(): pl.pallas_call(retreat_plane_kernel, in_specs=[anywhere] * 8 + [inside] *...  75.4 us
    ppermute x28, starting transfers between devices, shift(): return lax.ppermute(value, axis, [(i, i ^ distance) for i in range(count)])  34 us
    ppermute x28, waiting for transfers between devices, shift(): return lax.ppermute(value, axis, [(i, i ^ distance) for i in range(count)])  30 us
  transfers between devices with their start and end apart: 37, of which 11 were waited for; matrix products, arithmetic and copies ran while one was open for 4% of the time, Pallas kernels for 34%

profile of v4, /device:TPU:0, one launch (start us, length us, event | category | flops | bytes accessed | tf_op | source)
XLA Modules:
  0.0 915.0 jit_solution(9123775447743406027)
XLA Ops:
  10.4 2.6 reshape.290
  17.0 99.3 %shard_map.263 = (bf16[2048,2048]{1,0:T(8,128)(2,1)S(1)}, bf16[2048,1536]{1,0:T(8,128)(2,1)S(1)}, bf16[256,2048]{1,0:T(8,128)(2,1)}, bf16[512,128]{1,0:T(8,128)(2,1)S(1)}) custom-call(bf16[512,2048]{1,0:T(8,128)(2,1)S(1)} %bitcast.102, bf16[4,64,1536]{2,1,0:T(8,128)(2,1)S(1)} %reshape.291.qkv_pieces, bf16[4,64,2048]{2,1,0:T(8,128)(2,1)S(1)} %reshape.293.fc_pieces, ...), custom_call_target="tpu_custom_call" | custom-call | bytes 41943040 | tf_op jit(solution)/shard_map/pallas_call | solution.py:686
  116.3 3.3 copy-done.1
  119.6 2.8 copy-done.2
  131.4 24.6 %shard_map.264 = (bf16[2048,2048]{1,0:T(8,128)(2,1)}, bf16[2048,512]{1,0:T(8,128)(2,1)}, bf16[2048,512]{1,0:T(8,128)(2,1)}, bf16[2048,512]{1,0:T(8,128)(2,1)}, b...) custom-call(bf16[2048,2048]{1,0:T(8,128)(2,1)} %copy-done.1, f32[1,2048]{1,0:T(1,128)} %reshape.296.refs_1_.gain, ...), custom_call_target="tpu_custom_call" | custom-call | flops 12884901888 | bytes 33554432 | tf_op jit(solution)/shard_map/pallas_call | solution.py:63
  156.0 14.1 %collective-permute-done.1.cot_two = bf16[512,2048]{1,0:T(8,128)(2,1)S(1)} collective-permute-done((bf16[512,2048]{1,0:T(8,128)(2,1)}, bf16[512,2048]{1,0:T(8,128)(2,1)S(1)}, u32[]{:S(2)}, u32[]{:S(2)}) %collective-permute-start.1) | collective-permute-done | bytes 2097184 | tf_op jit(solution)/shard_map/ppermute | solution.py:1370
  171.5 98.7 %shard_map.265 = (f32[512,2048]{1,0:T(8,128)}, bf16[512,2048]{1,0:T(8,128)(2,1)}, bf16[2048,512]{1,0:T(8,128)(2,1)}, f32[4,1,2048]{2,1,0:T(1,128)}, bf16[512,2048]{1,0:T(8,128)(2,1)}) custom-call(bf16[2048,512]{1,0:T(8,128)(2,1)} %get-tuple-element.48.q, bf16[2048,512]{1,0:T(8,128)(2,1)} %get-tuple-element.49.k, bf16[512,2048]{1,0:T(8,128)(2,1)} %get-tuple-element.50.v_t, ...), custom_call_target="tpu_custom_call" | custom-call | flops 10737418240 | bytes 41943040 | tf_op jit(solution)/shard_map/pallas_call | solution.py:833
  270.2 16.8 %all-gather.6.cloned.1.call-done.fc = bf16[2048,2048]{1,0:T(8,128)(2,1)} async-done(((bf16[256,2048]{1,0:T(8,128)(2,1)}), bf16[2048,2048]{1,0:T(8,128)(2,1)}) %all-gather.6.cloned.1.call-update) | async-done | bytes 8388624 | tf_op jit(solution)/shard_map/all_gather | solution.py:1441
  287.0 230.3 %shard_map.266 = (f32[512,2048]{1,0:T(8,128)}, bf16[2048,2048]{1,0:T(8,128)(2,1)}, f32[4,2048]{1,0:T(4,128)}, f32[1,2048]{1,0:T(1,128)}, bf16[2048,2048]{1,0:T(8...) custom-call(bf16[512,2048]{1,0:T(8,128)(2,1)} %get-tuple-element.52., ...), custom_call_target="tpu_custom_call" | custom-call | flops 103079215104 | bytes 41943040 | tf_op jit(solution)/shard_map/pallas_call | solution.py:1095
  517.3 75.4 %shard_map.267 = (bf16[2048,1536]{1,0:T(8,128)(2,1)}, f32[2,512]{1,0:T(2,128)}, bf16[512,2048]{1,0:T(8,128)(2,1)}) custom-call(bf16[2048,2048]{1,0:T(8,128)(2,1)} %get-tuple-element.57.low_all, bf16[2048,512]{1,0:T(8,128)(2,1)} %get-tuple-element.48.q, bf16[2048,512]{1,0:T(8,128)(2,1)} %get-tuple-element.49.k, bf16[2048,512]{1,0:T(8,128)(2,1)} %get-tuple-element.58.v, ...), custom_call_target="tpu_custom_call" | custom-call | flops 21474836480 | bytes 41943040 | tf_op jit(solution)/shard_map/pallas_call | solution.py:1248
  592.7 19.6 %convolution_convert_fusion = bf16[2048,1536]{1,0:T(8,128)(2,1)} fusion(bf16[2048,2048]{1,0:T(8,128)(2,1)} %get-tuple-element.68, bf16[2048,1536]{1,0:T(8,128)(2,1)} %get-tuple-element.63.grads), kind=kOutput, calls=%fused_computation | convolution fusion | flops 12888047616 | bytes 20971520 | tf_op jit(solution)/shard_map/dot_general | solution.py:32
  613.9 9.7 %convolution_convert_fusion.1 = bf16[512,2048]{1,0:T(8,128)(2,1)} fusion(bf16[2048,512]{1,0:T(8,128)(2,1)S(1)} %copy-done.26, bf16[2048,2048]{1,0:T(8,128)(2,1)} %get-tuple-element.57.low_all), kind=kOutput, calls=%fused_computation.1 | convolution fusion | flops 4296015872 | bytes 12582912 | tf_op jit(solution)/shard_map/dot_general | solution.py:32
  626.4 82.4 %shard_map.268 = (f32[512,2048]{1,0:T(8,128)}, f32[2,2048]{1,0:T(2,128)}) custom-call(bf16[2048,1536]{1,0:T(8,128)(2,1)} %get-tuple-element.63.grads, bf16[2048,1536]{1,0:T(8,128)(2,1)} %copy-done.2, bf16[512,2048]{1,0:T(8,128)(2,1)} %bitcast.101, f32[512,2048]{1,0:T(8,128)} %get-tuple-element.64.grad_middle, f32[1,2048]{1,0:T(1,128)} %reshape.296.refs_1_.gain), custom_call_target="tpu_custom_call" | custom-call | flops 12884901888 | bytes 10485760 | tf_op jit(solution)/shard_map/pallas_call | solution.py:1347
  714.8 1.9 collective-permute-done.5
  718.0 2.9 collective-permute-start.11
  720.8 2.2 collective-permute-start.9
  723.1 2.1 collective-permute-start.7
  730.1 1.9 collective-permute-done.19
  733.2 2.8 collective-permute-start.25
  736.0 2.2 collective-permute-start.23
  738.3 1.9 dynamic-slice_bitcast_fusion.4
  740.2 2.1 collective-permute-start.21
  744.0 63.5 %reduce-scatter.9.cloned.1.call-done = bf16[256,2048]{1,0:T(8,128)(2,1)} async-done(((bf16[2048,2048]{1,0:T(8,128)(2,1)}), bf16[256,2048]{1,0:T(8,128)(2,1)}) %reduce-scatter.9.cloned.1.call-update) | async-done | bytes 1048592 | tf_op jit(solution)/shard_map/reduce_scatter | solution.py:1445
  807.5 2.0 dynamic-slice_bitcast_fusion
  809.5 2.4 collective-permute-start.15
  816.5 1.8 collective-permute-done.15.refs_3_
  821.2 9.2 %collective-permute-done.14.refs_2_ = bf16[64,1536]{1,0:T(8,128)(2,1)S(1)} collective-permute-done((bf16[64,1536]{1,0:T(8,128)(2,1)S(1)}, bf16[64,1536]{1,0:T(8,128)(2,1)S(1)}, u32[]{:S(2)}, u32[]{:S(2)}) %collective-permute-start.14) | collective-permute-done | bytes 196640 | tf_op jit(solution)/shard_map/ppermute | solution.py:1370
  831.1 2.7 shard_map.269
  833.9 63.9 %reduce-scatter.11.cloned.1.call-done = bf16[256,2048]{1,0:T(8,128)(2,1)} async-done(((bf16[2048,2048]{1,0:T(8,128)(2,1)}), bf16[256,2048]{1,0:T(8,128)(2,1)}) %reduce-scatter.11.cloned.1.call-update) | async-done | bytes 1048592 | tf_op jit(solution)/shard_map/reduce_scatter | solution.py:1445
  897.8 2.8 convert_element_type.45
  901.4 3.2 shard_map.270
  905.9 2.0 copy.80
  (186 shorter events, 46.1 us)
Async XLA Ops:
  7.2 163.2 %all-gather.4.cloned.1.call-start = ((), (), s32[]{:S(2)}) async-start(), calls=%async_computation.4 | async-start | bytes 2359296 | tf_op jit(solution)/shard_map/all_gather | solution.py:1441
  9.7 260.4 %all-gather.8.cloned.1.call-start = ((), (), s32[]{:S(2)}) async-start(), calls=%async_computation.6 | async-start | bytes 9437184 | tf_op jit(solution)/shard_map/all_gather | solution.py:1441
  122.4 164.6 %all-gather.6.cloned.1.call-start = ((), (), s32[]{:S(2)}) async-start(), calls=%async_computation.5 | async-start | bytes 9437184 | tf_op jit(solution)/shard_map/all_gather | solution.py:1441
  123.2 615.1 %reduce-scatter.5.cloned.1.call-start = ((), (), s32[]{:S(2)}) async-start(), calls=%async_computation.7 | async-start | bytes 7077888 | tf_op jit(solution)/shard_map/reduce_scatter | solution.py:1445
  123.2 46.9 %collective-permute-start.1 = (bf16[512,2048]{1,0:T(8,128)(2,1)}, bf16[512,2048]{1,0:T(8,128)(2,1)S(1)}, u32[]{:S(2)}, u32[]{:S(2)}) collective-permute-start(bf16[512,2048]{1,0:T(8,128)(2,1)} %bitcast.134), channel_id=1, source_target_pairs={{0,2},{1,3},{2,0},{3,1},{4,6},{5,7},{6,4},{7,5},{8,10},{9,11},{10,... | collective-permute-start | bytes 6291464 | tf_op jit(solution)/shard_map/ppermute | solution.py:1370
  124.1 46.2 %collective-permute-start = (bf16[512,2048]{1,0:T(8,128)(2,1)}, bf16[512,2048]{1,0:T(8,128)(2,1)}, u32[]{:S(2)}, u32[]{:S(2)}) collective-permute-start(bf16[512,2048]{1,0:T(8,128)(2,1)} %bitcast.135), channel_id=1, source_target_pairs={{0,1},{1,0},{2,3},{3,2},{4,5},{5,4},{6,7},{7,6},{8,9},{9,8},{10,11... | collective-permute-start | bytes 6291464 | tf_op jit(solution)/shard_map/ppermute | solution.py:1370
  612.4 130.0 %reduce-scatter.7.cloned.1.call-start = ((), (), s32[]{:S(2)}) async-start(), calls=%async_computation.8 | async-start | bytes 2359296 | tf_op jit(solution)/shard_map/reduce_scatter | solution.py:1445
  623.7 183.9 %reduce-scatter.9.cloned.1.call-start = ((), (), s32[]{:S(2)}) async-start(), calls=%async_computation.9 | async-start | bytes 9437184 | tf_op jit(solution)/shard_map/reduce_scatter | solution.py:1445
  624.2 273.5 %reduce-scatter.11.cloned.1.call-start = ((), (), s32[]{:S(2)}) async-start(), calls=%async_computation.10 | async-start | bytes 9437184 | tf_op jit(solution)/shard_map/reduce_scatter | solution.py:1445
  716.7 6.4 collective-permute-start.12
  716.8 6.3 collective-permute-start.6
  718.0 7.3 collective-permute-start.11
  720.8 5.5 collective-permute-start.10
  720.8 6.5 collective-permute-start.9
  723.1 5.7 collective-permute-start.8
  723.1 5.7 collective-permute-start.7
  725.3 4.7 collective-permute-start.17
  727.4 4.6 collective-permute-start.19
  732.0 8.2 collective-permute-start.26
  732.1 8.1 collective-permute-start.20
  733.2 9.2 %collective-permute-start.25 = (f32[512]{0:T(512)S(1)}, f32[512]{0:T(512)S(1)}, u32[]{:S(2)}, u32[]{:S(2)}) collective-permute-start(f32[512]{0:T(512)S(1)} %bitcast.124), channel_id=1, source_target_pairs={{0,24},{4,28},{8,16},{12,20},{16,8},{20,12},{24,0},{28,4},{1,25},{... | collective-permute-start | bytes 6152 | tf_op jit(solution)/shard_map/ppermute | solution.py:1370
  736.0 73.5 %collective-permute-start.24 = (f32[512]{0:T(512)S(1)}, f32[512]{0:T(512)S(1)}, u32[]{:S(2)}, u32[]{:S(2)}) collective-permute-start(f32[512]{0:T(512)S(1)} %bitcast.123), channel_id=1, source_target_pairs={{0,20},{4,16},{8,28},{12,24},{16,4},{20,0},{24,12},{28,8},{1,21},{... | collective-permute-start | bytes 6152 | tf_op jit(solution)/shard_map/ppermute | solution.py:1370
  736.0 75.8 %collective-permute-start.23 = (f32[512]{0:T(512)S(1)}, f32[512]{0:T(512)S(1)}, u32[]{:S(2)}, u32[]{:S(2)}) collective-permute-start(f32[512]{0:T(512)S(1)} %bitcast.122), channel_id=1, source_target_pairs={{0,16},{4,20},{8,24},{12,28},{16,0},{20,4},{24,8},{28,12},{1,17},{... | collective-permute-start | bytes 6152 | tf_op jit(solution)/shard_map/ppermute | solution.py:1370
  740.2 72.2 %collective-permute-start.22 = (f32[512]{0:T(512)S(1)}, f32[512]{0:T(512)S(1)}, u32[]{:S(2)}, u32[]{:S(2)}) collective-permute-start(f32[512]{0:T(512)S(1)} %bitcast.121), channel_id=1, source_target_pairs={{0,12},{4,8},{8,4},{12,0},{16,28},{20,24},{24,20},{28,16},{1,13},{... | collective-permute-start | bytes 6152 | tf_op jit(solution)/shard_map/ppermute | solution.py:1370
  740.2 73.7 %collective-permute-start.21 = (f32[512]{0:T(512)S(1)}, f32[512]{0:T(512)S(1)}, u32[]{:S(2)}, u32[]{:S(2)}) collective-permute-start(f32[512]{0:T(512)S(1)} %bitcast.120), channel_id=1, source_target_pairs={{0,8},{4,12},{8,0},{12,4},{16,24},{20,28},{24,16},{28,20},{1,9},{5... | collective-permute-start | bytes 6152 | tf_op jit(solution)/shard_map/ppermute | solution.py:1370
  742.4 73.6 %collective-permute-start.16 = (bf16[64,2048]{1,0:T(8,128)(2,1)}, bf16[64,2048]{1,0:T(8,128)(2,1)S(1)}, u32[]{:S(2)}, u32[]{:S(2)}) collective-permute-start(bf16[64,2048]{1,0:T(8,128)(2,1)} %reduce-scatter.7.cloned.1.call-done), channel_id=1, source_target_pairs={{0,0},{4,1},{2,2},{6,3},{1,4},{5,5},{3,6},{7,7},{8,8},{12,9},{10,1... | collective-permute-start | bytes 786440 | tf_op jit(solution)/shard_map/ppermute | solution.py:1598
  809.5 8.8 collective-permute-start.15
  811.9 88.7 %collective-permute-start.29 = (bf16[64,2048]{1,0:T(8,128)(2,1)S(1)}, bf16[64,2048]{1,0:T(8,128)(2,1)S(1)}, u32[]{:S(2)}, u32[]{:S(2)}) collective-permute-start(bf16[64,2048]{1,0:T(8,128)(2,1)S(1)} %get-tuple-element.80), channel_id=1, source_target_pairs={{0,3},{1,2},{2,1},{3,0},{4,7},{5,6},{6,5},{7,4},{8,11},{9,10},{10,... | collective-permute-start | bytes 786440 | tf_op jit(solution)/shard_map/ppermute | solution.py:1370
  812.5 88.1 %collective-permute-start.28 = (bf16[64,2048]{1,0:T(8,128)(2,1)S(1)}, bf16[64,2048]{1,0:T(8,128)(2,1)S(1)}, u32[]{:S(2)}, u32[]{:S(2)}) collective-permute-start(bf16[64,2048]{1,0:T(8,128)(2,1)S(1)} %get-tuple-element.81), channel_id=1, source_target_pairs={{0,2},{1,3},{2,0},{3,1},{4,6},{5,7},{6,4},{7,5},{8,10},{9,11},{10,... | collective-permute-start | bytes 786440 | tf_op jit(solution)/shard_map/ppermute | solution.py:1370
  813.9 86.7 %collective-permute-start.27 = (bf16[64,2048]{1,0:T(8,128)(2,1)S(1)}, bf16[64,2048]{1,0:T(8,128)(2,1)}, u32[]{:S(2)}, u32[]{:S(2)}) collective-permute-start(bf16[64,2048]{1,0:T(8,128)(2,1)S(1)} %get-tuple-element.82), channel_id=1, source_target_pairs={{0,1},{1,0},{2,3},{3,2},{4,5},{5,4},{6,7},{7,6},{8,9},{9,8},{10,11... | collective-permute-start | bytes 786440 | tf_op jit(solution)/shard_map/ppermute | solution.py:1370
  816.0 14.4 %collective-permute-start.14 = (bf16[64,1536]{1,0:T(8,128)(2,1)S(1)}, bf16[64,1536]{1,0:T(8,128)(2,1)S(1)}, u32[]{:S(2)}, u32[]{:S(2)}) collective-permute-start(bf16[64,1536]{1,0:T(8,128)(2,1)S(1)} %get-tuple-element.85), channel_id=1, source_target_pairs={{0,2},{1,3},{2,0},{3,1},{4,6},{5,7},{6,4},{7,5},{8,10},{9,11},{10,... | collective-permute-start | bytes 589832 | tf_op jit(solution)/shard_map/ppermute | solution.py:1370
  818.3 12.2 %collective-permute-start.13 = (bf16[64,1536]{1,0:T(8,128)(2,1)S(1)}, bf16[64,1536]{1,0:T(8,128)(2,1)S(1)}, u32[]{:S(2)}, u32[]{:S(2)}) collective-permute-start(bf16[64,1536]{1,0:T(8,128)(2,1)S(1)} %get-tuple-element.86), channel_id=1, source_target_pairs={{0,1},{1,0},{2,3},{3,2},{4,5},{5,4},{6,7},{7,6},{8,9},{9,8},{10,11... | collective-permute-start | bytes 589832 | tf_op jit(solution)/shard_map/ppermute | solution.py:1370
  (32 other events, 266.2 us)
Sparse Core Ops, SparseCore 0:
  10.2 40.5 all-gather.3
  122.5 82.2 all-gather.7
  206.4 80.5 all-gather.5
  612.5 67.3 reduce-scatter.4
  682.6 34.1 reduce-scatter.6
  718.9 88.5 reduce-scatter.8
  809.8 87.8 reduce-scatter.10

commit v5 on v4

--- a/solution.py
+++ b/solution.py
@@ -864,10 +864,128 @@
         ref[at : at + 1, columns] += total
 
 
+class LevelScatter:
+    def __init__(self, source, mate_in, summed, got, send, receive):
+        self.source, self.mate_in, self.summed, self.got = source, mate_in, summed, got
+        self.send, self.receive = send, receive
+        self.rows = mate_in.shape[0] // 4
+        self.place = lax.axis_index("dp")
+        self.level, self.core = lax.div(self.place, 2), lax.rem(self.place, 2)
+        self.mate = self.place + 1 - 2 * self.core
+
+    def greet(self):
+        greet("dp", self.mate)
+        count = jnp.int32(1)
+        for step in (1, 2):
+            up, down = self.level + step <= 3, self.level >= step
+            pl.when(up)(lambda step=step: greet("dp", self.place + 2 * step))
+            pl.when(down)(lambda step=step: greet("dp", self.place - 2 * step))
+            count = count + up.astype(jnp.int32) + down.astype(jnp.int32)
+        return count
+
+    def block(self, ref, at):
+        return ref.at[pl.ds(at * self.rows, self.rows)]
+
+    def swaps(self):
+        return [
+            remote(
+                self.block(self.source, 2 * at + 1 - self.core), self.block(self.mate_in, at),
+                self.send.at[at], self.receive.at[at], "dp", self.mate,
+            )
+            for at in range(4)
+        ]
+
+    def start(self):
+        for item in self.swaps():
+            item.start()
+
+    def add(self, first, second, out, grid, first_at, second_at, out_at):
+        def body(left, right, total):
+            total[...] = (left[...].astype(F32) + right[...].astype(F32)).astype(total.dtype)
+
+        spec = lambda at: pl.BlockSpec((self.rows, first.shape[1]), lambda i: (at(i), 0))
+        pltpu.emit_pipeline(
+            body, grid=(grid,), in_specs=[spec(first_at), spec(second_at)], out_specs=[spec(out_at)]
+        )(first, second, out)
+
+    def hop(self, at, slot, index, steps):
+        return remote(
+            self.block(self.summed, at), self.block(self.got, slot), self.send.at[4 + index], self.receive.at[4 + slot],
+            "dp", self.place + 2 * steps,
+        )
+
+    def hops(self):
+        level = self.level
+        return [
+            (level == 0, self.hop(3, 3, 0, 1)),
+            (level == 3, self.hop(0, 3, 0, -1)),
+            (level == 0, self.hop(2, 2, 1, 2)),
+            (level == 3, self.hop(1, 2, 1, -2)),
+            (level <= 2, self.hop(lax.rem(level + 1, 4), 0, 2, 1)),
+            (level >= 1, self.hop(lax.rem(level + 3, 4), 1, 3, -1)),
+        ]
+
+    def passes(self):
+        return [(self.level == 1, self.hop(3, 2, 1, 2)), (self.level == 2, self.hop(0, 2, 1, -2))]
+
+    def spread(self):
+        for item in self.swaps():
+            item.wait_recv()
+        self.add(
+            self.source, self.mate_in, self.summed, 4, lambda i: 2 * i + self.core, lambda i: i, lambda i: i
+        )
+        for condition, copy in self.hops():
+            pl.when(condition)(lambda copy=copy: copy.start())
+
+    def arrive(self, slot):
+        here = self.block(self.got, slot)
+        remote(here, here, self.send.at[0], self.receive.at[4 + slot], "dp", self.mate).wait_recv()
+
+    def pass_on(self):
+        for level, at in ((1, 3), (2, 0)):
+
+            @pl.when(self.level == level)
+            def _(at=at):
+                self.arrive(3)
+                self.add(self.summed, self.got, self.summed, 1, lambda i: at, lambda i: 3, lambda i: at)
+
+        for condition, copy in self.passes():
+            pl.when(condition)(lambda copy=copy: copy.start())
+
+    def finish(self, out):
+        level = self.level
+        pl.when(level >= 1)(lambda: self.arrive(0))
+        pl.when(level <= 2)(lambda: self.arrive(1))
+        self.arrive(2)
+        rows = min(64, self.rows)
+
+        def body(own, mate, below, above, far, total):
+            value = own[...].astype(F32) + mate[...].astype(F32) + far[...].astype(F32)
+            below_term, above_term = below[...].astype(F32), above[...].astype(F32)
+            value = value + jnp.where(level >= 1, below_term, 0.0) + jnp.where(level <= 2, above_term, 0.0)
+            total[...] = value.astype(total.dtype)
+
+        steps = self.rows // rows
+        spec = lambda at: pl.BlockSpec((rows, out.shape[1]), lambda i: (at * steps + i, 0))
+        pltpu.emit_pipeline(
+            body,
+            grid=(steps,),
+            in_specs=[spec(self.place), spec(level), spec(0), spec(1), spec(2)],
+            out_specs=[spec(0)],
+        )(self.source, self.mate_in, self.got, self.got, self.got, out)
+
+    def close(self):
+        for item in self.swaps():
+            item.wait_send()
+        for condition, copy in self.hops() + self.passes():
+            pl.when(condition)(lambda copy=copy: copy.wait_send())
+
+
 def plane_kernel(
     normed, cot_own, cot_one, cot_two, cot_three, fc, bias, down, middle, gain,
     grad_middle, low_all, sums, hidden_sums, active, hidden_grad, normed_all, cot_all, terms, grad_down, grad_fc,
-    normed_buf, cot_buf, sum_ref, joined, passed, arrived, load, local, send, receive,
+    mate_in, summed, got, down_share,
+    normed_buf, cot_buf, sum_ref, joined, passed, arrived, load, local, send, receive, level_send, level_receive,
 ):
     piece, width = normed.shape
     half = piece // 2
@@ -876,9 +994,10 @@
     tile = min(512, inner)
     last = inner // tile - 1
     one, two = neighbours()
+    scatter = LevelScatter(grad_down, mate_in, summed, got, level_send, level_receive)
     for device in (one, two):
         greet("seq", device)
-    pl.semaphore_wait(pltpu.get_barrier_semaphore(), 2)
+    pl.semaphore_wait(pltpu.get_barrier_semaphore(), 2 + scatter.greet())
 
     up, lower = pl.ds(0, half), pl.ds(half, half)
     rows = lambda k, start=0, size=piece: pl.ds(k * piece + start, size)
@@ -1017,7 +1136,24 @@
             out_specs=[pl.BlockSpec((piece, narrow), lambda k, j: (start + k, j))],
         )(active, down, terms)
 
-    multiply_down(0)
+    wide, tall = min(1024, width), min(1024, inner)
+
+    def outer_body(left, right, out):
+        out[...] = tn(left[...], right[...]).astype(BF16)
+
+    def outer(left, right, out, shape):
+        pltpu.emit_pipeline(
+            outer_body,
+            grid=(out.shape[0] // shape[0], out.shape[1] // shape[1]),
+            in_specs=[
+                pl.BlockSpec((length, shape[0]), lambda i, j: (0, i)),
+                pl.BlockSpec((length, shape[1]), lambda i, j: (0, j)),
+            ],
+            out_specs=[pl.BlockSpec(shape, lambda i, j: (i, j))],
+        )(left, right, out)
+
+    outer(active, cot_all, grad_down, (tall, wide))
+    scatter.start()
     for item in across:
         item.wait_recv()
     joined[0] = (cot_buf[1, half:].astype(F32) + passed[1].astype(F32)).astype(BF16)
@@ -1026,7 +1162,8 @@
     joined_two.start()
     for item in keeps:
         item.wait()
-    multiply_down(2)
+    multiply_down(0)
+    scatter.spread()
     for item in (plain_one, plain_two, joined_one, joined_two):
         item.wait_recv()
 
@@ -1054,28 +1191,15 @@
     low_one.start()
     low_two.start()
 
-    wide, tall = min(1024, width), min(1024, inner)
-
-    def outer_body(left, right, out):
-        out[...] = tn(left[...], right[...]).astype(BF16)
-
-    def outer(left, right, out, shape):
-        pltpu.emit_pipeline(
-            outer_body,
-            grid=(out.shape[0] // shape[0], out.shape[1] // shape[1]),
-            in_specs=[
-                pl.BlockSpec((length, shape[0]), lambda i, j: (0, i)),
-                pl.BlockSpec((length, shape[1]), lambda i, j: (0, j)),
-            ],
-            out_specs=[pl.BlockSpec(shape, lambda i, j: (i, j))],
-        )(left, right, out)
-
-    outer(active, cot_all, grad_down, (tall, wide))
+    multiply_down(2)
+    scatter.pass_on()
+    outer(normed_all, hidden_grad, grad_fc, (wide, tall))
     low_one.wait_recv()
     low_two.wait_recv()
     for item in low_three:
         item.start()
-    outer(normed_all, hidden_grad, grad_fc, (wide, tall))
+    scatter.finish(down_share)
+    scatter.close()
     for item in low_three:
         item.wait()
     for item in (
@@ -1095,11 +1219,12 @@
     return pl.pallas_call(
         plane_kernel,
         in_specs=[anywhere] * 6 + [inside, anywhere, anywhere, inside],
-        out_specs=[anywhere, anywhere, inside, inside] + [anywhere] * 7,
+        out_specs=[anywhere, anywhere, inside, inside] + [anywhere] * 11,
         out_shape=[
             shape(piece, width, F32), shape(length, width), shape(4, width, F32), shape(1, inner, F32),
             shape(length, inner), shape(length, inner), shape(length, width), shape(length, width),
             shape(length, width), shape(inner, width), shape(width, inner),
+            shape(inner // 2, width), shape(inner // 2, width), shape(inner // 2, width), shape(inner // 8, width, F32),
         ],
         scratch_shapes=[
             pltpu.VMEM((4, piece, width), BF16),
@@ -1108,7 +1233,7 @@
             pltpu.VMEM((2, half, width), BF16),
             pltpu.VMEM((2, half, width), BF16),
             pltpu.VMEM((3, piece, width), BF16),
-            dma((5,)), dma((8,)), dma((14,)), dma((14,)),
+            dma((5,)), dma((8,)), dma((14,)), dma((14,)), dma((8,)), dma((8,)),
         ],
         compiler_params=pltpu.CompilerParams(collective_id=1, has_side_effects=True, vmem_limit_bytes=60 * 2**20),
         cost_estimate=cost(12 * length * width * inner, 10 * length * width),
@@ -1558,11 +1683,12 @@
         )
 
     if in_plane:
-        grad_middle, low_all, sums_two, hidden_sums, _, _, _, _, down_terms, grad_down, grad_fc = feed_plane(
-            normed_two, (cot_own, *cots, cot_three), fc_full, fc_shift, down_full, middle, gain_two
-        )
+        results = feed_plane(normed_two, (cot_own, *cots, cot_three), fc_full, fc_shift, down_full, middle, gain_two)
+        grad_middle, low_all, sums_two, hidden_sums, down_terms, grad_fc, grad_down = [
+            results[i] for i in (0, 1, 2, 3, 8, 10, 14)
+        ]
         sums_two = [sums_two[i] for i in range(4)]
-        grad_down, grad_fc = scatter_dp(grad_down), scatter_dp(grad_fc)
+        grad_fc = scatter_dp(grad_fc)
         grads, qv_sums, block_out = retreat_plane(
             low_all, q, keys, values, keys_t, lse, down_terms, middle, key_bias, proj_full, down_shift
         )
@@ -1593,8 +1719,11 @@
         grad_q, low_all = shared
         grads = jnp.concatenate([grad_q, sums[0], sums[1]], axis=1)
         qv_sums = jnp.stack([jnp.sum(item.astype(F32), axis=0) for item in (grad_q, sums[1])])
+    grad_proj = tn(attended, low_all).astype(BF16)
+    if in_plane:
+        normed_one = after(normed_one, grad_fc, grad_proj)
     grad_qkv = scatter_dp(tn(normed_one, grads).astype(BF16))
-    grad_proj = scatter_dp(tn(attended, low_all).astype(BF16))
+    grad_proj = scatter_dp(grad_proj)
     grad_proj = lax.ppermute(grad_proj, BOTH, swap).astype(F32)
     if in_plane:
         tokens_grad, sums_one = closing(grads, qkv_full, tokens_own, grad_middle, gain_one)

time: 920 us -> 800 us (0.87)
  waiting for transfers between devices: 176 us -> 51.1 us
    reduce_scatter x4 -> x3, waiting for transfers between devices: 127 us -> 0.02 us  [scatter_dp(): return lax.psum_scatter(value, 'dp', scatter_dimension=0, tiled=True)]
  transfers between devices with their start and end apart: 37 -> 36, of which waited for: 11 -> 15; matrix products, arithmetic and copies ran while one was open for 4% -> 6% of each run, Pallas kernels for 34% -> 48%
where the time goes in v5:
time: 800 us; the launch traced here: 792 us
  Pallas kernels  615 us (77%)
  waiting for transfers between devices  51.1 us (6%)
  starting transfers between devices  45.2 us (6%)
  local copies, waits for them, and re-layouts  33.4 us (4%)
  matrix products  28.6 us (4%)
  between operations  15.6 us (2%)
    pallas_call x1, Pallas kernels, feed_plane(): pl.pallas_call(plane_kernel, in_specs=[anywhere] * 6 + [inside, anywhere,...  230 us
    pallas_call x1, Pallas kernels, opening(): pl.pallas_call(opening_kernel, in_specs=[inside] * 4, out_specs=[anywhere...  99.3 us
    pallas_call x1, Pallas kernels, attend_plane(): pl.pallas_call(attend_plane_kernel, in_specs=[anywhere] * 6 + [inside] *...  98.7 us
    pallas_call x1, Pallas kernels, closing(): pl.pallas_call(closing_kernel, in_specs=[inside, inside, anywhere, anywhe...  82.1 us
    pallas_call x1, Pallas kernels, retreat_plane(): pl.pallas_call(retreat_plane_kernel, in_specs=[anywhere] * 8 + [inside] *...  74.5 us
    ppermute x28, waiting for transfers between devices, shift(): return lax.ppermute(value, axis, [(i, i ^ distance) for i in range(count)])  33.5 us
    ppermute x28, starting transfers between devices, shift(): return lax.ppermute(value, axis, [(i, i ^ distance) for i in range(count)])  32.8 us
    dot_general x2, matrix products, tn(): lax.dot_general(left, right, (((0,), (0,)), ((), ())), preferred_element_...  28.6 us
  transfers between devices with their start and end apart: 36, of which 15 were waited for; matrix products, arithmetic and copies ran while one was open for 6% of the time, Pallas kernels for 48%

profile of v5, /device:TPU:0, one launch (start us, length us, event | category | flops | bytes accessed | tf_op | source)
XLA Modules:
  0.0 792.3 jit_solution(1931348293063434117)
XLA Ops:
  7.2 1.7 collective-permute-start.2
  10.4 2.6 reshape.290
  15.5 1.6 copy-done
  17.0 99.3 %shard_map.263 = (bf16[2048,2048]{1,0:T(8,128)(2,1)S(1)}, bf16[2048,1536]{1,0:T(8,128)(2,1)S(1)}, bf16[256,2048]{1,0:T(8,128)(2,1)}, bf16[512,128]{1,0:T(8,128)(2,1)S(1)}) custom-call(bf16[512,2048]{1,0:T(8,128)(2,1)S(1)} %bitcast.102, bf16[4,64,1536]{2,1,0:T(8,128)(2,1)S(1)} %reshape.291.qkv_pieces, bf16[4,64,2048]{2,1,0:T(8,128)(2,1)S(1)} %reshape.293.fc_pieces, ...), custom_call_target="tpu_custom_call" | custom-call | bytes 41943040 | tf_op jit(solution)/shard_map/pallas_call | solution.py:686
  116.3 3.3 copy-done.1
  119.6 2.8 copy-done.2
  130.7 24.7 %shard_map.264 = (bf16[2048,2048]{1,0:T(8,128)(2,1)}, bf16[2048,512]{1,0:T(8,128)(2,1)}, bf16[2048,512]{1,0:T(8,128)(2,1)}, bf16[2048,512]{1,0:T(8,128)(2,1)}, b...) custom-call(bf16[2048,2048]{1,0:T(8,128)(2,1)} %copy-done.1, f32[1,2048]{1,0:T(1,128)} %reshape.296.refs_1_.gain, ...), custom_call_target="tpu_custom_call" | custom-call | flops 12884901888 | bytes 33554432 | tf_op jit(solution)/shard_map/pallas_call | solution.py:63
  155.4 14.7 %collective-permute-done.1.cot_two = bf16[512,2048]{1,0:T(8,128)(2,1)S(1)} collective-permute-done((bf16[512,2048]{1,0:T(8,128)(2,1)}, bf16[512,2048]{1,0:T(8,128)(2,1)S(1)}, u32[]{:S(2)}, u32[]{:S(2)}) %collective-permute-start.1) | collective-permute-done | bytes 2097184 | tf_op jit(solution)/shard_map/ppermute | solution.py:1495
  171.4 98.7 %shard_map.265 = (f32[512,2048]{1,0:T(8,128)}, bf16[512,2048]{1,0:T(8,128)(2,1)}, bf16[2048,512]{1,0:T(8,128)(2,1)}, f32[4,1,2048]{2,1,0:T(1,128)}, bf16[512,2048]{1,0:T(8,128)(2,1)}) custom-call(bf16[2048,512]{1,0:T(8,128)(2,1)} %get-tuple-element.49.q, bf16[2048,512]{1,0:T(8,128)(2,1)} %get-tuple-element.50.k, bf16[512,2048]{1,0:T(8,128)(2,1)} %get-tuple-element.51.v_t, ...), custom_call_target="tpu_custom_call" | custom-call | flops 10737418240 | bytes 41943040 | tf_op jit(solution)/shard_map/pallas_call | solution.py:833
  270.2 16.8 %all-gather.6.cloned.1.call-done.fc = bf16[2048,2048]{1,0:T(8,128)(2,1)} async-done(((bf16[256,2048]{1,0:T(8,128)(2,1)}), bf16[2048,2048]{1,0:T(8,128)(2,1)}) %all-gather.6.cloned.1.call-update) | async-done | bytes 8388624 | tf_op jit(solution)/shard_map/all_gather | solution.py:1566
  287.0 230.1 %shard_map.266 = (f32[512,2048]{1,0:T(8,128)}, bf16[2048,2048]{1,0:T(8,128)(2,1)}, f32[4,2048]{1,0:T(4,128)}, f32[1,2048]{1,0:T(1,128)}, bf16[2048,2048]{1,0:T(8...) custom-call(bf16[512,2048]{1,0:T(8,128)(2,1)} %get-tuple-element.53., ...), custom_call_target="tpu_custom_call" | custom-call | flops 103079215104 | bytes 41943040 | tf_op jit(solution)/shard_map/pallas_call | solution.py:1219
  518.7 9.5 %convolution_convert_fusion.1 = bf16[512,2048]{1,0:T(8,128)(2,1)} fusion(bf16[2048,512]{1,0:T(8,128)(2,1)S(1)} %copy-done.25, bf16[2048,2048]{1,0:T(8,128)(2,1)} %get-tuple-element.58.low_all), kind=kOutput, calls=%fused_computation.1 | convolution fusion | flops 4296015872 | bytes 12582912 | tf_op jit(solution)/shard_map/dot_general | solution.py:32
  528.2 8.8 %reduce-scatter.6.cloned.1.call-start = ((), (), s32[]{:S(2)}) async-start(), calls=%async_computation.7 | async-start | bytes 7077888 | tf_op jit(solution)/shard_map/reduce_scatter | solution.py:1570
  537.0 74.5 %shard_map.267 = (bf16[2048,1536]{1,0:T(8,128)(2,1)}, f32[2,512]{1,0:T(2,128)}, bf16[512,2048]{1,0:T(8,128)(2,1)}) custom-call(bf16[2048,2048]{1,0:T(8,128)(2,1)} %get-tuple-element.58.low_all, bf16[2048,512]{1,0:T(8,128)(2,1)} %get-tuple-element.49.q, bf16[2048,512]{1,0:T(8,128)(2,1)} %get-tuple-element.50.k, bf16[2048,512]{1,0:T(8,128)(2,1)} %get-tuple-element.59.v, ...), custom_call_target="tpu_custom_call" | custom-call | flops 21474836480 | bytes 41943040 | tf_op jit(solution)/shard_map/pallas_call | solution.py:1373
  611.5 19.2 %convolution_convert_fusion = bf16[2048,1536]{1,0:T(8,128)(2,1)} fusion(bf16[2048,2048]{1,0:T(8,128)(2,1)} %get-tuple-element.72, bf16[2048,1536]{1,0:T(8,128)(2,1)} %get-tuple-element.64.grads), kind=kOutput, calls=%fused_computation | convolution fusion | flops 12888047616 | bytes 20971520 | tf_op jit(solution)/shard_map/dot_general | solution.py:32
  632.5 82.1 %shard_map.268 = (f32[512,2048]{1,0:T(8,128)}, f32[2,2048]{1,0:T(2,128)}) custom-call(bf16[2048,1536]{1,0:T(8,128)(2,1)} %get-tuple-element.64.grads, bf16[2048,1536]{1,0:T(8,128)(2,1)} %copy-done.2, bf16[512,2048]{1,0:T(8,128)(2,1)} %bitcast.101, f32[512,2048]{1,0:T(8,128)} %get-tuple-element.65.grad_middle, f32[1,2048]{1,0:T(1,128)} %reshape.296.refs_1_.gain), custom_call_target="tpu_custom_call" | custom-call | flops 12884901888 | bytes 10485760 | tf_op jit(solution)/shard_map/pallas_call | solution.py:1472
  715.9 1.7 collective-permute-start.3
  722.7 3.4 collective-permute-start.6
  733.6 1.5 collective-permute-start.19
  736.5 1.8 collective-permute-done.19
  738.9 2.5 collective-permute-start.20
  743.4 2.2 collective-permute-start.23
  748.6 1.7 collective-permute-start.16
  750.3 2.3 collective-permute-start.29
  754.4 2.0 dynamic-slice_bitcast_fusion.4
  756.4 2.3 collective-permute-start.15
  759.6 4.8 collective-permute-done.29.refs_3_
  765.8 2.4 collective-permute-done.28.refs_2_
  769.5 2.8 shard_map.270
  772.3 2.1 collective-permute-done.15.refs_3_
  776.9 2.6 shard_map.269
  780.8 2.1 copy.81
  (181 shorter events, 48.3 us)
Async XLA Ops:
  7.2 163.1 %all-gather.4.cloned.1.call-start = ((), (), s32[]{:S(2)}) async-start(), calls=%async_computation.3 | async-start | bytes 2359296 | tf_op jit(solution)/shard_map/all_gather | solution.py:1566
  9.7 260.4 %all-gather.8.cloned.1.call-start = ((), (), s32[]{:S(2)}) async-start(), calls=%async_computation.5 | async-start | bytes 9437184 | tf_op jit(solution)/shard_map/all_gather | solution.py:1566
  122.4 164.6 %all-gather.6.cloned.1.call-start = ((), (), s32[]{:S(2)}) async-start(), calls=%async_computation.4 | async-start | bytes 9437184 | tf_op jit(solution)/shard_map/all_gather | solution.py:1566
  123.1 488.3 %reduce-scatter.4.cloned.1.call-start = ((), (), s32[]{:S(2)}) async-start(), calls=%async_computation.6 | async-start | bytes 9437184 | tf_op jit(solution)/shard_map/reduce_scatter | solution.py:1570
  123.2 46.9 %collective-permute-start.1 = (bf16[512,2048]{1,0:T(8,128)(2,1)}, bf16[512,2048]{1,0:T(8,128)(2,1)S(1)}, u32[]{:S(2)}, u32[]{:S(2)}) collective-permute-start(bf16[512,2048]{1,0:T(8,128)(2,1)} %bitcast.134), channel_id=1, source_target_pairs={{0,2},{1,3},{2,0},{3,1},{4,6},{5,7},{6,4},{7,5},{8,10},{9,11},{10,... | collective-permute-start | bytes 6291464 | tf_op jit(solution)/shard_map/ppermute | solution.py:1495
  124.1 46.2 %collective-permute-start = (bf16[512,2048]{1,0:T(8,128)(2,1)}, bf16[512,2048]{1,0:T(8,128)(2,1)}, u32[]{:S(2)}, u32[]{:S(2)}) collective-permute-start(bf16[512,2048]{1,0:T(8,128)(2,1)} %bitcast.135), channel_id=1, source_target_pairs={{0,1},{1,0},{2,3},{3,2},{4,5},{5,4},{6,7},{7,6},{8,9},{9,8},{10,11... | collective-permute-start | bytes 6291464 | tf_op jit(solution)/shard_map/ppermute | solution.py:1495
  517.1 231.4 %reduce-scatter.8.cloned.1.call-start = ((), (), s32[]{:S(2)}) async-start(), calls=%async_computation.8 | async-start | bytes 2359296 | tf_op jit(solution)/shard_map/reduce_scatter | solution.py:1570
  528.2 226.2 %reduce-scatter.6.cloned.1.call-start = ((), (), s32[]{:S(2)}) async-start(), calls=%async_computation.7 | async-start | bytes 7077888 | tf_op jit(solution)/shard_map/reduce_scatter | solution.py:1570
  715.9 4.2 collective-permute-start.3
  718.0 4.5 collective-permute-start.5
  722.6 6.4 collective-permute-start.12
  722.7 7.7 collective-permute-start.6
  726.2 5.4 collective-permute-start.11
  726.7 6.0 collective-permute-start.10
  727.7 5.9 collective-permute-start.9
  729.0 6.1 collective-permute-start.8
  730.3 4.8 collective-permute-start.7
  733.6 4.6 collective-permute-start.19
  738.3 7.4 collective-permute-start.26
  738.9 7.7 collective-permute-start.20
  742.5 6.1 collective-permute-start.25
  743.4 6.9 collective-permute-start.24
  743.4 9.3 %collective-permute-start.23 = (f32[512]{0:T(512)S(1)}, f32[512]{0:T(512)S(1)}, u32[]{:S(2)}, u32[]{:S(2)}) collective-permute-start(f32[512]{0:T(512)S(1)} %bitcast.122), channel_id=1, source_target_pairs={{0,16},{4,20},{8,24},{12,28},{16,0},{20,4},{24,8},{28,12},{1,17},{... | collective-permute-start | bytes 6152 | tf_op jit(solution)/shard_map/ppermute | solution.py:1495
  745.6 7.0 collective-permute-start.22
  746.6 6.0 collective-permute-start.21
  748.6 10.2 %collective-permute-start.16 = (bf16[64,2048]{1,0:T(8,128)(2,1)}, bf16[64,2048]{1,0:T(8,128)(2,1)S(1)}, u32[]{:S(2)}, u32[]{:S(2)}) collective-permute-start(bf16[64,2048]{1,0:T(8,128)(2,1)} %reduce-scatter.8.cloned.1.call-done), channel_id=1, source_target_pairs={{0,0},{4,1},{2,2},{6,3},{1,4},{5,5},{3,6},{7,7},{8,8},{12,9},{10,1... | collective-permute-start | bytes 786440 | tf_op jit(solution)/shard_map/ppermute | solution.py:1727
  750.3 14.1 %collective-permute-start.29 = (bf16[64,2048]{1,0:T(8,128)(2,1)S(1)}, bf16[64,2048]{1,0:T(8,128)(2,1)S(1)}, u32[]{:S(2)}, u32[]{:S(2)}) collective-permute-start(bf16[64,2048]{1,0:T(8,128)(2,1)S(1)} %get-tuple-element.82), channel_id=1, source_target_pairs={{0,3},{1,2},{2,1},{3,0},{4,7},{5,6},{6,5},{7,4},{8,11},{9,10},{10,... | collective-permute-start | bytes 786440 | tf_op jit(solution)/shard_map/ppermute | solution.py:1495
  753.2 15.0 %collective-permute-start.28 = (bf16[64,2048]{1,0:T(8,128)(2,1)S(1)}, bf16[64,2048]{1,0:T(8,128)(2,1)}, u32[]{:S(2)}, u32[]{:S(2)}) collective-permute-start(bf16[64,2048]{1,0:T(8,128)(2,1)S(1)} %get-tuple-element.83), channel_id=1, source_target_pairs={{0,2},{1,3},{2,0},{3,1},{4,6},{5,7},{6,4},{7,5},{8,10},{9,11},{10,... | collective-permute-start | bytes 786440 | tf_op jit(solution)/shard_map/ppermute | solution.py:1495
  754.1 15.4 %collective-permute-start.27 = (bf16[64,2048]{1,0:T(8,128)(2,1)S(1)}, bf16[64,2048]{1,0:T(8,128)(2,1)}, u32[]{:S(2)}, u32[]{:S(2)}) collective-permute-start(bf16[64,2048]{1,0:T(8,128)(2,1)S(1)} %get-tuple-element.84), channel_id=1, source_target_pairs={{0,1},{1,0},{2,3},{3,2},{4,5},{5,4},{6,7},{7,6},{8,9},{9,8},{10,11... | collective-permute-start | bytes 786440 | tf_op jit(solution)/shard_map/ppermute | solution.py:1495
  756.4 18.0 %collective-permute-start.15 = (bf16[64,1536]{1,0:T(8,128)(2,1)}, bf16[64,1536]{1,0:T(8,128)(2,1)}, u32[]{:S(2)}, u32[]{:S(2)}) collective-permute-start(bf16[64,1536]{1,0:T(8,128)(2,1)} %get-tuple-element.86), channel_id=1, source_target_pairs={{0,3},{1,2},{2,1},{3,0},{4,7},{5,6},{6,5},{7,4},{8,11},{9,10},{10,... | collective-permute-start | bytes 589832 | tf_op jit(solution)/shard_map/ppermute | solution.py:1495
  758.8 16.2 %collective-permute-start.14 = (bf16[64,1536]{1,0:T(8,128)(2,1)S(1)}, bf16[64,1536]{1,0:T(8,128)(2,1)}, u32[]{:S(2)}, u32[]{:S(2)}) collective-permute-start(bf16[64,1536]{1,0:T(8,128)(2,1)S(1)} %get-tuple-element.87), channel_id=1, source_target_pairs={{0,2},{1,3},{2,0},{3,1},{4,6},{5,7},{6,4},{7,5},{8,10},{9,11},{10,... | collective-permute-start | bytes 589832 | tf_op jit(solution)/shard_map/ppermute | solution.py:1495
  764.4 11.9 %collective-permute-start.13 = (bf16[64,1536]{1,0:T(8,128)(2,1)S(1)}, bf16[64,1536]{1,0:T(8,128)(2,1)S(1)}, u32[]{:S(2)}, u32[]{:S(2)}) collective-permute-start(bf16[64,1536]{1,0:T(8,128)(2,1)S(1)} %get-tuple-element.88), channel_id=1, source_target_pairs={{0,1},{1,0},{2,3},{3,2},{4,5},{5,4},{6,7},{7,6},{8,9},{9,8},{10,11... | collective-permute-start | bytes 589832 | tf_op jit(solution)/shard_map/ppermute | solution.py:1495
  (30 other events, 333.1 us)
Sparse Core Ops, SparseCore 0:
  10.2 40.5 all-gather.3
  122.5 82.1 all-gather.7
  206.4 80.5 all-gather.5
  517.3 88.1 reduce-scatter.3
  607.6 34.1 reduce-scatter.7
  644.0 68.4 reduce-scatter.5

commit v6 on v5

--- a/solution.py
+++ b/solution.py
@@ -1398,15 +1398,26 @@
 
 
 def closing_kernel(
-    grads, weight, tokens, grad_middle, gain, tokens_grad, sums,
-    terms, passed, joined, arrived, send, receive,
+    grads, weight, normed_one, tokens, grad_middle, gain, sums_two, hidden_sums, qv_sums, fc_share,
+    tokens_grad, qkv_out, fc_out, small_out, grad_qkv, mate_in, summed, got, qkv_share,
+    terms, passed, joined, arrived, qkv_in, fc_in, mine, small_in, small_rows, small_got,
+    send, receive, level_send, level_receive, small_send, small_receive, load,
 ):
     piece, width = tokens.shape
     half = piece // 2
+    columns = grads.shape[1]
+    heads = columns // (3 * HEAD_DIM)
+    me, place = lax.axis_index("seq"), lax.axis_index("dp")
     one, two = neighbours()
-    for device in (one, two):
+    three = 3 - me
+    plane = (one, two, three)
+    others = [lax.rem(place + i, 8) for i in range(1, 8)]
+    for device in plane:
         greet("seq", device)
-    pl.semaphore_wait(pltpu.get_barrier_semaphore(), 2)
+    for device in others:
+        greet("dp", device)
+    pl.semaphore_wait(pltpu.get_barrier_semaphore(), 10)
+    scatter = LevelScatter(grad_qkv, mate_in, summed, got, level_send, level_receive)
     up, lower = pl.ds(0, half), pl.ds(half, half)
 
     def copy(index, source, target, device):
@@ -1417,31 +1428,59 @@
     plain_two = copy(3, terms.at[2, lower], arrived.at[1, lower], two)
     joined_one = copy(4, joined.at[0], arrived.at[0, lower], one)
     joined_two = copy(5, joined.at[1], arrived.at[1, up], two)
-
-    @pl.loop(0, 4)
-    def _(step):
-        at = 3 - step
-        terms[at] = nt(grads[pl.ds(pl.multiple_of(at * piece, piece), piece), :], weight[...]).astype(BF16)
-
-        @pl.when(step == 0)
-        def _():
-            for item in across:
-                item.start()
-
-        @pl.when(step == 1)
-        def _():
-            plain_two.start()
-
-        @pl.when(step == 2)
-        def _():
-            plain_one.start()
-
+    fine = qkv_in.shape[1]
+    rows_for = lambda ref, device: ref.at[pl.ds(device * fine, fine)]
+    fc_copies = [copy(6 + i, rows_for(fc_share, device), fc_in.at[i], device) for i, device in enumerate(plane)]
+    qkv_copies = [copy(9 + i, rows_for(qkv_share, device), qkv_in.at[i], device) for i, device in enumerate(plane)]
+    small_copies = [copy(12 + i, mine, small_in.at[i], device) for i, device in enumerate(plane)]
+    fc_own = pltpu.make_async_copy(rows_for(fc_share, me), fc_in.at[3], load.at[0])
+    qkv_own = pltpu.make_async_copy(rows_for(qkv_share, me), qkv_in.at[3], load.at[1])
+    row_copies = [
+        remote(small_rows.at[device], small_got.at[i], small_send.at[i], small_receive.at[i], "dp", device)
+        for i, device in enumerate(others)
+    ]
+
+    def back_term(at):
+        terms[at] = nt(grads[at * piece : (at + 1) * piece, :], weight[...]).astype(BF16)
+
+    back_term(3)
+    for item in across:
+        item.start()
+    tile = min(512, width)
+
+    def outer_body(left, out):
+        out[...] = tn(left[...], grads[...]).astype(BF16)
+
+    pltpu.emit_pipeline(
+        outer_body,
+        grid=(width // tile,),
+        in_specs=[pl.BlockSpec((normed_one.shape[0], tile), lambda i: (0, i))],
+        out_specs=[pl.BlockSpec((tile, columns), lambda i: (i, 0))],
+    )(normed_one, grad_qkv)
+    scatter.start()
+    fc_own.start()
+    back_term(2)
+    plain_two.start()
+    back_term(1)
+    plain_one.start()
     for item in across:
         item.wait_recv()
     joined[0] = (terms[1, half:].astype(F32) + passed[1].astype(F32)).astype(BF16)
     joined[1] = (terms[2, :half].astype(F32) + passed[0].astype(F32)).astype(BF16)
     joined_one.start()
     joined_two.start()
+    scatter.spread()
+    back_term(0)
+    for item in fc_copies:
+        item.start()
+    mine[...] = jnp.zeros_like(mine)
+    mine[2:6, :] = sums_two[...]
+    for head in range(heads):
+        at = (head * 2 + lax.rem(me, 2)) * 2 + lax.div(me, 2)
+        here = pl.ds(pl.multiple_of(at * HEAD_DIM, HEAD_DIM), HEAD_DIM)
+        for part in range(2):
+            mine[6 + part : 7 + part, here] = qv_sums[part : part + 1, head * HEAD_DIM : (head + 1) * HEAD_DIM]
+    scatter.pass_on()
     for item in (plain_one, plain_two, joined_one, joined_two):
         item.wait_recv()
     part = min(128, piece)
@@ -1453,37 +1492,95 @@
         unit, scale = norm_parts(token_tile[...].astype(F32))
         out[...] = middle_tile[...] + norm_backward(unit, scale, gain[...], upstream)
         for at, item in enumerate((upstream * unit, upstream)):
-            sum_rows(sums, at, slice(None), item, i == 0)
+            sum_rows(mine, at, slice(None), item, i == 0)
 
     line = pl.BlockSpec((part, width), lambda i: (i, 0))
     pltpu.emit_pipeline(norm_body, grid=(piece // part,), in_specs=[line] * 2, out_specs=[line])(
         tokens, grad_middle, tokens_grad
     )
-    for item in (*across, plain_one, plain_two, joined_one, joined_two):
+    for item in small_copies:
+        item.start()
+    scatter.finish(qkv_share)
+    for item in qkv_copies:
+        item.start()
+    qkv_own.start()
+    for item in small_copies:
+        item.wait_recv()
+    mine_total = mine[...] + small_in[0] + small_in[1] + small_in[2]
+    small_rows[...] = jnp.zeros_like(small_rows)
+    share, wide = width // 8, 2 * width // 8
+    for d in range(8):
+        small_rows[d, 0:6, 0:share] = mine_total[0:6, d * share : (d + 1) * share]
+        row, at = 6 + d // 4, (d % 4) * wide
+        small_rows[d, 6:7, :] = mine_total[row : row + 1, at : at + wide]
+        inner = hidden_sums.shape[1] // 8
+        small_rows[d, 7:8, 0:inner] = hidden_sums[:, d * inner : (d + 1) * inner]
+    for item in row_copies:
+        item.start()
+    sources = (*plane, me)
+    fc_own.wait()
+    for item in fc_copies:
+        item.wait_recv()
+    block = fc_in.shape[2] // 8
+    for i, source in enumerate(sources):
+        for d in range(8):
+            target = pl.ds(pl.multiple_of((d * 4 + source) * block, block), block)
+            fc_out[:, target] = fc_in[i, :, d * block : (d + 1) * block].astype(F32)
+    qkv_own.wait()
+    for item in qkv_copies:
+        item.wait_recv()
+    for i, source in enumerate(sources):
+        for part in range(3):
+            for head in range(heads):
+                at = part * HEADS + (head * 2 + lax.rem(source, 2)) * 2 + lax.div(source, 2)
+                target = pl.ds(pl.multiple_of(at * HEAD_DIM, HEAD_DIM), HEAD_DIM)
+                start = (part * heads + head) * HEAD_DIM
+                qkv_out[:, target] = qkv_in[i, :, start : start + HEAD_DIM].astype(F32)
+    for item in row_copies:
+        item.wait_recv()
+    total = small_rows[place]
+    for i in range(7):
+        total = total + small_got[i]
+    small_out[...] = total
+    for item in (*across, plain_one, plain_two, joined_one, joined_two, *fc_copies, *qkv_copies, *small_copies, *row_copies):
         item.wait_send()
-
-
-def closing(grads, weight, tokens, grad_middle, gain):
+    scatter.close()
+
+
+def closing(grads, weight, normed_one, tokens, grad_middle, gain, sums_two, hidden_sums, qv_sums, fc_share):
     piece, width = tokens.shape
-    half = piece // 2
+    columns, half = grads.shape[1], piece // 2
+    fine = fc_share.shape[0] // 4
+    wide = 2 * width // 8
     anywhere = pl.BlockSpec(memory_space=pl.ANY)
     inside = pl.BlockSpec(memory_space=pltpu.VMEM)
+    shape = lambda rows, columns, kind=BF16: jax.ShapeDtypeStruct((rows, columns), kind)
     dma = pltpu.SemaphoreType.DMA
     return pl.pallas_call(
         closing_kernel,
-        in_specs=[inside, inside, anywhere, anywhere, inside],
-        out_specs=[anywhere, inside],
-        out_shape=[jax.ShapeDtypeStruct((piece, width), F32), jax.ShapeDtypeStruct((2, width), F32)],
+        in_specs=[inside, inside, anywhere, anywhere, anywhere, inside, inside, inside, inside, anywhere],
+        out_specs=[anywhere, inside, inside, inside] + [anywhere] * 5,
+        out_shape=[
+            shape(piece, width, F32), shape(fine, 4 * columns, F32), shape(fine, 4 * fc_share.shape[1], F32),
+            shape(8, wide, F32), shape(width, columns), shape(width // 2, columns), shape(width // 2, columns),
+            shape(width // 2, columns), shape(width // 8, columns),
+        ],
         scratch_shapes=[
             pltpu.VMEM((4, piece, width), BF16),
             pltpu.VMEM((2, half, width), BF16),
             pltpu.VMEM((2, half, width), BF16),
             pltpu.VMEM((2, piece, width), BF16),
-            dma((6,)), dma((6,)),
+            pltpu.VMEM((4, fine, columns), BF16),
+            pltpu.VMEM((4, fine, fc_share.shape[1]), BF16),
+            pltpu.VMEM((8, width), F32),
+            pltpu.VMEM((3, 8, width), F32),
+            pltpu.VMEM((8, 8, wide), F32),
+            pltpu.VMEM((7, 8, wide), F32),
+            dma((15,)), dma((15,)), dma((8,)), dma((8,)), dma((7,)), dma((7,)), dma((2,)),
         ],
         compiler_params=pltpu.CompilerParams(collective_id=4, has_side_effects=True, vmem_limit_bytes=60 * 2**20),
-        cost_estimate=cost(8 * piece * width * grads.shape[1], 10 * piece * width),
-    )(grads, weight, tokens, grad_middle, gain)
+        cost_estimate=cost(16 * piece * width * columns, 10 * piece * width),
+    )(grads, weight, normed_one, tokens, grad_middle, gain, sums_two, hidden_sums, qv_sums, fc_share)
 
 
 def after(value, *others):
@@ -1687,7 +1784,6 @@
         grad_middle, low_all, sums_two, hidden_sums, down_terms, grad_fc, grad_down = [
             results[i] for i in (0, 1, 2, 3, 8, 10, 14)
         ]
-        sums_two = [sums_two[i] for i in range(4)]
         grad_fc = scatter_dp(grad_fc)
         grads, qv_sums, block_out = retreat_plane(
             low_all, q, keys, values, keys_t, lse, down_terms, middle, key_bias, proj_full, down_shift
@@ -1720,14 +1816,16 @@
         grads = jnp.concatenate([grad_q, sums[0], sums[1]], axis=1)
         qv_sums = jnp.stack([jnp.sum(item.astype(F32), axis=0) for item in (grad_q, sums[1])])
     grad_proj = tn(attended, low_all).astype(BF16)
+    grad_proj = scatter_dp(after(grad_proj, grad_fc) if in_plane else grad_proj)
+    grad_proj = lax.ppermute(grad_proj, BOTH, swap).astype(F32)
+    share = attn_gain.shape[0]
     if in_plane:
-        normed_one = after(normed_one, grad_fc, grad_proj)
-    grad_qkv = scatter_dp(tn(normed_one, grads).astype(BF16))
-    grad_proj = scatter_dp(grad_proj)
-    grad_proj = lax.ppermute(grad_proj, BOTH, swap).astype(F32)
-    if in_plane:
-        tokens_grad, sums_one = closing(grads, qkv_full, tokens_own, grad_middle, gain_one)
-        sums_one = [sums_one[i] for i in range(2)]
+        tokens_grad, grad_qkv_weight, grad_fc, smalls = closing(
+            grads, qkv_full, normed_one, tokens_own, grad_middle, gain_one, sums_two, hidden_sums, qv_sums, grad_fc
+        )[:4]
+        own = lambda row, size: lax.dynamic_slice_in_dim(smalls[row], seq_rank * size, size)
+        late = jnp.concatenate([own(0, share), own(1, share), own(6, 2 * share)])
+        early = jnp.concatenate([own(row, share) for row in range(2, 6)] + [smalls[7, :block]])
     else:
         back_terms = [None] * seq_count
         for k in order:
@@ -1736,33 +1834,33 @@
             tokens_back_kernel, scatter_blocks(back_terms), [tokens_own, grad_middle], [gain_one], [F32], 2
         )
 
-    blocks = exchange(grad_fc.reshape(seq_count, rows, dp_count * block), seq_rank)
-    if block % 128 == 0:
-        fc_places = lambda s: [(0, d, d * seq_count + s) for d in range(dp_count)]
-        grad_fc = lay_out(rank, [[item] for item in blocks], fc_weight.shape[1], (fc_places, block))
-    else:
-        blocks = [item.reshape(rows, dp_count, block) for item in by_rank(blocks, seq_rank)]
-        grad_fc = jnp.stack(blocks, axis=2).reshape(fc_weight.shape).astype(F32)
-    blocks = [[item] for item in exchange(grad_qkv.reshape(seq_count, rows, 3 * own_width), seq_rank)]
-    qkv_places = lambda s: [
-        (0, part * own_heads + head, part * HEADS + (head * sub + s % sub) * high + s // sub)
-        for part in range(3)
-        for head in range(own_heads)
-    ]
-    grad_qkv_weight = lay_out(rank, blocks, qkv_weight.shape[1], (qkv_places, HEAD_DIM))
-
-    def spread(vector):
-        return vector.reshape(dp_count, seq_count, -1)
-
-    here = (jnp.arange(seq_count) == seq_rank).astype(F32)
-    hidden_sums = hidden_sums.reshape(dp_count, 1, -1) * here[None, :, None]
-    early = jnp.concatenate([spread(item) for item in sums_two] + [hidden_sums], axis=2)
-    early = small_scatter(early, dp_rank, seq_rank)
-    here = (jnp.arange(sub) == rank_low)[:, None] & (jnp.arange(high) == rank_high)[None, :]
-    qv_sums = qv_sums.reshape(2, own_heads, 1, 1, HEAD_DIM) * here.astype(F32)[None, None, :, :, None]
-    late = jnp.concatenate([spread(item) for item in sums_one] + [spread(qv_sums)], axis=2)
-    late = small_scatter(late, dp_rank, seq_rank)
-    share = attn_gain.shape[0]
+        blocks = exchange(grad_fc.reshape(seq_count, rows, dp_count * block), seq_rank)
+        if block % 128 == 0:
+            fc_places = lambda s: [(0, d, d * seq_count + s) for d in range(dp_count)]
+            grad_fc = lay_out(rank, [[item] for item in blocks], fc_weight.shape[1], (fc_places, block))
+        else:
+            blocks = [item.reshape(rows, dp_count, block) for item in by_rank(blocks, seq_rank)]
+            grad_fc = jnp.stack(blocks, axis=2).reshape(fc_weight.shape).astype(F32)
+        grad_qkv = scatter_dp(tn(normed_one, grads).astype(BF16))
+        blocks = [[item] for item in exchange(grad_qkv.reshape(seq_count, rows, 3 * own_width), seq_rank)]
+        qkv_places = lambda s: [
+            (0, part * own_heads + head, part * HEADS + (head * sub + s % sub) * high + s // sub)
+            for part in range(3)
+            for head in range(own_heads)
+        ]
+        grad_qkv_weight = lay_out(rank, blocks, qkv_weight.shape[1], (qkv_places, HEAD_DIM))
+
+        def spread(vector):
+            return vector.reshape(dp_count, seq_count, -1)
+
+        here = (jnp.arange(seq_count) == seq_rank).astype(F32)
+        hidden_sums = hidden_sums.reshape(dp_count, 1, -1) * here[None, :, None]
+        early = jnp.concatenate([spread(item) for item in sums_two] + [hidden_sums], axis=2)
+        early = small_scatter(early, dp_rank, seq_rank)
+        here = (jnp.arange(sub) == rank_low)[:, None] & (jnp.arange(high) == rank_high)[None, :]
+        qv_sums = qv_sums.reshape(2, own_heads, 1, 1, HEAD_DIM) * here.astype(F32)[None, None, :, :, None]
+        late = jnp.concatenate([spread(item) for item in sums_one] + [spread(qv_sums)], axis=2)
+        late = small_scatter(late, dp_rank, seq_rank)
     return (
         block_out[None],
         tokens_grad[None],

time: 800 us -> 831 us (1.039)
  waiting for transfers between devices: 51.1 us -> 113 us
  starting transfers between devices: 45.2 us -> 6.23 us
  Pallas kernels: 615 us -> 644 us
  matrix products: 28.6 us -> 9.13 us
    reduce_scatter x3 -> x2, waiting for transfers between devices: 0.02 us -> 80.5 us  [scatter_dp(): return lax.psum_scatter(value, 'dp', scatter_dimension=0, tiled=True)]
    ppermute x28 -> x2, starting transfers between devices: 32.8 us -> 2.18 us  [shift(): return lax.ppermute(value, axis, [(i, i ^ distance) for i in range(count)])]
    pallas_call x1, Pallas kernels: 82.1 us -> 112 us  [closing(): pl.pallas_call(closing_kernel, in_specs=[inside, inside, anywhere, anywhe...]
    dot_general x2 -> x1, matrix products: 28.6 us -> 9.13 us  [tn(): lax.dot_general(left, right, (((0,), (0,)), ((), ())), preferred_element_...]
    ppermute x28 -> x2, waiting for transfers between devices: 33.5 us -> 15 us  [shift(): return lax.ppermute(value, axis, [(i, i ^ distance) for i in range(count)])]
    reduce_scatter x3 -> x2, starting transfers between devices: 8.85 us -> 0.08 us  [scatter_dp(): return lax.psum_scatter(value, 'dp', scatter_dimension=0, tiled=True)]
    unnamed x61 -> x49, local copies, waits for them, and re-layouts: 17.2 us -> 18 us
  transfers between devices with their start and end apart: 36 -> 9, of which waited for: 15 -> 4; matrix products, arithmetic and copies ran while one was open for 6% -> 3% of each run, Pallas kernels for 48% -> 50%
where the time goes in v6:
time: 831 us; the launch traced here: 822 us
  Pallas kernels  644 us (77%)
  waiting for transfers between devices  113 us (14%)
  local copies, waits for them, and re-layouts  31.5 us (4%)
  between operations  15 us (2%)
  matrix products  9.13 us (1%)
    pallas_call x1, Pallas kernels, feed_plane(): pl.pallas_call(plane_kernel, in_specs=[anywhere] * 6 + [inside, anywhere,...  234 us
    pallas_call x1, Pallas kernels, closing(): pl.pallas_call(closing_kernel, in_specs=[inside, inside, anywhere, anywhe...  112 us
    pallas_call x1, Pallas kernels, opening(): pl.pallas_call(opening_kernel, in_specs=[inside] * 4, out_specs=[anywhere...  99.3 us
    pallas_call x1, Pallas kernels, attend_plane(): pl.pallas_call(attend_plane_kernel, in_specs=[anywhere] * 6 + [inside] *...  98.7 us
    reduce_scatter x2, waiting for transfers between devices, scatter_dp(): return lax.psum_scatter(value, 'dp', scatter_dimension=0, tiled=True)  80.5 us
    pallas_call x1, Pallas kernels, retreat_plane(): pl.pallas_call(retreat_plane_kernel, in_specs=[anywhere] * 8 + [inside] *...  76.4 us
    pallas_call x1, Pallas kernels, call_on_block(): pl.pallas_call(body, grid=grid, in_specs=specs, out_specs=out_specs, out_...  24.7 us
    unnamed x49, local copies, waits for them, and re-layouts  18 us
  transfers between devices with their start and end apart: 9, of which 4 were waited for; matrix products, arithmetic and copies ran while one was open for 3% of the time, Pallas kernels for 50%

profile of v6, /device:TPU:0, one launch (start us, length us, event | category | flops | bytes accessed | tf_op | source)
XLA Modules:
  0.0 822.0 jit_solution(266838640711669622)
XLA Ops:
  7.2 1.7 collective-permute-start.2
  9.0 0.7 copy-done.9
  10.4 2.6 reshape.233
  13.7 0.8 reshape.235
  15.5 1.6 copy-done
  17.0 99.3 %shard_map.263 = (bf16[2048,2048]{1,0:T(8,128)(2,1)S(1)}, bf16[2048,1536]{1,0:T(8,128)(2,1)S(1)}, bf16[256,2048]{1,0:T(8,128)(2,1)}, bf16[512,128]{1,0:T(8,128)(2,1)S(1)}) custom-call(bf16[512,2048]{1,0:T(8,128)(2,1)S(1)} %bitcast.50, bf16[4,64,1536]{2,1,0:T(8,128)(2,1)S(1)} %reshape.234.qkv_pieces, bf16[4,64,2048]{2,1,0:T(8,128)(2,1)S(1)} %reshape.236.fc_pieces, ...), custom_call_target="tpu_custom_call" | custom-call | bytes 41943040 | tf_op jit(solution)/shard_map/pallas_call | solution.py:686
  116.3 3.2 copy-done.1
  119.6 2.8 copy-done.2
  123.1 0.9 collective-permute-start.1
  124.1 1.2 collective-permute-start
  129.6 1.1 broadcast_select_fusion.key_bias
  130.7 24.7 %shard_map.264 = (bf16[2048,2048]{1,0:T(8,128)(2,1)}, bf16[2048,512]{1,0:T(8,128)(2,1)}, bf16[2048,512]{1,0:T(8,128)(2,1)}, bf16[2048,512]{1,0:T(8,128)(2,1)}, b...) custom-call(bf16[2048,2048]{1,0:T(8,128)(2,1)} %copy-done.1, f32[1,2048]{1,0:T(1,128)} %reshape.239.refs_1_.gain, ...), custom_call_target="tpu_custom_call" | custom-call | flops 12884901888 | bytes 33554432 | tf_op jit(solution)/shard_map/pallas_call | solution.py:63
  155.3 14.7 %collective-permute-done.1.cot_two = bf16[512,2048]{1,0:T(8,128)(2,1)S(1)} collective-permute-done((bf16[512,2048]{1,0:T(8,128)(2,1)}, bf16[512,2048]{1,0:T(8,128)(2,1)S(1)}, u32[]{:S(2)}, u32[]{:S(2)}) %collective-permute-start.1) | collective-permute-done | bytes 2097184 | tf_op jit(solution)/shard_map/ppermute | solution.py:1592
  170.3 1.1 copy-done.20
  171.4 98.7 %shard_map.265 = (f32[512,2048]{1,0:T(8,128)}, bf16[512,2048]{1,0:T(8,128)(2,1)}, bf16[2048,512]{1,0:T(8,128)(2,1)}, f32[4,1,2048]{2,1,0:T(1,128)}, bf16[512,2048]{1,0:T(8,128)(2,1)}) custom-call(bf16[2048,512]{1,0:T(8,128)(2,1)} %get-tuple-element.51.q, bf16[2048,512]{1,0:T(8,128)(2,1)} %get-tuple-element.52.k, bf16[512,2048]{1,0:T(8,128)(2,1)} %get-tuple-element.53.v_t, ...), custom_call_target="tpu_custom_call" | custom-call | flops 10737418240 | bytes 41943040 | tf_op jit(solution)/shard_map/pallas_call | solution.py:833
  270.1 16.8 %all-gather.6.cloned.1.call-done.fc = bf16[2048,2048]{1,0:T(8,128)(2,1)} async-done(((bf16[256,2048]{1,0:T(8,128)(2,1)}), bf16[2048,2048]{1,0:T(8,128)(2,1)}) %all-gather.6.cloned.1.call-update) | async-done | bytes 8388624 | tf_op jit(solution)/shard_map/all_gather | solution.py:1663
  287.0 233.8 %shard_map.266 = (f32[512,2048]{1,0:T(8,128)}, bf16[2048,2048]{1,0:T(8,128)(2,1)}, f32[4,2048]{1,0:T(4,128)}, f32[1,2048]{1,0:T(1,128)}, bf16[2048,2048]{1,0:T(8...) custom-call(bf16[512,2048]{1,0:T(8,128)(2,1)} %get-tuple-element.55., ...), custom_call_target="tpu_custom_call" | custom-call | flops 103079215104 | bytes 41943040 | tf_op jit(solution)/shard_map/pallas_call | solution.py:1219
  520.8 0.7 reshape.246.down_shift
  521.5 0.8 copy-done.21
  522.3 9.1 %convolution_convert_fusion = bf16[512,2048]{1,0:T(8,128)(2,1)} fusion(bf16[2048,512]{1,0:T(8,128)(2,1)S(1)} %copy-done.21, bf16[2048,2048]{1,0:T(8,128)(2,1)} %get-tuple-element.60.low_all), kind=kOutput, calls=%fused_computation | convolution fusion | flops 4296015872 | bytes 12582912 | tf_op jit(solution)/shard_map/dot_general | solution.py:32
  531.5 80.5 %reduce-scatter.3.cloned.1.call-done.fc_share = bf16[256,2048]{1,0:T(8,128)(2,1)} async-done(((bf16[2048,2048]{1,0:T(8,128)(2,1)}), bf16[256,2048]{1,0:T(8,128)(2,1)}) %reduce-scatter.3.cloned.1.call-update) | async-done | bytes 1048592 | tf_op jit(solution)/shard_map/reduce_scatter | solution.py:1667
  612.0 76.4 %shard_map.267 = (bf16[2048,1536]{1,0:T(8,128)(2,1)}, f32[2,512]{1,0:T(2,128)}, bf16[512,2048]{1,0:T(8,128)(2,1)}) custom-call(bf16[2048,2048]{1,0:T(8,128)(2,1)} %get-tuple-element.60.low_all, bf16[2048,512]{1,0:T(8,128)(2,1)} %get-tuple-element.51.q, bf16[2048,512]{1,0:T(8,128)(2,1)} %get-tuple-element.52.k, bf16[2048,512]{1,0:T(8,128)(2,1)} %get-tuple-element.61.v, ...), custom_call_target="tpu_custom_call" | custom-call | flops 21474836480 | bytes 41943040 | tf_op jit(solution)/shard_map/pallas_call | solution.py:1373
  688.4 111.6 %shard_map.268 = (f32[512,2048]{1,0:T(8,128)}, f32[64,6144]{1,0:T(8,128)}, f32[64,8192]{1,0:T(8,128)}, f32[8,512]{1,0:T(8,128)}, bf16[2048,1536]{1,0:T(8,128)(2,...) custom-call(bf16[2048,1536]{1,0:T(8,128)(2,1)} %get-tuple-element.66, ...), custom_call_target="tpu_custom_call" | custom-call | flops 25769803776 | bytes 10485760 | tf_op jit(solution)/shard_map/pallas_call | solution.py:1559
  800.0 1.0 fusion.14
  801.6 2.1 collective-permute-start.3
  804.2 1.3 slice.82
  806.6 0.8 convert_element_type.17
  807.5 1.3 copy.60
  808.8 2.1 copy.61
  811.3 1.1 copy.62
  812.5 1.3 copy.63
  813.9 1.3 copy.64
  (83 shorter events, 9.7 us)
Async XLA Ops:
  7.2 6.4 copy-start.8
  7.2 163.1 %all-gather.4.cloned.1.call-start = ((), (), s32[]{:S(2)}) async-start(), calls=%async_computation.2 | async-start | bytes 2359296 | tf_op jit(solution)/shard_map/all_gather | solution.py:1663
  7.2 1.7 collective-permute-start.2
  9.0 0.7 copy-start.9
  9.7 260.4 %all-gather.8.cloned.1.call-start = ((), (), s32[]{:S(2)}) async-start(), calls=%async_computation.4 | async-start | bytes 9437184 | tf_op jit(solution)/shard_map/all_gather | solution.py:1663
  13.6 1.6 copy-start.11
  13.6 1.6 copy-start.12
  13.7 1.6 copy-start.13
  13.7 1.6 copy-start.14
  13.7 1.6 copy-start.15
  13.7 1.6 copy-start.16
  13.7 1.6 copy-start.17
  13.7 1.6 copy-start.18
  13.7 1.6 copy-start.19
  15.5 1.6 copy-start
  116.3 3.2 copy-start.1
  119.6 2.8 copy-start.2
  122.4 164.6 %all-gather.6.cloned.1.call-start = ((), (), s32[]{:S(2)}) async-start(), calls=%async_computation.3 | async-start | bytes 9437184 | tf_op jit(solution)/shard_map/all_gather | solution.py:1663
  123.1 488.8 %reduce-scatter.3.cloned.1.call-start = ((), (), s32[]{:S(2)}) async-start(), calls=%async_computation.5 | async-start | bytes 9437184 | tf_op jit(solution)/shard_map/reduce_scatter | solution.py:1667
  123.1 46.9 %collective-permute-start.1 = (bf16[512,2048]{1,0:T(8,128)(2,1)}, bf16[512,2048]{1,0:T(8,128)(2,1)S(1)}, u32[]{:S(2)}, u32[]{:S(2)}) collective-permute-start(bf16[512,2048]{1,0:T(8,128)(2,1)} %bitcast.59), channel_id=1, source_target_pairs={{0,2},{1,3},{2,0},{3,1},{4,6},{5,7},{6,4},{7,5},{8,10},{9,11},{10,... | collective-permute-start | bytes 6291464 | tf_op jit(solution)/shard_map/ppermute | solution.py:1592
  124.1 46.2 %collective-permute-start = (bf16[512,2048]{1,0:T(8,128)(2,1)}, bf16[512,2048]{1,0:T(8,128)(2,1)}, u32[]{:S(2)}, u32[]{:S(2)}) collective-permute-start(bf16[512,2048]{1,0:T(8,128)(2,1)} %bitcast.60), channel_id=1, source_target_pairs={{0,1},{1,0},{2,3},{3,2},{4,5},{5,4},{6,7},{7,6},{8,9},{9,8},{10,11... | collective-permute-start | bytes 6291464 | tf_op jit(solution)/shard_map/ppermute | solution.py:1592
  125.7 29.7 %copy-start.10 = (f32[1,2048]{1,0:T(1,128)}, f32[1,2048]{1,0:T(1,128)S(1)}, u32[]{:S(2)}) copy-start(f32[1,2048]{1,0:T(1,128)S(1)} %reshape.243.gain) | copy-start | bytes 24580
  170.1 1.3 copy-start.20
  520.7 1.6 copy-start.21
  520.8 280.8 %reduce-scatter.5.cloned.1.call-start = ((), (), s32[]{:S(2)}) async-start(), calls=%async_computation.6 | async-start | bytes 2359296 | tf_op jit(solution)/shard_map/reduce_scatter | solution.py:1667
  688.4 119.1 %copy-start.5 = (bf16[512,2048]{1,0:T(8,128)(2,1)S(1)}, bf16[512,2048]{1,0:T(8,128)(2,1)}, u32[]{:S(2)}) copy-start(bf16[512,2048]{1,0:T(8,128)(2,1)} %get-tuple-element.65) | copy-start | bytes 6291460
  801.6 7.2 copy-start.3
  801.6 5.1 collective-permute-start.3
  808.8 2.5 copy-start.7
  808.8 3.7 copy-start.6
  811.3 2.6 copy-start.4
Sparse Core Ops, SparseCore 0:
  10.2 40.5 all-gather.3
  122.5 82.1 all-gather.7
  206.3 80.5 all-gather.5
  520.9 90.9 reduce-scatter.2
  614.1 33.9 reduce-scatter.4

commit v7 on v4

--- a/solution.py
+++ b/solution.py
@@ -40,7 +40,7 @@
     return pl.CostEstimate(flops=int(flops), bytes_accessed=int(moved), transcendentals=int(exps))
 
 
-def call_on_block(kernel, grid, inputs, fresh, shared, previous, scratch, estimate, rank=None):
+def call_on_block(kernel, grid, inputs, fresh, shared, previous, scratch, estimate, rank=None, limit_mib=62):
     arrays = [item for item, _ in inputs]
     specs = [spec for _, spec in inputs]
     aliases = {}
@@ -62,7 +62,7 @@
     if rank is None:
         results = pl.pallas_call(
             body, grid=grid, in_specs=specs, out_specs=out_specs, out_shape=out_shape, scratch_shapes=scratch,
-            input_output_aliases=aliases, compiler_params=params(), cost_estimate=estimate,
+            input_output_aliases=aliases, compiler_params=params(limit_mib), cost_estimate=estimate,
         )(*arrays)
     else:
         results = pl.pallas_call(
@@ -70,7 +70,7 @@
             grid_spec=pltpu.PrefetchScalarGridSpec(
                 num_scalar_prefetch=1, grid=grid, in_specs=specs, out_specs=out_specs, scratch_shapes=scratch
             ),
-            out_shape=out_shape, input_output_aliases=aliases, compiler_params=params(), cost_estimate=estimate,
+            out_shape=out_shape, input_output_aliases=aliases, compiler_params=params(limit_mib), cost_estimate=estimate,
         )(rank, *arrays)
     return results[: len(fresh)], results[len(fresh) :]
 
@@ -91,20 +91,20 @@
     )
 
 
-def project_kernel(x, gain, shift_, wq, wk, wv, bias, normed, q, k, v, k_t, v_t):
+def project_kernel(x, vectors, wq, wk, wv, normed, q, k, v, k_t, v_t):
     columns = wq.shape[1]
-    rows = (norm_parts(x[...].astype(F32))[0] * gain[...] + shift_[...]).astype(BF16)
+    rows = (norm_parts(x[...].astype(F32))[0] * vectors[0:1, :] + vectors[1:2, :]).astype(BF16)
     normed[...] = rows
-    q[...] = (nn(rows, wq[...]) + bias[:, :columns]).astype(BF16)
+    q[...] = (nn(rows, wq[...]) + vectors[7:8, :columns]).astype(BF16)
     keys = nn(rows, wk[...])
     k[...] = keys.astype(BF16)
     k_t[...] = keys.T.astype(BF16)
-    values = nn(rows, wv[...]) + bias[:, columns:]
+    values = nn(rows, wv[...]) + vectors[7:8, columns : 2 * columns]
     v[...] = values.astype(BF16)
     v_t[...] = values.T.astype(BF16)
 
 
-def project(at, x, first, rows_here, gain, shift_, weight, bias, count, previous):
+def project(at, x, first, rows_here, vectors, weight, count, previous):
     width, columns = x.shape[1], weight.shape[1] // 3
     tile = min(256, rows_here)
     steps = rows_here // tile
@@ -113,10 +113,8 @@
     turned = pl.BlockSpec((columns, tile), lambda i: (0, at * steps + i))
     inputs = [
         (x, pl.BlockSpec((tile, width), lambda i: (first * steps + i, 0))),
-        (gain, whole((1, width))),
-        (shift_, whole((1, width))),
+        (vectors, whole(vectors.shape)),
         *[(weight, pl.BlockSpec((width, columns), lambda i, part=part: (0, part))) for part in range(3)],
-        (bias, whole((1, 2 * columns))),
     ]
     shape = lambda *dims: jax.ShapeDtypeStruct(dims, BF16)
     shared = [(shape(count, width), rows(width))] + [(shape(count, columns), rows(columns))] * 3
@@ -517,12 +515,246 @@
     pl.semaphore_signal(pltpu.get_barrier_semaphore(), inc=1, device_id={axis: device}, device_id_type=MESH)
 
 
+def flip(first, second):
+    low = lax.rem(first + second, 2)
+    high = lax.rem(lax.div(first, 2) + lax.div(second, 2), 2)
+    return 2 * high + low
+
+
+class LevelScatter:
+    def __init__(self, source, mate_in, summed, got, send, receive):
+        self.source, self.mate_in, self.summed, self.got = source, mate_in, summed, got
+        self.send, self.receive = send, receive
+        self.rows = mate_in.shape[0] // 4
+        self.place = lax.axis_index("dp")
+        self.level, self.core = lax.div(self.place, 2), lax.rem(self.place, 2)
+        self.mate = self.place + 1 - 2 * self.core
+
+    def greet(self):
+        greet("dp", self.mate)
+        count = jnp.int32(1)
+        for step in (1, 2):
+            up, down = self.level + step <= 3, self.level >= step
+            pl.when(up)(lambda step=step: greet("dp", self.place + 2 * step))
+            pl.when(down)(lambda step=step: greet("dp", self.place - 2 * step))
+            count = count + up.astype(jnp.int32) + down.astype(jnp.int32)
+        return count
+
+    def block(self, ref, at):
+        return ref.at[pl.ds(at * self.rows, self.rows)]
+
+    def swaps(self):
+        return [
+            remote(
+                self.block(self.source, 2 * at + 1 - self.core), self.block(self.mate_in, at),
+                self.send.at[at], self.receive.at[at], "dp", self.mate,
+            )
+            for at in range(4)
+        ]
+
+    def start(self):
+        for item in self.swaps():
+            item.start()
+
+    def add(self, first, second, out, grid, first_at, second_at, out_at):
+        def body(left, right, total):
+            total[...] = (left[...].astype(F32) + right[...].astype(F32)).astype(total.dtype)
+
+        spec = lambda at: pl.BlockSpec((self.rows, first.shape[1]), lambda i: (at(i), 0))
+        pltpu.emit_pipeline(
+            body, grid=(grid,), in_specs=[spec(first_at), spec(second_at)], out_specs=[spec(out_at)]
+        )(first, second, out)
+
+    def hop(self, at, slot, index, steps):
+        return remote(
+            self.block(self.summed, at), self.block(self.got, slot), self.send.at[4 + index], self.receive.at[4 + slot],
+            "dp", self.place + 2 * steps,
+        )
+
+    def hops(self):
+        level = self.level
+        return [
+            (level == 0, self.hop(3, 3, 0, 1)),
+            (level == 3, self.hop(0, 3, 0, -1)),
+            (level == 0, self.hop(2, 2, 1, 2)),
+            (level == 3, self.hop(1, 2, 1, -2)),
+            (level <= 2, self.hop(lax.rem(level + 1, 4), 0, 2, 1)),
+            (level >= 1, self.hop(lax.rem(level + 3, 4), 1, 3, -1)),
+        ]
+
+    def passes(self):
+        return [(self.level == 1, self.hop(3, 2, 1, 2)), (self.level == 2, self.hop(0, 2, 1, -2))]
+
+    def spread(self):
+        for item in self.swaps():
+            item.wait_recv()
+        self.add(
+            self.source, self.mate_in, self.summed, 4, lambda i: 2 * i + self.core, lambda i: i, lambda i: i
+        )
+        for condition, copy in self.hops():
+            pl.when(condition)(lambda copy=copy: copy.start())
+
+    def arrive(self, slot):
+        here = self.block(self.got, slot)
+        remote(here, here, self.send.at[0], self.receive.at[4 + slot], "dp", self.mate).wait_recv()
+
+    def pass_on(self):
+        for level, at in ((1, 3), (2, 0)):
+
+            @pl.when(self.level == level)
+            def _(at=at):
+                self.arrive(3)
+                self.add(self.summed, self.got, self.summed, 1, lambda i: at, lambda i: 3, lambda i: at)
+
+        for condition, copy in self.passes():
+            pl.when(condition)(lambda copy=copy: copy.start())
+
+    def finish(self, out):
+        level = self.level
+        pl.when(level >= 1)(lambda: self.arrive(0))
+        pl.when(level <= 2)(lambda: self.arrive(1))
+        self.arrive(2)
+        rows = min(64, self.rows)
+
+        def body(own, mate, below, above, far, total):
+            value = own[...].astype(F32) + mate[...].astype(F32) + far[...].astype(F32)
+            below_term, above_term = below[...].astype(F32), above[...].astype(F32)
+            value = value + jnp.where(level >= 1, below_term, 0.0) + jnp.where(level <= 2, above_term, 0.0)
+            total[...] = value.astype(total.dtype)
+
+        steps = self.rows // rows
+        spec = lambda at: pl.BlockSpec((rows, out.shape[1]), lambda i: (at * steps + i, 0))
+        pltpu.emit_pipeline(
+            body,
+            grid=(steps,),
+            in_specs=[spec(self.place), spec(level), spec(0), spec(1), spec(2)],
+            out_specs=[spec(0)],
+        )(self.source, self.mate_in, self.got, self.got, self.got, out)
+
+    def close(self):
+        for item in self.swaps():
+            item.wait_send()
+        for condition, copy in self.hops() + self.passes():
+            pl.when(condition)(lambda copy=copy: copy.wait_send())
+
+
+class NearScatter(LevelScatter):
+    def part(self, ref, at):
+        return ref[pl.ds(pl.multiple_of(at * self.rows, self.rows), self.rows), :].astype(F32)
+
+    def spread(self):
+        for item in self.swaps():
+            item.wait_recv()
+        for at in range(4):
+            total = self.part(self.source, 2 * at + self.core) + self.part(self.mate_in, at)
+            self.summed[at * self.rows : (at + 1) * self.rows, :] = total.astype(BF16)
+        for condition, copy in self.hops():
+            pl.when(condition)(lambda copy=copy: copy.start())
+
+    def pass_on(self):
+        for level, at in ((1, 3), (2, 0)):
+
+            @pl.when(self.level == level)
+            def _(at=at):
+                self.arrive(3)
+                total = self.part(self.summed, at) + self.part(self.got, 3)
+                self.summed[at * self.rows : (at + 1) * self.rows, :] = total.astype(BF16)
+
+        for condition, copy in self.passes():
+            pl.when(condition)(lambda copy=copy: copy.start())
+
+    def finish(self, out):
+        level = self.level
+        pl.when(level >= 1)(lambda: self.arrive(0))
+        pl.when(level <= 2)(lambda: self.arrive(1))
+        self.arrive(2)
+        value = self.part(self.source, self.place) + self.part(self.mate_in, level) + self.part(self.got, 2)
+        value = value + jnp.where(level >= 1, self.part(self.got, 0), 0.0)
+        value = value + jnp.where(level <= 2, self.part(self.got, 1), 0.0)
+        out[...] = value.astype(BF16)
+
+
+class LevelGather:
+    def __init__(self, own, full, send, receive, mate_send, mate_receive):
+        self.own, self.full, self.send, self.receive = own, full, send, receive
+        self.mate_send, self.mate_receive = mate_send, mate_receive
+        self.rows = own.shape[0]
+        self.place = lax.axis_index("dp")
+        self.level, self.core = lax.div(self.place, 2), lax.rem(self.place, 2)
+        self.mate = self.place + 1 - 2 * self.core
+
+    greet = LevelScatter.greet
+
+    def shard(self, level):
+        return self.full.at[pl.ds((2 * level + self.core) * self.rows, self.rows)]
+
+    def hop(self, index, steps, slot):
+        return remote(
+            self.own, self.shard(self.level), self.send.at[index], self.receive.at[slot], "dp", self.place + 2 * steps
+        )
+
+    def near(self):
+        return [(self.level <= 2, self.hop(0, 1, 0)), (self.level >= 1, self.hop(1, -1, 1))]
+
+    def second(self):
+        inner = (self.level == 1) | (self.level == 2)
+        lower, upper = self.shard(self.level - 1), self.shard(self.level + 1)
+        return [
+            (inner, remote(lower, lower, self.send.at[2], self.receive.at[2], "dp", self.place + 2)),
+            (inner, remote(upper, upper, self.send.at[3], self.receive.at[2], "dp", self.place - 2)),
+        ]
+
+    def passes(self):
+        first, last = self.shard(0), self.shard(3)
+        return [
+            (self.level == 2, remote(first, first, self.send.at[4], self.receive.at[3], "dp", self.place + 2)),
+            (self.level == 1, remote(last, last, self.send.at[4], self.receive.at[3], "dp", self.place - 2)),
+        ]
+
+    def across(self, index, level):
+        here = self.own if index == 4 else self.shard(level)
+        return remote(here, self.shard(level), self.mate_send.at[index], self.mate_receive.at[index], "dp", self.mate)
+
+    def arrivals(self, slots):
+        level = self.level
+        two_away = level + 2 - 4 * lax.div(level, 2)
+        every = [
+            (level >= 1, 0, level - 1),
+            (level <= 2, 1, level + 1),
+            (level >= 0, 2, two_away),
+            ((level == 0) | (level == 3), 3, 3 - level),
+        ]
+        return [item for item in every if item[1] in slots]
+
+    def start(self, hops):
+        for condition, copy in hops:
+            pl.when(condition)(lambda copy=copy: copy.start())
+
+    def take(self, slots):
+        for condition, slot, level in self.arrivals(slots):
+
+            @pl.when(condition)
+            def _(slot=slot, level=level):
+                here = self.shard(level)
+                remote(here, here, self.send.at[0], self.receive.at[slot], "dp", self.mate).wait_recv()
+                self.across(slot, level).start()
+
+    def finish(self, slots, hops):
+        for condition, slot, level in self.arrivals(slots):
+            pl.when(condition)(lambda slot=slot, level=level: self.across(slot, level).wait())
+        for condition, copy in hops:
+            pl.when(condition)(lambda copy=copy: copy.wait_send())
+
+
 def opening_kernel(
-    tokens, qkv_pieces, fc_pieces, small, token_all, qkv_full, fc_rows, small_full,
-    qkv_rows, small_rows, local, send, receive, up_send, up_receive, down_send, down_receive, mate_send, mate_receive,
+    tokens, cot, qkv_weight, fc_weight, small, down, proj,
+    token_all, qkv_full, fc_rows, cot_one, cot_two, down_full, proj_full, vectors, key_bias,
+    qkv_pieces, fc_pieces, token_buf, qkv_rows, small_rows, small_full, proj_rows, square, local, send, receive, up_send, up_receive, down_send, down_receive, mate_send, mate_receive,
+    level_send, level_receive, level_mate_send, level_mate_receive,
 ):
     piece = tokens.shape[0]
     half = piece // 2
+    gather = LevelGather(down, down_full, level_send, level_receive, level_mate_send, level_mate_receive)
     me, place = lax.axis_index("seq"), lax.axis_index("dp")
     one, two = neighbours()
     three = 3 - me
@@ -536,7 +768,22 @@
     greet("dp", mate)
     pl.when(above)(lambda: greet("dp", place + 2))
     pl.when(below)(lambda: greet("dp", place - 2))
-    pl.semaphore_wait(pltpu.get_barrier_semaphore(), 4 + above.astype(jnp.int32) + below.astype(jnp.int32))
+    swaps = core != lax.rem(me, 2)
+    partner = {"dp": mate, "seq": one}
+
+    @pl.when(swaps)
+    def _():
+        pl.semaphore_signal(pltpu.get_barrier_semaphore(), inc=1, device_id=partner, device_id_type=MESH)
+
+    heads = qkv_pieces.shape[2] // (3 * HEAD_DIM)
+    for rank in range(4):
+        for part in range(3):
+            for head in range(heads):
+                source = (part * HEADS + (head * 2 + rank % 2) * 2 + rank // 2) * HEAD_DIM
+                target = (part * heads + head) * HEAD_DIM
+                qkv_pieces[rank, :, target : target + HEAD_DIM] = qkv_weight[:, source : source + HEAD_DIM]
+    count = 4 + above.astype(jnp.int32) + below.astype(jnp.int32) + swaps.astype(jnp.int32)
+    pl.semaphore_wait(pltpu.get_barrier_semaphore(), count)
 
     def block(ref, at, start=0, size=piece):
         return ref.at[pl.ds(at * piece + start, size)]
@@ -561,9 +808,21 @@
         remote(block(token_all, 2, half, half), block(token_all, 3, half, half), send.at[12], receive.at[12], "seq", one),
     )
     first_kept = [pltpu.make_async_copy(qkv_own, qkv_mine, local.at[0]), pltpu.make_async_copy(small_own, small_mine, local.at[1])]
-    later_kept = [pltpu.make_async_copy(fc_own, fc_mine, local.at[2]), pltpu.make_async_copy(tokens, block(token_all, 0), local.at[3])]
-
-    chains = ((qkv_rows, qkv_full), (small_rows, small_full))
+    later_kept = [
+        pltpu.make_async_copy(fc_own, fc_mine, local.at[2]),
+        pltpu.make_async_copy(token_buf, block(token_all, 0), local.at[3]),
+    ]
+    token_load = pltpu.make_async_copy(tokens, token_buf, local.at[4])
+    cot_copies = (
+        remote(cot.at[pl.ds(0, half)], cot_one, send.at[13], receive.at[13], "seq", one),
+        remote(cot.at[pl.ds(0, half)], cot_two, send.at[14], receive.at[14], "seq", two),
+    )
+
+    proj_copy = pltpu.make_async_remote_copy(
+        src_ref=proj, dst_ref=proj_rows, send_sem=send.at[15], recv_sem=receive.at[15], device_id=partner,
+        device_id_type=MESH,
+    )
+    chains = ((qkv_rows, qkv_full), (small_rows, small_full), (proj_rows, proj_full))
 
     def shard(array, at):
         rows = chains[array][0].shape[0]
@@ -591,40 +850,58 @@
     def relay(step):
         @pl.when(rises(step))
         def _():
-            for array in (1, 0):
+            for array in (1, 0, 2):
                 rising(array, step, place + 2).start()
 
         @pl.when(falls(step))
         def _():
-            for array in (1, 0):
+            for array in (1, 0, 2):
                 falling(array, step, place - 2).start()
 
     def take(step):
         @pl.when(from_below(step))
         def _():
-            for array in (1, 0):
+            for array in (1, 0, 2):
                 got = shard(array, level - step)
                 remote(got, got, up_send.at[array, step - 1], up_receive.at[array, step - 1], "dp", mate).wait_recv()
                 across(array, step, level - step).start()
 
         @pl.when(from_above(step))
         def _():
-            for array in (1, 0):
+            for array in (1, 0, 2):
                 got = shard(array, level + step)
                 remote(got, got, down_send.at[array, step - 1], down_receive.at[array, step - 1], "dp", mate).wait_recv()
                 across(array, stages - 1 + step, level + step).start()
 
     for copy in qkv_copies + small_copies + first_kept:
         copy.start()
+    pl.when(swaps)(proj_copy.start)
+
+    @pl.when(jnp.logical_not(swaps))
+    def _():
+        proj_rows[...] = proj[...]
+
     token_one.start()
     token_two.start()
+    gather.start(gather.near())
+    gather.across(4, level).start()
+    down_kept = pltpu.make_async_copy(down, gather.shard(level), local.at[8])
+    down_kept.start()
+    token_load.start()
+    inner = fc_pieces.shape[2] // 8
+    for rank in range(4):
+        for d in range(8):
+            source = (d * 4 + rank) * inner
+            fc_pieces[rank, :, d * inner : (d + 1) * inner] = fc_weight[:, source : source + inner]
+    token_load.wait()
     for copy in qkv_copies + small_copies:
         copy.wait_recv()
+    pl.when(swaps)(proj_copy.wait_recv)
     for copy in first_kept:
         copy.wait()
     relay(1)
-    own_full = [pltpu.make_async_copy(chains[array][0], shard(array, level), local.at[4 + array]) for array in range(2)]
-    for array in range(2):
+    own_full = [pltpu.make_async_copy(chains[array][0], shard(array, level), local.at[5 + array]) for array in range(3)]
+    for array in range(3):
         across(array, 0, level).start()
         own_full[array].start()
     for copy in fc_copies + later_kept:
@@ -633,9 +910,12 @@
     relay(2)
     take(2)
     relay(3)
+    gather.take((0, 1))
     token_one.wait_recv()
     token_two.wait_recv()
     for copy in token_three:
+        copy.start()
+    for copy in cot_copies:
         copy.start()
     take(3)
     for copy in later_kept + own_full:
@@ -650,91 +930,136 @@
 
         @pl.when(rises(step))
         def _(step=step):
-            for array in range(2):
+            for array in range(3):
                 rising(array, step, place + 2).wait_send()
 
         @pl.when(falls(step))
         def _(step=step):
-            for array in range(2):
+            for array in range(3):
                 falling(array, step, place - 2).wait_send()
 
         @pl.when(from_below(step))
         def _(step=step):
-            for array in range(2):
+            for array in range(3):
                 across(array, step, level - step).wait()
 
         @pl.when(from_above(step))
         def _(step=step):
-            for array in range(2):
+            for array in range(3):
                 across(array, stages - 1 + step, level + step).wait()
 
-    for array in range(2):
+    for array in range(3):
         across(array, 0, level).wait()
     for copy in token_three:
         copy.wait()
-
-
-def opening(tokens, qkv_pieces, fc_pieces, small, dp_count):
+    down_kept.wait()
+    pl.when(swaps)(proj_copy.wait_send)
+    tile = lambda d, s: small_full[pl.ds(pl.multiple_of((d * 4 + s) * 16, 16), 16), :].astype(F32)
+    vectors[...] = jnp.zeros_like(vectors)
+    for d in range(8):
+        for pair in range(2):
+            both = tile(d, 2 * pair) + tile(d, 2 * pair + 1)
+            vectors[0:6, (2 * d + pair) * 128 : (2 * d + pair + 1) * 128] = both[0:6]
+        own = tile(d, me)
+        for i in range(2):
+            vectors[6:7, (2 * d + i) * 128 : (2 * d + i + 1) * 128] = own[7 + i : 8 + i]
+        bias = tile(d, 2 * lax.rem(me, 2) + lax.div(me, 2))
+        vectors[7:8, d * HEAD_DIM : (d + 1) * HEAD_DIM] = bias[6:7]
+    square[...] = jnp.zeros_like(square)
+    for i in range(4):
+        square[4 * i : 4 * i + 4, :] = tile(place, flip(me, i))[9:13]
+    turned = square[...].T
+    lane = lax.broadcasted_iota(jnp.int32, turned.shape, 1)
+    for i in range(16):
+        flag = jnp.sum(jnp.where(lane == i, turned, 0.0), axis=1, keepdims=True)
+        key_bias[i * 128 : (i + 1) * 128, :] = jnp.where(flag > 0, 0.0, NEG)
+    for copy in cot_copies:
+        copy.wait()
+    gather.finish((0, 1), gather.near())
+    gather.across(4, level).wait()
+
+
+def opening(tokens, cot, qkv_weight, fc_weight, small, down, proj, dp_count):
     piece, width = tokens.shape
     steps = dp_count // 2 - 1
-    anywhere = pl.BlockSpec(memory_space=pl.ANY)
+    anywhere = pl.BlockSpec(memory_space=pltpu.HBM)
     shape = lambda rows, columns: jax.ShapeDtypeStruct((rows, columns), BF16)
     dma = pltpu.SemaphoreType.DMA
     inside = pl.BlockSpec(memory_space=pltpu.VMEM)
-    rows, columns = 4 * qkv_pieces.shape[1], qkv_pieces.shape[2]
-    fine = 4 * small.shape[0]
+    own_rows, columns, inner = qkv_weight.shape[0], qkv_weight.shape[1] // 4, fc_weight.shape[1] // 4
+    rows, fine = 4 * own_rows, 4 * small.shape[0]
     return pl.pallas_call(
         opening_kernel,
-        in_specs=[inside] * 4,
-        out_specs=[anywhere] * 4,
+        in_specs=[anywhere] * 2 + [inside] * 5,
+        out_specs=[anywhere] * 7 + [inside] * 2,
         out_shape=[
             shape(4 * piece, width),
             shape(rows * dp_count, columns),
-            shape(4 * fc_pieces.shape[1], fc_pieces.shape[2]),
-            shape(fine * dp_count, small.shape[1]),
+            shape(rows, inner),
+            shape(piece // 2, width),
+            shape(piece // 2, width),
+            shape(down.shape[0] * dp_count, width),
+            shape(proj.shape[0] * dp_count, width),
+            jax.ShapeDtypeStruct((8, width), F32),
+            jax.ShapeDtypeStruct((4 * piece, 1), F32),
         ],
         scratch_shapes=[
-            pltpu.VMEM((rows, columns), BF16), pltpu.VMEM((fine, small.shape[1]), BF16),
-            dma((6,)), dma((13,)), dma((13,)), dma((2, steps)), dma((2, steps)), dma((2, steps)), dma((2, steps)),
-            dma((2, 2 * steps + 1)), dma((2, 2 * steps + 1)),
+            pltpu.VMEM((4, own_rows, columns), BF16), pltpu.VMEM((4, own_rows, inner), BF16),
+            pltpu.VMEM((piece, width), BF16),
+            pltpu.VMEM((rows, columns), BF16), pltpu.VMEM((fine, 128), BF16), pltpu.VMEM((fine * dp_count, 128), BF16),
+            pltpu.VMEM(proj.shape, BF16), pltpu.VMEM((128, 128), F32),
+            dma((9,)), dma((16,)), dma((16,)), dma((3, steps)), dma((3, steps)), dma((3, steps)), dma((3, steps)),
+            dma((3, 2 * steps + 1)), dma((3, 2 * steps + 1)), dma((5,)), dma((4,)), dma((5,)), dma((5,)),
         ],
-        compiler_params=pltpu.CompilerParams(collective_id=0, has_side_effects=True, vmem_limit_bytes=32 * 2**20),
+        compiler_params=pltpu.CompilerParams(collective_id=0, has_side_effects=True, vmem_limit_bytes=62 * 2**20),
         cost_estimate=cost(0, 10 * 4 * piece * width),
-    )(tokens, qkv_pieces, fc_pieces, small)
-
-
-def flip(first, second):
-    low = lax.rem(first + second, 2)
-    high = lax.rem(lax.div(first, 2) + lax.div(second, 2), 2)
-    return 2 * high + low
+    )(tokens, cot, qkv_weight, fc_weight, small, down, proj)
 
 
 def attend_plane_kernel(
-    q, k, v_t, tokens, cot_one, cot_two, key_bias, proj, vectors,
-    middle, normed, attended, lse, cot_three,
+    tokens, cot, token_all, weight, cot_one, down, down_in, key_bias, proj, vectors,
+    middle, normed, attended, lse, cot_three, down_full, normed_one, q, k, v, k_t, v_t, one_low, two_low,
     score_ref, joint, terms, passed, joined, arrived, send, receive,
+    level_send, level_receive, mate_send, mate_receive,
 ):
     piece, width = tokens.shape
     half = piece // 2
-    heads = q.shape[1] // HEAD_DIM
+    length, columns = q.shape
+    heads = columns // HEAD_DIM
     rank = lax.axis_index("seq")
     one, two = neighbours()
+    gather = LevelGather(down, down_full, level_send, level_receive, mate_send, mate_receive)
     for device in (one, two):
         greet("seq", device)
-    pl.semaphore_wait(pltpu.get_barrier_semaphore(), 2)
+    pl.semaphore_wait(pltpu.get_barrier_semaphore(), 2 + gather.greet())
     up, lower = pl.ds(0, half), pl.ds(half, half)
+    gather.start(gather.second())
 
     def copy(index, source, target, device):
         return remote(source, target, send.at[index], receive.at[index], "seq", device)
 
-    cot_copies = (copy(0, cot_one.at[up], cot_three.at[up], two), copy(1, cot_two.at[lower], cot_three.at[lower], one))
+    cot_copies = (copy(0, cot_one, cot_three.at[up], two), copy(1, two_low, cot_three.at[lower], one))
+    low_copies = (copy(8, cot.at[lower], one_low, one), copy(9, cot.at[lower], two_low, two))
     across = (copy(2, terms.at[3, up], passed.at[0], one), copy(3, terms.at[3, lower], passed.at[1], two))
     plain_one = copy(4, terms.at[1, up], arrived.at[0, up], one)
     plain_two = copy(5, terms.at[2, lower], arrived.at[1, lower], two)
     joined_one = copy(6, joined.at[0], arrived.at[0, lower], one)
     joined_two = copy(7, joined.at[1], arrived.at[1, up], two)
-    for item in cot_copies:
+    for item in low_copies:
         item.start()
+    cot_copies[0].start()
+    tile = min(256, piece)
+    rows = lambda n: pl.BlockSpec((tile, n), lambda i: (i, 0))
+    turned = pl.BlockSpec((columns, tile), lambda i: (0, i))
+    pltpu.emit_pipeline(
+        lambda x, wq, wk, wv, *out: project_kernel(x, vectors, wq, wk, wv, *out),
+        grid=(length // tile,),
+        in_specs=[rows(width)] + [pl.BlockSpec((width, columns), lambda i, part=part: (0, part)) for part in range(3)],
+        out_specs=[rows(width), rows(columns), rows(columns), rows(columns), turned, turned],
+    )(token_all, weight, weight, weight, normed_one, q, k, v, k_t, v_t)
+    for item in low_copies:
+        item.wait_recv()
+    cot_copies[1].start()
 
     def body(query_ref, key_ref, value_t, attended_tile, lse_tile):
         group, head = pl.program_id(0), pl.program_id(1)
@@ -777,6 +1102,11 @@
         @pl.when((head == heads - 1) & (group == 1))
         def _():
             plain_two.start()
+
+        @pl.when((head == 0) & (group == 3))
+        def _():
+            gather.take((2,))
+            gather.start(gather.passes())
 
         @pl.when((head == heads - 1) & (group == 2))
         def _():
@@ -788,7 +1118,6 @@
             joined_one.start()
             joined_two.start()
 
-    length = q.shape[0]
     pltpu.emit_pipeline(
         body,
         grid=(4, heads),
@@ -810,33 +1139,40 @@
     def norm_body(token_tile, middle_tile, normed_tile):
         here = pl.ds(pl.multiple_of(pl.program_id(0) * part, part), part)
         total = terms[0, here, :].astype(F32) + arrived[0, here, :].astype(F32) + arrived[1, here, :].astype(F32)
-        values = token_tile[...].astype(F32) + (total + vectors[0:1, :])
+        values = token_tile[...].astype(F32) + (total + vectors[2:3, :])
         middle_tile[...] = values
-        normed_tile[...] = (norm_parts(values)[0] * vectors[1:2, :] + vectors[2:3, :]).astype(BF16)
+        normed_tile[...] = (norm_parts(values)[0] * vectors[3:4, :] + vectors[4:5, :]).astype(BF16)
 
     line = pl.BlockSpec((part, width), lambda i: (i, 0))
     pltpu.emit_pipeline(norm_body, grid=(piece // part,), in_specs=[line], out_specs=[line] * 2)(tokens, middle, normed)
+    gather.take((3,))
+    gather.finish((2, 3), gather.second() + gather.passes())
     for item in cot_copies:
         item.wait()
+    for item in low_copies:
+        item.wait_send()
     for item in (*across, plain_one, plain_two, joined_one, joined_two):
         item.wait_send()
 
 
-def attend_plane(q, k, v_t, tokens, cots, key_bias, proj, vectors):
+def attend_plane(tokens, cot, token_all, weight, cot_one, down, down_in, key_bias, proj, vectors):
     piece, width = tokens.shape
-    length, columns = q.shape
+    length, columns = token_all.shape[0], proj.shape[0]
     heads, half = columns // HEAD_DIM, piece // 2
-    anywhere = pl.BlockSpec(memory_space=pl.ANY)
+    anywhere = pl.BlockSpec(memory_space=pltpu.HBM)
     inside = pl.BlockSpec(memory_space=pltpu.VMEM)
     shape = lambda *dims: jax.ShapeDtypeStruct(dims, BF16)
     dma = pltpu.SemaphoreType.DMA
     return pl.pallas_call(
         attend_plane_kernel,
-        in_specs=[anywhere] * 6 + [inside] * 3,
-        out_specs=[anywhere] * 5,
+        in_specs=[anywhere] * 7 + [inside] * 3,
+        out_specs=[anywhere] * 14,
+        input_output_aliases={6: 5},
         out_shape=[
             jax.ShapeDtypeStruct((piece, width), F32), shape(piece, width), shape(length, columns),
-            jax.ShapeDtypeStruct((heads, 1, length), F32), shape(piece, width),
+            jax.ShapeDtypeStruct((heads, 1, length), F32), shape(piece, width), shape(*down_in.shape),
+            shape(length, width), *[shape(length, columns)] * 3, *[shape(columns, length)] * 2,
+            *[shape(half, width)] * 2,
         ],
         scratch_shapes=[
             pltpu.VMEM((length, piece), F32),
@@ -845,11 +1181,11 @@
             pltpu.VMEM((2, half, width), BF16),
             pltpu.VMEM((2, half, width), BF16),
             pltpu.VMEM((2, piece, width), BF16),
-            dma((8,)), dma((8,)),
+            dma((10,)), dma((10,)), dma((5,)), dma((4,)), dma((5,)), dma((5,)),
         ],
-        compiler_params=pltpu.CompilerParams(collective_id=2, has_side_effects=True, vmem_limit_bytes=56 * 2**20),
+        compiler_params=pltpu.CompilerParams(collective_id=2, has_side_effects=True, vmem_limit_bytes=62 * 2**20),
         cost_estimate=cost(3 * length * length * columns + 2 * length * columns * width, 10 * length * width, heads * length * length // 2),
-    )(q, k, v_t, tokens, *cots, key_bias, proj, vectors)
+    )(tokens, cot, token_all, weight, cot_one, down, down_in, key_bias, proj, vectors)
 
 
 def sum_rows(ref, at, columns, value, first):
@@ -865,9 +1201,10 @@
 
 
 def plane_kernel(
-    normed, cot_own, cot_one, cot_two, cot_three, fc, bias, down, middle, gain,
+    normed, cot_own, one_up, one_low, two_up, two_low, cot_three, fc, down, middle, vectors,
     grad_middle, low_all, sums, hidden_sums, active, hidden_grad, normed_all, cot_all, terms, grad_down, grad_fc,
-    normed_buf, cot_buf, sum_ref, joined, passed, arrived, load, local, send, receive,
+    mate_in, summed, got, down_share,
+    normed_buf, cot_buf, sum_ref, joined, passed, arrived, load, local, send, receive, level_send, level_receive,
 ):
     piece, width = normed.shape
     half = piece // 2
@@ -876,79 +1213,91 @@
     tile = min(512, inner)
     last = inner // tile - 1
     one, two = neighbours()
+    scatter = LevelScatter(grad_down, mate_in, summed, got, level_send, level_receive)
     for device in (one, two):
         greet("seq", device)
-    pl.semaphore_wait(pltpu.get_barrier_semaphore(), 2)
-
-    up, lower = pl.ds(0, half), pl.ds(half, half)
+    pl.semaphore_wait(pltpu.get_barrier_semaphore(), 2 + scatter.greet())
+
     rows = lambda k, start=0, size=piece: pl.ds(k * piece + start, size)
+    first, second = pl.ds(0, half), pl.ds(half, half)
 
     def copy(index, source, target, device):
         return remote(source, target, send.at[index], receive.at[index], "seq", device)
 
-    normed_one = copy(0, normed, normed_buf.at[1], one)
-    normed_two = copy(1, normed, normed_buf.at[2], two)
-    normed_three = (
-        copy(2, normed_buf.at[1, up], normed_buf.at[3, up], two),
-        copy(3, normed_buf.at[2, lower], normed_buf.at[3, lower], one),
+    normed_first = (copy(0, normed.at[first], normed_buf.at[2], one), copy(1, normed.at[second], normed_buf.at[5], two))
+    normed_across = (copy(2, normed_buf.at[2], normed_buf.at[6], two), copy(3, normed_buf.at[5], normed_buf.at[7], one))
+    normed_last = (copy(4, normed.at[second], normed_buf.at[3], one), copy(5, normed.at[first], normed_buf.at[4], two))
+    across = (copy(6, cot_buf.at[6], passed.at[0], one), copy(7, cot_buf.at[7], passed.at[1], two))
+    plain = (copy(8, cot_buf.at[2], arrived.at[0, 0], one), copy(9, cot_buf.at[5], arrived.at[1, 1], two))
+    both = (copy(10, joined.at[0], arrived.at[0, 1], one), copy(11, joined.at[1], arrived.at[1, 0], two))
+    low_near = (
+        copy(12, low_all.at[rows(0)], low_all.at[rows(1)], one),
+        copy(13, low_all.at[rows(0)], low_all.at[rows(2)], two),
     )
-    across = (copy(4, cot_buf.at[3, up], passed.at[0], one), copy(5, cot_buf.at[3, lower], passed.at[1], two))
-    plain_one = copy(6, cot_buf.at[1, up], arrived.at[0, up], one)
-    plain_two = copy(7, cot_buf.at[2, lower], arrived.at[1, lower], two)
-    joined_one = copy(8, joined.at[0], arrived.at[0, lower], one)
-    joined_two = copy(9, joined.at[1], arrived.at[1, up], two)
-    low_one = copy(10, low_all.at[rows(0)], low_all.at[rows(1)], one)
-    low_two = copy(11, low_all.at[rows(0)], low_all.at[rows(2)], two)
     low_three = (
-        copy(12, low_all.at[rows(1, 0, half)], low_all.at[rows(3, 0, half)], two),
-        copy(13, low_all.at[rows(2, half, half)], low_all.at[rows(3, half, half)], one),
+        copy(14, low_all.at[rows(1, 0, half)], low_all.at[rows(3, 0, half)], two),
+        copy(15, low_all.at[rows(2, half, half)], low_all.at[rows(3, half, half)], one),
     )
 
-    loads = [
-        pltpu.make_async_copy(source, cot_buf.at[k], load.at[k])
-        for k, source in enumerate((cot_own, cot_one, cot_two, cot_three))
+    sources = (
+        cot_own.at[first], cot_own.at[second], one_up, one_low, two_up, two_low, cot_three.at[first], cot_three.at[second]
+    )
+    loads = [pltpu.make_async_copy(source, cot_buf.at[i], load.at[i]) for i, source in enumerate(sources)]
+    own = [
+        pltpu.make_async_copy(normed.at[part], normed_buf.at[i], load.at[8 + i]) for i, part in enumerate((first, second))
     ]
-    own = pltpu.make_async_copy(normed, normed_buf.at[0], load.at[4])
-    keeps = [pltpu.make_async_copy(normed_buf.at[k], normed_all.at[rows(k)], local.at[k]) for k in range(4)]
-    keeps_cot = [pltpu.make_async_copy(cot_buf.at[k], cot_all.at[rows(k)], local.at[4 + k]) for k in range(4)]
-
-    normed_one.start()
-    normed_two.start()
-    own.start()
-    for item in loads:
-        item.start()
+    keep_to = lambda target, i: target.at[pl.ds(i * half, half)]
+    keeps = [pltpu.make_async_copy(normed_buf.at[i], keep_to(normed_all, i), local.at[i]) for i in range(8)]
+    keeps_cot = [pltpu.make_async_copy(cot_buf.at[i], keep_to(cot_all, i), local.at[8 + i]) for i in range(8)]
+
+    def start(*items):
+        for item in items:
+            item.start()
+
+    def received(*items):
+        for item in items:
+            item.wait_recv()
+
+    start(*normed_first, *own, *loads)
+
+    place_of = lambda step: step + 2 * lax.div(step, 3) - 7 * lax.div(step, 6)
 
     def feed_body(fc_tile, down_tile, active_tile, hidden_tile):
-        k, j = pl.program_id(0), pl.program_id(1)
-
-        @pl.when((k == 0) & (j == 0))
+        step, j = pl.program_id(0), pl.program_id(1)
+        at = place_of(step)
+
+        @pl.when((step == 0) & (j == 0))
         def _():
-            own.wait()
-            keeps[0].start()
+            for item in own:
+                item.wait()
+            start(*keeps[:2])
             for item in loads:
                 item.wait()
-            for item in keeps_cot:
-                item.start()
-
-        @pl.when((k == 1) & (j == 0))
+            start(*keeps_cot)
+
+        @pl.when((step == 2) & (j == 0))
         def _():
-            normed_one.wait_recv()
-            normed_two.wait_recv()
-            for item in normed_three:
-                item.start()
-            keeps[1].start()
-            keeps[2].start()
-
-        @pl.when((k == 3) & (j == 0))
+            received(*normed_first)
+            start(*normed_across, keeps[2], keeps[5])
+
+        @pl.when((step == 4) & (j == 0))
         def _():
-            for item in normed_three:
-                item.wait_recv()
-            keeps[3].start()
+            received(*normed_across)
+            start(*normed_last, *keeps[6:])
+
+        @pl.when((step == 6) & (j == 0))
+        def _():
+            received(*normed_last)
+            start(*keeps[3:5])
+
+        @pl.when((step == 7) & (j == 0))
+        def _():
+            start(*plain)
 
         weights = fc_tile[...]
         columns = pl.ds(pl.multiple_of(j * tile, tile), tile)
-        hidden = nn(normed_buf[k], weights) + bias[:, columns]
-        grad_active = nt(cot_buf[k], down_tile[...])
+        hidden = nn(normed_buf[at], weights) + vectors[6:7, columns]
+        grad_active = nt(cot_buf[at], down_tile[...])
         square = hidden * hidden
         bent = jnp.tanh(math.sqrt(2 / math.pi) * (hidden + 0.044715 * (square * hidden)))
         share = 0.5 * (1.0 + bent)
@@ -958,7 +1307,7 @@
         )
         grad_hidden = (grad_active * slope).astype(BF16)
         hidden_tile[...] = grad_hidden
-        sum_rows(hidden_sums, 0, columns, grad_hidden.astype(F32), k == 0)
+        sum_rows(hidden_sums, 0, columns, grad_hidden.astype(F32), step == 0)
         term = nt(grad_hidden, weights)
 
         @pl.when(j == 0)
@@ -969,37 +1318,35 @@
         def _():
             sum_ref[...] += term
 
-        @pl.when((j == last) & (k == 0))
+        @pl.when((j == last) & (step == 0))
         def _():
             for item in keeps_cot:
                 item.wait()
-            arrived[2] = sum_ref[...].astype(BF16)
-
-        @pl.when((j == last) & (k == 1))
+
+        @pl.when(j == last)
         def _():
-            cot_buf[1] = sum_ref[...].astype(BF16)
-            plain_one.start()
-
-        @pl.when((j == last) & (k == 2))
+            cot_buf[at] = sum_ref[...].astype(BF16)
+
+        @pl.when((j == last) & (step == 5))
         def _():
-            cot_buf[2] = sum_ref[...].astype(BF16)
-            plain_two.start()
-
-        @pl.when((j == last) & (k == 3))
-        def _():
-            cot_buf[3] = sum_ref[...].astype(BF16)
-            for item in across:
-                item.start()
+            start(*across)
 
     pltpu.emit_pipeline(
         feed_body,
-        grid=(4, inner // tile),
+        grid=(8, inner // tile),
         in_specs=[
-            pl.BlockSpec((width, tile), lambda k, j: (0, j)),
-            pl.BlockSpec((tile, width), lambda k, j: (j, 0)),
+            pl.BlockSpec((width, tile), lambda s, j: (0, j)),
+            pl.BlockSpec((tile, width), lambda s, j: (j, 0)),
         ],
-        out_specs=[pl.BlockSpec((piece, tile), lambda k, j: (k, j))] * 2,
+        out_specs=[pl.BlockSpec((half, tile), lambda s, j: (place_of(s), j))] * 2,
     )(fc, down, active, hidden_grad)
+
+    received(*across)
+    joined[0] = (cot_buf[3].astype(F32) + passed[1].astype(F32)).astype(BF16)
+    joined[1] = (cot_buf[4].astype(F32) + passed[0].astype(F32)).astype(BF16)
+    start(*both)
+    for item in keeps:
+        item.wait()
 
     narrow = min(512, width)
 
@@ -1017,43 +1364,6 @@
             out_specs=[pl.BlockSpec((piece, narrow), lambda k, j: (start + k, j))],
         )(active, down, terms)
 
-    multiply_down(0)
-    for item in across:
-        item.wait_recv()
-    joined[0] = (cot_buf[1, half:].astype(F32) + passed[1].astype(F32)).astype(BF16)
-    joined[1] = (cot_buf[2, :half].astype(F32) + passed[0].astype(F32)).astype(BF16)
-    joined_one.start()
-    joined_two.start()
-    for item in keeps:
-        item.wait()
-    multiply_down(2)
-    for item in (plain_one, plain_two, joined_one, joined_two):
-        item.wait_recv()
-
-    part = min(128, piece)
-
-    def norm_body(middle_tile, cot_tile, grad_tile, low_tile):
-        i = pl.program_id(0)
-        here = pl.ds(pl.multiple_of(i * part, part), part)
-        upstream = (
-            arrived[2, here, :].astype(F32) + arrived[0, here, :].astype(F32) + arrived[1, here, :].astype(F32)
-        )
-        unit, scale = norm_parts(middle_tile[...])
-        cot = cot_tile[...].astype(F32)
-        grad = cot + norm_backward(unit, scale, gain[...], upstream)
-        rounded = grad.astype(BF16)
-        grad_tile[...] = grad
-        low_tile[...] = rounded
-        for at, item in enumerate((upstream * unit, upstream, rounded.astype(F32), cot)):
-            sum_rows(sums, at, slice(None), item, i == 0)
-
-    line = pl.BlockSpec((part, width), lambda i: (i, 0))
-    pltpu.emit_pipeline(norm_body, grid=(piece // part,), in_specs=[line] * 2, out_specs=[line] * 2)(
-        middle, cot_own, grad_middle, low_all
-    )
-    low_one.start()
-    low_two.start()
-
     wide, tall = min(1024, width), min(1024, inner)
 
     def outer_body(left, right, out):
@@ -1071,52 +1381,80 @@
         )(left, right, out)
 
     outer(active, cot_all, grad_down, (tall, wide))
-    low_one.wait_recv()
-    low_two.wait_recv()
-    for item in low_three:
-        item.start()
+    scatter.start()
+    multiply_down(0)
+    scatter.spread()
+    received(*plain, *both)
+    part = min(128, half)
+    steps = half // part
+
+    def norm_body(middle_tile, cot_tile, grad_tile, low_tile):
+        i = pl.program_id(0)
+        at = lax.div(i, steps)
+        here = pl.ds(pl.multiple_of(lax.rem(i, steps) * part, part), part)
+        upstream = (
+            cot_buf[at, here, :].astype(F32) + arrived[0, at, here, :].astype(F32) + arrived[1, at, here, :].astype(F32)
+        )
+        unit, scale = norm_parts(middle_tile[...])
+        cot = cot_tile[...].astype(F32)
+        grad = cot + norm_backward(unit, scale, vectors[3:4, :], upstream)
+        rounded = grad.astype(BF16)
+        grad_tile[...] = grad
+        low_tile[...] = rounded
+        for at, item in enumerate((upstream * unit, upstream, rounded.astype(F32), cot)):
+            sum_rows(sums, at, slice(None), item, i == 0)
+
+    line = pl.BlockSpec((part, width), lambda i: (i, 0))
+    pltpu.emit_pipeline(norm_body, grid=(piece // part,), in_specs=[line] * 2, out_specs=[line] * 2)(
+        middle, cot_own, grad_middle, low_all
+    )
+    start(*low_near)
+    multiply_down(2)
+    scatter.pass_on()
     outer(normed_all, hidden_grad, grad_fc, (wide, tall))
-    for item in low_three:
-        item.wait()
-    for item in (
-        normed_one, normed_two, *normed_three, *across, plain_one, plain_two, joined_one, joined_two, low_one, low_two
-    ):
+    received(*low_near)
+    start(*low_three)
+    scatter.finish(down_share)
+    scatter.close()
+    received(*low_three)
+    for item in (*normed_first, *normed_across, *normed_last, *across, *plain, *both, *low_near, *low_three):
         item.wait_send()
 
 
-def feed_plane(normed, cots, fc, bias, down, middle, gain):
+def feed_plane(normed, cots, fc, down, middle, vectors):
     piece, width = normed.shape
     inner = fc.shape[1]
     length, half = 4 * piece, piece // 2
-    anywhere = pl.BlockSpec(memory_space=pl.ANY)
+    anywhere = pl.BlockSpec(memory_space=pltpu.HBM)
     inside = pl.BlockSpec(memory_space=pltpu.VMEM)
     shape = lambda rows, columns, kind=BF16: jax.ShapeDtypeStruct((rows, columns), kind)
     dma = pltpu.SemaphoreType.DMA
     return pl.pallas_call(
         plane_kernel,
-        in_specs=[anywhere] * 6 + [inside, anywhere, anywhere, inside],
-        out_specs=[anywhere, anywhere, inside, inside] + [anywhere] * 7,
+        in_specs=[anywhere] * 10 + [inside],
+        out_specs=[anywhere, anywhere, inside, inside] + [anywhere] * 11,
         out_shape=[
             shape(piece, width, F32), shape(length, width), shape(4, width, F32), shape(1, inner, F32),
             shape(length, inner), shape(length, inner), shape(length, width), shape(length, width),
             shape(length, width), shape(inner, width), shape(width, inner),
+            shape(inner // 2, width), shape(inner // 2, width), shape(inner // 2, width), shape(inner // 8, width, F32),
         ],
         scratch_shapes=[
-            pltpu.VMEM((4, piece, width), BF16),
-            pltpu.VMEM((4, piece, width), BF16),
-            pltpu.VMEM((piece, width), F32),
+            pltpu.VMEM((8, half, width), BF16),
+            pltpu.VMEM((8, half, width), BF16),
+            pltpu.VMEM((half, width), F32),
             pltpu.VMEM((2, half, width), BF16),
             pltpu.VMEM((2, half, width), BF16),
-            pltpu.VMEM((3, piece, width), BF16),
-            dma((5,)), dma((8,)), dma((14,)), dma((14,)),
+            pltpu.VMEM((2, 2, half, width), BF16),
+            dma((10,)), dma((16,)), dma((16,)), dma((16,)), dma((8,)), dma((8,)),
         ],
         compiler_params=pltpu.CompilerParams(collective_id=1, has_side_effects=True, vmem_limit_bytes=60 * 2**20),
         cost_estimate=cost(12 * length * width * inner, 10 * length * width),
-    )(normed, *cots, fc, bias, down, middle, gain)
+    )(normed, *cots, fc, down, middle, vectors)
 
 
 def retreat_plane_kernel(
-    low_all, q, k, v, k_t, lse, terms, middle, key_bias, proj, down_shift,
+    low_all, q, k, v, k_t, lse, terms, middle, key_bias, proj, vectors,
     grads, column_sums, block_out,
     prob_ref, chance_ref, grad_ref, key_sum, value_sum, rounded, own, passed, joined, arrived,
     load, local, send, receive,
@@ -1229,7 +1567,7 @@
     def out_body(middle_tile, term_tile, out):
         here = pl.ds(pl.multiple_of(pl.program_id(0) * part, part), part)
         total = term_tile[...].astype(F32) + arrived[0, here, :].astype(F32) + arrived[1, here, :].astype(F32)
-        out[...] = (middle_tile[...] + (total + down_shift[...])).astype(BF16)
+        out[...] = (middle_tile[...] + (total + vectors[5:6, :])).astype(BF16)
 
     line = pl.BlockSpec((part, width), lambda i: (i, 0))
     pltpu.emit_pipeline(out_body, grid=(piece // part,), in_specs=[line] * 2, out_specs=[line])(middle, terms, block_out)
@@ -1238,11 +1576,11 @@
         item.wait_send()
 
 
-def retreat_plane(low_all, q, k, v, k_t, lse, terms, middle, key_bias, proj, down_shift):
+def retreat_plane(low_all, q, k, v, k_t, lse, terms, middle, key_bias, proj, vectors):
     piece, width = middle.shape
     length, columns = q.shape
     half = piece // 2
-    anywhere = pl.BlockSpec(memory_space=pl.ANY)
+    anywhere = pl.BlockSpec(memory_space=pltpu.HBM)
     inside = pl.BlockSpec(memory_space=pltpu.VMEM)
     dma = pltpu.SemaphoreType.DMA
     return pl.pallas_call(
@@ -1269,19 +1607,35 @@
         ],
         compiler_params=pltpu.CompilerParams(collective_id=3, has_side_effects=True, vmem_limit_bytes=60 * 2**20),
         cost_estimate=cost(8 * length * length * columns + 2 * length * columns * width, 10 * length * width),
-    )(low_all, q, k, v, k_t, lse, terms, middle, key_bias, proj, down_shift)
+    )(low_all, q, k, v, k_t, lse, terms, middle, key_bias, proj, vectors)
 
 
 def closing_kernel(
-    grads, weight, tokens, grad_middle, gain, tokens_grad, sums,
-    terms, passed, joined, arrived, send, receive,
+    grads, weight, normed_one, tokens, grad_middle, vectors, sums_two, hidden_sums, qv_sums, fc_share,
+    tokens_grad, qkv_out, fc_out, small_out,
+    terms, passed, joined, arrived, qkv_in, fc_in, mine, small_in, small_rows, small_got,
+    grad_qkv, mate_in, summed, got, qkv_share,
+    send, receive, level_send, level_receive, small_send, small_receive, load,
 ):
+    pieces = [[ref.at[i] for ref in (grad_qkv, mate_in, summed, got, qkv_share)] for i in range(2)]
     piece, width = tokens.shape
     half = piece // 2
+    columns = grads.shape[1]
+    heads = columns // (3 * HEAD_DIM)
+    me, place = lax.axis_index("seq"), lax.axis_index("dp")
     one, two = neighbours()
-    for device in (one, two):
+    three = 3 - me
+    plane = (one, two, three)
+    others = [lax.rem(place + i, 8) for i in range(1, 8)]
+    for device in plane:
         greet("seq", device)
-    pl.semaphore_wait(pltpu.get_barrier_semaphore(), 2)
+    for device in others:
+        greet("dp", device)
+    pl.semaphore_wait(pltpu.get_barrier_semaphore(), 10)
+    scatters = [
+        NearScatter(*refs[:4], level_send.at[i], level_receive.at[i]) for i, refs in enumerate(pieces)
+    ]
+    shares = [refs[4] for refs in pieces]
     up, lower = pl.ds(0, half), pl.ds(half, half)
 
     def copy(index, source, target, device):
@@ -1292,33 +1646,80 @@
     plain_two = copy(3, terms.at[2, lower], arrived.at[1, lower], two)
     joined_one = copy(4, joined.at[0], arrived.at[0, lower], one)
     joined_two = copy(5, joined.at[1], arrived.at[1, up], two)
-
-    @pl.loop(0, 4)
-    def _(step):
-        at = 3 - step
-        terms[at] = nt(grads[pl.ds(pl.multiple_of(at * piece, piece), piece), :], weight[...]).astype(BF16)
-
-        @pl.when(step == 0)
-        def _():
-            for item in across:
-                item.start()
-
-        @pl.when(step == 1)
-        def _():
-            plain_two.start()
-
-        @pl.when(step == 2)
-        def _():
-            plain_one.start()
-
+    fine = qkv_in.shape[2]
+    rows_for = lambda ref, device: ref.at[pl.ds(device * fine, fine)]
+    fc_copies = [copy(6 + i, rows_for(fc_share, device), fc_in.at[i], device) for i, device in enumerate(plane)]
+    qkv_copies = [
+        [copy(15 + 3 * part + i, rows_for(share, device), qkv_in.at[part, i], device) for i, device in enumerate(plane)]
+        for part, share in enumerate(shares)
+    ]
+    small_copies = [copy(9 + i, mine, small_in.at[i], device) for i, device in enumerate(plane)]
+    fc_own = pltpu.make_async_copy(rows_for(fc_share, me), fc_in.at[3], load.at[0])
+    qkv_own = [
+        pltpu.make_async_copy(rows_for(share, me), qkv_in.at[part, 3], load.at[1 + part])
+        for part, share in enumerate(shares)
+    ]
+    row_copies = [
+        remote(small_rows.at[device], small_got.at[i], small_send.at[i], small_receive.at[i], "dp", device)
+        for i, device in enumerate(others)
+    ]
+
+    def back_term(at):
+        for start in range(0, width, width // 2):
+            columns_here = slice(start, start + width // 2)
+            term = nt(grads[at * piece : (at + 1) * piece, :], weight[columns_here, :])
+            terms[at, :, columns_here] = term.astype(BF16)
+
+    tile = min(512, width)
+    narrow = columns // 2
+
+    def outer(part):
+        def body(left):
+            here = pl.ds(pl.multiple_of(pl.program_id(0) * tile, tile), tile)
+            grad_qkv[part, here, :] = tn(left[...], grads[:, part * narrow : (part + 1) * narrow]).astype(BF16)
+
+        pltpu.emit_pipeline(
+            body,
+            grid=(width // tile,),
+            in_specs=[pl.BlockSpec((normed_one.shape[0], tile), lambda i: (0, i))],
+        )(normed_one)
+
+    back_term(3)
+    for item in across:
+        item.start()
+    back_term(1)
+    plain_one.start()
+    outer(0)
+    scatters[0].start()
+    back_term(2)
+    plain_two.start()
+    scatters[0].spread()
+    outer(1)
+    scatters[1].start()
     for item in across:
         item.wait_recv()
     joined[0] = (terms[1, half:].astype(F32) + passed[1].astype(F32)).astype(BF16)
     joined[1] = (terms[2, :half].astype(F32) + passed[0].astype(F32)).astype(BF16)
     joined_one.start()
     joined_two.start()
+    scatters[1].spread()
+    scatters[0].pass_on()
+    fc_own.start()
+    back_term(0)
+    mine[...] = jnp.zeros_like(mine)
+    mine[2:6, :] = sums_two[...]
+    for head in range(heads):
+        at = (head * 2 + lax.rem(me, 2)) * 2 + lax.div(me, 2)
+        here = pl.ds(pl.multiple_of(at * HEAD_DIM, HEAD_DIM), HEAD_DIM)
+        for part in range(2):
+            mine[6 + part : 7 + part, here] = qv_sums[part : part + 1, head * HEAD_DIM : (head + 1) * HEAD_DIM]
+    scatters[1].pass_on()
+
+    scatters[0].finish(shares[0])
     for item in (plain_one, plain_two, joined_one, joined_two):
         item.wait_recv()
+    for item in fc_copies:
+        item.start()
     part = min(128, piece)
 
     def norm_body(token_tile, middle_tile, out):
@@ -1326,39 +1727,106 @@
         here = pl.ds(pl.multiple_of(i * part, part), part)
         upstream = terms[0, here, :].astype(F32) + arrived[0, here, :].astype(F32) + arrived[1, here, :].astype(F32)
         unit, scale = norm_parts(token_tile[...].astype(F32))
-        out[...] = middle_tile[...] + norm_backward(unit, scale, gain[...], upstream)
+        out[...] = middle_tile[...] + norm_backward(unit, scale, vectors[0:1, :], upstream)
         for at, item in enumerate((upstream * unit, upstream)):
-            sum_rows(sums, at, slice(None), item, i == 0)
+            sum_rows(mine, at, slice(None), item, i == 0)
 
     line = pl.BlockSpec((part, width), lambda i: (i, 0))
     pltpu.emit_pipeline(norm_body, grid=(piece // part,), in_specs=[line] * 2, out_specs=[line])(
         tokens, grad_middle, tokens_grad
     )
-    for item in (*across, plain_one, plain_two, joined_one, joined_two):
+    for item in small_copies:
+        item.start()
+    scatters[1].finish(shares[1])
+    for part in range(2):
+        for item in qkv_copies[part]:
+            item.start()
+        qkv_own[part].start()
+    for item in small_copies:
+        item.wait_recv()
+    mine_total = mine[...] + small_in[0] + small_in[1] + small_in[2]
+    small_rows[...] = jnp.zeros_like(small_rows)
+    share, wide = width // 8, 2 * width // 8
+    for d in range(8):
+        small_rows[d, 0:6, 0:share] = mine_total[0:6, d * share : (d + 1) * share]
+        row, at = 6 + d // 4, (d % 4) * wide
+        small_rows[d, 6:7, :] = mine_total[row : row + 1, at : at + wide]
+        inner = hidden_sums.shape[1] // 8
+        small_rows[d, 7:8, 0:inner] = hidden_sums[:, d * inner : (d + 1) * inner]
+    for item in row_copies:
+        item.start()
+    sources = (*plane, me)
+    fc_own.wait()
+    for item in fc_copies:
+        item.wait_recv()
+    block = fc_in.shape[2] // 8
+    for i, source in enumerate(sources):
+        for d in range(8):
+            target = pl.ds(pl.multiple_of((d * 4 + source) * block, block), block)
+            fc_out[:, target] = fc_in[i, :, d * block : (d + 1) * block].astype(F32)
+    for part in range(2):
+        qkv_own[part].wait()
+        for item in qkv_copies[part]:
+            item.wait_recv()
+    for i, source in enumerate(sources):
+        for part in range(3):
+            for head in range(heads):
+                at = part * HEADS + (head * 2 + lax.rem(source, 2)) * 2 + lax.div(source, 2)
+                target = pl.ds(pl.multiple_of(at * HEAD_DIM, HEAD_DIM), HEAD_DIM)
+                start = (part * heads + head) * HEAD_DIM
+                which, start = start // narrow, start % narrow
+                qkv_out[:, target] = qkv_in[which, i, :, start : start + HEAD_DIM].astype(F32)
+    for item in row_copies:
+        item.wait_recv()
+    total = small_rows[place]
+    for i in range(7):
+        total = total + small_got[i]
+    small_out[...] = total
+    for item in (*across, plain_one, plain_two, joined_one, joined_two, *fc_copies, *small_copies, *row_copies):
         item.wait_send()
-
-
-def closing(grads, weight, tokens, grad_middle, gain):
+    for part in range(2):
+        scatters[part].close()
+        for item in qkv_copies[part]:
+            item.wait_send()
+
+
+def closing(grads, weight, normed_one, tokens, grad_middle, vectors, sums_two, hidden_sums, qv_sums, fc_share):
     piece, width = tokens.shape
-    half = piece // 2
-    anywhere = pl.BlockSpec(memory_space=pl.ANY)
+    columns, half = grads.shape[1], piece // 2
+    fine = fc_share.shape[0] // 4
+    wide = 2 * width // 8
+    anywhere = pl.BlockSpec(memory_space=pltpu.HBM)
     inside = pl.BlockSpec(memory_space=pltpu.VMEM)
+    shape = lambda rows, columns, kind=BF16: jax.ShapeDtypeStruct((rows, columns), kind)
     dma = pltpu.SemaphoreType.DMA
     return pl.pallas_call(
         closing_kernel,
-        in_specs=[inside, inside, anywhere, anywhere, inside],
-        out_specs=[anywhere, inside],
-        out_shape=[jax.ShapeDtypeStruct((piece, width), F32), jax.ShapeDtypeStruct((2, width), F32)],
+        in_specs=[inside, inside, anywhere, anywhere, anywhere, inside, inside, inside, inside, anywhere],
+        out_specs=[anywhere, inside, inside, inside],
+        out_shape=[
+            shape(piece, width, F32), shape(fine, 4 * columns, F32), shape(fine, 4 * fc_share.shape[1], F32),
+            shape(8, wide, F32),
+        ],
         scratch_shapes=[
             pltpu.VMEM((4, piece, width), BF16),
             pltpu.VMEM((2, half, width), BF16),
             pltpu.VMEM((2, half, width), BF16),
             pltpu.VMEM((2, piece, width), BF16),
-            dma((6,)), dma((6,)),
+            pltpu.VMEM((2, 4, fine, columns // 2), BF16),
+            pltpu.VMEM((4, fine, fc_share.shape[1]), BF16),
+            pltpu.VMEM((8, width), F32),
+            pltpu.VMEM((3, 8, width), F32),
+            pltpu.VMEM((8, 8, wide), F32),
+            pltpu.VMEM((7, 8, wide), F32),
+            *[
+                pltpu.VMEM((2, count, columns // 2), BF16)
+                for count in (width, width // 2, width // 2, width // 2, width // 8)
+            ],
+            dma((21,)), dma((21,)), dma((2, 8)), dma((2, 8)), dma((7,)), dma((7,)), dma((3,)),
         ],
         compiler_params=pltpu.CompilerParams(collective_id=4, has_side_effects=True, vmem_limit_bytes=60 * 2**20),
-        cost_estimate=cost(8 * piece * width * grads.shape[1], 10 * piece * width),
-    )(grads, weight, tokens, grad_middle, gain)
+        cost_estimate=cost(16 * piece * width * columns, 10 * piece * width),
+    )(grads, weight, normed_one, tokens, grad_middle, vectors, sums_two, hidden_sums, qv_sums, fc_share)
 
 
 def after(value, *others):
@@ -1479,76 +1947,73 @@
         order = [3, 1, 2, 0]
 
     in_plane = seq_count == 4 and dp_count == 8
-    qkv_pieces = (
-        qkv_weight.reshape(rows, 3, own_heads, sub, high, HEAD_DIM)
-        .transpose(4, 3, 0, 1, 2, 5)
-        .reshape(seq_count, rows, 3 * own_width)
-    )
     tokens_own, cot_own = tokens[0], cotangent[0]
 
-    small = (attn_gain, attn_shift, qv_bias, proj_bias, mlp_gain, mlp_shift, fc_bias, down_bias)
-    sizes = [item.shape[0] for item in small]
     positions = seq_rank * piece + jnp.arange(piece, dtype=jnp.int32)
     own_flags = ((key_mask[0] == 1) & (positions < lengths[0])).astype(BF16)
-    packed = jnp.concatenate(small + (own_flags,))
-    fc_pieces = (
-        fc_weight.reshape(rows, dp_count, seq_count, block)
-        .transpose(2, 0, 1, 3)
-        .reshape(seq_count, rows, dp_count * block)
-    )
+    length = piece * seq_count
+    shared = None
     if in_plane:
-        room = -(-packed.shape[0] // 2048) * 2048
-        small_rows = jnp.pad(packed, (0, room - packed.shape[0])).reshape(room // 128, 128)
-        token_all, qkv_full, fc_rows, small_full = opening(
-            tokens_own, qkv_pieces, fc_pieces, small_rows, dp_count
+        six = jnp.stack([attn_gain, attn_shift, proj_bias, mlp_gain, mlp_shift, down_bias])
+        odd = (seq_rank & 1) != 0
+        six = jnp.concatenate([jnp.where(odd, 0, six), jnp.where(odd, six, 0)], axis=1)
+        small, start = 0, 0
+        for item in (six, qv_bias, fc_bias, own_flags):
+            item = item.reshape(-1, 128)
+            small = small + jnp.pad(item, ((start, 16 - start - item.shape[0]), (0, 0)))
+            start += item.shape[0]
+        token_all, qkv_full, fc_rows, cot_one, cot_two, down_full, proj_full, vectors, key_bias = opening(
+            tokens_own, cot_own, qkv_weight, fc_weight, small, down_weight, proj_weight, dp_count
         )
-        packed = small_full.reshape(dp_count, seq_count, room)
-        flags = lax.dynamic_index_in_dim(packed, dp_rank, axis=0, keepdims=False)
-        flags = jnp.concatenate(by_rank([flags[s, sum(sizes) : sum(sizes) + piece] for s in range(seq_count)], seq_rank))
-        packed = packed[:, :, : sum(sizes)].astype(F32)
+        fc_full = gather_dp(fc_rows)
     else:
-        qkv_full = gather_dp(jnp.concatenate(by_rank(exchange(qkv_pieces, seq_rank), seq_rank), axis=0))
+        small = (attn_gain, attn_shift, qv_bias, proj_bias, mlp_gain, mlp_shift, fc_bias, down_bias)
+        sizes = [item.shape[0] for item in small]
+        packed = jnp.concatenate(small + (own_flags,))
         blocks = gather_blocks(packed)
         flags = jnp.concatenate([item[-piece:] for item in blocks])
+        key_bias = jnp.where(flags > 0, 0.0, NEG).astype(F32)[:, None]
         packed = jnp.stack(by_rank([item[:-piece] for item in blocks], seq_rank))
         packed = jnp.stack(by_rank(gather_blocks(packed, "dp"), dp_rank)).astype(F32)
-        fc_rows = jnp.concatenate(by_rank(exchange(fc_pieces, seq_rank), seq_rank), axis=0)
-    key_bias = jnp.where(flags > 0, 0.0, NEG).astype(F32)[:, None]
-    parts, start = [], 0
-    for size in sizes:
-        parts.append(packed[:, :, start : start + size])
-        start += size
-    whole = [part.reshape(1, -1) for part in parts]
-    gain_one, shift_one, qv_full, proj_shift, gain_two, shift_two, _, down_shift = whole
-    fc_shift = lax.dynamic_index_in_dim(parts[6], seq_rank, axis=1, keepdims=False).reshape(1, -1)
-    rank_low, rank_high = seq_rank % sub, seq_rank // sub
-    qv_heads = qv_full.reshape(2, own_heads, sub, high, HEAD_DIM)
-    qv_own = lax.dynamic_index_in_dim(
-        lax.dynamic_index_in_dim(qv_heads, rank_low, axis=2, keepdims=False), rank_high, axis=2, keepdims=False
-    )
-    qv_own = qv_own.reshape(1, -1)
-
-    length = piece * seq_count
-    proj_full = gather_dp(lax.ppermute(proj_weight, BOTH, swap))
-    down_full = gather_dp(after(down_weight, fc_rows) if in_plane else down_weight)
-    fc_full = gather_dp(fc_rows)
-    shared = None
-    if in_plane:
-        cot_own, token_all = lax.optimization_barrier((cot_own, token_all))
-        cots = (shift(cot_own, "seq", 1), shift(cot_own, "seq", 2))
-        shared = project(0, token_all, 0, length, gain_one, shift_one, qkv_full, qv_own, length, None)
-    else:
+        parts, start = [], 0
+        for size in sizes:
+            parts.append(packed[:, :, start : start + size])
+            start += size
+        whole = [part.reshape(1, -1) for part in parts]
+        gain_one, shift_one, qv_full, proj_shift, gain_two, shift_two, _, down_shift = whole
+        fc_shift = lax.dynamic_index_in_dim(parts[6], seq_rank, axis=1, keepdims=False).reshape(1, -1)
+        rank_low, rank_high = seq_rank % sub, seq_rank // sub
+        qv_own = qv_full.reshape(2, own_heads, sub, high, HEAD_DIM)
+        qv_own = lax.dynamic_index_in_dim(qv_own, rank_low, axis=2, keepdims=False)
+        qv_own = lax.dynamic_index_in_dim(qv_own, rank_high, axis=2, keepdims=False).reshape(1, -1)
+        qv_own = jnp.pad(qv_own, ((0, 0), (0, width - 2 * own_width)))
+        vectors = jnp.concatenate([gain_one, shift_one, jnp.zeros((5, width), F32), qv_own], axis=0)
+        qkv_pieces = (
+            qkv_weight.reshape(rows, 3, own_heads, sub, high, HEAD_DIM)
+            .transpose(4, 3, 0, 1, 2, 5)
+            .reshape(seq_count, rows, 3 * own_width)
+        )
+        fc_pieces = (
+            fc_weight.reshape(rows, dp_count, seq_count, block)
+            .transpose(2, 0, 1, 3)
+            .reshape(seq_count, rows, dp_count * block)
+        )
+        qkv_full = gather_dp(jnp.concatenate(by_rank(exchange(qkv_pieces, seq_rank), seq_rank), axis=0))
+        proj_full = gather_dp(lax.ppermute(proj_weight, BOTH, swap))
+        down_full = gather_dp(down_weight)
+        fc_full = gather_dp(jnp.concatenate(by_rank(exchange(fc_pieces, seq_rank), seq_rank), axis=0))
         token_blocks = gather_blocks(tokens_own)
         cot_blocks = gather_blocks(after(cot_own, token_blocks[-1]))
         for k in range(seq_count):
-            shared = project(k, token_blocks[k], 0, piece, gain_one, shift_one, qkv_full, qv_own, length, shared)
-    normed_one, q, keys, values, keys_t, values_t = shared
+            shared = project(k, token_blocks[k], 0, piece, vectors, qkv_full, length, shared)
     if in_plane:
-        middle, normed_two, attended, lse, cot_three = attend_plane(
-            q, keys, values_t, tokens_own, cots, key_bias, proj_full,
-            jnp.concatenate([proj_shift, gain_two, shift_two], axis=0),
+        results = attend_plane(
+            tokens_own, cot_own, token_all, qkv_full, cot_one, down_weight, down_full, key_bias, proj_full, vectors
         )
+        middle, normed_two, attended, lse, cot_three, down_full = results[:6]
+        normed_one, q, keys, values, keys_t, values_t, one_low, two_low = results[6:]
     else:
+        normed_one, q, keys, values, keys_t, values_t = shared
         proj_terms, shared = [None] * seq_count, None
         for k in order:
             proj_terms[k], shared = attend(k, rank, q, keys, values_t, key_bias, proj_full, piece, shared)
@@ -1558,13 +2023,14 @@
         )
 
     if in_plane:
-        grad_middle, low_all, sums_two, hidden_sums, _, _, _, _, down_terms, grad_down, grad_fc = feed_plane(
-            normed_two, (cot_own, *cots, cot_three), fc_full, fc_shift, down_full, middle, gain_two
-        )
-        sums_two = [sums_two[i] for i in range(4)]
-        grad_down, grad_fc = scatter_dp(grad_down), scatter_dp(grad_fc)
+        cots = (cot_own, cot_one, one_low, cot_two, two_low, cot_three)
+        results = feed_plane(normed_two, cots, fc_full, down_full, middle, vectors)
+        grad_middle, low_all, sums_two, hidden_sums, down_terms, grad_fc, grad_down = [
+            results[i] for i in (0, 1, 2, 3, 8, 10, 14)
+        ]
+        grad_fc = scatter_dp(grad_fc)
         grads, qv_sums, block_out = retreat_plane(
-            low_all, q, keys, values, keys_t, lse, down_terms, middle, key_bias, proj_full, down_shift
+            low_all, q, keys, values, keys_t, lse, down_terms, middle, key_bias, proj_full, vectors
         )
     else:
         normed_blocks = gather_blocks(normed_two)
@@ -1593,12 +2059,17 @@
         grad_q, low_all = shared
         grads = jnp.concatenate([grad_q, sums[0], sums[1]], axis=1)
         qv_sums = jnp.stack([jnp.sum(item.astype(F32), axis=0) for item in (grad_q, sums[1])])
-    grad_qkv = scatter_dp(tn(normed_one, grads).astype(BF16))
-    grad_proj = scatter_dp(tn(attended, low_all).astype(BF16))
+    grad_proj = tn(after(attended, grads), low_all).astype(BF16)
+    grad_proj = scatter_dp(after(grad_proj, grad_fc) if in_plane else grad_proj)
     grad_proj = lax.ppermute(grad_proj, BOTH, swap).astype(F32)
+    share = attn_gain.shape[0]
     if in_plane:
-        tokens_grad, sums_one = closing(grads, qkv_full, tokens_own, grad_middle, gain_one)
-        sums_one = [sums_one[i] for i in range(2)]
+        tokens_grad, grad_qkv_weight, grad_fc, smalls = closing(
+            grads, qkv_full, normed_one, tokens_own, grad_middle, vectors, sums_two, hidden_sums, qv_sums, grad_fc
+        )[:4]
+        own = lambda row, size: lax.dynamic_slice_in_dim(smalls[row], seq_rank * size, size)
+        late = jnp.concatenate([own(0, share), own(1, share), own(6, 2 * share)])
+        early = jnp.concatenate([own(row, share) for row in range(2, 6)] + [smalls[7, :block]])
     else:
         back_terms = [None] * seq_count
         for k in order:
@@ -1607,33 +2078,33 @@
             tokens_back_kernel, scatter_blocks(back_terms), [tokens_own, grad_middle], [gain_one], [F32], 2
         )
 
-    blocks = exchange(grad_fc.reshape(seq_count, rows, dp_count * block), seq_rank)
-    if block % 128 == 0:
-        fc_places = lambda s: [(0, d, d * seq_count + s) for d in range(dp_count)]
-        grad_fc = lay_out(rank, [[item] for item in blocks], fc_weight.shape[1], (fc_places, block))
-    else:
-        blocks = [item.reshape(rows, dp_count, block) for item in by_rank(blocks, seq_rank)]
-        grad_fc = jnp.stack(blocks, axis=2).reshape(fc_weight.shape).astype(F32)
-    blocks = [[item] for item in exchange(grad_qkv.reshape(seq_count, rows, 3 * own_width), seq_rank)]
-    qkv_places = lambda s: [
-        (0, part * own_heads + head, part * HEADS + (head * sub + s % sub) * high + s // sub)
-        for part in range(3)
-        for head in range(own_heads)
-    ]
-    grad_qkv_weight = lay_out(rank, blocks, qkv_weight.shape[1], (qkv_places, HEAD_DIM))
-
-    def spread(vector):
-        return vector.reshape(dp_count, seq_count, -1)
-
-    here = (jnp.arange(seq_count) == seq_rank).astype(F32)
-    hidden_sums = hidden_sums.reshape(dp_count, 1, -1) * here[None, :, None]
-    early = jnp.concatenate([spread(item) for item in sums_two] + [hidden_sums], axis=2)
-    early = small_scatter(early, dp_rank, seq_rank)
-    here = (jnp.arange(sub) == rank_low)[:, None] & (jnp.arange(high) == rank_high)[None, :]
-    qv_sums = qv_sums.reshape(2, own_heads, 1, 1, HEAD_DIM) * here.astype(F32)[None, None, :, :, None]
-    late = jnp.concatenate([spread(item) for item in sums_one] + [spread(qv_sums)], axis=2)
-    late = small_scatter(late, dp_rank, seq_rank)
-    share = attn_gain.shape[0]
+        blocks = exchange(grad_fc.reshape(seq_count, rows, dp_count * block), seq_rank)
+        if block % 128 == 0:
+            fc_places = lambda s: [(0, d, d * seq_count + s) for d in range(dp_count)]
+            grad_fc = lay_out(rank, [[item] for item in blocks], fc_weight.shape[1], (fc_places, block))
+        else:
+            blocks = [item.reshape(rows, dp_count, block) for item in by_rank(blocks, seq_rank)]
+            grad_fc = jnp.stack(blocks, axis=2).reshape(fc_weight.shape).astype(F32)
+        grad_qkv = scatter_dp(tn(normed_one, grads).astype(BF16))
+        blocks = [[item] for item in exchange(grad_qkv.reshape(seq_count, rows, 3 * own_width), seq_rank)]
+        qkv_places = lambda s: [
+            (0, part * own_heads + head, part * HEADS + (head * sub + s % sub) * high + s // sub)
+            for part in range(3)
+            for head in range(own_heads)
+        ]
+        grad_qkv_weight = lay_out(rank, blocks, qkv_weight.shape[1], (qkv_places, HEAD_DIM))
+
+        def spread(vector):
+            return vector.reshape(dp_count, seq_count, -1)
+
+        here = (jnp.arange(seq_count) == seq_rank).astype(F32)
+        hidden_sums = hidden_sums.reshape(dp_count, 1, -1) * here[None, :, None]
+        early = jnp.concatenate([spread(item) for item in sums_two] + [hidden_sums], axis=2)
+        early = small_scatter(early, dp_rank, seq_rank)
+        here = (jnp.arange(sub) == rank_low)[:, None] & (jnp.arange(high) == rank_high)[None, :]
+        qv_sums = qv_sums.reshape(2, own_heads, 1, 1, HEAD_DIM) * here.astype(F32)[None, None, :, :, None]
+        late = jnp.concatenate([spread(item) for item in sums_one] + [spread(qv_sums)], axis=2)
+        late = small_scatter(late, dp_rank, seq_rank)
     return (
         block_out[None],
         tokens_grad[None],

time: 920 us -> 715 us (0.78)
  waiting for transfers between devices: 176 us -> 3.82 us
  Pallas kernels: 617 us -> 659 us
  starting transfers between devices: 37.6 us -> 2.24 us
  local copies, waits for them, and re-layouts: 33.3 us -> 13 us
  matrix products: 29.3 us -> 9.12 us
    reduce_scatter x4 -> x2, waiting for transfers between devices: 127 us -> 3.74 us  [scatter_dp(): return lax.psum_scatter(value, 'dp', scatter_dimension=0, tiled=True)]
    ppermute x29 -> x0, starting transfers between devices: 35.8 us -> none  [the longest x28 34 us: shift(): return lax.ppermute(value, axis, [(i, i ^ distance) for i in range(count)])]
    ppermute x29 -> x0, waiting for transfers between devices: 30 us -> none  [the longest x28 30 us: shift(): return lax.ppermute(value, axis, [(i, i ^ distance) for i in range(count)])]
    pallas_call x1, Pallas kernels: 82.4 us -> 106 us  [closing(): pl.pallas_call(closing_kernel, in_specs=[inside, inside, anywhere, anywhe...]
    dot_general x2 -> x1, matrix products: 29.3 us -> 9.12 us  [tn(): lax.dot_general(left, right, (((0,), (0,)), ((), ())), preferred_element_...]
    pallas_call x6 -> x3, Pallas kernels: 459 us -> 476 us  [the longest x1 224 us: feed_plane(): pl.pallas_call(plane_kernel, in_specs=[anywhere] * 10 + [inside], out_spe...]
    all_gather x3 -> x1, waiting for transfers between devices: 16.9 us -> 0.02 us  [gather_dp(): return lax.all_gather(value, 'dp', axis=0, tiled=True)]
  transfers between devices with their start and end apart: 37 -> 4, of which waited for: 11 -> 1; matrix products, arithmetic and copies ran while one was open for 4% -> 2% of each run, Pallas kernels for 34% -> 44%
where the time goes in v7:
time: 715 us; the launch traced here: 705 us
  Pallas kernels  659 us (92%)
  between operations  14.9 us (2%)
  local copies, waits for them, and re-layouts  13 us (2%)
  matrix products  9.12 us (1%)
    pallas_call x1, Pallas kernels, feed_plane(): pl.pallas_call(plane_kernel, in_specs=[anywhere] * 10 + [inside], out_spe...  224 us
    pallas_call x1, Pallas kernels, opening(): pl.pallas_call(opening_kernel, in_specs=[anywhere] * 2 + [inside] * 5, ou...  127 us
    pallas_call x1, Pallas kernels, attend_plane(): pl.pallas_call(attend_plane_kernel, in_specs=[anywhere] * 7 + [inside] *...  126 us
    pallas_call x1, Pallas kernels, closing(): pl.pallas_call(closing_kernel, in_specs=[inside, inside, anywhere, anywhe...  106 us
    pallas_call x1, Pallas kernels, retreat_plane(): pl.pallas_call(retreat_plane_kernel, in_specs=[anywhere] * 8 + [inside] *...  76.2 us
  transfers between devices with their start and end apart: 4, of which 1 were waited for; matrix products, arithmetic and copies ran while one was open for 2% of the time, Pallas kernels for 44%

profile of v7, /device:TPU:0, one launch (start us, length us, event | category | flops | bytes accessed | tf_op | source)
XLA Modules:
  0.0 705.1 jit_solution(12003169705747073582)
XLA Ops:
  7.2 0.0 all-gather.2.cloned.1.call-start
  7.9 0.7 compare_reduce_fusion
  8.6 0.8 stack.27
  9.4 1.3 fusion.2.small
  10.7 126.8 %shard_map.263 = (bf16[2048,2048]{1,0:T(8,128)(2,1)}, bf16[2048,1536]{1,0:T(8,128)(2,1)}, bf16[256,2048]{1,0:T(8,128)(2,1)}, bf16[256,2048]{1,0:T(8,128)(2,1)}, ...) custom-call(bf16[512,2048]{1,0:T(8,128)(2,1)} %bitcast.37, ...), custom_call_target="tpu_custom_call" | custom-call | bytes 41943040 | tf_op jit(solution)/shard_map/pallas_call | solution.py:991
  137.5 0.0 all-gather.2.cloned.1.call-update
  137.5 0.0 reduce-scatter.3.cloned.1.call-start
  137.6 126.1 %shard_map.264 = (f32[512,2048]{1,0:T(8,128)}, bf16[512,2048]{1,0:T(8,128)(2,1)}, bf16[2048,512]{1,0:T(8,128)(2,1)}, f32[4,1,2048]{2,1,0:T(1,128)}, bf16[512,204...) custom-call(bf16[512,2048]{1,0:T(8,128)(2,1)} %bitcast.38, ...), custom_call_target="tpu_custom_call", output_to_operand_aliasing={{5}: (6, {})} | custom-call | flops 10737418240 | bytes 41943040 | tf_op jit(solution)/shard_map/pallas_call | solution.py:1166
  263.7 0.0 all-gather.2.cloned.1.call-done.fc
  263.8 223.5 %shard_map.265 = (f32[512,2048]{1,0:T(8,128)}, bf16[2048,2048]{1,0:T(8,128)(2,1)}, f32[4,2048]{1,0:T(4,128)}, f32[1,2048]{1,0:T(1,128)}, bf16[2048,2048]{1,0:T(8...) custom-call(bf16[512,2048]{1,0:T(8,128)(2,1)} %get-tuple-element.59., ...), custom_call_target="tpu_custom_call" | custom-call | flops 103079215104 | bytes 41943040 | tf_op jit(solution)/shard_map/pallas_call | solution.py:1432
  487.3 0.0 reduce-scatter.3.cloned.1.call-update
  487.3 0.0 reduce-scatter.5.cloned.1.call-start
  487.4 76.2 %shard_map.266 = (bf16[2048,1536]{1,0:T(8,128)(2,1)}, f32[2,512]{1,0:T(2,128)}, bf16[512,2048]{1,0:T(8,128)(2,1)}) custom-call(bf16[2048,2048]{1,0:T(8,128)(2,1)} %get-tuple-element.67.low_all, bf16[2048,512]{1,0:T(8,128)(2,1)} %get-tuple-element.68.q, bf16[2048,512]{1,0:T(8,128)(2,1)} %get-tuple-element.69.k, bf16[2048,512]{1,0:T(8,128)(2,1)} %get-tuple-element.70.v, ...), custom_call_target="tpu_custom_call" | custom-call | flops 21474836480 | bytes 41943040 | tf_op jit(solution)/shard_map/pallas_call | solution.py:1586
  563.6 9.1 %convolution_convert_fusion = bf16[512,2048]{1,0:T(8,128)(2,1)} fusion(bf16[2048,512]{1,0:T(8,128)(2,1)S(1)} %copy-done.5, bf16[2048,2048]{1,0:T(8,128)(2,1)} %get-tuple-element.67.low_all), kind=kOutput, calls=%fused_computation | convolution fusion | flops 4296015872 | bytes 12582912 | tf_op jit(solution)/shard_map/dot_general | solution.py:32
  572.7 3.7 reduce-scatter.3.cloned.1.call-done.fc_share
  576.5 106.4 %shard_map.267 = (f32[512,2048]{1,0:T(8,128)}, f32[64,6144]{1,0:T(8,128)}, f32[64,8192]{1,0:T(8,128)}, f32[8,512]{1,0:T(8,128)}) custom-call(bf16[2048,1536]{1,0:T(8,128)(2,1)} %get-tuple-element.75.grads, bf16[2048,1536]{1,0:T(8,128)(2,1)} %get-tuple-element.53.weight, bf16[2048,2048]{1,0:T(8,128)(2,1)} %get-tuple-element.76.normed_one, ...), custom_call_target="tpu_custom_call" | custom-call | flops 25769803776 | bytes 10485760 | tf_op jit(solution)/shard_map/pallas_call | solution.py:1802
  683.0 1.0 fusion.14
  683.9 0.6 fusion.12
  684.5 2.1 collective-permute-start
  686.7 0.5 fusion.9
  687.2 1.3 slice.30
  688.4 0.6 fusion.10
  689.0 0.6 fusion.7
  689.6 0.8 convert_element_type.21
  690.4 1.3 copy.38
  691.8 2.1 copy.39
  693.9 0.4 copy-done.4
  694.3 1.1 copy.40
  695.4 0.0 copy-done.3
  695.5 1.3 copy.41
  696.8 0.1 copy-done.1
  696.9 1.3 copy.42
  (14 shorter events, 0.1 us)
Async XLA Ops:
  7.2 256.6 %all-gather.2.cloned.1.call-start = ((), (), s32[]{:S(2)}) async-start(), calls=%async_computation.2 | async-start | bytes 9437184 | tf_op jit(solution)/shard_map/all_gather | solution.py:1909
  137.5 438.9 %reduce-scatter.3.cloned.1.call-start = ((), (), s32[]{:S(2)}) async-start(), calls=%async_computation.3 | async-start | bytes 9437184 | tf_op jit(solution)/shard_map/reduce_scatter | solution.py:1913
  487.3 197.2 %reduce-scatter.5.cloned.1.call-start = ((), (), s32[]{:S(2)}) async-start(), calls=%async_computation.4 | async-start | bytes 2359296 | tf_op jit(solution)/shard_map/reduce_scatter | solution.py:1913
  487.4 76.2 %copy-start.5 = (bf16[2048,512]{1,0:T(8,128)(2,1)S(1)}, bf16[2048,512]{1,0:T(8,128)(2,1)}, u32[]{:S(2)}) copy-start(bf16[2048,512]{1,0:T(8,128)(2,1)} %get-tuple-element.86) | copy-start | bytes 6291460
  576.5 113.9 %copy-start.2 = (bf16[512,2048]{1,0:T(8,128)(2,1)S(1)}, bf16[512,2048]{1,0:T(8,128)(2,1)}, u32[]{:S(2)}) copy-start(bf16[512,2048]{1,0:T(8,128)(2,1)} %get-tuple-element.74) | copy-start | bytes 6291460
  684.5 7.2 %copy-start = (f32[512,2048]{1,0:T(8,128)S(1)}, f32[512,2048]{1,0:T(8,128)}, u32[]{:S(2)}) copy-start(f32[512,2048]{1,0:T(8,128)} %get-tuple-element.82) | copy-start | bytes 12582916
  684.5 5.1 collective-permute-start
  691.8 2.5 copy-start.4
  691.8 3.7 copy-start.3
  694.3 2.6 copy-start.1
Sparse Core Ops, SparseCore 0:
  137.7 101.8 all-gather.1
  487.4 88.9 reduce-scatter.2
  579.3 36.7 reduce-scatter.4

commit v8 on v7

--- a/solution.py
+++ b/solution.py
@@ -582,16 +582,27 @@
             (level >= 1, self.hop(lax.rem(level + 3, 4), 1, 3, -1)),
         ]
 
+    def first_hops(self):
+        hops, inner = self.hops(), (self.level == 1) | (self.level == 2)
+        return hops[:2] + [(inner, hops[4][1]), (inner, hops[5][1])]
+
+    def later_hops(self):
+        hops = self.hops()
+        return hops[2:4] + [(self.level == 0, hops[4][1]), (self.level == 3, hops[5][1])]
+
     def passes(self):
         return [(self.level == 1, self.hop(3, 2, 1, 2)), (self.level == 2, self.hop(0, 2, 1, -2))]
 
-    def spread(self):
+    def combine(self):
         for item in self.swaps():
             item.wait_recv()
         self.add(
             self.source, self.mate_in, self.summed, 4, lambda i: 2 * i + self.core, lambda i: i, lambda i: i
         )
-        for condition, copy in self.hops():
+
+    def spread(self):
+        self.combine()
+        for condition, copy in self.first_hops():
             pl.when(condition)(lambda copy=copy: copy.start())
 
     def arrive(self, slot):
@@ -606,7 +617,7 @@
                 self.arrive(3)
                 self.add(self.summed, self.got, self.summed, 1, lambda i: at, lambda i: 3, lambda i: at)
 
-        for condition, copy in self.passes():
+        for condition, copy in self.passes() + self.later_hops():
             pl.when(condition)(lambda copy=copy: copy.start())
 
     def finish(self, out):
@@ -638,6 +649,66 @@
             pl.when(condition)(lambda copy=copy: copy.wait_send())
 
 
+class LateScatter(LevelScatter):
+    def __init__(self, summed, got, through, own, send, receive, load):
+        self.summed, self.got, self.through, self.own = summed, got, through, own
+        self.send, self.receive, self.load = send, receive, load
+        self.rows = own.shape[0]
+        self.place = lax.axis_index("dp")
+        self.level, self.core = lax.div(self.place, 2), lax.rem(self.place, 2)
+        self.mate = self.place + 1 - 2 * self.core
+
+    def loads(self):
+        passed_on = 3 * lax.rem(self.level, 2)
+        return (
+            pltpu.make_async_copy(self.block(self.summed, self.level), self.own, self.load.at[0]),
+            pltpu.make_async_copy(self.block(self.summed, passed_on), self.through, self.load.at[1]),
+        )
+
+    def passes(self):
+        target = self.block(self.got, 2)
+        send, receive = self.send.at[4 + 1], self.receive.at[4 + 2]
+        return [
+            (self.level == 1, remote(self.through, target, send, receive, "dp", self.place + 4)),
+            (self.level == 2, remote(self.through, target, send, receive, "dp", self.place - 4)),
+        ]
+
+    def start(self):
+        for condition, copy in self.first_hops():
+            pl.when(condition)(lambda copy=copy: copy.start())
+        for item in self.loads():
+            item.start()
+
+    def part(self, slot):
+        return self.got[slot * self.rows : (slot + 1) * self.rows, :].astype(F32)
+
+    def pass_on(self):
+        for item in self.loads():
+            item.wait()
+
+        @pl.when((self.level == 1) | (self.level == 2))
+        def _():
+            self.arrive(3)
+            self.through[...] = (self.through[...].astype(F32) + self.part(3)).astype(BF16)
+
+        for condition, copy in self.passes() + self.later_hops():
+            pl.when(condition)(lambda copy=copy: copy.start())
+
+    def finish(self, out):
+        level = self.level
+        pl.when(level >= 1)(lambda: self.arrive(0))
+        pl.when(level <= 2)(lambda: self.arrive(1))
+        self.arrive(2)
+        value = self.own[...].astype(F32) + self.part(2)
+        value = value + jnp.where(level >= 1, self.part(0), 0.0)
+        value = value + jnp.where(level <= 2, self.part(1), 0.0)
+        out[...] = value.astype(BF16)
+
+    def close(self):
+        for condition, copy in self.hops() + self.passes():
+            pl.when(condition)(lambda copy=copy: copy.wait_send())
+
+
 class NearScatter(LevelScatter):
     def part(self, ref, at):
         return ref[pl.ds(pl.multiple_of(at * self.rows, self.rows), self.rows), :].astype(F32)
@@ -648,7 +719,7 @@
         for at in range(4):
             total = self.part(self.source, 2 * at + self.core) + self.part(self.mate_in, at)
             self.summed[at * self.rows : (at + 1) * self.rows, :] = total.astype(BF16)
-        for condition, copy in self.hops():
+        for condition, copy in self.first_hops():
             pl.when(condition)(lambda copy=copy: copy.start())
 
     def pass_on(self):
@@ -660,7 +731,7 @@
                 total = self.part(self.summed, at) + self.part(self.got, 3)
                 self.summed[at * self.rows : (at + 1) * self.rows, :] = total.astype(BF16)
 
-        for condition, copy in self.passes():
+        for condition, copy in self.passes() + self.later_hops():
             pl.when(condition)(lambda copy=copy: copy.start())
 
     def finish(self, out):
@@ -906,6 +977,8 @@
         own_full[array].start()
     for copy in fc_copies + later_kept:
         copy.start()
+    for copy in cot_copies:
+        copy.start()
     take(1)
     relay(2)
     take(2)
@@ -914,8 +987,6 @@
     token_one.wait_recv()
     token_two.wait_recv()
     for copy in token_three:
-        copy.start()
-    for copy in cot_copies:
         copy.start()
     take(3)
     for copy in later_kept + own_full:
@@ -1203,8 +1274,8 @@
 def plane_kernel(
     normed, cot_own, one_up, one_low, two_up, two_low, cot_three, fc, down, middle, vectors,
     grad_middle, low_all, sums, hidden_sums, active, hidden_grad, normed_all, cot_all, terms, grad_down, grad_fc,
-    mate_in, summed, got, down_share,
-    normed_buf, cot_buf, sum_ref, joined, passed, arrived, load, local, send, receive, level_send, level_receive,
+    mate_in, summed, got, down_share, fc_mate, fc_summed,
+    normed_buf, cot_buf, sum_ref, joined, passed, arrived, load, local, send, receive, level_send, level_receive, fc_send, fc_receive,
 ):
     piece, width = normed.shape
     half = piece // 2
@@ -1214,6 +1285,7 @@
     last = inner // tile - 1
     one, two = neighbours()
     scatter = LevelScatter(grad_down, mate_in, summed, got, level_send, level_receive)
+    fc_scatter = LevelScatter(grad_fc, fc_mate, fc_summed, None, fc_send, fc_receive)
     for device in (one, two):
         greet("seq", device)
     pl.semaphore_wait(pltpu.get_barrier_semaphore(), 2 + scatter.greet())
@@ -1412,10 +1484,14 @@
     multiply_down(2)
     scatter.pass_on()
     outer(normed_all, hidden_grad, grad_fc, (wide, tall))
+    fc_scatter.start()
     received(*low_near)
     start(*low_three)
+    fc_scatter.combine()
     scatter.finish(down_share)
     scatter.close()
+    for item in fc_scatter.swaps():
+        item.wait_send()
     received(*low_three)
     for item in (*normed_first, *normed_across, *normed_last, *across, *plain, *both, *low_near, *low_three):
         item.wait_send()
@@ -1432,12 +1508,13 @@
     return pl.pallas_call(
         plane_kernel,
         in_specs=[anywhere] * 10 + [inside],
-        out_specs=[anywhere, anywhere, inside, inside] + [anywhere] * 11,
+        out_specs=[anywhere, anywhere, inside, inside] + [anywhere] * 13,
         out_shape=[
             shape(piece, width, F32), shape(length, width), shape(4, width, F32), shape(1, inner, F32),
             shape(length, inner), shape(length, inner), shape(length, width), shape(length, width),
             shape(length, width), shape(inner, width), shape(width, inner),
             shape(inner // 2, width), shape(inner // 2, width), shape(inner // 2, width), shape(inner // 8, width, F32),
+            shape(width // 2, inner), shape(width // 2, inner),
         ],
         scratch_shapes=[
             pltpu.VMEM((8, half, width), BF16),
@@ -1446,7 +1523,7 @@
             pltpu.VMEM((2, half, width), BF16),
             pltpu.VMEM((2, half, width), BF16),
             pltpu.VMEM((2, 2, half, width), BF16),
-            dma((10,)), dma((16,)), dma((16,)), dma((16,)), dma((8,)), dma((8,)),
+            dma((10,)), dma((16,)), dma((16,)), dma((16,)), dma((8,)), dma((8,)), dma((4,)), dma((4,)),
         ],
         compiler_params=pltpu.CompilerParams(collective_id=1, has_side_effects=True, vmem_limit_bytes=60 * 2**20),
         cost_estimate=cost(12 * length * width * inner, 10 * length * width),
@@ -1454,10 +1531,10 @@
 
 
 def retreat_plane_kernel(
-    low_all, q, k, v, k_t, lse, terms, middle, key_bias, proj, vectors,
-    grads, column_sums, block_out,
+    low_all, q, k, v, k_t, lse, terms, middle, fc_summed, attended, key_bias, proj, vectors,
+    grads, column_sums, block_out, grad_proj, fc_share,
     prob_ref, chance_ref, grad_ref, key_sum, value_sum, rounded, own, passed, joined, arrived,
-    load, local, send, receive,
+    level_got, level_through, level_own, load, local, send, receive, level_send, level_receive, level_load,
 ):
     piece, width = middle.shape
     half = piece // 2
@@ -1465,9 +1542,10 @@
     heads = columns // HEAD_DIM
     rank = lax.axis_index("seq")
     one, two = neighbours()
+    scatter = LateScatter(fc_summed, level_got, level_through, level_own, level_send, level_receive, level_load)
     for device in (one, two):
         greet("seq", device)
-    pl.semaphore_wait(pltpu.get_barrier_semaphore(), 2)
+    pl.semaphore_wait(pltpu.get_barrier_semaphore(), 2 + scatter.greet())
     up, lower = pl.ds(0, half), pl.ds(half, half)
     rows = lambda at, start=0, size=piece: pl.ds(at * piece + start, size)
 
@@ -1488,6 +1566,7 @@
     )
     for item in (*across, plain_one, plain_two, *loads):
         item.start()
+    scatter.start()
     key_sum[...] = jnp.zeros_like(key_sum)
     value_sum[...] = jnp.zeros_like(value_sum)
 
@@ -1510,6 +1589,10 @@
             joined[1] = (own[1].astype(F32) + passed[0].astype(F32)).astype(BF16)
             joined_one.start()
             joined_two.start()
+
+        @pl.when((at == 1) & (head == 3))
+        def _():
+            scatter.pass_on()
 
         query, grad, base = query_ref[...], grad_ref[:, here], lse_ref[0]
 
@@ -1560,6 +1643,20 @@
     column_sums[1:2, :] = jnp.sum(values.astype(F32), axis=0, keepdims=True)
     keep = pltpu.make_async_copy(rounded, grads.at[:, pl.ds(columns, 2 * columns)], local.at[0])
     keep.start()
+    tile = min(512, width)
+
+    def outer_body(left, right, out):
+        out[...] = tn(left[...], right[...]).astype(BF16)
+
+    pltpu.emit_pipeline(
+        outer_body,
+        grid=(width // tile,),
+        in_specs=[
+            pl.BlockSpec((length, columns), lambda i: (0, 0)),
+            pl.BlockSpec((length, tile), lambda i: (0, i)),
+        ],
+        out_specs=[pl.BlockSpec((columns, tile), lambda i: (0, i))],
+    )(attended, low_all, grad_proj)
     for item in (plain_one, plain_two, joined_one, joined_two):
         item.wait_recv()
     part = min(128, piece)
@@ -1571,26 +1668,30 @@
 
     line = pl.BlockSpec((part, width), lambda i: (i, 0))
     pltpu.emit_pipeline(out_body, grid=(piece // part,), in_specs=[line] * 2, out_specs=[line])(middle, terms, block_out)
+    scatter.finish(fc_share)
+    scatter.close()
     keep.wait()
     for item in (*across, plain_one, plain_two, joined_one, joined_two):
         item.wait_send()
 
 
-def retreat_plane(low_all, q, k, v, k_t, lse, terms, middle, key_bias, proj, vectors):
+def retreat_plane(low_all, q, k, v, k_t, lse, terms, middle, fc_summed, attended, key_bias, proj, vectors):
     piece, width = middle.shape
     length, columns = q.shape
-    half = piece // 2
+    half, inner = piece // 2, fc_summed.shape[1]
     anywhere = pl.BlockSpec(memory_space=pltpu.HBM)
     inside = pl.BlockSpec(memory_space=pltpu.VMEM)
     dma = pltpu.SemaphoreType.DMA
     return pl.pallas_call(
         retreat_plane_kernel,
-        in_specs=[anywhere] * 8 + [inside] * 3,
-        out_specs=[anywhere, inside, anywhere],
+        in_specs=[anywhere] * 10 + [inside] * 3,
+        out_specs=[anywhere, inside, anywhere, anywhere, inside],
         out_shape=[
             jax.ShapeDtypeStruct((length, 3 * columns), BF16),
             jax.ShapeDtypeStruct((2, columns), F32),
             jax.ShapeDtypeStruct((piece, width), BF16),
+            jax.ShapeDtypeStruct((columns, width), BF16),
+            jax.ShapeDtypeStruct((width // 8, inner), BF16),
         ],
         scratch_shapes=[
             pltpu.VMEM((length, piece), F32),
@@ -1603,11 +1704,14 @@
             pltpu.VMEM((2, half, width), BF16),
             pltpu.VMEM((2, half, width), BF16),
             pltpu.VMEM((2, piece, width), BF16),
-            dma((2,)), dma((1,)), dma((6,)), dma((6,)),
+            pltpu.VMEM((width // 2, inner), BF16),
+            pltpu.VMEM((width // 8, inner), BF16),
+            pltpu.VMEM((width // 8, inner), BF16),
+            dma((2,)), dma((1,)), dma((6,)), dma((6,)), dma((8,)), dma((8,)), dma((2,)),
         ],
-        compiler_params=pltpu.CompilerParams(collective_id=3, has_side_effects=True, vmem_limit_bytes=60 * 2**20),
+        compiler_params=pltpu.CompilerParams(collective_id=3, has_side_effects=True, vmem_limit_bytes=62 * 2**20),
         cost_estimate=cost(8 * length * length * columns + 2 * length * columns * width, 10 * length * width),
-    )(low_all, q, k, v, k_t, lse, terms, middle, key_bias, proj, vectors)
+    )(low_all, q, k, v, k_t, lse, terms, middle, fc_summed, attended, key_bias, proj, vectors)
 
 
 def closing_kernel(
@@ -2025,12 +2129,11 @@
     if in_plane:
         cots = (cot_own, cot_one, one_low, cot_two, two_low, cot_three)
         results = feed_plane(normed_two, cots, fc_full, down_full, middle, vectors)
-        grad_middle, low_all, sums_two, hidden_sums, down_terms, grad_fc, grad_down = [
-            results[i] for i in (0, 1, 2, 3, 8, 10, 14)
+        grad_middle, low_all, sums_two, hidden_sums, down_terms, grad_down, fc_summed = [
+            results[i] for i in (0, 1, 2, 3, 8, 14, 16)
         ]
-        grad_fc = scatter_dp(grad_fc)
-        grads, qv_sums, block_out = retreat_plane(
-            low_all, q, keys, values, keys_t, lse, down_terms, middle, key_bias, proj_full, vectors
+        grads, qv_sums, block_out, grad_proj, grad_fc = retreat_plane(
+            low_all, q, keys, values, keys_t, lse, down_terms, middle, fc_summed, attended, key_bias, proj_full, vectors
         )
     else:
         normed_blocks = gather_blocks(normed_two)
@@ -2059,9 +2162,8 @@
         grad_q, low_all = shared
         grads = jnp.concatenate([grad_q, sums[0], sums[1]], axis=1)
         qv_sums = jnp.stack([jnp.sum(item.astype(F32), axis=0) for item in (grad_q, sums[1])])
-    grad_proj = tn(after(attended, grads), low_all).astype(BF16)
-    grad_proj = scatter_dp(after(grad_proj, grad_fc) if in_plane else grad_proj)
-    grad_proj = lax.ppermute(grad_proj, BOTH, swap).astype(F32)
+        grad_proj = tn(attended, low_all).astype(BF16)
+    grad_proj = lax.ppermute(scatter_dp(grad_proj), BOTH, swap).astype(F32)
     share = attn_gain.shape[0]
     if in_plane:
         tokens_grad, grad_qkv_weight, grad_fc, smalls = closing(

time: 715 us -> 711 us (level)
  matrix products: 9.12 us -> 0 us
  Pallas kernels: 659 us -> 668 us
    pallas_call x1, Pallas kernels: 76.2 us -> 86.4 us  [retreat_plane(): pl.pallas_call(retreat_plane_kernel, in_specs=[anywhere] * 10 + [inside]...]
    dot_general x1 -> x0, matrix products: 9.12 us -> none  [tn(): lax.dot_general(left, right, (((0,), (0,)), ((), ())), preferred_element_...]
  transfers between devices with their start and end apart: 4 -> 3, of which waited for: 1 -> 0; matrix products, arithmetic and copies ran while one was open for 2% -> 1% of each run, Pallas kernels for 44% -> 34%
where the time goes in v8:
time: 711 us; the launch traced here: 701 us
  Pallas kernels  668 us (94%)
  between operations  15.2 us (2%)
  local copies, waits for them, and re-layouts  13 us (2%)
    pallas_call x1, Pallas kernels, feed_plane(): pl.pallas_call(plane_kernel, in_specs=[anywhere] * 10 + [inside], out_spe...  223 us
    pallas_call x1, Pallas kernels, attend_plane(): pl.pallas_call(attend_plane_kernel, in_specs=[anywhere] * 7 + [inside] *...  130 us
    pallas_call x1, Pallas kernels, opening(): pl.pallas_call(opening_kernel, in_specs=[anywhere] * 2 + [inside] * 5, ou...  122 us
    pallas_call x1, Pallas kernels, closing(): pl.pallas_call(closing_kernel, in_specs=[inside, inside, anywhere, anywhe...  107 us
    pallas_call x1, Pallas kernels, retreat_plane(): pl.pallas_call(retreat_plane_kernel, in_specs=[anywhere] * 10 + [inside]...  86.4 us
  transfers between devices with their start and end apart: 3, of which 0 were waited for; matrix products, arithmetic and copies ran while one was open for 1% of the time, Pallas kernels for 34%

profile of v8, /device:TPU:0, one launch (start us, length us, event | category | flops | bytes accessed | tf_op | source)
XLA Modules:
  0.0 701.1 jit_solution(11128787558378741671)
XLA Ops:
  7.2 0.0 all-gather.2.cloned.1.call-start
  7.9 0.7 compare_reduce_fusion
  8.6 0.8 stack.27
  9.4 1.3 fusion.2.small
  10.7 122.2 %shard_map.263 = (bf16[2048,2048]{1,0:T(8,128)(2,1)}, bf16[2048,1536]{1,0:T(8,128)(2,1)}, bf16[256,2048]{1,0:T(8,128)(2,1)}, bf16[256,2048]{1,0:T(8,128)(2,1)}, ...) custom-call(bf16[512,2048]{1,0:T(8,128)(2,1)} %bitcast.35, ...), custom_call_target="tpu_custom_call" | custom-call | bytes 41943040 | tf_op jit(solution)/shard_map/pallas_call | solution.py:1062
  132.9 0.0 all-gather.2.cloned.1.call-update
  133.0 0.0 reduce-scatter.2.cloned.1.call-start
  133.0 129.7 %shard_map.264 = (f32[512,2048]{1,0:T(8,128)}, bf16[512,2048]{1,0:T(8,128)(2,1)}, bf16[2048,512]{1,0:T(8,128)(2,1)}, f32[4,1,2048]{2,1,0:T(1,128)}, bf16[512,204...) custom-call(bf16[512,2048]{1,0:T(8,128)(2,1)} %bitcast.36, ...), custom_call_target="tpu_custom_call", output_to_operand_aliasing={{5}: (6, {})} | custom-call | flops 10737418240 | bytes 41943040 | tf_op jit(solution)/shard_map/pallas_call | solution.py:1237
  262.8 0.0 all-gather.2.cloned.1.call-done.fc
  262.8 222.7 %shard_map.265 = (f32[512,2048]{1,0:T(8,128)}, bf16[2048,2048]{1,0:T(8,128)(2,1)}, f32[4,2048]{1,0:T(4,128)}, f32[1,2048]{1,0:T(1,128)}, bf16[2048,2048]{1,0:T(8...) custom-call(bf16[512,2048]{1,0:T(8,128)(2,1)} %get-tuple-element.59., ...), custom_call_target="tpu_custom_call" | custom-call | flops 103079215104 | bytes 41943040 | tf_op jit(solution)/shard_map/pallas_call | solution.py:1508
  485.5 86.4 %shard_map.266 = (bf16[2048,1536]{1,0:T(8,128)(2,1)}, f32[2,512]{1,0:T(2,128)}, bf16[512,2048]{1,0:T(8,128)(2,1)}, bf16[512,2048]{1,0:T(8,128)(2,1)}, bf16[256,2048]{1,0:T(8,128)(2,1)}) custom-call(bf16[2048,2048]{1,0:T(8,128)(2,1)} %get-tuple-element.67.low_all, bf16[2048,512]{1,0:T(8,128)(2,1)} %get-tuple-element.68.q, ...), custom_call_target="tpu_custom_call" | custom-call | flops 21474836480 | bytes 41943040 | tf_op jit(solution)/shard_map/pallas_call | solution.py:1685
  571.9 0.0 reduce-scatter.2.cloned.1.call-update
  572.0 0.0 copy-start.2
  572.0 106.6 %shard_map.267 = (f32[512,2048]{1,0:T(8,128)}, f32[64,6144]{1,0:T(8,128)}, f32[64,8192]{1,0:T(8,128)}, f32[8,512]{1,0:T(8,128)}) custom-call(bf16[2048,1536]{1,0:T(8,128)(2,1)} %get-tuple-element.77.grads, bf16[2048,1536]{1,0:T(8,128)(2,1)} %get-tuple-element.53.weight, bf16[2048,2048]{1,0:T(8,128)(2,1)} %get-tuple-element.78.normed_one, ...), custom_call_target="tpu_custom_call" | custom-call | flops 25769803776 | bytes 10485760 | tf_op jit(solution)/shard_map/pallas_call | solution.py:1906
  678.6 1.0 fusion.14
  679.6 0.6 fusion.12
  680.2 2.1 collective-permute-start
  682.3 0.5 fusion.9
  682.8 1.3 slice.30
  684.0 0.6 fusion.10
  684.6 0.6 fusion.7
  685.2 0.0 collective-permute-done
  685.2 0.8 convert_element_type.17
  686.1 0.0 copy-done.2
  686.1 1.3 copy.38
  687.4 2.1 copy.39
  689.5 0.4 copy-done.4
  689.9 1.1 copy.40
  691.1 0.0 copy-done.3
  691.1 1.3 copy.41
  692.4 0.1 copy-done.1
  692.5 1.3 copy.42
  (8 shorter events, 0.0 us)
Async XLA Ops:
  7.2 255.6 %all-gather.2.cloned.1.call-start = ((), (), s32[]{:S(2)}) async-start(), calls=%async_computation.1 | async-start | bytes 9437184 | tf_op jit(solution)/shard_map/all_gather | solution.py:2013
  133.0 547.2 %reduce-scatter.2.cloned.1.call-start = ((), (), s32[]{:S(2)}) async-start(), calls=%async_computation.2 | async-start | bytes 2359296 | tf_op jit(solution)/shard_map/reduce_scatter | solution.py:2017
  572.0 114.1 %copy-start.2 = (bf16[512,2048]{1,0:T(8,128)(2,1)S(1)}, bf16[512,2048]{1,0:T(8,128)(2,1)}, u32[]{:S(2)}) copy-start(bf16[512,2048]{1,0:T(8,128)(2,1)} %get-tuple-element.76) | copy-start | bytes 6291460
  680.2 7.2 %copy-start = (f32[512,2048]{1,0:T(8,128)S(1)}, f32[512,2048]{1,0:T(8,128)}, u32[]{:S(2)}) copy-start(f32[512,2048]{1,0:T(8,128)} %get-tuple-element.84) | copy-start | bytes 12582916
  680.2 5.1 collective-permute-start
  687.4 2.5 copy-start.4
  687.4 3.7 copy-start.3
  689.9 2.6 copy-start.1
Sparse Core Ops, SparseCore 0:
  133.1 99.6 all-gather.1
  572.1 34.6 reduce-scatter.1

commit v9 on v8

--- a/solution.py
+++ b/solution.py
@@ -1564,7 +1564,7 @@
         pltpu.make_async_copy(terms.at[rows(1, half, half)], own.at[0], load.at[0]),
         pltpu.make_async_copy(terms.at[rows(2, 0, half)], own.at[1], load.at[1]),
     )
-    for item in (*across, plain_one, plain_two, *loads):
+    for item in (*across, *loads):
         item.start()
     scatter.start()
     key_sum[...] = jnp.zeros_like(key_sum)
@@ -1587,8 +1587,8 @@
                 item.wait()
             joined[0] = (own[0].astype(F32) + passed[1].astype(F32)).astype(BF16)
             joined[1] = (own[1].astype(F32) + passed[0].astype(F32)).astype(BF16)
-            joined_one.start()
-            joined_two.start()
+            for item in (plain_one, plain_two, joined_one, joined_two):
+                item.start()
 
         @pl.when((at == 1) & (head == 3))
         def _():
@@ -1715,16 +1715,24 @@
 
 
 def closing_kernel(
-    grads, weight, normed_one, tokens, grad_middle, vectors, sums_two, hidden_sums, qv_sums, fc_share,
+    grads_in, weight_in, normed_one, tokens, grad_middle, vectors, sums_two, hidden_sums, qv_sums, fc_share,
     tokens_grad, qkv_out, fc_out, small_out,
     terms, passed, joined, arrived, qkv_in, fc_in, mine, small_in, small_rows, small_got,
-    grad_qkv, mate_in, summed, got, qkv_share,
+    grad_qkv, mate_in, summed, got, qkv_share, grads, weight,
     send, receive, level_send, level_receive, small_send, small_receive, load,
 ):
     pieces = [[ref.at[i] for ref in (grad_qkv, mate_in, summed, got, qkv_share)] for i in range(2)]
     piece, width = tokens.shape
     half = piece // 2
     columns = grads.shape[1]
+    farthest, others_in = pl.ds(3 * piece, piece), pl.ds(0, 3 * piece)
+    early = (
+        pltpu.make_async_copy(weight_in, weight, load.at[3]),
+        pltpu.make_async_copy(grads_in.at[farthest], grads.at[farthest], load.at[4]),
+    )
+    later = pltpu.make_async_copy(grads_in.at[others_in], grads.at[others_in], load.at[5])
+    for item in (*early, later):
+        item.start()
     heads = columns // (3 * HEAD_DIM)
     me, place = lax.axis_index("seq"), lax.axis_index("dp")
     one, two = neighbours()
@@ -1788,9 +1796,12 @@
             in_specs=[pl.BlockSpec((normed_one.shape[0], tile), lambda i: (0, i))],
         )(normed_one)
 
+    for item in early:
+        item.wait()
     back_term(3)
     for item in across:
         item.start()
+    later.wait()
     back_term(1)
     plain_one.start()
     outer(0)
@@ -1905,7 +1916,7 @@
     dma = pltpu.SemaphoreType.DMA
     return pl.pallas_call(
         closing_kernel,
-        in_specs=[inside, inside, anywhere, anywhere, anywhere, inside, inside, inside, inside, anywhere],
+        in_specs=[anywhere] * 5 + [inside] * 4 + [anywhere],
         out_specs=[anywhere, inside, inside, inside],
         out_shape=[
             shape(piece, width, F32), shape(fine, 4 * columns, F32), shape(fine, 4 * fc_share.shape[1], F32),
@@ -1926,7 +1937,9 @@
                 pltpu.VMEM((2, count, columns // 2), BF16)
                 for count in (width, width // 2, width // 2, width // 2, width // 8)
             ],
-            dma((21,)), dma((21,)), dma((2, 8)), dma((2, 8)), dma((7,)), dma((7,)), dma((3,)),
+            pltpu.VMEM(grads.shape, BF16),
+            pltpu.VMEM(weight.shape, BF16),
+            dma((21,)), dma((21,)), dma((2, 8)), dma((2, 8)), dma((7,)), dma((7,)), dma((6,)),
         ],
         compiler_params=pltpu.CompilerParams(collective_id=4, has_side_effects=True, vmem_limit_bytes=60 * 2**20),
         cost_estimate=cost(16 * piece * width * columns, 10 * piece * width),

time: 711 us -> 706 us (level)
  no operation moved by 1% of the time
where the time goes in v9:
time: 706 us; the launch traced here: 696 us
  Pallas kernels  663 us (94%)
  between operations  15.2 us (2%)
  local copies, waits for them, and re-layouts  13 us (2%)
    pallas_call x1, Pallas kernels, feed_plane(): pl.pallas_call(plane_kernel, in_specs=[anywhere] * 10 + [inside], out_spe...  223 us
    pallas_call x1, Pallas kernels, attend_plane(): pl.pallas_call(attend_plane_kernel, in_specs=[anywhere] * 7 + [inside] *...  130 us
    pallas_call x1, Pallas kernels, opening(): pl.pallas_call(opening_kernel, in_specs=[anywhere] * 2 + [inside] * 5, ou...  122 us
    pallas_call x1, Pallas kernels, closing(): pl.pallas_call(closing_kernel, in_specs=[anywhere] * 5 + [inside] * 4 + [...  105 us
    pallas_call x1, Pallas kernels, retreat_plane(): pl.pallas_call(retreat_plane_kernel, in_specs=[anywhere] * 10 + [inside]...  83.9 us
  transfers between devices with their start and end apart: 3, of which 0 were waited for; matrix products, arithmetic and copies ran while one was open for 1% of the time, Pallas kernels for 34%

profile of v9, /device:TPU:0, one launch (start us, length us, event | category | flops | bytes accessed | tf_op | source)
XLA Modules:
  0.0 696.4 jit_solution(7658431184458528978)
XLA Ops:
  7.2 0.0 all-gather.2.cloned.1.call-start
  7.9 0.7 compare_reduce_fusion
  8.6 0.8 stack.27
  9.4 1.3 fusion.2.small
  10.7 122.2 %shard_map.263 = (bf16[2048,2048]{1,0:T(8,128)(2,1)}, bf16[2048,1536]{1,0:T(8,128)(2,1)}, bf16[256,2048]{1,0:T(8,128)(2,1)}, bf16[256,2048]{1,0:T(8,128)(2,1)}, ...) custom-call(bf16[512,2048]{1,0:T(8,128)(2,1)} %bitcast.35, ...), custom_call_target="tpu_custom_call" | custom-call | bytes 41943040 | tf_op jit(solution)/shard_map/pallas_call | solution.py:1062
  132.9 0.0 all-gather.2.cloned.1.call-update
  133.0 0.0 reduce-scatter.2.cloned.1.call-start
  133.0 129.7 %shard_map.264 = (f32[512,2048]{1,0:T(8,128)}, bf16[512,2048]{1,0:T(8,128)(2,1)}, bf16[2048,512]{1,0:T(8,128)(2,1)}, f32[4,1,2048]{2,1,0:T(1,128)}, bf16[512,204...) custom-call(bf16[512,2048]{1,0:T(8,128)(2,1)} %bitcast.36, ...), custom_call_target="tpu_custom_call", output_to_operand_aliasing={{5}: (6, {})} | custom-call | flops 10737418240 | bytes 41943040 | tf_op jit(solution)/shard_map/pallas_call | solution.py:1237
  262.8 0.0 all-gather.2.cloned.1.call-done.fc
  262.8 222.7 %shard_map.265 = (f32[512,2048]{1,0:T(8,128)}, bf16[2048,2048]{1,0:T(8,128)(2,1)}, f32[4,2048]{1,0:T(4,128)}, f32[1,2048]{1,0:T(1,128)}, bf16[2048,2048]{1,0:T(8...) custom-call(bf16[512,2048]{1,0:T(8,128)(2,1)} %get-tuple-element.59., ...), custom_call_target="tpu_custom_call" | custom-call | flops 103079215104 | bytes 41943040 | tf_op jit(solution)/shard_map/pallas_call | solution.py:1508
  485.5 83.9 %shard_map.266 = (bf16[2048,1536]{1,0:T(8,128)(2,1)}, f32[2,512]{1,0:T(2,128)}, bf16[512,2048]{1,0:T(8,128)(2,1)}, bf16[512,2048]{1,0:T(8,128)(2,1)}, bf16[256,2048]{1,0:T(8,128)(2,1)}) custom-call(bf16[2048,2048]{1,0:T(8,128)(2,1)} %get-tuple-element.67.low_all, bf16[2048,512]{1,0:T(8,128)(2,1)} %get-tuple-element.68.q, ...), custom_call_target="tpu_custom_call" | custom-call | flops 21474836480 | bytes 41943040 | tf_op jit(solution)/shard_map/pallas_call | solution.py:1685
  569.4 0.0 reduce-scatter.2.cloned.1.call-update
  569.4 0.0 copy-start.2
  569.4 104.5 %shard_map.267 = (f32[512,2048]{1,0:T(8,128)}, f32[64,6144]{1,0:T(8,128)}, f32[64,8192]{1,0:T(8,128)}, f32[8,512]{1,0:T(8,128)}) custom-call(bf16[2048,1536]{1,0:T(8,128)(2,1)} %get-tuple-element.77.grads_in, bf16[2048,1536]{1,0:T(8,128)(2,1)} %get-tuple-element.53.weight.weight_in, bf16[2048,2048]{1,0:T(8,128)(2,1)} %get-tuple-element.78.normed_one, ...), custom_call_target="tpu_custom_call" | custom-call | flops 25769803776 | bytes 10485760 | tf_op jit(solution)/shard_map/pallas_call | solution.py:1917
  673.9 1.0 fusion.14
  674.9 0.6 fusion.12
  675.5 2.1 collective-permute-start
  677.6 0.5 fusion.9
  678.1 1.3 slice.30
  679.4 0.6 fusion.10
  680.0 0.6 fusion.7
  680.6 0.0 collective-permute-done
  680.6 0.8 convert_element_type.17
  681.4 0.0 copy-done.2
  681.4 1.3 copy.38
  682.7 2.1 copy.39
  684.9 0.4 copy-done.4
  685.3 1.1 copy.40
  686.4 0.0 copy-done.3
  686.4 1.3 copy.41
  687.8 0.1 copy-done.1
  687.8 1.3 copy.42
  (8 shorter events, 0.0 us)
Async XLA Ops:
  7.2 255.6 %all-gather.2.cloned.1.call-start = ((), (), s32[]{:S(2)}) async-start(), calls=%async_computation.1 | async-start | bytes 9437184 | tf_op jit(solution)/shard_map/all_gather | solution.py:2026
  133.0 542.5 %reduce-scatter.2.cloned.1.call-start = ((), (), s32[]{:S(2)}) async-start(), calls=%async_computation.2 | async-start | bytes 2359296 | tf_op jit(solution)/shard_map/reduce_scatter | solution.py:2030
  569.4 112.0 %copy-start.2 = (bf16[512,2048]{1,0:T(8,128)(2,1)S(1)}, bf16[512,2048]{1,0:T(8,128)(2,1)}, u32[]{:S(2)}) copy-start(bf16[512,2048]{1,0:T(8,128)(2,1)} %get-tuple-element.76) | copy-start | bytes 6291460
  675.5 7.2 %copy-start = (f32[512,2048]{1,0:T(8,128)S(1)}, f32[512,2048]{1,0:T(8,128)}, u32[]{:S(2)}) copy-start(f32[512,2048]{1,0:T(8,128)} %get-tuple-element.84) | copy-start | bytes 12582916
  675.5 5.1 collective-permute-start
  682.7 2.5 copy-start.4
  682.7 3.7 copy-start.3
  685.3 2.6 copy-start.1
Sparse Core Ops, SparseCore 0:
  133.1 99.6 all-gather.1
  569.5 40.2 reduce-scatter.1

commit v10 on v9

--- a/solution.py
+++ b/solution.py
@@ -818,13 +818,21 @@
 
 
 def opening_kernel(
-    tokens, cot, qkv_weight, fc_weight, small, down, proj,
+    tokens, cot, qkv_in, fc_in, small, down_in, proj_in,
     token_all, qkv_full, fc_rows, cot_one, cot_two, down_full, proj_full, vectors, key_bias,
-    qkv_pieces, fc_pieces, token_buf, qkv_rows, small_rows, small_full, proj_rows, square, local, send, receive, up_send, up_receive, down_send, down_receive, mate_send, mate_receive,
+    qkv_weight, fc_weight, down, proj, entry, qkv_pieces, fc_pieces, token_buf, qkv_rows, small_rows, small_full, proj_rows, square, local, send, receive, up_send, up_receive, down_send, down_receive, mate_send, mate_receive,
     level_send, level_receive, level_mate_send, level_mate_receive,
 ):
     piece = tokens.shape[0]
     half = piece // 2
+    entries = [
+        pltpu.make_async_copy(source, target, entry.at[i])
+        for i, (source, target) in enumerate(
+            ((qkv_in, qkv_weight), (proj_in, proj), (down_in, down), (fc_in, fc_weight))
+        )
+    ]
+    for copy in entries:
+        copy.start()
     gather = LevelGather(down, down_full, level_send, level_receive, level_mate_send, level_mate_receive)
     me, place = lax.axis_index("seq"), lax.axis_index("dp")
     one, two = neighbours()
@@ -847,6 +855,7 @@
         pl.semaphore_signal(pltpu.get_barrier_semaphore(), inc=1, device_id=partner, device_id_type=MESH)
 
     heads = qkv_pieces.shape[2] // (3 * HEAD_DIM)
+    entries[0].wait()
     for rank in range(4):
         for part in range(3):
             for head in range(heads):
@@ -946,6 +955,7 @@
 
     for copy in qkv_copies + small_copies + first_kept:
         copy.start()
+    entries[1].wait()
     pl.when(swaps)(proj_copy.start)
 
     @pl.when(jnp.logical_not(swaps))
@@ -954,11 +964,13 @@
 
     token_one.start()
     token_two.start()
+    entries[2].wait()
     gather.start(gather.near())
     gather.across(4, level).start()
     down_kept = pltpu.make_async_copy(down, gather.shard(level), local.at[8])
     down_kept.start()
     token_load.start()
+    entries[3].wait()
     inner = fc_pieces.shape[2] // 8
     for rank in range(4):
         for d in range(8):
@@ -1061,7 +1073,7 @@
     rows, fine = 4 * own_rows, 4 * small.shape[0]
     return pl.pallas_call(
         opening_kernel,
-        in_specs=[anywhere] * 2 + [inside] * 5,
+        in_specs=[anywhere] * 4 + [inside] + [anywhere] * 2,
         out_specs=[anywhere] * 7 + [inside] * 2,
         out_shape=[
             shape(4 * piece, width),
@@ -1075,6 +1087,7 @@
             jax.ShapeDtypeStruct((4 * piece, 1), F32),
         ],
         scratch_shapes=[
+            *[pltpu.VMEM(item.shape, BF16) for item in (qkv_weight, fc_weight, down, proj)], dma((4,)),
             pltpu.VMEM((4, own_rows, columns), BF16), pltpu.VMEM((4, own_rows, inner), BF16),
             pltpu.VMEM((piece, width), BF16),
             pltpu.VMEM((rows, columns), BF16), pltpu.VMEM((fine, 128), BF16), pltpu.VMEM((fine * dp_count, 128), BF16),
@@ -1088,13 +1101,18 @@
 
 
 def attend_plane_kernel(
-    tokens, cot, token_all, weight, cot_one, down, down_in, key_bias, proj, vectors,
+    tokens, cot, token_all, weight, cot_one, down, down_in, bias_in, proj_in, vectors,
     middle, normed, attended, lse, cot_three, down_full, normed_one, q, k, v, k_t, v_t, one_low, two_low,
-    score_ref, joint, terms, passed, joined, arrived, send, receive,
+    key_bias, proj, entry, score_ref, joint, terms, passed, joined, arrived, send, receive,
     level_send, level_receive, mate_send, mate_receive,
 ):
     piece, width = tokens.shape
     half = piece // 2
+    entries = (
+        pltpu.make_async_copy(bias_in, key_bias, entry.at[0]), pltpu.make_async_copy(proj_in, proj, entry.at[1])
+    )
+    for item in entries:
+        item.start()
     length, columns = q.shape
     heads = columns // HEAD_DIM
     rank = lax.axis_index("seq")
@@ -1131,6 +1149,8 @@
     for item in low_copies:
         item.wait_recv()
     cot_copies[1].start()
+    for item in entries:
+        item.wait()
 
     def body(query_ref, key_ref, value_t, attended_tile, lse_tile):
         group, head = pl.program_id(0), pl.program_id(1)
@@ -1236,7 +1256,7 @@
     dma = pltpu.SemaphoreType.DMA
     return pl.pallas_call(
         attend_plane_kernel,
-        in_specs=[anywhere] * 7 + [inside] * 3,
+        in_specs=[anywhere] * 9 + [inside],
         out_specs=[anywhere] * 14,
         input_output_aliases={6: 5},
         out_shape=[
@@ -1246,6 +1266,9 @@
             *[shape(half, width)] * 2,
         ],
         scratch_shapes=[
+            pltpu.VMEM(key_bias.shape, F32),
+            pltpu.VMEM(proj.shape, BF16),
+            dma((2,)),
             pltpu.VMEM((length, piece), F32),
             pltpu.VMEM((piece, columns), BF16),
             pltpu.VMEM((4, piece, width), BF16),
@@ -1531,13 +1554,18 @@
 
 
 def retreat_plane_kernel(
-    low_all, q, k, v, k_t, lse, terms, middle, fc_summed, attended, key_bias, proj, vectors,
+    low_all, q, k, v, k_t, lse, terms, middle, fc_summed, attended, bias_in, proj_in, vectors,
     grads, column_sums, block_out, grad_proj, fc_share,
-    prob_ref, chance_ref, grad_ref, key_sum, value_sum, rounded, own, passed, joined, arrived,
+    key_bias, proj, entry, prob_ref, chance_ref, grad_ref, key_sum, value_sum, rounded, own, passed, joined, arrived,
     level_got, level_through, level_own, load, local, send, receive, level_send, level_receive, level_load,
 ):
     piece, width = middle.shape
     half = piece // 2
+    entries = (
+        pltpu.make_async_copy(bias_in, key_bias, entry.at[0]), pltpu.make_async_copy(proj_in, proj, entry.at[1])
+    )
+    for item in entries:
+        item.start()
     length, columns = q.shape
     heads = columns // HEAD_DIM
     rank = lax.axis_index("seq")
@@ -1569,6 +1597,8 @@
     scatter.start()
     key_sum[...] = jnp.zeros_like(key_sum)
     value_sum[...] = jnp.zeros_like(value_sum)
+    for item in entries:
+        item.wait()
 
     def body(low_ref, query_ref, key_ref, value_ref, key_t, lse_ref, query_out):
         at, head = pl.program_id(0), pl.program_id(1)
@@ -1684,7 +1714,7 @@
     dma = pltpu.SemaphoreType.DMA
     return pl.pallas_call(
         retreat_plane_kernel,
-        in_specs=[anywhere] * 10 + [inside] * 3,
+        in_specs=[anywhere] * 12 + [inside],
         out_specs=[anywhere, inside, anywhere, anywhere, inside],
         out_shape=[
             jax.ShapeDtypeStruct((length, 3 * columns), BF16),
@@ -1694,6 +1724,9 @@
             jax.ShapeDtypeStruct((width // 8, inner), BF16),
         ],
         scratch_shapes=[
+            pltpu.VMEM(key_bias.shape, F32),
+            pltpu.VMEM(proj.shape, BF16),
+            dma((2,)),
             pltpu.VMEM((length, piece), F32),
             pltpu.VMEM((length, piece), F32),
             pltpu.VMEM((piece, columns), BF16),

time: 706 us -> 703 us (level)
  no operation moved by 1% of the time
where the time goes in v10:
time: 703 us; the launch traced here: 694 us
  Pallas kernels  660 us (94%)
  between operations  15.2 us (2%)
  local copies, waits for them, and re-layouts  13 us (2%)
    pallas_call x1, Pallas kernels, feed_plane(): pl.pallas_call(plane_kernel, in_specs=[anywhere] * 10 + [inside], out_spe...  223 us
    pallas_call x1, Pallas kernels, attend_plane(): pl.pallas_call(attend_plane_kernel, in_specs=[anywhere] * 9 + [inside], o...  129 us
    pallas_call x1, Pallas kernels, opening(): pl.pallas_call(opening_kernel, in_specs=[anywhere] * 4 + [inside] + [anyw...  121 us
    pallas_call x1, Pallas kernels, closing(): pl.pallas_call(closing_kernel, in_specs=[anywhere] * 5 + [inside] * 4 + [...  105 us
    pallas_call x1, Pallas kernels, retreat_plane(): pl.pallas_call(retreat_plane_kernel, in_specs=[anywhere] * 12 + [inside],...  82.8 us
  transfers between devices with their start and end apart: 3, of which 0 were waited for; matrix products, arithmetic and copies ran while one was open for 1% of the time, Pallas kernels for 34%

profile of v10, /device:TPU:0, one launch (start us, length us, event | category | flops | bytes accessed | tf_op | source)
XLA Modules:
  0.0 693.8 jit_solution(5558902654112679984)
XLA Ops:
  7.2 0.0 all-gather.2.cloned.1.call-start
  7.9 0.7 compare_reduce_fusion
  8.6 0.8 stack.27
  9.4 1.3 fusion.2.small
  10.7 121.1 %shard_map.263 = (bf16[2048,2048]{1,0:T(8,128)(2,1)}, bf16[2048,1536]{1,0:T(8,128)(2,1)}, bf16[256,2048]{1,0:T(8,128)(2,1)}, bf16[256,2048]{1,0:T(8,128)(2,1)}, ...) custom-call(bf16[512,2048]{1,0:T(8,128)(2,1)} %bitcast.35, ...), custom_call_target="tpu_custom_call" | custom-call | bytes 41943040 | tf_op jit(solution)/shard_map/pallas_call | solution.py:1074
  131.8 0.0 all-gather.2.cloned.1.call-update
  131.9 0.0 reduce-scatter.2.cloned.1.call-start
  131.9 128.7 %shard_map.264 = (f32[512,2048]{1,0:T(8,128)}, bf16[512,2048]{1,0:T(8,128)(2,1)}, bf16[2048,512]{1,0:T(8,128)(2,1)}, f32[4,1,2048]{2,1,0:T(1,128)}, bf16[512,204...) custom-call(bf16[512,2048]{1,0:T(8,128)(2,1)} %bitcast.36, ...), custom_call_target="tpu_custom_call", output_to_operand_aliasing={{5}: (6, {})} | custom-call | flops 10737418240 | bytes 41943040 | tf_op jit(solution)/shard_map/pallas_call | solution.py:1257
  260.6 0.0 all-gather.2.cloned.1.call-done.fc
  260.7 222.7 %shard_map.265 = (f32[512,2048]{1,0:T(8,128)}, bf16[2048,2048]{1,0:T(8,128)(2,1)}, f32[4,2048]{1,0:T(4,128)}, f32[1,2048]{1,0:T(1,128)}, bf16[2048,2048]{1,0:T(8...) custom-call(bf16[512,2048]{1,0:T(8,128)(2,1)} %get-tuple-element.59., ...), custom_call_target="tpu_custom_call" | custom-call | flops 103079215104 | bytes 41943040 | tf_op jit(solution)/shard_map/pallas_call | solution.py:1531
  483.4 82.8 %shard_map.266 = (bf16[2048,1536]{1,0:T(8,128)(2,1)}, f32[2,512]{1,0:T(2,128)}, bf16[512,2048]{1,0:T(8,128)(2,1)}, bf16[512,2048]{1,0:T(8,128)(2,1)}, bf16[256,2048]{1,0:T(8,128)(2,1)}) custom-call(bf16[2048,2048]{1,0:T(8,128)(2,1)} %get-tuple-element.67.low_all, bf16[2048,512]{1,0:T(8,128)(2,1)} %get-tuple-element.68.q, ...), custom_call_target="tpu_custom_call" | custom-call | flops 21474836480 | bytes 41943040 | tf_op jit(solution)/shard_map/pallas_call | solution.py:1715
  566.2 0.0 reduce-scatter.2.cloned.1.call-update
  566.3 0.0 copy-start.2
  566.3 105.0 %shard_map.267 = (f32[512,2048]{1,0:T(8,128)}, f32[64,6144]{1,0:T(8,128)}, f32[64,8192]{1,0:T(8,128)}, f32[8,512]{1,0:T(8,128)}) custom-call(bf16[2048,1536]{1,0:T(8,128)(2,1)} %get-tuple-element.77.grads_in, bf16[2048,1536]{1,0:T(8,128)(2,1)} %get-tuple-element.53.weight.weight_in, bf16[2048,2048]{1,0:T(8,128)(2,1)} %get-tuple-element.78.normed_one, ...), custom_call_target="tpu_custom_call" | custom-call | flops 25769803776 | bytes 10485760 | tf_op jit(solution)/shard_map/pallas_call | solution.py:1950
  671.3 1.0 fusion.14
  672.3 0.6 fusion.12
  672.9 2.1 collective-permute-start
  675.0 0.5 fusion.9
  675.5 1.3 slice.30
  676.8 0.6 fusion.10
  677.4 0.6 fusion.7
  677.9 0.0 collective-permute-done
  677.9 0.8 convert_element_type.17
  678.8 0.0 copy-done.2
  678.8 1.3 copy.38
  680.1 2.1 copy.39
  682.2 0.4 copy-done.4
  682.6 1.1 copy.40
  683.8 0.0 copy-done.3
  683.8 1.3 copy.41
  685.1 0.1 copy-done.1
  685.2 1.3 copy.42
  (8 shorter events, 0.0 us)
Async XLA Ops:
  7.2 253.5 %all-gather.2.cloned.1.call-start = ((), (), s32[]{:S(2)}) async-start(), calls=%async_computation.1 | async-start | bytes 9437184 | tf_op jit(solution)/shard_map/all_gather | solution.py:2059
  131.9 541.0 %reduce-scatter.2.cloned.1.call-start = ((), (), s32[]{:S(2)}) async-start(), calls=%async_computation.2 | async-start | bytes 2359296 | tf_op jit(solution)/shard_map/reduce_scatter | solution.py:2063
  566.3 112.5 %copy-start.2 = (bf16[512,2048]{1,0:T(8,128)(2,1)S(1)}, bf16[512,2048]{1,0:T(8,128)(2,1)}, u32[]{:S(2)}) copy-start(bf16[512,2048]{1,0:T(8,128)(2,1)} %get-tuple-element.76) | copy-start | bytes 6291460
  672.9 7.2 %copy-start = (f32[512,2048]{1,0:T(8,128)S(1)}, f32[512,2048]{1,0:T(8,128)}, u32[]{:S(2)}) copy-start(f32[512,2048]{1,0:T(8,128)} %get-tuple-element.84) | copy-start | bytes 12582916
  672.9 5.1 collective-permute-start
  680.1 2.5 copy-start.4
  680.1 3.7 copy-start.3
  682.6 2.6 copy-start.1
Sparse Core Ops, SparseCore 0:
  132.0 98.6 all-gather.1
  566.4 40.4 reduce-scatter.1

commit v11 on v10

--- a/solution.py
+++ b/solution.py
@@ -1866,6 +1866,12 @@
     scatters[0].finish(shares[0])
     for item in (plain_one, plain_two, joined_one, joined_two):
         item.wait_recv()
+    def share_out(part):
+        for item in qkv_copies[part]:
+            item.start()
+        qkv_own[part].start()
+
+    share_out(0)
     for item in fc_copies:
         item.start()
     part = min(128, piece)
@@ -1886,10 +1892,7 @@
     for item in small_copies:
         item.start()
     scatters[1].finish(shares[1])
-    for part in range(2):
-        for item in qkv_copies[part]:
-            item.start()
-        qkv_own[part].start()
+    share_out(1)
     for item in small_copies:
         item.wait_recv()
     mine_total = mine[...] + small_in[0] + small_in[1] + small_in[2]

time: 703 us -> 705 us (level)
  no operation moved by 1% of the time
where the time goes in v11:
time: 705 us; the launch traced here: 695 us
  Pallas kernels  662 us (94%)
  between operations  15.2 us (2%)
  local copies, waits for them, and re-layouts  13 us (2%)
    pallas_call x1, Pallas kernels, feed_plane(): pl.pallas_call(plane_kernel, in_specs=[anywhere] * 10 + [inside], out_spe...  223 us
    pallas_call x1, Pallas kernels, attend_plane(): pl.pallas_call(attend_plane_kernel, in_specs=[anywhere] * 9 + [inside], o...  129 us
    pallas_call x1, Pallas kernels, opening(): pl.pallas_call(opening_kernel, in_specs=[anywhere] * 4 + [inside] + [anyw...  121 us
    pallas_call x1, Pallas kernels, closing(): pl.pallas_call(closing_kernel, in_specs=[anywhere] * 5 + [inside] * 4 + [...  106 us
    pallas_call x1, Pallas kernels, retreat_plane(): pl.pallas_call(retreat_plane_kernel, in_specs=[anywhere] * 12 + [inside],...  82.8 us
  transfers between devices with their start and end apart: 3, of which 0 were waited for; matrix products, arithmetic and copies ran while one was open for 1% of the time, Pallas kernels for 34%

profile of v11, /device:TPU:0, one launch (start us, length us, event | category | flops | bytes accessed | tf_op | source)
XLA Modules:
  0.0 695.0 jit_solution(14682616404184829170)
XLA Ops:
  7.2 0.0 all-gather.2.cloned.1.call-start
  7.9 0.7 compare_reduce_fusion
  8.6 0.8 stack.27
  9.4 1.3 fusion.2.small
  10.7 121.1 %shard_map.263 = (bf16[2048,2048]{1,0:T(8,128)(2,1)}, bf16[2048,1536]{1,0:T(8,128)(2,1)}, bf16[256,2048]{1,0:T(8,128)(2,1)}, bf16[256,2048]{1,0:T(8,128)(2,1)}, ...) custom-call(bf16[512,2048]{1,0:T(8,128)(2,1)} %bitcast.35, ...), custom_call_target="tpu_custom_call" | custom-call | bytes 41943040 | tf_op jit(solution)/shard_map/pallas_call | solution.py:1074
  131.8 0.0 all-gather.2.cloned.1.call-update
  131.9 0.0 reduce-scatter.2.cloned.1.call-start
  131.9 128.7 %shard_map.264 = (f32[512,2048]{1,0:T(8,128)}, bf16[512,2048]{1,0:T(8,128)(2,1)}, bf16[2048,512]{1,0:T(8,128)(2,1)}, f32[4,1,2048]{2,1,0:T(1,128)}, bf16[512,204...) custom-call(bf16[512,2048]{1,0:T(8,128)(2,1)} %bitcast.36, ...), custom_call_target="tpu_custom_call", output_to_operand_aliasing={{5}: (6, {})} | custom-call | flops 10737418240 | bytes 41943040 | tf_op jit(solution)/shard_map/pallas_call | solution.py:1257
  260.6 0.0 all-gather.2.cloned.1.call-done.fc
  260.7 222.7 %shard_map.265 = (f32[512,2048]{1,0:T(8,128)}, bf16[2048,2048]{1,0:T(8,128)(2,1)}, f32[4,2048]{1,0:T(4,128)}, f32[1,2048]{1,0:T(1,128)}, bf16[2048,2048]{1,0:T(8...) custom-call(bf16[512,2048]{1,0:T(8,128)(2,1)} %get-tuple-element.59., ...), custom_call_target="tpu_custom_call" | custom-call | flops 103079215104 | bytes 41943040 | tf_op jit(solution)/shard_map/pallas_call | solution.py:1531
  483.4 82.8 %shard_map.266 = (bf16[2048,1536]{1,0:T(8,128)(2,1)}, f32[2,512]{1,0:T(2,128)}, bf16[512,2048]{1,0:T(8,128)(2,1)}, bf16[512,2048]{1,0:T(8,128)(2,1)}, bf16[256,2048]{1,0:T(8,128)(2,1)}) custom-call(bf16[2048,2048]{1,0:T(8,128)(2,1)} %get-tuple-element.67.low_all, bf16[2048,512]{1,0:T(8,128)(2,1)} %get-tuple-element.68.q, ...), custom_call_target="tpu_custom_call" | custom-call | flops 21474836480 | bytes 41943040 | tf_op jit(solution)/shard_map/pallas_call | solution.py:1715
  566.2 0.0 reduce-scatter.2.cloned.1.call-update
  566.3 0.0 copy-start.2
  566.3 106.3 %shard_map.267 = (f32[512,2048]{1,0:T(8,128)}, f32[64,6144]{1,0:T(8,128)}, f32[64,8192]{1,0:T(8,128)}, f32[8,512]{1,0:T(8,128)}) custom-call(bf16[2048,1536]{1,0:T(8,128)(2,1)} %get-tuple-element.77.grads_in, bf16[2048,1536]{1,0:T(8,128)(2,1)} %get-tuple-element.53.weight.weight_in, bf16[2048,2048]{1,0:T(8,128)(2,1)} %get-tuple-element.78.normed_one, ...), custom_call_target="tpu_custom_call" | custom-call | flops 25769803776 | bytes 10485760 | tf_op jit(solution)/shard_map/pallas_call | solution.py:1953
  672.5 1.0 fusion.14
  673.5 0.6 fusion.12
  674.1 2.1 collective-permute-start
  676.2 0.5 fusion.9
  676.8 1.3 slice.30
  678.0 0.6 fusion.10
  678.6 0.6 fusion.7
  679.2 0.0 collective-permute-done
  679.2 0.8 convert_element_type.17
  680.0 0.0 copy-done.2
  680.0 1.3 copy.38
  681.3 2.1 copy.39
  683.5 0.4 copy-done.4
  683.9 1.1 copy.40
  685.0 0.0 copy-done.3
  685.1 1.3 copy.41
  686.4 0.1 copy-done.1
  686.4 1.3 copy.42
  (8 shorter events, 0.0 us)
Async XLA Ops:
  7.2 253.5 %all-gather.2.cloned.1.call-start = ((), (), s32[]{:S(2)}) async-start(), calls=%async_computation.1 | async-start | bytes 9437184 | tf_op jit(solution)/shard_map/all_gather | solution.py:2062
  131.9 542.3 %reduce-scatter.2.cloned.1.call-start = ((), (), s32[]{:S(2)}) async-start(), calls=%async_computation.2 | async-start | bytes 2359296 | tf_op jit(solution)/shard_map/reduce_scatter | solution.py:2066
  566.3 113.7 %copy-start.2 = (bf16[512,2048]{1,0:T(8,128)(2,1)S(1)}, bf16[512,2048]{1,0:T(8,128)(2,1)}, u32[]{:S(2)}) copy-start(bf16[512,2048]{1,0:T(8,128)(2,1)} %get-tuple-element.76) | copy-start | bytes 6291460
  674.1 7.2 %copy-start = (f32[512,2048]{1,0:T(8,128)S(1)}, f32[512,2048]{1,0:T(8,128)}, u32[]{:S(2)}) copy-start(f32[512,2048]{1,0:T(8,128)} %get-tuple-element.84) | copy-start | bytes 12582916
  674.1 5.1 collective-permute-start
  681.3 2.5 copy-start.4
  681.3 3.7 copy-start.3
  683.9 2.6 copy-start.1
Sparse Core Ops, SparseCore 0:
  132.0 98.6 all-gather.1
  566.4 40.4 reduce-scatter.1
